TPU v7x, 32 devices: a whole 2x2x4 slice. The times are simulated.
32 devices in a mesh: pair: 2 (over y), virt: 16 (over z, x, core).
Axes of the slice: x: 2, y: 2, z: 4, core: 2. Of those that a mesh axis runs over, the one named last changes fastest.
Arguments:
- amplitudes: bfloat16 [2048, 65536], P('pair', 'virt'), may hold values from -6 to 6
- integrals: bfloat16 [65536, 1024], P('virt', 'pair'), may hold values from -0.0234375 to 0.0234375
- occ_pairs: int32 [2048, 2], P(('pair', 'virt')), may hold values from 0 to 95, as said below
- partners: int32 [2048], P(('pair', 'virt')), may hold values from 0 to 2047, as said below
- virt_list: int32 [32], replicated, may hold values from 0 to 511
- eps_occ: float32 [96], replicated, may hold values from -2 to -0.5
- eps_virt: float32 [512], replicated, may hold values from 0.2 to 3
Outputs:
- update: float32 [2048, 1024], P(('pair', 'virt'))
Inputs may be any that keep to these rules, and one draw needn't show every extreme that they name: Row r holds the pair (i, j) with i != j; row partners[r] holds (j, i), partners[partners[r]] = r, and partners[r] lies in the same index of pair and in the index of virt 16 / 2 away under the placement of the output rows. `occ_pairs`: the two orbitals of a row differ.
All inputs are finite; a program needn't handle non-finite values.
Results may differ from a plain program's by a relative error of at most 0.0003.
Values may be sent and summed in bfloat16 or wider, within the bound.
No kernel may reach another device: no remote copies, remote signals or barrier semaphores. Data moves between devices by JAX's collectives and lax.ppermute only.
A program may use at most 192 MiB of HBM per device.

v0:
```python
import jax
import jax.numpy as jnp
from jax import lax
from jax.sharding import PartitionSpec as P


def passed_along(value, axis, steps):
    count = lax.axis_size(axis)
    pairs = [(source, (source + steps) % count) for source in range(count)]
    return lax.ppermute(value, axis, pairs)


def transpose_block(values, width):
    count = values.shape[0]
    return values.reshape(count, width, width).transpose(0, 2, 1).reshape(count, width * width)


def add_transposed(mine, partners, width):
    other = passed_along(mine, "virt", lax.axis_size("virt") // 2)
    local_rows = partners % mine.shape[0]
    flipped = jnp.take(other, local_rows, axis=0)
    return mine + transpose_block(flipped, width)


def columns_product(amplitudes, integrals):
    return jnp.dot(
        amplitudes,
        lax.all_gather(integrals, "pair", axis=1, tiled=True),
        preferred_element_type=jnp.float32,
    )


def per_device(amplitudes, integrals, occ_pairs, partners, virt_list, eps_occ, eps_virt):
    width = virt_list.shape[0]
    partial_value = columns_product(amplitudes, integrals)
    mine = lax.psum_scatter(partial_value, "virt", scatter_dimension=0, tiled=True)
    total = add_transposed(mine, partners, width)
    occ_ids = jnp.arange(eps_occ.shape[0], dtype=jnp.int32)
    occ_match = occ_pairs[:, :, None] == occ_ids[None, None, :]
    occ_sum = jnp.sum(jnp.where(occ_match, eps_occ[None, None, :], 0.0), axis=(1, 2))
    virt_ids = jnp.arange(eps_virt.shape[0], dtype=jnp.int32)
    virt_match = virt_list[:, None] == virt_ids[None, :]
    virt_energy = jnp.sum(jnp.where(virt_match, eps_virt[None, :], 0.0), axis=1)
    virt_sum = (virt_energy[:, None] + virt_energy[None, :]).reshape(-1)
    denominator = virt_sum[None, :] - occ_sum[:, None]
    return total / denominator


def solution(mesh):
    placed = (
        P("pair", "virt"),
        P("virt", "pair"),
        P(("pair", "virt"), None),
        P(("pair", "virt")),
        P(),
        P(),
        P(),
    )
    return jax.shard_map(
        per_device, mesh=mesh, in_specs=placed, out_specs=P(("pair", "virt"), None), check_vma=False
    )
```

profile of v0, /device:TPU:0, one launch (start us, length us, event | category | flops | bytes accessed | tf_op | source)
XLA Modules:
  0.0 226.6 jit_solution(5362928926961314063)
XLA Ops:
  6.5 0.0 all-gather.2.cloned.1.call-start
  6.5 0.7 all-gather.2.cloned.1.call-update
  7.3 0.0 copy-start
  7.3 0.0 copy-start.2
  7.3 0.0 copy-start.4
  7.3 0.0 copy-start.1
  7.3 0.0 copy-start.3
  7.3 0.0 reduce-scatter.2.cloned.1.call-start
  7.4 108.3 %all-gather.2.cloned.1.call-done = bf16[4096,1024]{1,0:T(8,128)(2,1)} async-done(((bf16[4096,512]{1,0:T(8,128)(2,1)}), bf16[4096,1024]{1,0:T(8,128)(2,1)}) %all-gather.2.cloned.1.call-update) | async-done | bytes 8388624 | tf_op jit(solution)/shard_map/all_gather | solution.py:28
  115.6 15.0 %fusion.1 = f32[1024,1024]{1,0:T(8,128)} fusion(bf16[1024,4096]{1,0:T(8,128)(2,1)} %param.7, bf16[4096,1024]{1,0:T(8,128)(2,1)} %all-gather.2.cloned.1.call-done), kind=kOutput, calls=%fused_computation.15 | convolution fusion | flops 8589934592 | bytes 20971520 | tf_op jit(solution)/shard_map/dot_general | solution.py:26
  130.7 0.0 reduce-scatter.2.cloned.1.call-update
  130.7 0.0 copy-done
  130.7 0.0 copy-done.2
  130.7 0.2 select_reduce_fusion.1
  130.9 0.1 broadcast_add_fusion
  131.0 72.5 %reduce-scatter.2.cloned.1.call-done = f32[64,1024]{1,0:T(8,128)} async-done(((f32[1024,1024]{1,0:T(8,128)}), f32[64,1024]{1,0:T(8,128)}) %reduce-scatter.2.cloned.1.call-update) | async-done | bytes 262160 | tf_op jit(solution)/shard_map/reduce_scatter | solution.py:36
  203.5 1.5 collective-permute-start
  205.0 0.0 copy-done.4
  205.0 0.1 add.43
  205.1 0.0 copy-done.1
  205.1 0.0 copy-done.3
  205.1 0.2 select_reduce_fusion
  205.3 11.3 %collective-permute-done = f32[64,1024]{1,0:T(8,128)S(1)} collective-permute-done((f32[64,1024]{1,0:T(8,128)}, f32[64,1024]{1,0:T(8,128)S(1)}, u32[]{:S(2)}, u32[]{:S(2)}) %collective-permute-start) | collective-permute-done | bytes 262176 | tf_op jit(solution)/shard_map/ppermute | solution.py:10
  216.5 0.7 gather_fusion
  217.2 0.2 copy.14
  217.5 0.3 copy.15
  217.8 0.2 copy.16
  218.0 1.8 subtract_divide_fusion
  (3 shorter events, 0.1 us)
Async XLA Ops:
  6.5 109.1 %all-gather.2.cloned.1.call-start = ((), (), s32[]{:S(2)}) async-start(), calls=%async_computation.1 | async-start | bytes 12582912 | tf_op jit(solution)/shard_map/all_gather | solution.py:28
  7.3 123.5 %copy-start = (f32[512]{0:T(512)S(1)}, f32[512]{0:T(512)}, u32[]{:S(2)}) copy-start(f32[512]{0:T(512)} %param.13) | copy-start | bytes 6148
  7.3 123.5 %copy-start.2 = (s32[32]{0:T(128)S(1)}, s32[32]{0:T(128)}, u32[]{:S(2)}) copy-start(s32[32]{0:T(128)} %param.11) | copy-start | bytes 388
  7.3 197.7 %copy-start.4 = (s32[64]{0:T(128)S(1)}, s32[64]{0:T(128)}, u32[]{:S(2)}) copy-start(s32[64]{0:T(128)} %param.10) | copy-start | bytes 772
  7.3 197.8 %copy-start.1 = (s32[64,2]{0,1:T(2,128)S(1)}, s32[64,2]{0,1:T(2,128)}, u32[]{:S(2)}) copy-start(s32[64,2]{0,1:T(2,128)} %param.9) | copy-start | bytes 1540
  7.3 197.8 %copy-start.3 = (f32[96]{0:T(128)S(1)}, f32[96]{0:T(128)}, u32[]{:S(2)}) copy-start(f32[96]{0:T(128)} %param.12) | copy-start | bytes 1156
  7.3 196.2 %reduce-scatter.2.cloned.1.call-start = ((), (), s32[]{:S(2)}) async-start(), calls=%async_computation.2 | async-start | bytes 4456448 | tf_op jit(solution)/shard_map/reduce_scatter | solution.py:36
  203.5 13.0 %collective-permute-start = (f32[64,1024]{1,0:T(8,128)}, f32[64,1024]{1,0:T(8,128)S(1)}, u32[]{:S(2)}, u32[]{:S(2)}) collective-permute-start(f32[64,1024]{1,0:T(8,128)} %reduce-scatter.2.cloned.1.call-done), channel_id=1, source_target_pairs={{0,8},{1,9},{2,10},{3,11},{4,12},{5,13},{6,14},{7,15},{8,0},{9,1},... | collective-permute-start | bytes 786440 | tf_op jit(solution)/shard_map/ppermute | solution.py:10
Sparse Core Ops, SparseCore 0:
  8.9 106.6 all-gather.1
  130.8 72.5 reduce-scatter.1
where the time goes:
time: 227 us
  waiting for transfers between devices  193 us (85%)
  matrix products  15 us (7%)
  between operations  13.5 us (6%)
    all_gather x1, waiting for transfers between devices, columns_product(): lax.all_gather(integrals, 'pair', axis=1, tiled=True)  108 us
    reduce_scatter x1, waiting for transfers between devices, per_device(): lax.psum_scatter(partial_value, 'virt', scatter_dimension=0, tiled=True)  72.5 us
    dot_general x1, matrix products, columns_product(): jnp.dot(amplitudes, lax.all_gather(integrals, 'pair', axis=1, tiled=True)...  15 us
    ppermute x1, waiting for transfers between devices, passed_along(): return lax.ppermute(value, axis, pairs)  11.3 us
  transfers between devices with their start and end apart: 3, of which 3 were waited for; matrix products, arithmetic and copies ran while one was open for 0% of the time, Pallas kernels for 0%

commit v1 on v0

--- a/solution.py
+++ b/solution.py
@@ -15,26 +15,62 @@
     return values.reshape(count, width, width).transpose(0, 2, 1).reshape(count, width * width)
 
 
-def add_transposed(mine, partners, width):
-    other = passed_along(mine, "virt", lax.axis_size("virt") // 2)
-    local_rows = partners % mine.shape[0]
-    flipped = jnp.take(other, local_rows, axis=0)
-    return mine + transpose_block(flipped, width)
+def column_cuts(columns):
+    half, quarter = columns // 2, columns // 4
+    return [(0, half), (half, half + quarter), (half + quarter, columns)]
 
 
-def columns_product(amplitudes, integrals):
-    return jnp.dot(
-        amplitudes,
-        lax.all_gather(integrals, "pair", axis=1, tiled=True),
-        preferred_element_type=jnp.float32,
-    )
+def in_column_order(blocks, count):
+    own = lax.axis_index("pair")
+    ordered = []
+    for place in range(count):
+        block = blocks[place]
+        for index in range(1, count):
+            block = jnp.where(own == index, blocks[(place - index) % count], block)
+        ordered.append(block)
+    return jnp.concatenate(ordered, axis=1)
 
 
 def per_device(amplitudes, integrals, occ_pairs, partners, virt_list, eps_occ, eps_virt):
     width = virt_list.shape[0]
-    partial_value = columns_product(amplitudes, integrals)
-    mine = lax.psum_scatter(partial_value, "virt", scatter_dimension=0, tiled=True)
-    total = add_transposed(mine, partners, width)
+    count = lax.axis_size("pair")
+    half = lax.axis_size("virt") // 2
+    cuts = column_cuts(integrals.shape[1])
+    def multiplied(columns):
+        return jnp.dot(amplitudes, columns, preferred_element_type=jnp.float32)
+
+    def sent(low, high):
+        return [passed_along(integrals[:, low:high], "pair", -shift) for shift in range(1, count)]
+
+    def after(value, earlier):
+        return lax.optimization_barrier((value, earlier))[0]
+
+    def summed(partial_value):
+        mine = lax.psum_scatter(partial_value, "virt", scatter_dimension=0, tiled=True)
+        return mine, passed_along(mine, "virt", half)
+
+    in_flight = [sent(*cuts[0])]
+    own_product = multiplied(integrals)
+    sums = [[summed(own_product)]] + [[] for _ in range(1, count)]
+    integrals = after(integrals, own_product)
+    in_flight.append(sent(*cuts[1]))
+    last_product = own_product
+    for step in range(len(cuts)):
+        arrived = after(in_flight[step], last_product)
+        products = [multiplied(piece) for piece in arrived]
+        for shift in range(1, count):
+            sums[shift].append(summed(products[shift - 1]))
+        last_product = products
+        if step + 2 < len(cuts):
+            integrals = after(integrals, products)
+            in_flight.append(sent(*cuts[step + 2]))
+
+    mine = in_column_order([jnp.concatenate([m for m, _ in parts], axis=1) for parts in sums], count)
+    other = in_column_order([jnp.concatenate([o for _, o in parts], axis=1) for parts in sums], count)
+
+    flipped = jnp.take(other, partners % mine.shape[0], axis=0)
+    total = mine + transpose_block(flipped, width)
+
     occ_ids = jnp.arange(eps_occ.shape[0], dtype=jnp.int32)
     occ_match = occ_pairs[:, :, None] == occ_ids[None, None, :]
     occ_sum = jnp.sum(jnp.where(occ_match, eps_occ[None, None, :], 0.0), axis=(1, 2))

time: 227 us -> 341 us (1.50)
  waiting for transfers between devices: 193 us -> 275 us
  matrix products: 15 us -> 31 us
  starting transfers between devices: 1.54 us -> 10.8 us
  local copies, waits for them, and re-layouts: 1.45 us -> 8.22 us
    reduce_scatter x1 -> x4, waiting for transfers between devices: 72.5 us -> 199 us  [summed(): lax.psum_scatter(partial_value, 'virt', scatter_dimension=0, tiled=True)]
    all_gather x1 -> x0, waiting for transfers between devices: 108 us -> none  [columns_product(): lax.all_gather(integrals, 'pair', axis=1, tiled=True)]
    ppermute x1 -> x7, waiting for transfers between devices: 11.3 us -> 75.6 us  [passed_along(): return lax.ppermute(value, axis, pairs)]
    dot_general x1 -> x4, matrix products: 15 us -> 31 us  [multiplied(): return jnp.dot(amplitudes, columns, preferred_element_type=jnp.float32)]
    ppermute x1 -> x7, starting transfers between devices: 1.5 us -> 10.6 us  [passed_along(): return lax.ppermute(value, axis, pairs)]
    slice x0 -> x3, local copies, waits for them, and re-layouts: none -> 4.31 us  [sent(): integrals[:, low:high]]
  transfers between devices with their start and end apart: 3 -> 11, of which waited for: 3 -> 9; matrix products, arithmetic and copies ran while one was open for 0% -> 9% of each run, Pallas kernels for 0% -> 0%
where the time goes in v1:
time: 341 us
  waiting for transfers between devices  275 us (81%)
  matrix products  31 us (9%)
  between operations  13.3 us (4%)
  starting transfers between devices  10.8 us (3%)
  local copies, waits for them, and re-layouts  8.22 us (2%)
    reduce_scatter x4, waiting for transfers between devices, summed(): lax.psum_scatter(partial_value, 'virt', scatter_dimension=0, tiled=True)  199 us
    ppermute x7, waiting for transfers between devices, passed_along(): return lax.ppermute(value, axis, pairs)  75.6 us
    dot_general x4, matrix products, multiplied(): return jnp.dot(amplitudes, columns, preferred_element_type=jnp.float32)  31 us
    ppermute x7, starting transfers between devices, passed_along(): return lax.ppermute(value, axis, pairs)  10.6 us
  transfers between devices with their start and end apart: 11, of which 9 were waited for; matrix products, arithmetic and copies ran while one was open for 9% of the time, Pallas kernels for 0%

profile of v1, /device:TPU:0, one launch (start us, length us, event | category | flops | bytes accessed | tf_op | source)
XLA Modules:
  0.0 341.0 jit_solution(6690338497998888570)
XLA Ops:
  6.5 1.7 slice.9
  8.3 3.0 collective-permute-start
  11.3 10.4 %fusion.2 = f32[1024,512]{1,0:T(8,128)} fusion(bf16[1024,4096]{1,0:T(8,128)(2,1)} %param.7, bf16[4096,512]{1,0:T(8,128)(2,1)} %param.8), kind=kOutput, calls=%fused_computation.30 | convolution fusion | flops 4294967296 | bytes 14680064 | tf_op jit(solution)/shard_map/dot_general | solution.py:40
  21.7 1.3 slice.10
  23.0 0.1 collective-permute-start.1
  23.1 34.8 %collective-permute-done = bf16[4096,256]{1,0:T(8,128)(2,1)} collective-permute-done((bf16[4096,256]{1,0:T(8,128)(2,1)S(1)}, bf16[4096,256]{1,0:T(8,128)(2,1)}, u32[]{:S(2)}, u32[]{:S(2)}) %collective-permute-start) | collective-permute-done | bytes 2097184 | tf_op jit(solution)/shard_map/ppermute | solution.py:10
  57.9 7.3 %convolution_bitcast_fusion = f32[1024,256]{1,0:T(8,128)} fusion(bf16[1024,4096]{1,0:T(8,128)(2,1)} %param.7, bf16[4096,256]{1,0:T(8,128)(2,1)} %collective-permute-done), kind=kOutput, calls=%fused_computation.1 | convolution fusion | flops 2147483648 | bytes 11534336 | tf_op jit(solution)/shard_map/dot_general | solution.py:40
  65.1 14.4 %collective-permute-done.1 = bf16[4096,128]{1,0:T(8,128)(2,1)} collective-permute-done((bf16[4096,128]{1,0:T(8,128)(2,1)S(1)}, bf16[4096,128]{1,0:T(8,128)(2,1)}, u32[]{:S(2)}, u32[]{:S(2)}) %collective-permute-start.1) | collective-permute-done | bytes 1048608 | tf_op jit(solution)/shard_map/ppermute | solution.py:10
  79.5 6.7 %convolution_bitcast_fusion.2 = f32[1024,128]{1,0:T(8,128)} fusion(bf16[1024,4096]{1,0:T(8,128)(2,1)} %param.7, bf16[4096,128]{1,0:T(8,128)(2,1)} %collective-permute-done.1), kind=kOutput, calls=%fused_computation.3 | convolution fusion | flops 1073741824 | bytes 9961472 | tf_op jit(solution)/shard_map/dot_general | solution.py:40
  86.3 0.0 reduce-scatter.7.cloned.1.call-update
  86.3 0.0 copy-start.4
  86.3 0.0 copy-start.1
  86.3 0.0 copy-start.3
  86.3 0.0 reduce-scatter.11.cloned.1.call-start
  86.4 0.7 reduce-scatter.11.cloned.1.call-update
  87.1 0.0 reduce-scatter.5.cloned.1.call-start
  87.1 1.3 slice.11
  88.4 1.8 collective-permute-start.2
  90.2 0.0 reduce-scatter.5.cloned.1.call-update
  90.2 0.0 reduce-scatter.9.cloned.1.call-start
  90.3 0.2 select_reduce_fusion.1
  90.5 0.1 broadcast_add_fusion
  90.6 22.3 %collective-permute-done.2 = bf16[4096,128]{1,0:T(8,128)(2,1)S(1)} collective-permute-done((bf16[4096,128]{1,0:T(8,128)(2,1)S(1)}, bf16[4096,128]{1,0:T(8,128)(2,1)S(1)}, u32[]{:S(2)}, u32[]{:S(2)}) %collective-permute-start.2) | collective-permute-done | bytes 1048608 | tf_op jit(solution)/shard_map/ppermute | solution.py:10
  112.8 6.6 %convolution_bitcast_fusion.1 = f32[1024,128]{1,0:T(8,128)} fusion(bf16[1024,4096]{1,0:T(8,128)(2,1)} %param.7, bf16[4096,128]{1,0:T(8,128)(2,1)S(1)} %collective-permute-done.2), kind=kOutput, calls=%fused_computation.2 | convolution fusion | flops 1073741824 | bytes 9961472 | tf_op jit(solution)/shard_map/dot_general | solution.py:40
  119.4 0.0 reduce-scatter.9.cloned.1.call-update
  119.5 0.1 add.49
  119.6 0.2 select_reduce_fusion
  119.7 23.9 %reduce-scatter.7.cloned.1.call-done = f32[64,128]{1,0:T(8,128)} async-done(((f32[1024,128]{1,0:T(8,128)}), f32[64,128]{1,0:T(8,128)}) %reduce-scatter.7.cloned.1.call-update) | async-done | bytes 32784 | tf_op jit(solution)/shard_map/reduce_scatter | solution.py:49
  143.7 1.4 collective-permute-start.4
  145.1 63.4 %reduce-scatter.11.cloned.1.call-done = f32[64,512]{1,0:T(8,128)} async-done(((f32[1024,512]{1,0:T(8,128)}), f32[64,512]{1,0:T(8,128)}) %reduce-scatter.11.cloned.1.call-update) | async-done | bytes 131088 | tf_op jit(solution)/shard_map/reduce_scatter | solution.py:49
  208.5 1.4 collective-permute-start.6
  209.9 58.6 %reduce-scatter.5.cloned.1.call-done = f32[64,256]{1,0:T(8,128)} async-done(((f32[1024,256]{1,0:T(8,128)}), f32[64,256]{1,0:T(8,128)}) %reduce-scatter.5.cloned.1.call-update) | async-done | bytes 65552 | tf_op jit(solution)/shard_map/reduce_scatter | solution.py:49
  268.6 1.4 collective-permute-start.3
  270.0 0.9 constant_dynamic-update-slice_fusion.2
  270.8 0.8 constant_dynamic-update-slice_fusion.1
  271.6 2.3 collective-permute-done.3
  273.9 0.0 collective-permute-done.4
  274.0 53.2 %reduce-scatter.9.cloned.1.call-done = f32[64,128]{1,0:T(8,128)} async-done(((f32[1024,128]{1,0:T(8,128)}), f32[64,128]{1,0:T(8,128)}) %reduce-scatter.9.cloned.1.call-update) | async-done | bytes 32784 | tf_op jit(solution)/shard_map/reduce_scatter | solution.py:49
  327.2 1.5 collective-permute-start.5
  328.6 0.8 constant_dynamic-update-slice_fusion
  329.4 0.9 broadcast_select_fusion.3
  330.3 1.8 collective-permute-done.5
  332.2 0.0 collective-permute-done.6
  332.2 0.7 gather_fusion
  332.9 0.2 copy.23
  333.2 0.3 copy.24
  333.5 0.2 copy.25
  333.7 0.8 fusion
  (16 shorter events, 0.1 us)
Async XLA Ops:
  6.5 137.1 %reduce-scatter.7.cloned.1.call-start = ((), (), s32[]{:S(2)}) async-start(), calls=%async_computation.5 | async-start | bytes 557056 | tf_op jit(solution)/shard_map/reduce_scatter | solution.py:49
  8.3 49.6 %collective-permute-start = (bf16[4096,256]{1,0:T(8,128)(2,1)S(1)}, bf16[4096,256]{1,0:T(8,128)(2,1)}, u32[]{:S(2)}, u32[]{:S(2)}) collective-permute-start(bf16[4096,256]{1,0:T(8,128)(2,1)S(1)} %slice.9), channel_id=1, source_target_pairs={{0,16},{16,0},{1,17},{17,1},{2,18},{18,2},{3,19},{19,3},{4,20},{20... | collective-permute-start | bytes 6291464 | tf_op jit(solution)/shard_map/ppermute | solution.py:10
  23.0 56.5 %collective-permute-start.1 = (bf16[4096,128]{1,0:T(8,128)(2,1)S(1)}, bf16[4096,128]{1,0:T(8,128)(2,1)}, u32[]{:S(2)}, u32[]{:S(2)}) collective-permute-start(bf16[4096,128]{1,0:T(8,128)(2,1)S(1)} %slice.10), channel_id=1, source_target_pairs={{0,16},{16,0},{1,17},{17,1},{2,18},{18,2},{3,19},{19,3},{4,20},{20... | collective-permute-start | bytes 3145736 | tf_op jit(solution)/shard_map/ppermute | solution.py:10
  65.1 25.2 %copy-start = (f32[512]{0:T(512)S(1)}, f32[512]{0:T(512)}, u32[]{:S(2)}) copy-start(f32[512]{0:T(512)} %param.13) | copy-start | bytes 6148
  65.1 25.2 %copy-start.2 = (s32[32]{0:T(128)S(1)}, s32[32]{0:T(128)}, u32[]{:S(2)}) copy-start(s32[32]{0:T(128)} %param.11) | copy-start | bytes 388
  86.3 33.2 %copy-start.4 = (s32[64]{0:T(128)S(1)}, s32[64]{0:T(128)}, u32[]{:S(2)}) copy-start(s32[64]{0:T(128)} %param.10) | copy-start | bytes 772
  86.3 33.3 %copy-start.1 = (s32[64,2]{0,1:T(2,128)S(1)}, s32[64,2]{0,1:T(2,128)}, u32[]{:S(2)}) copy-start(s32[64,2]{0,1:T(2,128)} %param.9) | copy-start | bytes 1540
  86.3 33.3 %copy-start.3 = (f32[96]{0:T(128)S(1)}, f32[96]{0:T(128)}, u32[]{:S(2)}) copy-start(f32[96]{0:T(128)} %param.12) | copy-start | bytes 1156
  86.3 122.2 %reduce-scatter.11.cloned.1.call-start = ((), (), s32[]{:S(2)}) async-start(), calls=%async_computation.7 | async-start | bytes 2228224 | tf_op jit(solution)/shard_map/reduce_scatter | solution.py:49
  87.1 181.5 %reduce-scatter.5.cloned.1.call-start = ((), (), s32[]{:S(2)}) async-start(), calls=%async_computation.4 | async-start | bytes 1114112 | tf_op jit(solution)/shard_map/reduce_scatter | solution.py:49
  88.4 24.4 %collective-permute-start.2 = (bf16[4096,128]{1,0:T(8,128)(2,1)S(1)}, bf16[4096,128]{1,0:T(8,128)(2,1)S(1)}, u32[]{:S(2)}, u32[]{:S(2)}) collective-permute-start(bf16[4096,128]{1,0:T(8,128)(2,1)S(1)} %slice.11), channel_id=1, source_target_pairs={{0,16},{16,0},{1,17},{17,1},{2,18},{18,2},{3,19},{19,3},{4,20},{20... | collective-permute-start | bytes 3145736 | tf_op jit(solution)/shard_map/ppermute | solution.py:10
  90.2 236.9 %reduce-scatter.9.cloned.1.call-start = ((), (), s32[]{:S(2)}) async-start(), calls=%async_computation.6 | async-start | bytes 557056 | tf_op jit(solution)/shard_map/reduce_scatter | solution.py:49
  143.7 130.3 %collective-permute-start.4 = (f32[64,128]{1,0:T(8,128)}, f32[64,128]{1,0:T(8,128)S(1)}, u32[]{:S(2)}, u32[]{:S(2)}) collective-permute-start(f32[64,128]{1,0:T(8,128)} %reduce-scatter.7.cloned.1.call-done), channel_id=1, source_target_pairs={{0,8},{1,9},{2,10},{3,11},{4,12},{5,13},{6,14},{7,15},{8,0},{9,1},... | collective-permute-start | bytes 98312 | tf_op jit(solution)/shard_map/ppermute | solution.py:10
  208.5 123.7 %collective-permute-start.6 = (f32[64,512]{1,0:T(8,128)}, f32[64,512]{1,0:T(8,128)S(1)}, u32[]{:S(2)}, u32[]{:S(2)}) collective-permute-start(f32[64,512]{1,0:T(8,128)} %reduce-scatter.11.cloned.1.call-done), channel_id=1, source_target_pairs={{0,8},{1,9},{2,10},{3,11},{4,12},{5,13},{6,14},{7,15},{8,0},{9,1},... | collective-permute-start | bytes 393224 | tf_op jit(solution)/shard_map/ppermute | solution.py:10
  268.6 5.4 %collective-permute-start.3 = (f32[64,256]{1,0:T(8,128)}, f32[64,256]{1,0:T(8,128)S(1)}, u32[]{:S(2)}, u32[]{:S(2)}) collective-permute-start(f32[64,256]{1,0:T(8,128)} %reduce-scatter.5.cloned.1.call-done), channel_id=1, source_target_pairs={{0,8},{1,9},{2,10},{3,11},{4,12},{5,13},{6,14},{7,15},{8,0},{9,1},... | collective-permute-start | bytes 196616 | tf_op jit(solution)/shard_map/ppermute | solution.py:10
  327.2 5.0 %collective-permute-start.5 = (f32[64,128]{1,0:T(8,128)}, f32[64,128]{1,0:T(8,128)S(1)}, u32[]{:S(2)}, u32[]{:S(2)}) collective-permute-start(f32[64,128]{1,0:T(8,128)} %reduce-scatter.9.cloned.1.call-done), channel_id=1, source_target_pairs={{0,8},{1,9},{2,10},{3,11},{4,12},{5,13},{6,14},{7,15},{8,0},{9,1},... | collective-permute-start | bytes 98312 | tf_op jit(solution)/shard_map/ppermute | solution.py:10
Sparse Core Ops, SparseCore 0:
  86.4 57.2 reduce-scatter.6
  147.9 60.6 reduce-scatter.10
  212.1 56.3 reduce-scatter.4
  272.4 54.7 reduce-scatter.8

commit v2 on v0

--- a/solution.py
+++ b/solution.py
@@ -1,7 +1,14 @@
+import functools
+
 import jax
 import jax.numpy as jnp
 from jax import lax
+from jax.experimental import pallas as pl
+from jax.experimental.pallas import tpu as pltpu
 from jax.sharding import PartitionSpec as P
+
+PRODUCT_BYTES = 51 * 1024 * 1024
+SUM_BYTES = 8 * 1024 * 1024
 
 
 def passed_along(value, axis, steps):
@@ -15,26 +22,145 @@
     return values.reshape(count, width, width).transpose(0, 2, 1).reshape(count, width * width)
 
 
-def add_transposed(mine, partners, width):
-    other = passed_along(mine, "virt", lax.axis_size("virt") // 2)
-    local_rows = partners % mine.shape[0]
-    flipped = jnp.take(other, local_rows, axis=0)
-    return mine + transpose_block(flipped, width)
+def column_cuts(columns):
+    part = columns // 4
+    return [(low, low + part) for low in range(0, columns, part)]
 
 
-def columns_product(amplitudes, integrals):
-    return jnp.dot(
-        amplitudes,
-        lax.all_gather(integrals, "pair", axis=1, tiled=True),
-        preferred_element_type=jnp.float32,
-    )
+def after(value, earlier):
+    return lax.optimization_barrier((value, earlier))[0]
+
+
+def in_column_order(blocks, count):
+    own = lax.axis_index("pair")
+    ordered = []
+    for place in range(count):
+        block = blocks[place]
+        for index in range(1, count):
+            block = jnp.where(own == index, blocks[(place - index) % count], block)
+        ordered.append(block)
+    return jnp.concatenate(ordered, axis=1)
+
+
+def product_kernel(steps, order, bit_ref, a_ref, b_ref, keep_ref, send_ref, total_ref):
+    step = pl.program_id(0)
+    term = jnp.dot(a_ref[...], b_ref[...], preferred_element_type=jnp.float32)
+
+    @pl.when(step == 0)
+    def _():
+        total_ref[...] = term
+
+    @pl.when(step > 0)
+    def _():
+        total_ref[...] += term
+
+    @pl.when(step == steps - 1)
+    def _():
+        rows = keep_ref.shape[0] // len(order)
+        for out_ref, bit in ((keep_ref, bit_ref[0]), (send_ref, 1 - bit_ref[0])):
+            for place, block in enumerate(order):
+                start = pl.multiple_of((block + bit) * rows, rows)
+                out_ref[place * rows : (place + 1) * rows, :] = total_ref[pl.ds(start, rows), :]
+
+
+def multiplied(amplitudes, columns, bit, order):
+    rows, depth = amplitudes.shape
+    width = columns.shape[1]
+    steps = 4
+    part = depth // steps
+    shape = jax.ShapeDtypeStruct((rows // 2, width), jnp.float32)
+    return pl.pallas_call(
+        functools.partial(product_kernel, steps, order),
+        grid=(steps,),
+        out_shape=[shape] * 2,
+        in_specs=[
+            pl.BlockSpec(memory_space=pltpu.SMEM),
+            pl.BlockSpec((rows, part), lambda k: (0, k)),
+            pl.BlockSpec((part, width), lambda k: (k, 0)),
+        ],
+        out_specs=[pl.BlockSpec(shape.shape, lambda k: (0, 0))] * 2,
+        scratch_shapes=[pltpu.VMEM((rows, width), jnp.float32)],
+        compiler_params=pltpu.CompilerParams(vmem_limit_bytes=PRODUCT_BYTES),
+        cost_estimate=pl.CostEstimate(flops=0, bytes_accessed=0, transcendentals=0),
+    )(bit, amplitudes, columns)
+
+
+def halve_kernel(bit_ref, mine_ref, came_ref, keep_ref, send_ref):
+    rows = keep_ref.shape[0]
+    for out_ref, bit in ((keep_ref, bit_ref[0]), (send_ref, 1 - bit_ref[0])):
+        part = pl.ds(pl.multiple_of(bit * rows, rows), rows)
+        out_ref[...] = mine_ref[part, :] + came_ref[part, :]
+
+
+def halved(mine, came, bit):
+    rows, width = mine.shape
+    shape = jax.ShapeDtypeStruct((rows // 2, width), jnp.float32)
+    return pl.pallas_call(
+        halve_kernel,
+        out_shape=[shape] * 2,
+        in_specs=[pl.BlockSpec(memory_space=pltpu.SMEM)] + [pl.BlockSpec(memory_space=pltpu.VMEM)] * 2,
+        out_specs=[pl.BlockSpec(memory_space=pltpu.VMEM)] * 2,
+        compiler_params=pltpu.CompilerParams(vmem_limit_bytes=SUM_BYTES),
+        cost_estimate=pl.CostEstimate(flops=0, bytes_accessed=0, transcendentals=0),
+    )(bit, mine, came)
+
+
+def flipped_along(value, axis, bits):
+    count = lax.axis_size(axis)
+    return lax.ppermute(value, axis, [(source, source ^ bits) for source in range(count)])
+
+
+def exchanged_sum(parts, bits):
+    stages = []
+    for level in range(1, len(bits)):
+        keep, send = parts
+        came = flipped_along(send, "virt", 1 << (level - 1))
+        parts = halved(keep, came, bits[level]) if level < len(bits) - 1 else [keep + came]
+        stages.append(parts[0])
+    total = parts[0]
+    return total + flipped_along(total, "virt", 1 << (len(bits) - 1)), stages
 
 
 def per_device(amplitudes, integrals, occ_pairs, partners, virt_list, eps_occ, eps_virt):
     width = virt_list.shape[0]
-    partial_value = columns_product(amplitudes, integrals)
-    mine = lax.psum_scatter(partial_value, "virt", scatter_dimension=0, tiled=True)
-    total = add_transposed(mine, partners, width)
+    count = lax.axis_size("pair")
+    size = lax.axis_size("virt")
+    rows = amplitudes.shape[0] // size
+    cuts = column_cuts(integrals.shape[1])
+    me = lax.axis_index("virt").astype(jnp.int32)
+    levels = size.bit_length() - 1
+    bits = [((me >> level) & 1).reshape(1) for level in range(levels)]
+    order = [sum(((place >> (levels - 1 - level)) & 1) << level for level in range(1, levels)) for place in range(size // 2)]
+    upper = me >= size // 2
+
+    def sent(piece):
+        return [passed_along(piece, "pair", -shift) for shift in range(1, count)]
+
+    first = integrals[:, cuts[0][0] : cuts[0][1]]
+    rest = after(integrals, first)
+    pieces = [first] + [rest[:, low:high] for low, high in cuts[1:]]
+    in_flight = [sent(pieces[0]), sent(pieces[1])]
+    own_product = multiplied(amplitudes, after(rest, pieces), bits[0], order)
+    own_sum, own_stages = exchanged_sum(own_product, bits)
+    sums = [[own_sum]] + [[] for _ in range(1, count)]
+    earlier = own_product
+    for step in range(len(cuts)):
+        if step > 0:
+            earlier = (earlier, (own_stages + [own_sum])[min(step - 1 if step < 3 else len(own_stages), len(own_stages))])
+        arrived, earlier = lax.optimization_barrier((in_flight[step], earlier))
+        if step + 2 < len(cuts):
+            in_flight.append(sent(after(pieces[step + 2], arrived)))
+        for shift in range(1, count):
+            product = multiplied(amplitudes, arrived[shift - 1], bits[0], order)
+            earlier, stages = exchanged_sum(product, bits)
+            sums[shift].append(earlier)
+
+    both = in_column_order([jnp.concatenate(parts, axis=1) for parts in sums], count)
+    mine = jnp.where(upper, both[rows:], both[:rows])
+    other = jnp.where(upper, both[:rows], both[rows:])
+    flipped = jnp.take(other, partners % mine.shape[0], axis=0)
+    total = mine + transpose_block(flipped, width)
+
     occ_ids = jnp.arange(eps_occ.shape[0], dtype=jnp.int32)
     occ_match = occ_pairs[:, :, None] == occ_ids[None, None, :]
     occ_sum = jnp.sum(jnp.where(occ_match, eps_occ[None, None, :], 0.0), axis=(1, 2))

time: 227 us -> 146 us (0.64)
  waiting for transfers between devices: 193 us -> 64.3 us
  Pallas kernels: 0 us -> 35.9 us
  starting transfers between devices: 1.54 us -> 36 us
  matrix products: 15 us -> 0 us
  between operations: 13.5 us -> 0.28 us
  local copies, waits for them, and re-layouts: 1.45 us -> 7.37 us
    all_gather x1 -> x0, waiting for transfers between devices: 108 us -> none  [columns_product(): lax.all_gather(integrals, 'pair', axis=1, tiled=True)]
    reduce_scatter x1 -> x0, waiting for transfers between devices: 72.5 us -> none  [per_device(): lax.psum_scatter(partial_value, 'virt', scatter_dimension=0, tiled=True)]
    ppermute x0 -> x20, waiting for transfers between devices: none -> 52.9 us  [flipped_along(): lax.ppermute(value, axis, [(source, source ^ bits) for source in range(co...]
    pallas_call x0 -> x15, Pallas kernels: none -> 35.9 us  [the longest x5 32.7 us: multiplied(): pl.pallas_call(functools.partial(product_kernel, steps, order), grid=(ste...]
    ppermute x0 -> x20, starting transfers between devices: none -> 29.4 us  [flipped_along(): lax.ppermute(value, axis, [(source, source ^ bits) for source in range(co...]
    dot_general x1 -> x0, matrix products: 15 us -> none  [columns_product(): jnp.dot(amplitudes, lax.all_gather(integrals, 'pair', axis=1, tiled=True)...]
    slice x0 -> x2, local copies, waits for them, and re-layouts: none -> 5.9 us  [the longest x1 3.61 us: per_device(): pieces = [first] + [rest[:, low:high] for low, high in cuts[1:]]]
    ppermute x1 -> x4, starting transfers between devices: 1.5 us -> 6.55 us  [passed_along(): return lax.ppermute(value, axis, pairs)]
  transfers between devices with their start and end apart: 3 -> 24, of which waited for: 3 -> 15; matrix products, arithmetic and copies ran while one was open for 0% -> 3% of each run, Pallas kernels for 0% -> 21%
where the time goes in v2:
time: 146 us; the launch traced here: 145 us
  waiting for transfers between devices  64.3 us (44%)
  starting transfers between devices  36 us (25%)
  Pallas kernels  35.9 us (25%)
  local copies, waits for them, and re-layouts  7.37 us (5%)
  other arithmetic  1.55 us (1%)
    ppermute x20, waiting for transfers between devices, flipped_along(): lax.ppermute(value, axis, [(source, source ^ bits) for source in range(co...  52.9 us
    pallas_call x5, Pallas kernels, multiplied(): pl.pallas_call(functools.partial(product_kernel, steps, order), grid=(ste...  32.7 us
    ppermute x20, starting transfers between devices, flipped_along(): lax.ppermute(value, axis, [(source, source ^ bits) for source in range(co...  29.4 us
    ppermute x4, waiting for transfers between devices, passed_along(): return lax.ppermute(value, axis, pairs)  11.4 us
    ppermute x4, starting transfers between devices, passed_along(): return lax.ppermute(value, axis, pairs)  6.55 us
    slice x1, local copies, waits for them, and re-layouts, per_device(): pieces = [first] + [rest[:, low:high] for low, high in cuts[1:]]  3.61 us
    pallas_call x10, Pallas kernels, halved(): pl.pallas_call(halve_kernel, out_shape=[shape] * 2, in_specs=[pl.BlockSpe...  3.19 us
  transfers between devices with their start and end apart: 24, of which 15 were waited for; matrix products, arithmetic and copies ran while one was open for 3% of the time, Pallas kernels for 21%

profile of v2, /device:TPU:0, one launch (start us, length us, event | category | flops | bytes accessed | tf_op | source)
XLA Modules:
  0.0 145.3 jit_solution(5317023148882822359)
XLA Ops:
  0.0 2.3 %slice.20 = bf16[4096,128]{1,0:T(8,128)(2,1)} slice(bf16[4096,512]{1,0:T(8,128)(2,1)} %b_ref), slice={[0:4096], [0:128]} | slice | bytes 2097152 | tf_op jit(solution)/shard_map/slice | solution.py:139
  2.3 3.0 %collective-permute-start = (bf16[4096,128]{1,0:T(8,128)(2,1)}, bf16[4096,128]{1,0:T(8,128)(2,1)S(1)}, u32[]{:S(2)}, u32[]{:S(2)}) collective-permute-start(bf16[4096,128]{1,0:T(8,128)(2,1)} %slice.20), channel_id=1, source_target_pairs={{0,16},{16,0},{1,17},{17,1},{2,18},{18,2},{3,19},{19,3},{4,20},{20... | collective-permute-start | bytes 3145736 | tf_op jit(solution)/shard_map/ppermute | solution.py:17
  5.3 3.6 %fusion.4 = (bf16[4096,128]{1,0:T(8,128)(2,1)}, bf16[4096,128]{1,0:T(8,128)(2,1)}, bf16[4096,128]{1,0:T(8,128)(2,1)}) fusion(bf16[4096,512]{1,0:T(8,128)(2,1)} %b_ref), kind=kLoop, calls=%fused_computation.23 | loop fusion | bytes 6291456 | tf_op jit(solution)/shard_map/slice | solution.py:141
  8.9 9.2 %shard_map.73 = (f32[512,512]{1,0:T(8,128)S(1)}, f32[512,512]{1,0:T(8,128)}) custom-call(s32[1]{0:T(128)} %bitcast.2.bit_ref, bf16[1024,4096]{1,0:T(8,128)(2,1)} %a_ref.9, bf16[4096,512]{1,0:T(8,128)(2,1)} %b_ref), custom_call_target="tpu_custom_call" | custom-call | tf_op jit(solution)/shard_map/pallas_call | solution.py:72
  18.1 11.3 %collective-permute-done.b_ref = bf16[4096,128]{1,0:T(8,128)(2,1)S(1)} collective-permute-done((bf16[4096,128]{1,0:T(8,128)(2,1)}, bf16[4096,128]{1,0:T(8,128)(2,1)S(1)}, u32[]{:S(2)}, u32[]{:S(2)}) %collective-permute-start) | collective-permute-done | bytes 1048608 | tf_op jit(solution)/shard_map/ppermute | solution.py:17
  29.4 6.4 %shard_map.74 = (f32[512,128]{1,0:T(8,128)S(1)}, f32[512,128]{1,0:T(8,128)}) custom-call(s32[1]{0:T(128)} %bitcast.2.bit_ref, bf16[1024,4096]{1,0:T(8,128)(2,1)} %a_ref.9, bf16[4096,128]{1,0:T(8,128)(2,1)S(1)} %collective-permute-done.b_ref), custom_call_target="tpu_custom_call" | custom-call | tf_op jit(solution)/shard_map/pallas_call | solution.py:72
  35.8 2.1 %collective-permute-start.11 = (bf16[4096,128]{1,0:T(8,128)(2,1)}, bf16[4096,128]{1,0:T(8,128)(2,1)S(1)}, u32[]{:S(2)}, u32[]{:S(2)}) collective-permute-start(bf16[4096,128]{1,0:T(8,128)(2,1)} %get-tuple-element.62), channel_id=1, source_target_pairs={{0,16},{16,0},{1,17},{17,1},{2,18},{18,2},{3,19},{19,3},{4,20},{20... | collective-permute-start | bytes 3145736 | tf_op jit(solution)/shard_map/ppermute | solution.py:17
  37.9 1.6 %shard_map.75 = (f32[256,128]{1,0:T(8,128)S(1)}, f32[256,128]{1,0:T(8,128)}) custom-call(s32[1]{0:T(128)} %bitcast.1.bit_ref, f32[512,128]{1,0:T(8,128)S(1)} %get-tuple-element.48.mine_ref, f32[512,128]{1,0:T(8,128)} %collective-permute-done.1.came_ref), custom_call_target="tpu_custom_call" | custom-call | tf_op jit(solution)/shard_map/pallas_call | solution.py:98
  39.5 1.8 %collective-permute-start.2 = (f32[256,128]{1,0:T(8,128)}, f32[256,128]{1,0:T(8,128)S(1)}, u32[]{:S(2)}, u32[]{:S(2)}) collective-permute-start(f32[256,128]{1,0:T(8,128)} %get-tuple-element.51), channel_id=1, source_target_pairs={{0,2},{1,3},{2,0},{3,1},{4,6},{5,7},{6,4},{7,5},{8,10},{9,11},{10,... | collective-permute-start | bytes 393224 | tf_op jit(solution)/shard_map/ppermute | solution.py:110
  41.3 4.0 %collective-permute-done.2.came_ref = f32[256,128]{1,0:T(8,128)S(1)} collective-permute-done((f32[256,128]{1,0:T(8,128)}, f32[256,128]{1,0:T(8,128)S(1)}, u32[]{:S(2)}, u32[]{:S(2)}) %collective-permute-start.2) | collective-permute-done | bytes 131104 | tf_op jit(solution)/shard_map/ppermute | solution.py:110
  45.4 1.9 %collective-permute-start.3 = (f32[128,128]{1,0:T(8,128)S(1)}, f32[128,128]{1,0:T(8,128)S(1)}, u32[]{:S(2)}, u32[]{:S(2)}) collective-permute-start(f32[128,128]{1,0:T(8,128)S(1)} %get-tuple-element.53), channel_id=1, source_target_pairs={{0,4},{1,5},{2,6},{3,7},{4,0},{5,1},{6,2},{7,3},{8,12},{9,13},{10,... | collective-permute-start | bytes 196616 | tf_op jit(solution)/shard_map/ppermute | solution.py:110
  47.3 2.4 %collective-permute-done.3 = f32[128,128]{1,0:T(8,128)S(1)} collective-permute-done((f32[128,128]{1,0:T(8,128)S(1)}, f32[128,128]{1,0:T(8,128)S(1)}, u32[]{:S(2)}, u32[]{:S(2)}) %collective-permute-start.3) | collective-permute-done | bytes 65568 | tf_op jit(solution)/shard_map/ppermute | solution.py:110
  49.7 2.9 %collective-permute-start.4 = (f32[128,128]{1,0:T(8,128)S(1)}, f32[128,128]{1,0:T(8,128)S(1)}, u32[]{:S(2)}, u32[]{:S(2)}) collective-permute-start(f32[128,128]{1,0:T(8,128)S(1)} %add.65), channel_id=1, source_target_pairs={{0,8},{1,9},{2,10},{3,11},{4,12},{5,13},{6,14},{7,15},{8,0},{9,1},... | collective-permute-start | bytes 196616 | tf_op jit(solution)/shard_map/ppermute | solution.py:110
  52.6 1.3 shard_map.77
  54.0 1.0 collective-permute-done.4
  55.0 5.8 %shard_map.78 = (f32[512,128]{1,0:T(8,128)S(1)}, f32[512,128]{1,0:T(8,128)S(1)}) custom-call(s32[1]{0:T(128)} %bitcast.2.bit_ref, bf16[1024,4096]{1,0:T(8,128)(2,1)} %a_ref.9, bf16[4096,128]{1,0:T(8,128)(2,1)S(1)} %collective-permute-done.5.b_ref), custom_call_target="tpu_custom_call" | custom-call | tf_op jit(solution)/shard_map/pallas_call | solution.py:72
  60.8 1.8 %collective-permute-start.12 = (f32[256,512]{1,0:T(8,128)S(1)}, f32[256,512]{1,0:T(8,128)S(1)}, u32[]{:S(2)}, u32[]{:S(2)}) collective-permute-start(f32[256,512]{1,0:T(8,128)S(1)} %get-tuple-element.63), channel_id=1, source_target_pairs={{0,2},{1,3},{2,0},{3,1},{4,6},{5,7},{6,4},{7,5},{8,10},{9,11},{10,... | collective-permute-start | bytes 1572872 | tf_op jit(solution)/shard_map/ppermute | solution.py:110
  62.6 1.5 %collective-permute-start.17 = (bf16[4096,128]{1,0:T(8,128)(2,1)S(1)}, bf16[4096,128]{1,0:T(8,128)(2,1)S(1)}, u32[]{:S(2)}, u32[]{:S(2)}) collective-permute-start(bf16[4096,128]{1,0:T(8,128)(2,1)S(1)} %copy-done), channel_id=1, source_target_pairs={{0,16},{16,0},{1,17},{17,1},{2,18},{18,2},{3,19},{19,3},{4,20},{20... | collective-permute-start | bytes 3145736 | tf_op jit(solution)/shard_map/ppermute | solution.py:17
  64.2 0.6 collective-permute-start.8
  64.8 13.2 %collective-permute-done.8.came_ref = f32[256,128]{1,0:T(8,128)S(1)} collective-permute-done((f32[256,128]{1,0:T(8,128)S(1)}, f32[256,128]{1,0:T(8,128)S(1)}, u32[]{:S(2)}, u32[]{:S(2)}) %collective-permute-start.8) | collective-permute-done | bytes 131104 | tf_op jit(solution)/shard_map/ppermute | solution.py:110
  78.0 1.9 %collective-permute-start.9 = (f32[128,128]{1,0:T(8,128)S(1)}, f32[128,128]{1,0:T(8,128)S(1)}, u32[]{:S(2)}, u32[]{:S(2)}) collective-permute-start(f32[128,128]{1,0:T(8,128)S(1)} %get-tuple-element.61), channel_id=1, source_target_pairs={{0,4},{1,5},{2,6},{3,7},{4,0},{5,1},{6,2},{7,3},{8,12},{9,13},{10,... | collective-permute-start | bytes 196616 | tf_op jit(solution)/shard_map/ppermute | solution.py:110
  79.9 2.4 %collective-permute-done.9 = f32[128,128]{1,0:T(8,128)S(1)} collective-permute-done((f32[128,128]{1,0:T(8,128)S(1)}, f32[128,128]{1,0:T(8,128)S(1)}, u32[]{:S(2)}, u32[]{:S(2)}) %collective-permute-start.9) | collective-permute-done | bytes 65568 | tf_op jit(solution)/shard_map/ppermute | solution.py:110
  82.3 3.1 %collective-permute-start.10 = (f32[128,128]{1,0:T(8,128)S(1)}, f32[128,128]{1,0:T(8,128)S(1)}, u32[]{:S(2)}, u32[]{:S(2)}) collective-permute-start(f32[128,128]{1,0:T(8,128)S(1)} %add.67), channel_id=1, source_target_pairs={{0,8},{1,9},{2,10},{3,11},{4,12},{5,13},{6,14},{7,15},{8,0},{9,1},... | collective-permute-start | bytes 196616 | tf_op jit(solution)/shard_map/ppermute | solution.py:110
  85.5 2.4 %collective-permute-done.10 = f32[128,128]{1,0:T(8,128)S(1)} collective-permute-done((f32[128,128]{1,0:T(8,128)S(1)}, f32[128,128]{1,0:T(8,128)S(1)}, u32[]{:S(2)}, u32[]{:S(2)}) %collective-permute-start.10) | collective-permute-done | bytes 65568 | tf_op jit(solution)/shard_map/ppermute | solution.py:110
  87.9 5.7 %shard_map.82 = (f32[512,128]{1,0:T(8,128)S(1)}, f32[512,128]{1,0:T(8,128)S(1)}) custom-call(s32[1]{0:T(128)} %bitcast.2.bit_ref, bf16[1024,4096]{1,0:T(8,128)(2,1)} %a_ref.9, bf16[4096,128]{1,0:T(8,128)(2,1)S(1)} %collective-permute-done.11.b_ref), custom_call_target="tpu_custom_call" | custom-call | tf_op jit(solution)/shard_map/pallas_call | solution.py:72
  93.7 1.8 %collective-permute-start.18 = (f32[128,512]{1,0:T(8,128)S(1)}, f32[128,512]{1,0:T(8,128)S(1)}, u32[]{:S(2)}, u32[]{:S(2)}) collective-permute-start(f32[128,512]{1,0:T(8,128)S(1)} %get-tuple-element.73), channel_id=1, source_target_pairs={{0,4},{1,5},{2,6},{3,7},{4,0},{5,1},{6,2},{7,3},{8,12},{9,13},{10,... | collective-permute-start | bytes 786440 | tf_op jit(solution)/shard_map/ppermute | solution.py:110
  95.5 1.6 %collective-permute-start.14 = (f32[256,128]{1,0:T(8,128)S(1)}, f32[256,128]{1,0:T(8,128)S(1)}, u32[]{:S(2)}, u32[]{:S(2)}) collective-permute-start(f32[256,128]{1,0:T(8,128)S(1)} %get-tuple-element.69), channel_id=1, source_target_pairs={{0,2},{1,3},{2,0},{3,1},{4,6},{5,7},{6,4},{7,5},{8,10},{9,11},{10,... | collective-permute-start | bytes 393224 | tf_op jit(solution)/shard_map/ppermute | solution.py:110
  97.1 5.3 %collective-permute-done.18 = f32[128,512]{1,0:T(8,128)S(1)} collective-permute-done((f32[128,512]{1,0:T(8,128)S(1)}, f32[128,512]{1,0:T(8,128)S(1)}, u32[]{:S(2)}, u32[]{:S(2)}) %collective-permute-start.18) | collective-permute-done | bytes 262176 | tf_op jit(solution)/shard_map/ppermute | solution.py:110
  102.5 3.1 %collective-permute-start.19 = (f32[128,512]{1,0:T(8,128)S(1)}, f32[128,512]{1,0:T(8,128)S(1)}, u32[]{:S(2)}, u32[]{:S(2)}) collective-permute-start(f32[128,512]{1,0:T(8,128)S(1)} %add.71), channel_id=1, source_target_pairs={{0,8},{1,9},{2,10},{3,11},{4,12},{5,13},{6,14},{7,15},{8,0},{9,1},... | collective-permute-start | bytes 786440 | tf_op jit(solution)/shard_map/ppermute | solution.py:110
  105.6 1.8 %collective-permute-start.15 = (f32[128,128]{1,0:T(8,128)S(1)}, f32[128,128]{1,0:T(8,128)S(1)}, u32[]{:S(2)}, u32[]{:S(2)}) collective-permute-start(f32[128,128]{1,0:T(8,128)S(1)} %get-tuple-element.71), channel_id=1, source_target_pairs={{0,4},{1,5},{2,6},{3,7},{4,0},{5,1},{6,2},{7,3},{8,12},{9,13},{10,... | collective-permute-start | bytes 196616 | tf_op jit(solution)/shard_map/ppermute | solution.py:110
  107.4 5.2 %collective-permute-done.15 = f32[128,128]{1,0:T(8,128)S(1)} collective-permute-done((f32[128,128]{1,0:T(8,128)S(1)}, f32[128,128]{1,0:T(8,128)S(1)}, u32[]{:S(2)}, u32[]{:S(2)}) %collective-permute-start.15) | collective-permute-done | bytes 65568 | tf_op jit(solution)/shard_map/ppermute | solution.py:110
  112.6 2.4 %collective-permute-start.16 = (f32[128,128]{1,0:T(8,128)S(1)}, f32[128,128]{1,0:T(8,128)S(1)}, u32[]{:S(2)}, u32[]{:S(2)}) collective-permute-start(f32[128,128]{1,0:T(8,128)S(1)} %add.69), channel_id=1, source_target_pairs={{0,8},{1,9},{2,10},{3,11},{4,12},{5,13},{6,14},{7,15},{8,0},{9,1},... | collective-permute-start | bytes 196616 | tf_op jit(solution)/shard_map/ppermute | solution.py:110
  115.0 3.9 %collective-permute-done.19 = f32[128,512]{1,0:T(8,128)S(1)} collective-permute-done((f32[128,512]{1,0:T(8,128)S(1)}, f32[128,512]{1,0:T(8,128)S(1)}, u32[]{:S(2)}, u32[]{:S(2)}) %collective-permute-start.19) | collective-permute-done | bytes 262176 | tf_op jit(solution)/shard_map/ppermute | solution.py:110
  119.0 1.4 collective-permute-done.16
  120.4 5.7 %shard_map.85 = (f32[512,128]{1,0:T(8,128)S(1)}, f32[512,128]{1,0:T(8,128)S(1)}) custom-call(s32[1]{0:T(128)} %bitcast.2.bit_ref, bf16[1024,4096]{1,0:T(8,128)(2,1)} %a_ref.9, bf16[4096,128]{1,0:T(8,128)(2,1)S(1)} %collective-permute-done.17.b_ref), custom_call_target="tpu_custom_call" | custom-call | tf_op jit(solution)/shard_map/pallas_call | solution.py:72
  126.2 0.2 select_reduce_fusion.1
  126.5 1.2 collective-permute-done.20.came_ref
  127.7 1.6 %collective-permute-start.21 = (f32[256,128]{1,0:T(8,128)S(1)}, f32[256,128]{1,0:T(8,128)S(1)}, u32[]{:S(2)}, u32[]{:S(2)}) collective-permute-start(f32[256,128]{1,0:T(8,128)S(1)} %get-tuple-element.78), channel_id=1, source_target_pairs={{0,2},{1,3},{2,0},{3,1},{4,6},{5,7},{6,4},{7,5},{8,10},{9,11},{10,... | collective-permute-start | bytes 393224 | tf_op jit(solution)/shard_map/ppermute | solution.py:110
  129.3 4.0 %collective-permute-done.21.came_ref = f32[256,128]{1,0:T(8,128)S(1)} collective-permute-done((f32[256,128]{1,0:T(8,128)S(1)}, f32[256,128]{1,0:T(8,128)S(1)}, u32[]{:S(2)}, u32[]{:S(2)}) %collective-permute-start.21) | collective-permute-done | bytes 131104 | tf_op jit(solution)/shard_map/ppermute | solution.py:110
  133.4 0.8 collective-permute-start.22
  134.3 3.4 %collective-permute-done.22 = f32[128,128]{1,0:T(8,128)S(1)} collective-permute-done((f32[128,128]{1,0:T(8,128)S(1)}, f32[128,128]{1,0:T(8,128)S(1)}, u32[]{:S(2)}, u32[]{:S(2)}) %collective-permute-start.22) | collective-permute-done | bytes 65568 | tf_op jit(solution)/shard_map/ppermute | solution.py:110
  137.7 2.1 %collective-permute-start.23 = (f32[128,128]{1,0:T(8,128)S(1)}, f32[128,128]{1,0:T(8,128)S(1)}, u32[]{:S(2)}, u32[]{:S(2)}) collective-permute-start(f32[128,128]{1,0:T(8,128)S(1)} %add.73), channel_id=1, source_target_pairs={{0,8},{1,9},{2,10},{3,11},{4,12},{5,13},{6,14},{7,15},{8,0},{9,1},... | collective-permute-start | bytes 196616 | tf_op jit(solution)/shard_map/ppermute | solution.py:110
  139.9 3.1 %collective-permute-done.23 = f32[128,128]{1,0:T(8,128)S(1)} collective-permute-done((f32[128,128]{1,0:T(8,128)S(1)}, f32[128,128]{1,0:T(8,128)S(1)}, u32[]{:S(2)}, u32[]{:S(2)}) %collective-permute-start.23) | collective-permute-done | bytes 65568 | tf_op jit(solution)/shard_map/ppermute | solution.py:110
  143.1 0.7 gather_fusion
  143.7 0.2 copy.14
  144.0 0.3 copy.15
  144.3 0.2 copy.16
  144.5 0.8 subtract_divide_fusion
  (53 shorter events, 1.1 us)
Async XLA Ops:
  2.3 27.2 %collective-permute-start = (bf16[4096,128]{1,0:T(8,128)(2,1)}, bf16[4096,128]{1,0:T(8,128)(2,1)S(1)}, u32[]{:S(2)}, u32[]{:S(2)}) collective-permute-start(bf16[4096,128]{1,0:T(8,128)(2,1)} %slice.20), channel_id=1, source_target_pairs={{0,16},{16,0},{1,17},{17,1},{2,18},{18,2},{3,19},{19,3},{4,20},{20... | collective-permute-start | bytes 3145736 | tf_op jit(solution)/shard_map/ppermute | solution.py:17
  18.1 34.5 %collective-permute-start.6 = (f32[512,512]{1,0:T(8,128)}, f32[512,512]{1,0:T(8,128)}, u32[]{:S(2)}, u32[]{:S(2)}) collective-permute-start(f32[512,512]{1,0:T(8,128)} %get-tuple-element.46), channel_id=1, source_target_pairs={{0,1},{1,0},{2,3},{3,2},{4,5},{5,4},{6,7},{7,6},{8,9},{9,8},{10,11... | collective-permute-start | bytes 3145736 | tf_op jit(solution)/shard_map/ppermute | solution.py:110
  18.1 36.9 %collective-permute-start.5 = (bf16[4096,128]{1,0:T(8,128)(2,1)}, bf16[4096,128]{1,0:T(8,128)(2,1)S(1)}, u32[]{:S(2)}, u32[]{:S(2)}) collective-permute-start(bf16[4096,128]{1,0:T(8,128)(2,1)} %get-tuple-element.85), channel_id=1, source_target_pairs={{0,16},{16,0},{1,17},{17,1},{2,18},{18,2},{3,19},{19,3},{4,20},{20... | collective-permute-start | bytes 3145736 | tf_op jit(solution)/shard_map/ppermute | solution.py:17
  35.8 2.1 %collective-permute-start.1 = (f32[512,128]{1,0:T(8,128)}, f32[512,128]{1,0:T(8,128)}, u32[]{:S(2)}, u32[]{:S(2)}) collective-permute-start(f32[512,128]{1,0:T(8,128)} %get-tuple-element.49), channel_id=1, source_target_pairs={{0,1},{1,0},{2,3},{3,2},{4,5},{5,4},{6,7},{7,6},{8,9},{9,8},{10,11... | collective-permute-start | bytes 786440 | tf_op jit(solution)/shard_map/ppermute | solution.py:110
  35.8 52.1 %collective-permute-start.11 = (bf16[4096,128]{1,0:T(8,128)(2,1)}, bf16[4096,128]{1,0:T(8,128)(2,1)S(1)}, u32[]{:S(2)}, u32[]{:S(2)}) collective-permute-start(bf16[4096,128]{1,0:T(8,128)(2,1)} %get-tuple-element.62), channel_id=1, source_target_pairs={{0,16},{16,0},{1,17},{17,1},{2,18},{18,2},{3,19},{19,3},{4,20},{20... | collective-permute-start | bytes 3145736 | tf_op jit(solution)/shard_map/ppermute | solution.py:17
  39.5 5.8 %collective-permute-start.2 = (f32[256,128]{1,0:T(8,128)}, f32[256,128]{1,0:T(8,128)S(1)}, u32[]{:S(2)}, u32[]{:S(2)}) collective-permute-start(f32[256,128]{1,0:T(8,128)} %get-tuple-element.51), channel_id=1, source_target_pairs={{0,2},{1,3},{2,0},{3,1},{4,6},{5,7},{6,4},{7,5},{8,10},{9,11},{10,... | collective-permute-start | bytes 393224 | tf_op jit(solution)/shard_map/ppermute | solution.py:110
  45.4 4.3 %collective-permute-start.3 = (f32[128,128]{1,0:T(8,128)S(1)}, f32[128,128]{1,0:T(8,128)S(1)}, u32[]{:S(2)}, u32[]{:S(2)}) collective-permute-start(f32[128,128]{1,0:T(8,128)S(1)} %get-tuple-element.53), channel_id=1, source_target_pairs={{0,4},{1,5},{2,6},{3,7},{4,0},{5,1},{6,2},{7,3},{8,12},{9,13},{10,... | collective-permute-start | bytes 196616 | tf_op jit(solution)/shard_map/ppermute | solution.py:110
  49.7 5.2 %collective-permute-start.4 = (f32[128,128]{1,0:T(8,128)S(1)}, f32[128,128]{1,0:T(8,128)S(1)}, u32[]{:S(2)}, u32[]{:S(2)}) collective-permute-start(f32[128,128]{1,0:T(8,128)S(1)} %add.65), channel_id=1, source_target_pairs={{0,8},{1,9},{2,10},{3,11},{4,12},{5,13},{6,14},{7,15},{8,0},{9,1},... | collective-permute-start | bytes 196616 | tf_op jit(solution)/shard_map/ppermute | solution.py:110
  55.0 7.7 %copy-start = (bf16[4096,128]{1,0:T(8,128)(2,1)S(1)}, bf16[4096,128]{1,0:T(8,128)(2,1)}, u32[]{:S(2)}) copy-start(bf16[4096,128]{1,0:T(8,128)(2,1)} %get-tuple-element.72) | copy-start | bytes 3145732
  60.8 3.4 %collective-permute-start.7 = (f32[512,128]{1,0:T(8,128)S(1)}, f32[512,128]{1,0:T(8,128)S(1)}, u32[]{:S(2)}, u32[]{:S(2)}) collective-permute-start(f32[512,128]{1,0:T(8,128)S(1)} %get-tuple-element.57), channel_id=1, source_target_pairs={{0,1},{1,0},{2,3},{3,2},{4,5},{5,4},{6,7},{7,6},{8,9},{9,8},{10,11... | collective-permute-start | bytes 786440 | tf_op jit(solution)/shard_map/ppermute | solution.py:110
  60.8 24.6 %collective-permute-start.12 = (f32[256,512]{1,0:T(8,128)S(1)}, f32[256,512]{1,0:T(8,128)S(1)}, u32[]{:S(2)}, u32[]{:S(2)}) collective-permute-start(f32[256,512]{1,0:T(8,128)S(1)} %get-tuple-element.63), channel_id=1, source_target_pairs={{0,2},{1,3},{2,0},{3,1},{4,6},{5,7},{6,4},{7,5},{8,10},{9,11},{10,... | collective-permute-start | bytes 1572872 | tf_op jit(solution)/shard_map/ppermute | solution.py:110
  62.6 57.8 %collective-permute-start.17 = (bf16[4096,128]{1,0:T(8,128)(2,1)S(1)}, bf16[4096,128]{1,0:T(8,128)(2,1)S(1)}, u32[]{:S(2)}, u32[]{:S(2)}) collective-permute-start(bf16[4096,128]{1,0:T(8,128)(2,1)S(1)} %copy-done), channel_id=1, source_target_pairs={{0,16},{16,0},{1,17},{17,1},{2,18},{18,2},{3,19},{19,3},{4,20},{20... | collective-permute-start | bytes 3145736 | tf_op jit(solution)/shard_map/ppermute | solution.py:17
  64.2 13.8 %collective-permute-start.8 = (f32[256,128]{1,0:T(8,128)S(1)}, f32[256,128]{1,0:T(8,128)S(1)}, u32[]{:S(2)}, u32[]{:S(2)}) collective-permute-start(f32[256,128]{1,0:T(8,128)S(1)} %get-tuple-element.59), channel_id=1, source_target_pairs={{0,2},{1,3},{2,0},{3,1},{4,6},{5,7},{6,4},{7,5},{8,10},{9,11},{10,... | collective-permute-start | bytes 393224 | tf_op jit(solution)/shard_map/ppermute | solution.py:110
  78.0 4.3 %collective-permute-start.9 = (f32[128,128]{1,0:T(8,128)S(1)}, f32[128,128]{1,0:T(8,128)S(1)}, u32[]{:S(2)}, u32[]{:S(2)}) collective-permute-start(f32[128,128]{1,0:T(8,128)S(1)} %get-tuple-element.61), channel_id=1, source_target_pairs={{0,4},{1,5},{2,6},{3,7},{4,0},{5,1},{6,2},{7,3},{8,12},{9,13},{10,... | collective-permute-start | bytes 196616 | tf_op jit(solution)/shard_map/ppermute | solution.py:110
  82.3 5.6 %collective-permute-start.10 = (f32[128,128]{1,0:T(8,128)S(1)}, f32[128,128]{1,0:T(8,128)S(1)}, u32[]{:S(2)}, u32[]{:S(2)}) collective-permute-start(f32[128,128]{1,0:T(8,128)S(1)} %add.67), channel_id=1, source_target_pairs={{0,8},{1,9},{2,10},{3,11},{4,12},{5,13},{6,14},{7,15},{8,0},{9,1},... | collective-permute-start | bytes 196616 | tf_op jit(solution)/shard_map/ppermute | solution.py:110
  93.6 1.9 %collective-permute-start.13 = (f32[512,128]{1,0:T(8,128)S(1)}, f32[512,128]{1,0:T(8,128)S(1)}, u32[]{:S(2)}, u32[]{:S(2)}) collective-permute-start(f32[512,128]{1,0:T(8,128)S(1)} %get-tuple-element.67), channel_id=1, source_target_pairs={{0,1},{1,0},{2,3},{3,2},{4,5},{5,4},{6,7},{7,6},{8,9},{9,8},{10,11... | collective-permute-start | bytes 786440 | tf_op jit(solution)/shard_map/ppermute | solution.py:110
  93.7 8.7 %collective-permute-start.18 = (f32[128,512]{1,0:T(8,128)S(1)}, f32[128,512]{1,0:T(8,128)S(1)}, u32[]{:S(2)}, u32[]{:S(2)}) collective-permute-start(f32[128,512]{1,0:T(8,128)S(1)} %get-tuple-element.73), channel_id=1, source_target_pairs={{0,4},{1,5},{2,6},{3,7},{4,0},{5,1},{6,2},{7,3},{8,12},{9,13},{10,... | collective-permute-start | bytes 786440 | tf_op jit(solution)/shard_map/ppermute | solution.py:110
  95.5 10.0 %collective-permute-start.14 = (f32[256,128]{1,0:T(8,128)S(1)}, f32[256,128]{1,0:T(8,128)S(1)}, u32[]{:S(2)}, u32[]{:S(2)}) collective-permute-start(f32[256,128]{1,0:T(8,128)S(1)} %get-tuple-element.69), channel_id=1, source_target_pairs={{0,2},{1,3},{2,0},{3,1},{4,6},{5,7},{6,4},{7,5},{8,10},{9,11},{10,... | collective-permute-start | bytes 393224 | tf_op jit(solution)/shard_map/ppermute | solution.py:110
  102.5 16.5 %collective-permute-start.19 = (f32[128,512]{1,0:T(8,128)S(1)}, f32[128,512]{1,0:T(8,128)S(1)}, u32[]{:S(2)}, u32[]{:S(2)}) collective-permute-start(f32[128,512]{1,0:T(8,128)S(1)} %add.71), channel_id=1, source_target_pairs={{0,8},{1,9},{2,10},{3,11},{4,12},{5,13},{6,14},{7,15},{8,0},{9,1},... | collective-permute-start | bytes 786440 | tf_op jit(solution)/shard_map/ppermute | solution.py:110
  105.6 7.0 %collective-permute-start.15 = (f32[128,128]{1,0:T(8,128)S(1)}, f32[128,128]{1,0:T(8,128)S(1)}, u32[]{:S(2)}, u32[]{:S(2)}) collective-permute-start(f32[128,128]{1,0:T(8,128)S(1)} %get-tuple-element.71), channel_id=1, source_target_pairs={{0,4},{1,5},{2,6},{3,7},{4,0},{5,1},{6,2},{7,3},{8,12},{9,13},{10,... | collective-permute-start | bytes 196616 | tf_op jit(solution)/shard_map/ppermute | solution.py:110
  112.6 7.7 %collective-permute-start.16 = (f32[128,128]{1,0:T(8,128)S(1)}, f32[128,128]{1,0:T(8,128)S(1)}, u32[]{:S(2)}, u32[]{:S(2)}) collective-permute-start(f32[128,128]{1,0:T(8,128)S(1)} %add.69), channel_id=1, source_target_pairs={{0,8},{1,9},{2,10},{3,11},{4,12},{5,13},{6,14},{7,15},{8,0},{9,1},... | collective-permute-start | bytes 196616 | tf_op jit(solution)/shard_map/ppermute | solution.py:110
  120.4 5.8 %copy-start.1 = (f32[512]{0:T(512)S(1)}, f32[512]{0:T(512)}, u32[]{:S(2)}) copy-start(f32[512]{0:T(512)} %param.13) | copy-start | bytes 6148
  120.4 5.8 %copy-start.3 = (s32[32]{0:T(128)S(1)}, s32[32]{0:T(128)}, u32[]{:S(2)}) copy-start(s32[32]{0:T(128)} %param.11) | copy-start | bytes 388
  120.4 8.9 %copy-start.5 = (s32[64]{0:T(128)S(1)}, s32[64]{0:T(128)}, u32[]{:S(2)}) copy-start(s32[64]{0:T(128)} %param.10) | copy-start | bytes 772
  120.4 13.8 %copy-start.2 = (s32[64,2]{0,1:T(2,128)S(1)}, s32[64,2]{0,1:T(2,128)}, u32[]{:S(2)}) copy-start(s32[64,2]{0,1:T(2,128)} %param.9) | copy-start | bytes 1540
  120.4 13.8 %copy-start.4 = (f32[96]{0:T(128)S(1)}, f32[96]{0:T(128)}, u32[]{:S(2)}) copy-start(f32[96]{0:T(128)} %param.12) | copy-start | bytes 1156
  126.1 1.6 %collective-permute-start.20 = (f32[512,128]{1,0:T(8,128)S(1)}, f32[512,128]{1,0:T(8,128)S(1)}, u32[]{:S(2)}, u32[]{:S(2)}) collective-permute-start(f32[512,128]{1,0:T(8,128)S(1)} %get-tuple-element.76), channel_id=1, source_target_pairs={{0,1},{1,0},{2,3},{3,2},{4,5},{5,4},{6,7},{7,6},{8,9},{9,8},{10,11... | collective-permute-start | bytes 786440 | tf_op jit(solution)/shard_map/ppermute | solution.py:110
  127.7 5.6 %collective-permute-start.21 = (f32[256,128]{1,0:T(8,128)S(1)}, f32[256,128]{1,0:T(8,128)S(1)}, u32[]{:S(2)}, u32[]{:S(2)}) collective-permute-start(f32[256,128]{1,0:T(8,128)S(1)} %get-tuple-element.78), channel_id=1, source_target_pairs={{0,2},{1,3},{2,0},{3,1},{4,6},{5,7},{6,4},{7,5},{8,10},{9,11},{10,... | collective-permute-start | bytes 393224 | tf_op jit(solution)/shard_map/ppermute | solution.py:110
  133.4 4.3 %collective-permute-start.22 = (f32[128,128]{1,0:T(8,128)S(1)}, f32[128,128]{1,0:T(8,128)S(1)}, u32[]{:S(2)}, u32[]{:S(2)}) collective-permute-start(f32[128,128]{1,0:T(8,128)S(1)} %get-tuple-element.80), channel_id=1, source_target_pairs={{0,4},{1,5},{2,6},{3,7},{4,0},{5,1},{6,2},{7,3},{8,12},{9,13},{10,... | collective-permute-start | bytes 196616 | tf_op jit(solution)/shard_map/ppermute | solution.py:110
  137.7 5.2 %collective-permute-start.23 = (f32[128,128]{1,0:T(8,128)S(1)}, f32[128,128]{1,0:T(8,128)S(1)}, u32[]{:S(2)}, u32[]{:S(2)}) collective-permute-start(f32[128,128]{1,0:T(8,128)S(1)} %add.73), channel_id=1, source_target_pairs={{0,8},{1,9},{2,10},{3,11},{4,12},{5,13},{6,14},{7,15},{8,0},{9,1},... | collective-permute-start | bytes 196616 | tf_op jit(solution)/shard_map/ppermute | solution.py:110

commit v3 on v2

--- a/solution.py
+++ b/solution.py
@@ -7,6 +7,7 @@
 from jax.experimental.pallas import tpu as pltpu
 from jax.sharding import PartitionSpec as P
 
+DEPTH_CUTS = 4
 PRODUCT_BYTES = 51 * 1024 * 1024
 SUM_BYTES = 8 * 1024 * 1024
 
@@ -23,8 +24,8 @@
 
 
 def column_cuts(columns):
-    part = columns // 4
-    return [(low, low + part) for low in range(0, columns, part)]
+    half, quarter = columns // 2, columns // 4
+    return [(0, half), (half, half + quarter), (half + quarter, columns)]
 
 
 def after(value, earlier):
@@ -42,13 +43,15 @@
     return jnp.concatenate(ordered, axis=1)
 
 
-def product_kernel(steps, order, bit_ref, a_ref, b_ref, keep_ref, send_ref, total_ref):
+def product_kernel(steps, order, has_base, bit_ref, a_ref, b_ref, *refs):
+    base_ref = refs[0] if has_base else None
+    keep_ref, send_ref, total_ref = refs[-3:]
     step = pl.program_id(0)
     term = jnp.dot(a_ref[...], b_ref[...], preferred_element_type=jnp.float32)
 
     @pl.when(step == 0)
     def _():
-        total_ref[...] = term
+        total_ref[...] = term + base_ref[...] if has_base else term
 
     @pl.when(step > 0)
     def _():
@@ -63,26 +66,58 @@
                 out_ref[place * rows : (place + 1) * rows, :] = total_ref[pl.ds(start, rows), :]
 
 
-def multiplied(amplitudes, columns, bit, order):
+def multiplied(amplitudes, columns, bit, order, first=0, base=None):
     rows, depth = amplitudes.shape
     width = columns.shape[1]
-    steps = 4
-    part = depth // steps
+    part = depth // DEPTH_CUTS
+    steps = columns.shape[0] // part
     shape = jax.ShapeDtypeStruct((rows // 2, width), jnp.float32)
+    bases = [] if base is None else [base]
     return pl.pallas_call(
-        functools.partial(product_kernel, steps, order),
+        functools.partial(product_kernel, steps, order, base is not None),
         grid=(steps,),
         out_shape=[shape] * 2,
         in_specs=[
             pl.BlockSpec(memory_space=pltpu.SMEM),
-            pl.BlockSpec((rows, part), lambda k: (0, k)),
+            pl.BlockSpec((rows, part), lambda k: (0, k + first)),
             pl.BlockSpec((part, width), lambda k: (k, 0)),
-        ],
+        ]
+        + [pl.BlockSpec((rows, width), lambda k: (0, 0)) for _ in bases],
         out_specs=[pl.BlockSpec(shape.shape, lambda k: (0, 0))] * 2,
         scratch_shapes=[pltpu.VMEM((rows, width), jnp.float32)],
         compiler_params=pltpu.CompilerParams(vmem_limit_bytes=PRODUCT_BYTES),
         cost_estimate=pl.CostEstimate(flops=0, bytes_accessed=0, transcendentals=0),
-    )(bit, amplitudes, columns)
+    )(bit, amplitudes, columns, *bases)
+
+
+def plain_kernel(a_ref, b_ref, out_ref):
+    term = jnp.dot(a_ref[...], b_ref[...], preferred_element_type=jnp.float32)
+
+    @pl.when(pl.program_id(0) == 0)
+    def _():
+        out_ref[...] = term
+
+    @pl.when(pl.program_id(0) > 0)
+    def _():
+        out_ref[...] += term
+
+
+def plain_product(amplitudes, columns):
+    rows, depth = amplitudes.shape
+    width = columns.shape[1]
+    part = depth // DEPTH_CUTS
+    return pl.pallas_call(
+        plain_kernel,
+        grid=(columns.shape[0] // part,),
+        out_shape=jax.ShapeDtypeStruct((rows, width), jnp.float32),
+        in_specs=[
+            pl.BlockSpec((rows, part), lambda k: (0, k)),
+            pl.BlockSpec((part, width), lambda k: (k, 0)),
+        ],
+        out_specs=pl.BlockSpec((rows, width), lambda k: (0, 0)),
+        compiler_params=pltpu.CompilerParams(vmem_limit_bytes=PRODUCT_BYTES),
+        cost_estimate=pl.CostEstimate(flops=0, bytes_accessed=0, transcendentals=0),
+    )(amplitudes, columns)
 
 
 def halve_kernel(bit_ref, mine_ref, came_ref, keep_ref, send_ref):
@@ -110,11 +145,13 @@
     return lax.ppermute(value, axis, [(source, source ^ bits) for source in range(count)])
 
 
-def exchanged_sum(parts, bits):
+def exchanged_sum(parts, bits, gates=()):
     stages = []
     for level in range(1, len(bits)):
         keep, send = parts
         came = flipped_along(send, "virt", 1 << (level - 1))
+        if level in gates:
+            came = after(came, gates[level])
         parts = halved(keep, came, bits[level]) if level < len(bits) - 1 else [keep + came]
         stages.append(parts[0])
     total = parts[0]
@@ -138,22 +175,33 @@
 
     first = integrals[:, cuts[0][0] : cuts[0][1]]
     rest = after(integrals, first)
-    pieces = [first] + [rest[:, low:high] for low, high in cuts[1:]]
+    low, high = cuts[-1]
+    late = integrals.shape[0] // DEPTH_CUTS * (DEPTH_CUTS - 1)
+    pieces = [first] + [rest[:, low:high] for low, high in cuts[1:-1]] + [rest[:late, low:high], rest[late:, low:high]]
     in_flight = [sent(pieces[0]), sent(pieces[1])]
     own_product = multiplied(amplitudes, after(rest, pieces), bits[0], order)
     own_sum, own_stages = exchanged_sum(own_product, bits)
     sums = [[own_sum]] + [[] for _ in range(1, count)]
-    earlier = own_product
-    for step in range(len(cuts)):
-        if step > 0:
-            earlier = (earlier, (own_stages + [own_sum])[min(step - 1 if step < 3 else len(own_stages), len(own_stages))])
+    earlier, gates = own_stages[2], {}
+    for step in range(len(pieces)):
+        if step == 1:
+            earlier = (earlier, own_sum)
         arrived, earlier = lax.optimization_barrier((in_flight[step], earlier))
-        if step + 2 < len(cuts):
+        if step + 2 < len(pieces):
             in_flight.append(sent(after(pieces[step + 2], arrived)))
+        if step == len(pieces) - 2:
+            bases = [plain_product(amplitudes, columns) for columns in arrived]
+            earlier = (gates[2], bases)
+            gates = {}
+            continue
         for shift in range(1, count):
-            product = multiplied(amplitudes, arrived[shift - 1], bits[0], order)
-            earlier, stages = exchanged_sum(product, bits)
-            sums[shift].append(earlier)
+            if step < len(cuts) - 1:
+                product = multiplied(amplitudes, arrived[shift - 1], bits[0], order)
+            else:
+                product = multiplied(amplitudes, arrived[shift - 1], bits[0], order, DEPTH_CUTS - 1, bases[shift - 1])
+            total, stages = exchanged_sum(product, bits, gates)
+            sums[shift].append(total)
+            earlier, gates = stages[1], {1: stages[2], 2: total}
 
     both = in_column_order([jnp.concatenate(parts, axis=1) for parts in sums], count)
     mine = jnp.where(upper, both[rows:], both[:rows])

time: 146 us -> 130 us (0.89)
  Pallas kernels: 35.9 us -> 27.4 us
  starting transfers between devices: 36 us -> 28.7 us
    ppermute x20 -> x16, starting transfers between devices: 29.4 us -> 22.2 us  [flipped_along(): lax.ppermute(value, axis, [(source, source ^ bits) for source in range(co...]
    pallas_call x5, Pallas kernels: 32.7 us -> 27 us  [the longest x4 22.3 us: multiplied(): pl.pallas_call(functools.partial(product_kernel, steps, order, base is no...]
    pallas_call x10 -> x8, Pallas kernels: 3.19 us -> 0.34 us  [halved(): pl.pallas_call(halve_kernel, out_shape=[shape] * 2, in_specs=[pl.BlockSpe...]
    slice x1 -> x3, local copies, waits for them, and re-layouts: 3.61 us -> 2.21 us  [the longest x1 1.17 us: per_device(): rest[:, low:high]]
    ppermute x20 -> x16, waiting for transfers between devices: 52.9 us -> 52.4 us  [flipped_along(): lax.ppermute(value, axis, [(source, source ^ bits) for source in range(co...]
  transfers between devices with their start and end apart: 24 -> 20, of which waited for: 15 -> 13; matrix products, arithmetic and copies ran while one was open for 3% -> 2% of each run, Pallas kernels for 21% -> 19%
where the time goes in v3:
time: 130 us; the launch traced here: 129 us
  waiting for transfers between devices  64.4 us (50%)
  starting transfers between devices  28.7 us (22%)
  Pallas kernels  27.4 us (21%)
  local copies, waits for them, and re-layouts  6.9 us (5%)
  other arithmetic  1.54 us (1%)
    ppermute x16, waiting for transfers between devices, flipped_along(): lax.ppermute(value, axis, [(source, source ^ bits) for source in range(co...  52.4 us
    pallas_call x4, Pallas kernels, multiplied(): pl.pallas_call(functools.partial(product_kernel, steps, order, base is no...  22.3 us
    ppermute x16, starting transfers between devices, flipped_along(): lax.ppermute(value, axis, [(source, source ^ bits) for source in range(co...  22.2 us
    ppermute x4, waiting for transfers between devices, passed_along(): return lax.ppermute(value, axis, pairs)  12 us
    ppermute x4, starting transfers between devices, passed_along(): return lax.ppermute(value, axis, pairs)  6.52 us
    pallas_call x1, Pallas kernels, plain_product(): pl.pallas_call(plain_kernel, grid=(columns.shape[0] // part,), out_shape=...  4.7 us
    slice x1, local copies, waits for them, and re-layouts, per_device(): first = integrals[:, cuts[0][0]:cuts[0][1]]  3.22 us
  transfers between devices with their start and end apart: 20, of which 13 were waited for; matrix products, arithmetic and copies ran while one was open for 2% of the time, Pallas kernels for 19%

profile of v3, /device:TPU:0, one launch (start us, length us, event | category | flops | bytes accessed | tf_op | source)
XLA Modules:
  0.0 129.3 jit_solution(165154899565838573)
XLA Ops:
  0.0 3.2 %slice.20 = bf16[4096,256]{1,0:T(8,128)(2,1)} slice(bf16[4096,512]{1,0:T(8,128)(2,1)} %b_ref), slice={[0:4096], [0:256]} | slice | bytes 4194304 | tf_op jit(solution)/shard_map/slice | solution.py:176
  3.2 3.0 %collective-permute-start = (bf16[4096,256]{1,0:T(8,128)(2,1)}, bf16[4096,256]{1,0:T(8,128)(2,1)}, u32[]{:S(2)}, u32[]{:S(2)}) collective-permute-start(bf16[4096,256]{1,0:T(8,128)(2,1)} %slice.20), channel_id=1, source_target_pairs={{0,16},{16,0},{1,17},{17,1},{2,18},{18,2},{3,19},{19,3},{4,20},{20... | collective-permute-start | bytes 6291464 | tf_op jit(solution)/shard_map/ppermute | solution.py:18
  6.2 1.2 slice.21
  7.4 1.0 slice.22
  8.4 8.3 %shard_map.73 = (f32[512,512]{1,0:T(8,128)S(1)}, f32[512,512]{1,0:T(8,128)S(1)}) custom-call(s32[1]{0:T(128)} %bitcast.2.bit_ref, bf16[1024,4096]{1,0:T(8,128)(2,1)} %a_ref.9, bf16[4096,512]{1,0:T(8,128)(2,1)} %b_ref), custom_call_target="tpu_custom_call" | custom-call | tf_op jit(solution)/shard_map/pallas_call | solution.py:76
  16.8 2.6 %collective-permute-done.1.came_ref = f32[512,512]{1,0:T(8,128)S(1)} collective-permute-done((f32[512,512]{1,0:T(8,128)S(1)}, f32[512,512]{1,0:T(8,128)S(1)}, u32[]{:S(2)}, u32[]{:S(2)}) %collective-permute-start.1) | collective-permute-done | bytes 1048608 | tf_op jit(solution)/shard_map/ppermute | solution.py:145
  19.4 0.1 shard_map.74
  19.5 1.6 %collective-permute-start.2 = (f32[256,512]{1,0:T(8,128)S(1)}, f32[256,512]{1,0:T(8,128)S(1)}, u32[]{:S(2)}, u32[]{:S(2)}) collective-permute-start(f32[256,512]{1,0:T(8,128)S(1)} %get-tuple-element.44), channel_id=1, source_target_pairs={{0,2},{1,3},{2,0},{3,1},{4,6},{5,7},{6,4},{7,5},{8,10},{9,11},{10,... | collective-permute-start | bytes 1572872 | tf_op jit(solution)/shard_map/ppermute | solution.py:145
  21.1 12.5 %collective-permute-done.2.came_ref = f32[256,512]{1,0:T(8,128)S(1)} collective-permute-done((f32[256,512]{1,0:T(8,128)S(1)}, f32[256,512]{1,0:T(8,128)S(1)}, u32[]{:S(2)}, u32[]{:S(2)}) %collective-permute-start.2) | collective-permute-done | bytes 524320 | tf_op jit(solution)/shard_map/ppermute | solution.py:145
  33.6 1.6 %collective-permute-start.3 = (f32[128,512]{1,0:T(8,128)S(1)}, f32[128,512]{1,0:T(8,128)S(1)}, u32[]{:S(2)}, u32[]{:S(2)}) collective-permute-start(f32[128,512]{1,0:T(8,128)S(1)} %get-tuple-element.46), channel_id=1, source_target_pairs={{0,4},{1,5},{2,6},{3,7},{4,0},{5,1},{6,2},{7,3},{8,12},{9,13},{10,... | collective-permute-start | bytes 786440 | tf_op jit(solution)/shard_map/ppermute | solution.py:145
  35.2 0.5 collective-permute-start.8
  35.8 5.5 %collective-permute-done.3 = f32[128,512]{1,0:T(8,128)S(1)} collective-permute-done((f32[128,512]{1,0:T(8,128)S(1)}, f32[128,512]{1,0:T(8,128)S(1)}, u32[]{:S(2)}, u32[]{:S(2)}) %collective-permute-start.3) | collective-permute-done | bytes 262176 | tf_op jit(solution)/shard_map/ppermute | solution.py:145
  41.3 11.6 %collective-permute-done.b_ref = bf16[4096,256]{1,0:T(8,128)(2,1)} collective-permute-done((bf16[4096,256]{1,0:T(8,128)(2,1)}, bf16[4096,256]{1,0:T(8,128)(2,1)}, u32[]{:S(2)}, u32[]{:S(2)}) %collective-permute-start) | collective-permute-done | bytes 2097184 | tf_op jit(solution)/shard_map/ppermute | solution.py:18
  53.0 6.1 %shard_map.76 = (f32[512,256]{1,0:T(8,128)S(1)}, f32[512,256]{1,0:T(8,128)S(1)}) custom-call(s32[1]{0:T(128)} %bitcast.2.bit_ref, bf16[1024,4096]{1,0:T(8,128)(2,1)} %a_ref.9, bf16[4096,256]{1,0:T(8,128)(2,1)} %collective-permute-done.b_ref), custom_call_target="tpu_custom_call" | custom-call | tf_op jit(solution)/shard_map/pallas_call | solution.py:76
  59.0 0.1 collective-permute-start.4
  59.1 3.2 %collective-permute-start.9 = (f32[128,512]{1,0:T(8,128)S(1)}, f32[128,512]{1,0:T(8,128)S(1)}, u32[]{:S(2)}, u32[]{:S(2)}) collective-permute-start(f32[128,512]{1,0:T(8,128)S(1)} %add.59), channel_id=1, source_target_pairs={{0,8},{1,9},{2,10},{3,11},{4,12},{5,13},{6,14},{7,15},{8,0},{9,1},... | collective-permute-start | bytes 786440 | tf_op jit(solution)/shard_map/ppermute | solution.py:145
  62.4 1.6 %collective-permute-start.5 = (f32[256,256]{1,0:T(8,128)S(1)}, f32[256,256]{1,0:T(8,128)S(1)}, u32[]{:S(2)}, u32[]{:S(2)}) collective-permute-start(f32[256,256]{1,0:T(8,128)S(1)} %get-tuple-element.51), channel_id=1, source_target_pairs={{0,2},{1,3},{2,0},{3,1},{4,6},{5,7},{6,4},{7,5},{8,10},{9,11},{10,... | collective-permute-start | bytes 786440 | tf_op jit(solution)/shard_map/ppermute | solution.py:145
  63.9 1.5 %collective-permute-start.15 = (bf16[3072,128]{1,0:T(8,128)(2,1)S(1)}, bf16[3072,128]{1,0:T(8,128)(2,1)S(1)}, u32[]{:S(2)}, u32[]{:S(2)}) collective-permute-start(bf16[3072,128]{1,0:T(8,128)(2,1)S(1)} %copy-done.1), channel_id=1, source_target_pairs={{0,16},{16,0},{1,17},{17,1},{2,18},{18,2},{3,19},{19,3},{4,20},{20... | collective-permute-start | bytes 2359304 | tf_op jit(solution)/shard_map/ppermute | solution.py:18
  65.5 9.4 %collective-permute-done.9 = f32[128,512]{1,0:T(8,128)S(1)} collective-permute-done((f32[128,512]{1,0:T(8,128)S(1)}, f32[128,512]{1,0:T(8,128)S(1)}, u32[]{:S(2)}, u32[]{:S(2)}) %collective-permute-start.9) | collective-permute-done | bytes 262176 | tf_op jit(solution)/shard_map/ppermute | solution.py:145
  74.9 0.4 collective-permute-done.8.b_ref
  75.3 5.7 %shard_map.79 = (f32[512,128]{1,0:T(8,128)S(1)}, f32[512,128]{1,0:T(8,128)S(1)}) custom-call(s32[1]{0:T(128)} %bitcast.2.bit_ref, bf16[1024,4096]{1,0:T(8,128)(2,1)} %a_ref.9, bf16[4096,128]{1,0:T(8,128)(2,1)S(1)} %collective-permute-done.8.b_ref), custom_call_target="tpu_custom_call" | custom-call | tf_op jit(solution)/shard_map/pallas_call | solution.py:76
  81.1 2.2 %collective-permute-start.6 = (f32[128,256]{1,0:T(8,128)S(1)}, f32[128,256]{1,0:T(8,128)S(1)}, u32[]{:S(2)}, u32[]{:S(2)}) collective-permute-start(f32[128,256]{1,0:T(8,128)S(1)} %get-tuple-element.53), channel_id=1, source_target_pairs={{0,4},{1,5},{2,6},{3,7},{4,0},{5,1},{6,2},{7,3},{8,12},{9,13},{10,... | collective-permute-start | bytes 393224 | tf_op jit(solution)/shard_map/ppermute | solution.py:145
  83.3 4.1 %collective-permute-done.6 = f32[128,256]{1,0:T(8,128)S(1)} collective-permute-done((f32[128,256]{1,0:T(8,128)S(1)}, f32[128,256]{1,0:T(8,128)S(1)}, u32[]{:S(2)}, u32[]{:S(2)}) %collective-permute-start.6) | collective-permute-done | bytes 131104 | tf_op jit(solution)/shard_map/ppermute | solution.py:145
  87.4 2.8 %collective-permute-start.7 = (f32[128,256]{1,0:T(8,128)S(1)}, f32[128,256]{1,0:T(8,128)S(1)}, u32[]{:S(2)}, u32[]{:S(2)}) collective-permute-start(f32[128,256]{1,0:T(8,128)S(1)} %add.60), channel_id=1, source_target_pairs={{0,8},{1,9},{2,10},{3,11},{4,12},{5,13},{6,14},{7,15},{8,0},{9,1},... | collective-permute-start | bytes 393224 | tf_op jit(solution)/shard_map/ppermute | solution.py:145
  90.2 1.6 %collective-permute-start.11 = (f32[256,128]{1,0:T(8,128)S(1)}, f32[256,128]{1,0:T(8,128)S(1)}, u32[]{:S(2)}, u32[]{:S(2)}) collective-permute-start(f32[256,128]{1,0:T(8,128)S(1)} %get-tuple-element.59), channel_id=1, source_target_pairs={{0,2},{1,3},{2,0},{3,1},{4,6},{5,7},{6,4},{7,5},{8,10},{9,11},{10,... | collective-permute-start | bytes 393224 | tf_op jit(solution)/shard_map/ppermute | solution.py:145
  91.8 1.5 %collective-permute-start.14 = (bf16[1024,128]{1,0:T(8,128)(2,1)S(1)}, bf16[1024,128]{1,0:T(8,128)(2,1)S(1)}, u32[]{:S(2)}, u32[]{:S(2)}) collective-permute-start(bf16[1024,128]{1,0:T(8,128)(2,1)S(1)} %slice.23), channel_id=1, source_target_pairs={{0,16},{16,0},{1,17},{17,1},{2,18},{18,2},{3,19},{19,3},{4,20},{20... | collective-permute-start | bytes 786440 | tf_op jit(solution)/shard_map/ppermute | solution.py:18
  93.3 3.1 %collective-permute-done.7 = f32[128,256]{1,0:T(8,128)S(1)} collective-permute-done((f32[128,256]{1,0:T(8,128)S(1)}, f32[128,256]{1,0:T(8,128)S(1)}, u32[]{:S(2)}, u32[]{:S(2)}) %collective-permute-start.7) | collective-permute-done | bytes 131104 | tf_op jit(solution)/shard_map/ppermute | solution.py:145
  96.5 0.7 collective-permute-start.12
  97.2 3.6 %collective-permute-done.12 = f32[128,128]{1,0:T(8,128)S(1)} collective-permute-done((f32[128,128]{1,0:T(8,128)S(1)}, f32[128,128]{1,0:T(8,128)S(1)}, u32[]{:S(2)}, u32[]{:S(2)}) %collective-permute-start.12) | collective-permute-done | bytes 65568 | tf_op jit(solution)/shard_map/ppermute | solution.py:145
  100.8 2.1 %collective-permute-start.13 = (f32[128,128]{1,0:T(8,128)S(1)}, f32[128,128]{1,0:T(8,128)S(1)}, u32[]{:S(2)}, u32[]{:S(2)}) collective-permute-start(f32[128,128]{1,0:T(8,128)S(1)} %add.63), channel_id=1, source_target_pairs={{0,8},{1,9},{2,10},{3,11},{4,12},{5,13},{6,14},{7,15},{8,0},{9,1},... | collective-permute-start | bytes 196616 | tf_op jit(solution)/shard_map/ppermute | solution.py:145
  102.9 4.7 %shard_map.82.refs_0_ = f32[1024,128]{1,0:T(8,128)S(1)} custom-call(bf16[1024,4096]{1,0:T(8,128)(2,1)} %a_ref.9, bf16[3072,128]{1,0:T(8,128)(2,1)S(1)} %collective-permute-done.15.b_ref), custom_call_target="tpu_custom_call" | custom-call | tf_op jit(solution)/shard_map/pallas_call | solution.py:109
  107.7 2.4 %shard_map.83 = (f32[512,128]{1,0:T(8,128)S(1)}, f32[512,128]{1,0:T(8,128)S(1)}) custom-call(s32[1]{0:T(128)} %bitcast.2.bit_ref, bf16[1024,4096]{1,0:T(8,128)(2,1)} %a_ref.9, bf16[1024,128]{1,0:T(8,128)(2,1)S(1)} %collective-permute-done.14.b_ref, f32[1024,128]{1,0:T(8,128)S(1)} %shard_map.82.refs_0_), custom_call_target="tpu_custom_call" | custom-call | tf_op jit(solution)/shard_map/pallas_call | solution.py:76
  110.2 0.2 select_reduce_fusion.1
  110.4 0.1 broadcast_add_fusion
  110.5 0.1 add.73
  110.5 1.2 collective-permute-done.16.came_ref
  111.7 1.6 %collective-permute-start.17 = (f32[256,128]{1,0:T(8,128)S(1)}, f32[256,128]{1,0:T(8,128)S(1)}, u32[]{:S(2)}, u32[]{:S(2)}) collective-permute-start(f32[256,128]{1,0:T(8,128)S(1)} %get-tuple-element.70), channel_id=1, source_target_pairs={{0,2},{1,3},{2,0},{3,1},{4,6},{5,7},{6,4},{7,5},{8,10},{9,11},{10,... | collective-permute-start | bytes 393224 | tf_op jit(solution)/shard_map/ppermute | solution.py:145
  113.3 4.0 %collective-permute-done.17.came_ref = f32[256,128]{1,0:T(8,128)S(1)} collective-permute-done((f32[256,128]{1,0:T(8,128)S(1)}, f32[256,128]{1,0:T(8,128)S(1)}, u32[]{:S(2)}, u32[]{:S(2)}) %collective-permute-start.17) | collective-permute-done | bytes 131104 | tf_op jit(solution)/shard_map/ppermute | solution.py:145
  117.3 2.1 %collective-permute-start.18 = (f32[128,128]{1,0:T(8,128)S(1)}, f32[128,128]{1,0:T(8,128)S(1)}, u32[]{:S(2)}, u32[]{:S(2)}) collective-permute-start(f32[128,128]{1,0:T(8,128)S(1)} %get-tuple-element.72), channel_id=1, source_target_pairs={{0,4},{1,5},{2,6},{3,7},{4,0},{5,1},{6,2},{7,3},{8,12},{9,13},{10,... | collective-permute-start | bytes 196616 | tf_op jit(solution)/shard_map/ppermute | solution.py:145
  119.4 0.2 select_reduce_fusion
  119.6 2.1 %collective-permute-done.18 = f32[128,128]{1,0:T(8,128)S(1)} collective-permute-done((f32[128,128]{1,0:T(8,128)S(1)}, f32[128,128]{1,0:T(8,128)S(1)}, u32[]{:S(2)}, u32[]{:S(2)}) %collective-permute-start.18) | collective-permute-done | bytes 65568 | tf_op jit(solution)/shard_map/ppermute | solution.py:145
  121.7 0.9 collective-permute-start.19
  122.6 4.3 %collective-permute-done.19 = f32[128,128]{1,0:T(8,128)S(1)} collective-permute-done((f32[128,128]{1,0:T(8,128)S(1)}, f32[128,128]{1,0:T(8,128)S(1)}, u32[]{:S(2)}, u32[]{:S(2)}) %collective-permute-start.19) | collective-permute-done | bytes 65568 | tf_op jit(solution)/shard_map/ppermute | solution.py:145
  127.0 0.7 gather_fusion
  127.7 0.2 copy.14
  128.0 0.3 copy.15
  128.3 0.2 copy.16
  128.5 0.8 subtract_divide_fusion
  (45 shorter events, 0.8 us)
Async XLA Ops:
  0.0 6.2 %copy-start = (bf16[4096,512]{1,0:T(8,128)(2,1)S(1)}, bf16[4096,512]{1,0:T(8,128)(2,1)}, u32[]{:S(2)}) copy-start(bf16[4096,512]{1,0:T(8,128)(2,1)} %b_ref) | copy-start | bytes 12582916
  3.2 49.7 %collective-permute-start = (bf16[4096,256]{1,0:T(8,128)(2,1)}, bf16[4096,256]{1,0:T(8,128)(2,1)}, u32[]{:S(2)}, u32[]{:S(2)}) collective-permute-start(bf16[4096,256]{1,0:T(8,128)(2,1)} %slice.20), channel_id=1, source_target_pairs={{0,16},{16,0},{1,17},{17,1},{2,18},{18,2},{3,19},{19,3},{4,20},{20... | collective-permute-start | bytes 6291464 | tf_op jit(solution)/shard_map/ppermute | solution.py:18
  16.7 2.7 %collective-permute-start.1 = (f32[512,512]{1,0:T(8,128)S(1)}, f32[512,512]{1,0:T(8,128)S(1)}, u32[]{:S(2)}, u32[]{:S(2)}) collective-permute-start(f32[512,512]{1,0:T(8,128)S(1)} %get-tuple-element.42), channel_id=1, source_target_pairs={{0,1},{1,0},{2,3},{3,2},{4,5},{5,4},{6,7},{7,6},{8,9},{9,8},{10,11... | collective-permute-start | bytes 3145736 | tf_op jit(solution)/shard_map/ppermute | solution.py:145
  19.5 14.0 %collective-permute-start.2 = (f32[256,512]{1,0:T(8,128)S(1)}, f32[256,512]{1,0:T(8,128)S(1)}, u32[]{:S(2)}, u32[]{:S(2)}) collective-permute-start(f32[256,512]{1,0:T(8,128)S(1)} %get-tuple-element.44), channel_id=1, source_target_pairs={{0,2},{1,3},{2,0},{3,1},{4,6},{5,7},{6,4},{7,5},{8,10},{9,11},{10,... | collective-permute-start | bytes 1572872 | tf_op jit(solution)/shard_map/ppermute | solution.py:145
  33.6 7.7 %collective-permute-start.3 = (f32[128,512]{1,0:T(8,128)S(1)}, f32[128,512]{1,0:T(8,128)S(1)}, u32[]{:S(2)}, u32[]{:S(2)}) collective-permute-start(f32[128,512]{1,0:T(8,128)S(1)} %get-tuple-element.46), channel_id=1, source_target_pairs={{0,4},{1,5},{2,6},{3,7},{4,0},{5,1},{6,2},{7,3},{8,12},{9,13},{10,... | collective-permute-start | bytes 786440 | tf_op jit(solution)/shard_map/ppermute | solution.py:145
  35.2 40.1 %collective-permute-start.8 = (bf16[4096,128]{1,0:T(8,128)(2,1)}, bf16[4096,128]{1,0:T(8,128)(2,1)S(1)}, u32[]{:S(2)}, u32[]{:S(2)}) collective-permute-start(bf16[4096,128]{1,0:T(8,128)(2,1)} %slice.21), channel_id=1, source_target_pairs={{0,16},{16,0},{1,17},{17,1},{2,18},{18,2},{3,19},{19,3},{4,20},{20... | collective-permute-start | bytes 3145736 | tf_op jit(solution)/shard_map/ppermute | solution.py:18
  41.3 22.6 %copy-start.1 = (bf16[3072,128]{1,0:T(8,128)(2,1)S(1)}, bf16[3072,128]{1,0:T(8,128)(2,1)}, u32[]{:S(2)}) copy-start(bf16[3072,128]{1,0:T(8,128)(2,1)} %slice.22) | copy-start | bytes 2359300
  59.0 3.3 %collective-permute-start.4 = (f32[512,256]{1,0:T(8,128)S(1)}, f32[512,256]{1,0:T(8,128)S(1)}, u32[]{:S(2)}, u32[]{:S(2)}) collective-permute-start(f32[512,256]{1,0:T(8,128)S(1)} %get-tuple-element.49), channel_id=1, source_target_pairs={{0,1},{1,0},{2,3},{3,2},{4,5},{5,4},{6,7},{7,6},{8,9},{9,8},{10,11... | collective-permute-start | bytes 1572872 | tf_op jit(solution)/shard_map/ppermute | solution.py:145
  59.1 15.7 %collective-permute-start.9 = (f32[128,512]{1,0:T(8,128)S(1)}, f32[128,512]{1,0:T(8,128)S(1)}, u32[]{:S(2)}, u32[]{:S(2)}) collective-permute-start(f32[128,512]{1,0:T(8,128)S(1)} %add.59), channel_id=1, source_target_pairs={{0,8},{1,9},{2,10},{3,11},{4,12},{5,13},{6,14},{7,15},{8,0},{9,1},... | collective-permute-start | bytes 786440 | tf_op jit(solution)/shard_map/ppermute | solution.py:145
  62.4 12.5 %collective-permute-start.5 = (f32[256,256]{1,0:T(8,128)S(1)}, f32[256,256]{1,0:T(8,128)S(1)}, u32[]{:S(2)}, u32[]{:S(2)}) collective-permute-start(f32[256,256]{1,0:T(8,128)S(1)} %get-tuple-element.51), channel_id=1, source_target_pairs={{0,2},{1,3},{2,0},{3,1},{4,6},{5,7},{6,4},{7,5},{8,10},{9,11},{10,... | collective-permute-start | bytes 786440 | tf_op jit(solution)/shard_map/ppermute | solution.py:145
  63.9 39.0 %collective-permute-start.15 = (bf16[3072,128]{1,0:T(8,128)(2,1)S(1)}, bf16[3072,128]{1,0:T(8,128)(2,1)S(1)}, u32[]{:S(2)}, u32[]{:S(2)}) collective-permute-start(bf16[3072,128]{1,0:T(8,128)(2,1)S(1)} %copy-done.1), channel_id=1, source_target_pairs={{0,16},{16,0},{1,17},{17,1},{2,18},{18,2},{3,19},{19,3},{4,20},{20... | collective-permute-start | bytes 2359304 | tf_op jit(solution)/shard_map/ppermute | solution.py:18
  81.0 9.2 %collective-permute-start.10 = (f32[512,128]{1,0:T(8,128)S(1)}, f32[512,128]{1,0:T(8,128)S(1)}, u32[]{:S(2)}, u32[]{:S(2)}) collective-permute-start(f32[512,128]{1,0:T(8,128)S(1)} %get-tuple-element.56), channel_id=1, source_target_pairs={{0,1},{1,0},{2,3},{3,2},{4,5},{5,4},{6,7},{7,6},{8,9},{9,8},{10,11... | collective-permute-start | bytes 786440 | tf_op jit(solution)/shard_map/ppermute | solution.py:145
  81.1 6.3 %collective-permute-start.6 = (f32[128,256]{1,0:T(8,128)S(1)}, f32[128,256]{1,0:T(8,128)S(1)}, u32[]{:S(2)}, u32[]{:S(2)}) collective-permute-start(f32[128,256]{1,0:T(8,128)S(1)} %get-tuple-element.53), channel_id=1, source_target_pairs={{0,4},{1,5},{2,6},{3,7},{4,0},{5,1},{6,2},{7,3},{8,12},{9,13},{10,... | collective-permute-start | bytes 393224 | tf_op jit(solution)/shard_map/ppermute | solution.py:145
  87.4 9.0 %collective-permute-start.7 = (f32[128,256]{1,0:T(8,128)S(1)}, f32[128,256]{1,0:T(8,128)S(1)}, u32[]{:S(2)}, u32[]{:S(2)}) collective-permute-start(f32[128,256]{1,0:T(8,128)S(1)} %add.60), channel_id=1, source_target_pairs={{0,8},{1,9},{2,10},{3,11},{4,12},{5,13},{6,14},{7,15},{8,0},{9,1},... | collective-permute-start | bytes 393224 | tf_op jit(solution)/shard_map/ppermute | solution.py:145
  90.2 6.2 %collective-permute-start.11 = (f32[256,128]{1,0:T(8,128)S(1)}, f32[256,128]{1,0:T(8,128)S(1)}, u32[]{:S(2)}, u32[]{:S(2)}) collective-permute-start(f32[256,128]{1,0:T(8,128)S(1)} %get-tuple-element.59), channel_id=1, source_target_pairs={{0,2},{1,3},{2,0},{3,1},{4,6},{5,7},{6,4},{7,5},{8,10},{9,11},{10,... | collective-permute-start | bytes 393224 | tf_op jit(solution)/shard_map/ppermute | solution.py:145
  91.8 15.9 %collective-permute-start.14 = (bf16[1024,128]{1,0:T(8,128)(2,1)S(1)}, bf16[1024,128]{1,0:T(8,128)(2,1)S(1)}, u32[]{:S(2)}, u32[]{:S(2)}) collective-permute-start(bf16[1024,128]{1,0:T(8,128)(2,1)S(1)} %slice.23), channel_id=1, source_target_pairs={{0,16},{16,0},{1,17},{17,1},{2,18},{18,2},{3,19},{19,3},{4,20},{20... | collective-permute-start | bytes 786440 | tf_op jit(solution)/shard_map/ppermute | solution.py:18
  96.5 4.3 %collective-permute-start.12 = (f32[128,128]{1,0:T(8,128)S(1)}, f32[128,128]{1,0:T(8,128)S(1)}, u32[]{:S(2)}, u32[]{:S(2)}) collective-permute-start(f32[128,128]{1,0:T(8,128)S(1)} %get-tuple-element.62), channel_id=1, source_target_pairs={{0,4},{1,5},{2,6},{3,7},{4,0},{5,1},{6,2},{7,3},{8,12},{9,13},{10,... | collective-permute-start | bytes 196616 | tf_op jit(solution)/shard_map/ppermute | solution.py:145
  100.8 6.8 %collective-permute-start.13 = (f32[128,128]{1,0:T(8,128)S(1)}, f32[128,128]{1,0:T(8,128)S(1)}, u32[]{:S(2)}, u32[]{:S(2)}) collective-permute-start(f32[128,128]{1,0:T(8,128)S(1)} %add.63), channel_id=1, source_target_pairs={{0,8},{1,9},{2,10},{3,11},{4,12},{5,13},{6,14},{7,15},{8,0},{9,1},... | collective-permute-start | bytes 196616 | tf_op jit(solution)/shard_map/ppermute | solution.py:145
  107.7 2.5 %copy-start.2 = (f32[512]{0:T(512)S(1)}, f32[512]{0:T(512)}, u32[]{:S(2)}) copy-start(f32[512]{0:T(512)} %param.13) | copy-start | bytes 6148
  107.7 2.5 %copy-start.4 = (s32[32]{0:T(128)S(1)}, s32[32]{0:T(128)}, u32[]{:S(2)}) copy-start(s32[32]{0:T(128)} %param.11) | copy-start | bytes 388
  107.7 5.6 %copy-start.6 = (s32[64]{0:T(128)S(1)}, s32[64]{0:T(128)}, u32[]{:S(2)}) copy-start(s32[64]{0:T(128)} %param.10) | copy-start | bytes 772
  107.7 11.7 %copy-start.3 = (s32[64,2]{0,1:T(2,128)S(1)}, s32[64,2]{0,1:T(2,128)}, u32[]{:S(2)}) copy-start(s32[64,2]{0,1:T(2,128)} %param.9) | copy-start | bytes 1540
  107.7 11.7 %copy-start.5 = (f32[96]{0:T(128)S(1)}, f32[96]{0:T(128)}, u32[]{:S(2)}) copy-start(f32[96]{0:T(128)} %param.12) | copy-start | bytes 1156
  110.1 1.6 %collective-permute-start.16 = (f32[512,128]{1,0:T(8,128)S(1)}, f32[512,128]{1,0:T(8,128)S(1)}, u32[]{:S(2)}, u32[]{:S(2)}) collective-permute-start(f32[512,128]{1,0:T(8,128)S(1)} %get-tuple-element.68), channel_id=1, source_target_pairs={{0,1},{1,0},{2,3},{3,2},{4,5},{5,4},{6,7},{7,6},{8,9},{9,8},{10,11... | collective-permute-start | bytes 786440 | tf_op jit(solution)/shard_map/ppermute | solution.py:145
  111.7 5.6 %collective-permute-start.17 = (f32[256,128]{1,0:T(8,128)S(1)}, f32[256,128]{1,0:T(8,128)S(1)}, u32[]{:S(2)}, u32[]{:S(2)}) collective-permute-start(f32[256,128]{1,0:T(8,128)S(1)} %get-tuple-element.70), channel_id=1, source_target_pairs={{0,2},{1,3},{2,0},{3,1},{4,6},{5,7},{6,4},{7,5},{8,10},{9,11},{10,... | collective-permute-start | bytes 393224 | tf_op jit(solution)/shard_map/ppermute | solution.py:145
  117.3 4.3 %collective-permute-start.18 = (f32[128,128]{1,0:T(8,128)S(1)}, f32[128,128]{1,0:T(8,128)S(1)}, u32[]{:S(2)}, u32[]{:S(2)}) collective-permute-start(f32[128,128]{1,0:T(8,128)S(1)} %get-tuple-element.72), channel_id=1, source_target_pairs={{0,4},{1,5},{2,6},{3,7},{4,0},{5,1},{6,2},{7,3},{8,12},{9,13},{10,... | collective-permute-start | bytes 196616 | tf_op jit(solution)/shard_map/ppermute | solution.py:145
  121.7 5.2 %collective-permute-start.19 = (f32[128,128]{1,0:T(8,128)S(1)}, f32[128,128]{1,0:T(8,128)S(1)}, u32[]{:S(2)}, u32[]{:S(2)}) collective-permute-start(f32[128,128]{1,0:T(8,128)S(1)} %add.65), channel_id=1, source_target_pairs={{0,8},{1,9},{2,10},{3,11},{4,12},{5,13},{6,14},{7,15},{8,0},{9,1},... | collective-permute-start | bytes 196616 | tf_op jit(solution)/shard_map/ppermute | solution.py:145

commit v4 on v3

--- a/solution.py
+++ b/solution.py
@@ -8,6 +8,7 @@
 from jax.sharding import PartitionSpec as P
 
 DEPTH_CUTS = 4
+OWN_SPLITS = 2
 PRODUCT_BYTES = 51 * 1024 * 1024
 SUM_BYTES = 8 * 1024 * 1024
 
@@ -43,9 +44,9 @@
     return jnp.concatenate(ordered, axis=1)
 
 
-def product_kernel(steps, order, has_base, bit_ref, a_ref, b_ref, *refs):
+def product_kernel(steps, order, splits, has_base, bit_ref, a_ref, b_ref, *refs):
     base_ref = refs[0] if has_base else None
-    keep_ref, send_ref, total_ref = refs[-3:]
+    out_refs, total_ref = refs[-1 - 2 * splits : -1], refs[-1]
     step = pl.program_id(0)
     term = jnp.dot(a_ref[...], b_ref[...], preferred_element_type=jnp.float32)
 
@@ -59,31 +60,34 @@
 
     @pl.when(step == steps - 1)
     def _():
-        rows = keep_ref.shape[0] // len(order)
-        for out_ref, bit in ((keep_ref, bit_ref[0]), (send_ref, 1 - bit_ref[0])):
+        rows, width = out_refs[0].shape
+        rows = rows // len(order)
+        for index, out_ref in enumerate(out_refs):
+            bit = 1 - bit_ref[0] if index % 2 else bit_ref[0]
+            columns = slice(index // 2 * width, (index // 2 + 1) * width)
             for place, block in enumerate(order):
                 start = pl.multiple_of((block + bit) * rows, rows)
-                out_ref[place * rows : (place + 1) * rows, :] = total_ref[pl.ds(start, rows), :]
-
-
-def multiplied(amplitudes, columns, bit, order, first=0, base=None):
+                out_ref[place * rows : (place + 1) * rows, :] = total_ref[pl.ds(start, rows), columns]
+
+
+def multiplied(amplitudes, columns, bit, order, first=0, base=None, splits=1):
     rows, depth = amplitudes.shape
     width = columns.shape[1]
     part = depth // DEPTH_CUTS
     steps = columns.shape[0] // part
-    shape = jax.ShapeDtypeStruct((rows // 2, width), jnp.float32)
+    shape = jax.ShapeDtypeStruct((rows // 2, width // splits), jnp.float32)
     bases = [] if base is None else [base]
     return pl.pallas_call(
-        functools.partial(product_kernel, steps, order, base is not None),
+        functools.partial(product_kernel, steps, order, splits, base is not None),
         grid=(steps,),
-        out_shape=[shape] * 2,
+        out_shape=[shape] * (2 * splits),
         in_specs=[
             pl.BlockSpec(memory_space=pltpu.SMEM),
             pl.BlockSpec((rows, part), lambda k: (0, k + first)),
             pl.BlockSpec((part, width), lambda k: (k, 0)),
         ]
         + [pl.BlockSpec((rows, width), lambda k: (0, 0)) for _ in bases],
-        out_specs=[pl.BlockSpec(shape.shape, lambda k: (0, 0))] * 2,
+        out_specs=[pl.BlockSpec(shape.shape, lambda k: (0, 0))] * (2 * splits),
         scratch_shapes=[pltpu.VMEM((rows, width), jnp.float32)],
         compiler_params=pltpu.CompilerParams(vmem_limit_bytes=PRODUCT_BYTES),
         cost_estimate=pl.CostEstimate(flops=0, bytes_accessed=0, transcendentals=0),
@@ -179,20 +183,17 @@
     late = integrals.shape[0] // DEPTH_CUTS * (DEPTH_CUTS - 1)
     pieces = [first] + [rest[:, low:high] for low, high in cuts[1:-1]] + [rest[:late, low:high], rest[late:, low:high]]
     in_flight = [sent(pieces[0]), sent(pieces[1])]
-    own_product = multiplied(amplitudes, after(rest, pieces), bits[0], order)
-    own_sum, own_stages = exchanged_sum(own_product, bits)
-    sums = [[own_sum]] + [[] for _ in range(1, count)]
-    earlier, gates = own_stages[2], {}
+    own_product = multiplied(amplitudes, after(rest, pieces), bits[0], order, splits=OWN_SPLITS)
+    own_sums = [exchanged_sum(own_product[2 * part : 2 * part + 2], bits)[0] for part in range(OWN_SPLITS)]
+    sums = [own_sums] + [[] for _ in range(1, count)]
+    earlier, gates = own_sums, {}
     for step in range(len(pieces)):
-        if step == 1:
-            earlier = (earlier, own_sum)
         arrived, earlier = lax.optimization_barrier((in_flight[step], earlier))
         if step + 2 < len(pieces):
             in_flight.append(sent(after(pieces[step + 2], arrived)))
         if step == len(pieces) - 2:
             bases = [plain_product(amplitudes, columns) for columns in arrived]
-            earlier = (gates[2], bases)
-            gates = {}
+            earlier = (stages[2], bases)
             continue
         for shift in range(1, count):
             if step < len(cuts) - 1:
@@ -201,7 +202,7 @@
                 product = multiplied(amplitudes, arrived[shift - 1], bits[0], order, DEPTH_CUTS - 1, bases[shift - 1])
             total, stages = exchanged_sum(product, bits, gates)
             sums[shift].append(total)
-            earlier, gates = stages[1], {1: stages[2], 2: total}
+            earlier, gates = stages[2] if step < len(cuts) - 2 else stages[1], {1: total}
 
     both = in_column_order([jnp.concatenate(parts, axis=1) for parts in sums], count)
     mine = jnp.where(upper, both[rows:], both[:rows])

time: 130 us -> 130 us (level)
  starting transfers between devices: 28.7 us -> 33.8 us
  waiting for transfers between devices: 64.4 us -> 59.5 us
    ppermute x4, waiting for transfers between devices: 12 us -> 4.24 us  [passed_along(): return lax.ppermute(value, axis, pairs)]
    ppermute x16 -> x20, starting transfers between devices: 22.2 us -> 27.3 us  [flipped_along(): lax.ppermute(value, axis, [(source, source ^ bits) for source in range(co...]
    ppermute x16 -> x20, waiting for transfers between devices: 52.4 us -> 55.3 us  [flipped_along(): lax.ppermute(value, axis, [(source, source ^ bits) for source in range(co...]
  transfers between devices with their start and end apart: 20 -> 24, of which waited for: 13 -> 17; matrix products, arithmetic and copies ran while one was open for 2% -> 3% of each run, Pallas kernels for 19% -> 19%
where the time goes in v4:
time: 130 us
  waiting for transfers between devices  59.5 us (46%)
  starting transfers between devices  33.8 us (26%)
  Pallas kernels  27.4 us (21%)
  local copies, waits for them, and re-layouts  7.61 us (6%)
  other arithmetic  1.54 us (1%)
    ppermute x20, waiting for transfers between devices, flipped_along(): lax.ppermute(value, axis, [(source, source ^ bits) for source in range(co...  55.3 us
    ppermute x20, starting transfers between devices, flipped_along(): lax.ppermute(value, axis, [(source, source ^ bits) for source in range(co...  27.3 us
    pallas_call x4, Pallas kernels, multiplied(): pl.pallas_call(functools.partial(product_kernel, steps, order, splits, ba...  22.3 us
    ppermute x4, starting transfers between devices, passed_along(): return lax.ppermute(value, axis, pairs)  6.51 us
    pallas_call x1, Pallas kernels, plain_product(): pl.pallas_call(plain_kernel, grid=(columns.shape[0] // part,), out_shape=...  4.7 us
    ppermute x4, waiting for transfers between devices, passed_along(): return lax.ppermute(value, axis, pairs)  4.24 us
    slice x1, local copies, waits for them, and re-layouts, per_device(): first = integrals[:, cuts[0][0]:cuts[0][1]]  3.24 us
  transfers between devices with their start and end apart: 24, of which 17 were waited for; matrix products, arithmetic and copies ran while one was open for 3% of the time, Pallas kernels for 19%

profile of v4, /device:TPU:0, one launch (start us, length us, event | category | flops | bytes accessed | tf_op | source)
XLA Modules:
  0.0 130.2 jit_solution(8048787141866419140)
XLA Ops:
  0.0 3.2 %slice.20 = bf16[4096,256]{1,0:T(8,128)(2,1)} slice(bf16[4096,512]{1,0:T(8,128)(2,1)} %b_ref), slice={[0:4096], [0:256]} | slice | bytes 4194304 | tf_op jit(solution)/shard_map/slice | solution.py:180
  3.2 3.0 %collective-permute-start = (bf16[4096,256]{1,0:T(8,128)(2,1)}, bf16[4096,256]{1,0:T(8,128)(2,1)}, u32[]{:S(2)}, u32[]{:S(2)}) collective-permute-start(bf16[4096,256]{1,0:T(8,128)(2,1)} %slice.20), channel_id=1, source_target_pairs={{0,16},{16,0},{1,17},{17,1},{2,18},{18,2},{3,19},{19,3},{4,20},{20... | collective-permute-start | bytes 6291464 | tf_op jit(solution)/shard_map/ppermute | solution.py:19
  6.2 1.1 slice.21
  7.4 1.0 slice.22
  8.4 0.7 slice.23
  9.1 8.2 %shard_map.73 = (f32[512,256]{1,0:T(8,128)S(1)}, f32[512,256]{1,0:T(8,128)S(1)}, f32[512,256]{1,0:T(8,128)S(1)}, f32[512,256]{1,0:T(8,128)S(1)}) custom-call(s32[1]{0:T(128)} %bitcast.2.bit_ref, bf16[1024,4096]{1,0:T(8,128)(2,1)} %a_ref.9, bf16[4096,512]{1,0:T(8,128)(2,1)} %b_ref), custom_call_target="tpu_custom_call" | custom-call | tf_op jit(solution)/shard_map/pallas_call | solution.py:80
  17.4 0.5 collective-permute-start.5
  17.9 1.4 %collective-permute-done.1.came_ref = f32[512,256]{1,0:T(8,128)S(1)} collective-permute-done((f32[512,256]{1,0:T(8,128)S(1)}, f32[512,256]{1,0:T(8,128)S(1)}, u32[]{:S(2)}, u32[]{:S(2)}) %collective-permute-start.1) | collective-permute-done | bytes 524320 | tf_op jit(solution)/shard_map/ppermute | solution.py:149
  19.4 1.6 %collective-permute-start.2 = (f32[256,256]{1,0:T(8,128)S(1)}, f32[256,256]{1,0:T(8,128)S(1)}, u32[]{:S(2)}, u32[]{:S(2)}) collective-permute-start(f32[256,256]{1,0:T(8,128)S(1)} %get-tuple-element.50), channel_id=1, source_target_pairs={{0,2},{1,3},{2,0},{3,1},{4,6},{5,7},{6,4},{7,5},{8,10},{9,11},{10,... | collective-permute-start | bytes 786440 | tf_op jit(solution)/shard_map/ppermute | solution.py:149
  21.0 0.7 collective-permute-start.6
  21.7 6.9 %collective-permute-done.2.came_ref = f32[256,256]{1,0:T(8,128)S(1)} collective-permute-done((f32[256,256]{1,0:T(8,128)S(1)}, f32[256,256]{1,0:T(8,128)S(1)}, u32[]{:S(2)}, u32[]{:S(2)}) %collective-permute-start.2) | collective-permute-done | bytes 262176 | tf_op jit(solution)/shard_map/ppermute | solution.py:149
  28.6 1.6 %collective-permute-start.3 = (f32[128,256]{1,0:T(8,128)S(1)}, f32[128,256]{1,0:T(8,128)S(1)}, u32[]{:S(2)}, u32[]{:S(2)}) collective-permute-start(f32[128,256]{1,0:T(8,128)S(1)} %get-tuple-element.52), channel_id=1, source_target_pairs={{0,4},{1,5},{2,6},{3,7},{4,0},{5,1},{6,2},{7,3},{8,12},{9,13},{10,... | collective-permute-start | bytes 393224 | tf_op jit(solution)/shard_map/ppermute | solution.py:149
  30.3 3.1 %collective-permute-done.6.came_ref = f32[256,256]{1,0:T(8,128)S(1)} collective-permute-done((f32[256,256]{1,0:T(8,128)S(1)}, f32[256,256]{1,0:T(8,128)S(1)}, u32[]{:S(2)}, u32[]{:S(2)}) %collective-permute-start.6) | collective-permute-done | bytes 262176 | tf_op jit(solution)/shard_map/ppermute | solution.py:149
  33.5 1.6 %collective-permute-start.7 = (f32[128,256]{1,0:T(8,128)S(1)}, f32[128,256]{1,0:T(8,128)S(1)}, u32[]{:S(2)}, u32[]{:S(2)}) collective-permute-start(f32[128,256]{1,0:T(8,128)S(1)} %get-tuple-element.58), channel_id=1, source_target_pairs={{0,4},{1,5},{2,6},{3,7},{4,0},{5,1},{6,2},{7,3},{8,12},{9,13},{10,... | collective-permute-start | bytes 393224 | tf_op jit(solution)/shard_map/ppermute | solution.py:149
  35.1 2.6 %collective-permute-start.4 = (f32[128,256]{1,0:T(8,128)S(1)}, f32[128,256]{1,0:T(8,128)S(1)}, u32[]{:S(2)}, u32[]{:S(2)}) collective-permute-start(f32[128,256]{1,0:T(8,128)S(1)} %add.65), channel_id=1, source_target_pairs={{0,8},{1,9},{2,10},{3,11},{4,12},{5,13},{6,14},{7,15},{8,0},{9,1},... | collective-permute-start | bytes 393224 | tf_op jit(solution)/shard_map/ppermute | solution.py:149
  37.8 2.2 %collective-permute-done.7 = f32[128,256]{1,0:T(8,128)S(1)} collective-permute-done((f32[128,256]{1,0:T(8,128)S(1)}, f32[128,256]{1,0:T(8,128)S(1)}, u32[]{:S(2)}, u32[]{:S(2)}) %collective-permute-start.7) | collective-permute-done | bytes 131104 | tf_op jit(solution)/shard_map/ppermute | solution.py:149
  40.0 2.4 %collective-permute-start.8 = (f32[128,256]{1,0:T(8,128)S(1)}, f32[128,256]{1,0:T(8,128)S(1)}, u32[]{:S(2)}, u32[]{:S(2)}) collective-permute-start(f32[128,256]{1,0:T(8,128)S(1)} %add.67), channel_id=1, source_target_pairs={{0,8},{1,9},{2,10},{3,11},{4,12},{5,13},{6,14},{7,15},{8,0},{9,1},... | collective-permute-start | bytes 393224 | tf_op jit(solution)/shard_map/ppermute | solution.py:149
  42.4 0.5 collective-permute-start.13
  42.9 4.3 %collective-permute-done.4 = f32[128,256]{1,0:T(8,128)S(1)} collective-permute-done((f32[128,256]{1,0:T(8,128)S(1)}, f32[128,256]{1,0:T(8,128)S(1)}, u32[]{:S(2)}, u32[]{:S(2)}) %collective-permute-start.4) | collective-permute-done | bytes 131104 | tf_op jit(solution)/shard_map/ppermute | solution.py:149
  47.2 1.9 %collective-permute-done.8 = f32[128,256]{1,0:T(8,128)S(1)} collective-permute-done((f32[128,256]{1,0:T(8,128)S(1)}, f32[128,256]{1,0:T(8,128)S(1)}, u32[]{:S(2)}, u32[]{:S(2)}) %collective-permute-start.8) | collective-permute-done | bytes 131104 | tf_op jit(solution)/shard_map/ppermute | solution.py:149
  49.1 3.9 %collective-permute-done.b_ref = bf16[4096,256]{1,0:T(8,128)(2,1)} collective-permute-done((bf16[4096,256]{1,0:T(8,128)(2,1)}, bf16[4096,256]{1,0:T(8,128)(2,1)}, u32[]{:S(2)}, u32[]{:S(2)}) %collective-permute-start) | collective-permute-done | bytes 2097184 | tf_op jit(solution)/shard_map/ppermute | solution.py:19
  53.0 6.1 %shard_map.78 = (f32[512,256]{1,0:T(8,128)S(1)}, f32[512,256]{1,0:T(8,128)S(1)}) custom-call(s32[1]{0:T(128)} %bitcast.2.bit_ref, bf16[1024,4096]{1,0:T(8,128)(2,1)} %a_ref.9, bf16[4096,256]{1,0:T(8,128)(2,1)} %collective-permute-done.b_ref), custom_call_target="tpu_custom_call" | custom-call | tf_op jit(solution)/shard_map/pallas_call | solution.py:80
  59.1 1.9 %collective-permute-done.9.came_ref = f32[512,256]{1,0:T(8,128)S(1)} collective-permute-done((f32[512,256]{1,0:T(8,128)S(1)}, f32[512,256]{1,0:T(8,128)S(1)}, u32[]{:S(2)}, u32[]{:S(2)}) %collective-permute-start.9) | collective-permute-done | bytes 524320 | tf_op jit(solution)/shard_map/ppermute | solution.py:149
  61.1 2.1 %collective-permute-start.10 = (f32[256,256]{1,0:T(8,128)S(1)}, f32[256,256]{1,0:T(8,128)S(1)}, u32[]{:S(2)}, u32[]{:S(2)}) collective-permute-start(f32[256,256]{1,0:T(8,128)S(1)} %get-tuple-element.63), channel_id=1, source_target_pairs={{0,2},{1,3},{2,0},{3,1},{4,6},{5,7},{6,4},{7,5},{8,10},{9,11},{10,... | collective-permute-start | bytes 786440 | tf_op jit(solution)/shard_map/ppermute | solution.py:149
  63.2 1.5 %collective-permute-start.19 = (bf16[3072,128]{1,0:T(8,128)(2,1)S(1)}, bf16[3072,128]{1,0:T(8,128)(2,1)S(1)}, u32[]{:S(2)}, u32[]{:S(2)}) collective-permute-start(bf16[3072,128]{1,0:T(8,128)(2,1)S(1)} %copy-done.1), channel_id=1, source_target_pairs={{0,16},{16,0},{1,17},{17,1},{2,18},{18,2},{3,19},{19,3},{4,20},{20... | collective-permute-start | bytes 2359304 | tf_op jit(solution)/shard_map/ppermute | solution.py:19
  64.7 5.1 %collective-permute-done.10.came_ref = f32[256,256]{1,0:T(8,128)S(1)} collective-permute-done((f32[256,256]{1,0:T(8,128)S(1)}, f32[256,256]{1,0:T(8,128)S(1)}, u32[]{:S(2)}, u32[]{:S(2)}) %collective-permute-start.10) | collective-permute-done | bytes 262176 | tf_op jit(solution)/shard_map/ppermute | solution.py:149
  69.8 1.9 %collective-permute-start.11 = (f32[128,256]{1,0:T(8,128)S(1)}, f32[128,256]{1,0:T(8,128)S(1)}, u32[]{:S(2)}, u32[]{:S(2)}) collective-permute-start(f32[128,256]{1,0:T(8,128)S(1)} %get-tuple-element.65), channel_id=1, source_target_pairs={{0,4},{1,5},{2,6},{3,7},{4,0},{5,1},{6,2},{7,3},{8,12},{9,13},{10,... | collective-permute-start | bytes 393224 | tf_op jit(solution)/shard_map/ppermute | solution.py:149
  71.7 3.2 %collective-permute-done.11 = f32[128,256]{1,0:T(8,128)S(1)} collective-permute-done((f32[128,256]{1,0:T(8,128)S(1)}, f32[128,256]{1,0:T(8,128)S(1)}, u32[]{:S(2)}, u32[]{:S(2)}) %collective-permute-start.11) | collective-permute-done | bytes 131104 | tf_op jit(solution)/shard_map/ppermute | solution.py:149
  75.0 0.4 collective-permute-done.13.b_ref
  75.3 5.7 %shard_map.81 = (f32[512,128]{1,0:T(8,128)S(1)}, f32[512,128]{1,0:T(8,128)S(1)}) custom-call(s32[1]{0:T(128)} %bitcast.2.bit_ref, bf16[1024,4096]{1,0:T(8,128)(2,1)} %a_ref.9, bf16[4096,128]{1,0:T(8,128)(2,1)S(1)} %collective-permute-done.13.b_ref), custom_call_target="tpu_custom_call" | custom-call | tf_op jit(solution)/shard_map/pallas_call | solution.py:80
  81.1 3.2 %collective-permute-start.12 = (f32[128,256]{1,0:T(8,128)S(1)}, f32[128,256]{1,0:T(8,128)S(1)}, u32[]{:S(2)}, u32[]{:S(2)}) collective-permute-start(f32[128,256]{1,0:T(8,128)S(1)} %add.69), channel_id=1, source_target_pairs={{0,8},{1,9},{2,10},{3,11},{4,12},{5,13},{6,14},{7,15},{8,0},{9,1},... | collective-permute-start | bytes 393224 | tf_op jit(solution)/shard_map/ppermute | solution.py:149
  84.3 1.5 %collective-permute-start.18 = (bf16[1024,128]{1,0:T(8,128)(2,1)S(1)}, bf16[1024,128]{1,0:T(8,128)(2,1)S(1)}, u32[]{:S(2)}, u32[]{:S(2)}) collective-permute-start(bf16[1024,128]{1,0:T(8,128)(2,1)S(1)} %copy-done.2), channel_id=1, source_target_pairs={{0,16},{16,0},{1,17},{17,1},{2,18},{18,2},{3,19},{19,3},{4,20},{20... | collective-permute-start | bytes 786440 | tf_op jit(solution)/shard_map/ppermute | solution.py:19
  85.8 5.4 %collective-permute-done.12 = f32[128,256]{1,0:T(8,128)S(1)} collective-permute-done((f32[128,256]{1,0:T(8,128)S(1)}, f32[128,256]{1,0:T(8,128)S(1)}, u32[]{:S(2)}, u32[]{:S(2)}) %collective-permute-start.12) | collective-permute-done | bytes 131104 | tf_op jit(solution)/shard_map/ppermute | solution.py:149
  91.3 1.6 %collective-permute-start.15 = (f32[256,128]{1,0:T(8,128)S(1)}, f32[256,128]{1,0:T(8,128)S(1)}, u32[]{:S(2)}, u32[]{:S(2)}) collective-permute-start(f32[256,128]{1,0:T(8,128)S(1)} %get-tuple-element.71), channel_id=1, source_target_pairs={{0,2},{1,3},{2,0},{3,1},{4,6},{5,7},{6,4},{7,5},{8,10},{9,11},{10,... | collective-permute-start | bytes 393224 | tf_op jit(solution)/shard_map/ppermute | solution.py:149
  92.9 3.7 %collective-permute-done.15.came_ref = f32[256,128]{1,0:T(8,128)S(1)} collective-permute-done((f32[256,128]{1,0:T(8,128)S(1)}, f32[256,128]{1,0:T(8,128)S(1)}, u32[]{:S(2)}, u32[]{:S(2)}) %collective-permute-start.15) | collective-permute-done | bytes 131104 | tf_op jit(solution)/shard_map/ppermute | solution.py:149
  96.6 1.0 collective-permute-start.16
  97.6 4.7 %shard_map.84.refs_0_ = f32[1024,128]{1,0:T(8,128)S(1)} custom-call(bf16[1024,4096]{1,0:T(8,128)(2,1)} %a_ref.9, bf16[3072,128]{1,0:T(8,128)(2,1)S(1)} %collective-permute-done.19.b_ref), custom_call_target="tpu_custom_call" | custom-call | tf_op jit(solution)/shard_map/pallas_call | solution.py:113
  102.4 2.4 %shard_map.85 = (f32[512,128]{1,0:T(8,128)S(1)}, f32[512,128]{1,0:T(8,128)S(1)}) custom-call(s32[1]{0:T(128)} %bitcast.2.bit_ref, bf16[1024,4096]{1,0:T(8,128)(2,1)} %a_ref.9, bf16[1024,128]{1,0:T(8,128)(2,1)S(1)} %collective-permute-done.18.b_ref, f32[1024,128]{1,0:T(8,128)S(1)} %shard_map.84.refs_0_), custom_call_target="tpu_custom_call" | custom-call | tf_op jit(solution)/shard_map/pallas_call | solution.py:80
  105.1 3.4 %collective-permute-start.17 = (f32[128,128]{1,0:T(8,128)S(1)}, f32[128,128]{1,0:T(8,128)S(1)}, u32[]{:S(2)}, u32[]{:S(2)}) collective-permute-start(f32[128,128]{1,0:T(8,128)S(1)} %add.71), channel_id=1, source_target_pairs={{0,8},{1,9},{2,10},{3,11},{4,12},{5,13},{6,14},{7,15},{8,0},{9,1},... | collective-permute-start | bytes 196616 | tf_op jit(solution)/shard_map/ppermute | solution.py:149
  108.7 3.8 %collective-permute-done.17 = f32[128,128]{1,0:T(8,128)S(1)} collective-permute-done((f32[128,128]{1,0:T(8,128)S(1)}, f32[128,128]{1,0:T(8,128)S(1)}, u32[]{:S(2)}, u32[]{:S(2)}) %collective-permute-start.17) | collective-permute-done | bytes 65568 | tf_op jit(solution)/shard_map/ppermute | solution.py:149
  112.5 1.4 %collective-permute-start.21 = (f32[256,128]{1,0:T(8,128)S(1)}, f32[256,128]{1,0:T(8,128)S(1)}, u32[]{:S(2)}, u32[]{:S(2)}) collective-permute-start(f32[256,128]{1,0:T(8,128)S(1)} %get-tuple-element.82), channel_id=1, source_target_pairs={{0,2},{1,3},{2,0},{3,1},{4,6},{5,7},{6,4},{7,5},{8,10},{9,11},{10,... | collective-permute-start | bytes 393224 | tf_op jit(solution)/shard_map/ppermute | solution.py:149
  113.9 4.1 %collective-permute-done.21.came_ref = f32[256,128]{1,0:T(8,128)S(1)} collective-permute-done((f32[256,128]{1,0:T(8,128)S(1)}, f32[256,128]{1,0:T(8,128)S(1)}, u32[]{:S(2)}, u32[]{:S(2)}) %collective-permute-start.21) | collective-permute-done | bytes 131104 | tf_op jit(solution)/shard_map/ppermute | solution.py:149
  118.4 4.1 %collective-permute-done.22 = f32[128,128]{1,0:T(8,128)S(1)} collective-permute-done((f32[128,128]{1,0:T(8,128)S(1)}, f32[128,128]{1,0:T(8,128)S(1)}, u32[]{:S(2)}, u32[]{:S(2)}) %collective-permute-start.22) | collective-permute-done | bytes 65568 | tf_op jit(solution)/shard_map/ppermute | solution.py:149
  122.4 1.1 collective-permute-start.23
  123.6 4.2 %collective-permute-done.23 = f32[128,128]{1,0:T(8,128)S(1)} collective-permute-done((f32[128,128]{1,0:T(8,128)S(1)}, f32[128,128]{1,0:T(8,128)S(1)}, u32[]{:S(2)}, u32[]{:S(2)}) %collective-permute-start.23) | collective-permute-done | bytes 65568 | tf_op jit(solution)/shard_map/ppermute | solution.py:149
  127.9 0.7 gather_fusion
  128.9 0.3 copy.15
  129.4 0.8 subtract_divide_fusion
  (59 shorter events, 1.9 us)
Async XLA Ops:
  0.0 6.2 %copy-start = (bf16[4096,512]{1,0:T(8,128)(2,1)S(1)}, bf16[4096,512]{1,0:T(8,128)(2,1)}, u32[]{:S(2)}) copy-start(bf16[4096,512]{1,0:T(8,128)(2,1)} %b_ref) | copy-start | bytes 12582916
  3.2 49.7 %collective-permute-start = (bf16[4096,256]{1,0:T(8,128)(2,1)}, bf16[4096,256]{1,0:T(8,128)(2,1)}, u32[]{:S(2)}, u32[]{:S(2)}) collective-permute-start(bf16[4096,256]{1,0:T(8,128)(2,1)} %slice.20), channel_id=1, source_target_pairs={{0,16},{16,0},{1,17},{17,1},{2,18},{18,2},{3,19},{19,3},{4,20},{20... | collective-permute-start | bytes 6291464 | tf_op jit(solution)/shard_map/ppermute | solution.py:19
  17.4 2.0 %collective-permute-start.1 = (f32[512,256]{1,0:T(8,128)S(1)}, f32[512,256]{1,0:T(8,128)S(1)}, u32[]{:S(2)}, u32[]{:S(2)}) collective-permute-start(f32[512,256]{1,0:T(8,128)S(1)} %get-tuple-element.48), channel_id=1, source_target_pairs={{0,1},{1,0},{2,3},{3,2},{4,5},{5,4},{6,7},{7,6},{8,9},{9,8},{10,11... | collective-permute-start | bytes 1572872 | tf_op jit(solution)/shard_map/ppermute | solution.py:149
  17.4 3.5 %collective-permute-start.5 = (f32[512,256]{1,0:T(8,128)S(1)}, f32[512,256]{1,0:T(8,128)S(1)}, u32[]{:S(2)}, u32[]{:S(2)}) collective-permute-start(f32[512,256]{1,0:T(8,128)S(1)} %get-tuple-element.54), channel_id=1, source_target_pairs={{0,1},{1,0},{2,3},{3,2},{4,5},{5,4},{6,7},{7,6},{8,9},{9,8},{10,11... | collective-permute-start | bytes 1572872 | tf_op jit(solution)/shard_map/ppermute | solution.py:149
  19.4 9.2 %collective-permute-start.2 = (f32[256,256]{1,0:T(8,128)S(1)}, f32[256,256]{1,0:T(8,128)S(1)}, u32[]{:S(2)}, u32[]{:S(2)}) collective-permute-start(f32[256,256]{1,0:T(8,128)S(1)} %get-tuple-element.50), channel_id=1, source_target_pairs={{0,2},{1,3},{2,0},{3,1},{4,6},{5,7},{6,4},{7,5},{8,10},{9,11},{10,... | collective-permute-start | bytes 786440 | tf_op jit(solution)/shard_map/ppermute | solution.py:149
  21.0 12.4 %collective-permute-start.6 = (f32[256,256]{1,0:T(8,128)S(1)}, f32[256,256]{1,0:T(8,128)S(1)}, u32[]{:S(2)}, u32[]{:S(2)}) collective-permute-start(f32[256,256]{1,0:T(8,128)S(1)} %get-tuple-element.56), channel_id=1, source_target_pairs={{0,2},{1,3},{2,0},{3,1},{4,6},{5,7},{6,4},{7,5},{8,10},{9,11},{10,... | collective-permute-start | bytes 786440 | tf_op jit(solution)/shard_map/ppermute | solution.py:149
  28.6 6.5 %collective-permute-start.3 = (f32[128,256]{1,0:T(8,128)S(1)}, f32[128,256]{1,0:T(8,128)S(1)}, u32[]{:S(2)}, u32[]{:S(2)}) collective-permute-start(f32[128,256]{1,0:T(8,128)S(1)} %get-tuple-element.52), channel_id=1, source_target_pairs={{0,4},{1,5},{2,6},{3,7},{4,0},{5,1},{6,2},{7,3},{8,12},{9,13},{10,... | collective-permute-start | bytes 393224 | tf_op jit(solution)/shard_map/ppermute | solution.py:149
  33.5 6.5 %collective-permute-start.7 = (f32[128,256]{1,0:T(8,128)S(1)}, f32[128,256]{1,0:T(8,128)S(1)}, u32[]{:S(2)}, u32[]{:S(2)}) collective-permute-start(f32[128,256]{1,0:T(8,128)S(1)} %get-tuple-element.58), channel_id=1, source_target_pairs={{0,4},{1,5},{2,6},{3,7},{4,0},{5,1},{6,2},{7,3},{8,12},{9,13},{10,... | collective-permute-start | bytes 393224 | tf_op jit(solution)/shard_map/ppermute | solution.py:149
  35.1 12.1 %collective-permute-start.4 = (f32[128,256]{1,0:T(8,128)S(1)}, f32[128,256]{1,0:T(8,128)S(1)}, u32[]{:S(2)}, u32[]{:S(2)}) collective-permute-start(f32[128,256]{1,0:T(8,128)S(1)} %add.65), channel_id=1, source_target_pairs={{0,8},{1,9},{2,10},{3,11},{4,12},{5,13},{6,14},{7,15},{8,0},{9,1},... | collective-permute-start | bytes 393224 | tf_op jit(solution)/shard_map/ppermute | solution.py:149
  40.0 9.1 %collective-permute-start.8 = (f32[128,256]{1,0:T(8,128)S(1)}, f32[128,256]{1,0:T(8,128)S(1)}, u32[]{:S(2)}, u32[]{:S(2)}) collective-permute-start(f32[128,256]{1,0:T(8,128)S(1)} %add.67), channel_id=1, source_target_pairs={{0,8},{1,9},{2,10},{3,11},{4,12},{5,13},{6,14},{7,15},{8,0},{9,1},... | collective-permute-start | bytes 393224 | tf_op jit(solution)/shard_map/ppermute | solution.py:149
  42.4 32.9 %collective-permute-start.13 = (bf16[4096,128]{1,0:T(8,128)(2,1)}, bf16[4096,128]{1,0:T(8,128)(2,1)S(1)}, u32[]{:S(2)}, u32[]{:S(2)}) collective-permute-start(bf16[4096,128]{1,0:T(8,128)(2,1)} %slice.21), channel_id=1, source_target_pairs={{0,16},{16,0},{1,17},{17,1},{2,18},{18,2},{3,19},{19,3},{4,20},{20... | collective-permute-start | bytes 3145736 | tf_op jit(solution)/shard_map/ppermute | solution.py:19
  49.1 14.1 %copy-start.1 = (bf16[3072,128]{1,0:T(8,128)(2,1)S(1)}, bf16[3072,128]{1,0:T(8,128)(2,1)}, u32[]{:S(2)}) copy-start(bf16[3072,128]{1,0:T(8,128)(2,1)} %slice.22) | copy-start | bytes 2359300
  59.1 2.0 %collective-permute-start.9 = (f32[512,256]{1,0:T(8,128)S(1)}, f32[512,256]{1,0:T(8,128)S(1)}, u32[]{:S(2)}, u32[]{:S(2)}) collective-permute-start(f32[512,256]{1,0:T(8,128)S(1)} %get-tuple-element.61), channel_id=1, source_target_pairs={{0,1},{1,0},{2,3},{3,2},{4,5},{5,4},{6,7},{7,6},{8,9},{9,8},{10,11... | collective-permute-start | bytes 1572872 | tf_op jit(solution)/shard_map/ppermute | solution.py:149
  61.1 8.7 %collective-permute-start.10 = (f32[256,256]{1,0:T(8,128)S(1)}, f32[256,256]{1,0:T(8,128)S(1)}, u32[]{:S(2)}, u32[]{:S(2)}) collective-permute-start(f32[256,256]{1,0:T(8,128)S(1)} %get-tuple-element.63), channel_id=1, source_target_pairs={{0,2},{1,3},{2,0},{3,1},{4,6},{5,7},{6,4},{7,5},{8,10},{9,11},{10,... | collective-permute-start | bytes 786440 | tf_op jit(solution)/shard_map/ppermute | solution.py:149
  63.2 34.4 %collective-permute-start.19 = (bf16[3072,128]{1,0:T(8,128)(2,1)S(1)}, bf16[3072,128]{1,0:T(8,128)(2,1)S(1)}, u32[]{:S(2)}, u32[]{:S(2)}) collective-permute-start(bf16[3072,128]{1,0:T(8,128)(2,1)S(1)} %copy-done.1), channel_id=1, source_target_pairs={{0,16},{16,0},{1,17},{17,1},{2,18},{18,2},{3,19},{19,3},{4,20},{20... | collective-permute-start | bytes 2359304 | tf_op jit(solution)/shard_map/ppermute | solution.py:19
  69.8 5.1 %collective-permute-start.11 = (f32[128,256]{1,0:T(8,128)S(1)}, f32[128,256]{1,0:T(8,128)S(1)}, u32[]{:S(2)}, u32[]{:S(2)}) collective-permute-start(f32[128,256]{1,0:T(8,128)S(1)} %get-tuple-element.65), channel_id=1, source_target_pairs={{0,4},{1,5},{2,6},{3,7},{4,0},{5,1},{6,2},{7,3},{8,12},{9,13},{10,... | collective-permute-start | bytes 393224 | tf_op jit(solution)/shard_map/ppermute | solution.py:149
  74.9 9.4 %copy-start.2 = (bf16[1024,128]{1,0:T(8,128)(2,1)S(1)}, bf16[1024,128]{1,0:T(8,128)(2,1)}, u32[]{:S(2)}) copy-start(bf16[1024,128]{1,0:T(8,128)(2,1)} %slice.23) | copy-start | bytes 786436
  81.0 10.2 %collective-permute-start.14 = (f32[512,128]{1,0:T(8,128)S(1)}, f32[512,128]{1,0:T(8,128)S(1)}, u32[]{:S(2)}, u32[]{:S(2)}) collective-permute-start(f32[512,128]{1,0:T(8,128)S(1)} %get-tuple-element.68), channel_id=1, source_target_pairs={{0,1},{1,0},{2,3},{3,2},{4,5},{5,4},{6,7},{7,6},{8,9},{9,8},{10,11... | collective-permute-start | bytes 786440 | tf_op jit(solution)/shard_map/ppermute | solution.py:149
  81.1 10.1 %collective-permute-start.12 = (f32[128,256]{1,0:T(8,128)S(1)}, f32[128,256]{1,0:T(8,128)S(1)}, u32[]{:S(2)}, u32[]{:S(2)}) collective-permute-start(f32[128,256]{1,0:T(8,128)S(1)} %add.69), channel_id=1, source_target_pairs={{0,8},{1,9},{2,10},{3,11},{4,12},{5,13},{6,14},{7,15},{8,0},{9,1},... | collective-permute-start | bytes 393224 | tf_op jit(solution)/shard_map/ppermute | solution.py:149
  84.3 18.1 %collective-permute-start.18 = (bf16[1024,128]{1,0:T(8,128)(2,1)S(1)}, bf16[1024,128]{1,0:T(8,128)(2,1)S(1)}, u32[]{:S(2)}, u32[]{:S(2)}) collective-permute-start(bf16[1024,128]{1,0:T(8,128)(2,1)S(1)} %copy-done.2), channel_id=1, source_target_pairs={{0,16},{16,0},{1,17},{17,1},{2,18},{18,2},{3,19},{19,3},{4,20},{20... | collective-permute-start | bytes 786440 | tf_op jit(solution)/shard_map/ppermute | solution.py:19
  91.3 5.3 %collective-permute-start.15 = (f32[256,128]{1,0:T(8,128)S(1)}, f32[256,128]{1,0:T(8,128)S(1)}, u32[]{:S(2)}, u32[]{:S(2)}) collective-permute-start(f32[256,128]{1,0:T(8,128)S(1)} %get-tuple-element.71), channel_id=1, source_target_pairs={{0,2},{1,3},{2,0},{3,1},{4,6},{5,7},{6,4},{7,5},{8,10},{9,11},{10,... | collective-permute-start | bytes 393224 | tf_op jit(solution)/shard_map/ppermute | solution.py:149
  96.6 5.7 %collective-permute-start.16 = (f32[128,128]{1,0:T(8,128)S(1)}, f32[128,128]{1,0:T(8,128)S(1)}, u32[]{:S(2)}, u32[]{:S(2)}) collective-permute-start(f32[128,128]{1,0:T(8,128)S(1)} %get-tuple-element.73), channel_id=1, source_target_pairs={{0,4},{1,5},{2,6},{3,7},{4,0},{5,1},{6,2},{7,3},{8,12},{9,13},{10,... | collective-permute-start | bytes 196616 | tf_op jit(solution)/shard_map/ppermute | solution.py:149
  102.4 2.5 %copy-start.3 = (f32[512]{0:T(512)S(1)}, f32[512]{0:T(512)}, u32[]{:S(2)}) copy-start(f32[512]{0:T(512)} %param.13) | copy-start | bytes 6148
  102.4 2.5 %copy-start.5 = (s32[32]{0:T(128)S(1)}, s32[32]{0:T(128)}, u32[]{:S(2)}) copy-start(s32[32]{0:T(128)} %param.11) | copy-start | bytes 388
  102.4 11.5 %copy-start.7 = (s32[64]{0:T(128)S(1)}, s32[64]{0:T(128)}, u32[]{:S(2)}) copy-start(s32[64]{0:T(128)} %param.10) | copy-start | bytes 772
  102.4 15.8 %copy-start.4 = (s32[64,2]{0,1:T(2,128)S(1)}, s32[64,2]{0,1:T(2,128)}, u32[]{:S(2)}) copy-start(s32[64,2]{0,1:T(2,128)} %param.9) | copy-start | bytes 1540
  102.4 15.8 %copy-start.6 = (f32[96]{0:T(128)S(1)}, f32[96]{0:T(128)}, u32[]{:S(2)}) copy-start(f32[96]{0:T(128)} %param.12) | copy-start | bytes 1156
  104.8 7.7 %collective-permute-start.20 = (f32[512,128]{1,0:T(8,128)S(1)}, f32[512,128]{1,0:T(8,128)S(1)}, u32[]{:S(2)}, u32[]{:S(2)}) collective-permute-start(f32[512,128]{1,0:T(8,128)S(1)} %get-tuple-element.79), channel_id=1, source_target_pairs={{0,1},{1,0},{2,3},{3,2},{4,5},{5,4},{6,7},{7,6},{8,9},{9,8},{10,11... | collective-permute-start | bytes 786440 | tf_op jit(solution)/shard_map/ppermute | solution.py:149
  105.1 7.4 %collective-permute-start.17 = (f32[128,128]{1,0:T(8,128)S(1)}, f32[128,128]{1,0:T(8,128)S(1)}, u32[]{:S(2)}, u32[]{:S(2)}) collective-permute-start(f32[128,128]{1,0:T(8,128)S(1)} %add.71), channel_id=1, source_target_pairs={{0,8},{1,9},{2,10},{3,11},{4,12},{5,13},{6,14},{7,15},{8,0},{9,1},... | collective-permute-start | bytes 196616 | tf_op jit(solution)/shard_map/ppermute | solution.py:149
  112.5 5.6 %collective-permute-start.21 = (f32[256,128]{1,0:T(8,128)S(1)}, f32[256,128]{1,0:T(8,128)S(1)}, u32[]{:S(2)}, u32[]{:S(2)}) collective-permute-start(f32[256,128]{1,0:T(8,128)S(1)} %get-tuple-element.82), channel_id=1, source_target_pairs={{0,2},{1,3},{2,0},{3,1},{4,6},{5,7},{6,4},{7,5},{8,10},{9,11},{10,... | collective-permute-start | bytes 393224 | tf_op jit(solution)/shard_map/ppermute | solution.py:149
  118.1 4.3 %collective-permute-start.22 = (f32[128,128]{1,0:T(8,128)S(1)}, f32[128,128]{1,0:T(8,128)S(1)}, u32[]{:S(2)}, u32[]{:S(2)}) collective-permute-start(f32[128,128]{1,0:T(8,128)S(1)} %get-tuple-element.84), channel_id=1, source_target_pairs={{0,4},{1,5},{2,6},{3,7},{4,0},{5,1},{6,2},{7,3},{8,12},{9,13},{10,... | collective-permute-start | bytes 196616 | tf_op jit(solution)/shard_map/ppermute | solution.py:149
  122.4 5.4 %collective-permute-start.23 = (f32[128,128]{1,0:T(8,128)S(1)}, f32[128,128]{1,0:T(8,128)S(1)}, u32[]{:S(2)}, u32[]{:S(2)}) collective-permute-start(f32[128,128]{1,0:T(8,128)S(1)} %add.73), channel_id=1, source_target_pairs={{0,8},{1,9},{2,10},{3,11},{4,12},{5,13},{6,14},{7,15},{8,0},{9,1},... | collective-permute-start | bytes 196616 | tf_op jit(solution)/shard_map/ppermute | solution.py:149

commit v5 on v4

--- a/solution.py
+++ b/solution.py
@@ -8,6 +8,8 @@
 from jax.sharding import PartitionSpec as P
 
 DEPTH_CUTS = 4
+ROW_CUTS = 4
+FREE = pl.CostEstimate(flops=0, bytes_accessed=0, transcendentals=0)
 OWN_SPLITS = 2
 PRODUCT_BYTES = 51 * 1024 * 1024
 SUM_BYTES = 8 * 1024 * 1024
@@ -44,19 +46,37 @@
     return jnp.concatenate(ordered, axis=1)
 
 
-def product_kernel(steps, order, splits, has_base, bit_ref, a_ref, b_ref, *refs):
-    base_ref = refs[0] if has_base else None
+def add_product(a_refs, b_ref, total_ref, base_ref):
+    columns = b_ref[...]
+    rows = a_refs[0].shape[0]
+    for index, a_ref in enumerate(a_refs):
+        part = slice(index * rows, (index + 1) * rows)
+        term = jnp.dot(a_ref[...], columns, preferred_element_type=jnp.float32)
+
+        @pl.when(pl.program_id(0) == 0)
+        def _():
+            total_ref[part, :] = term if base_ref is None else term + base_ref[part, :]
+
+        @pl.when(pl.program_id(0) > 0)
+        def _():
+            total_ref[part, :] += term
+
+
+def row_blocks(rows, part, first):
+    return [pl.BlockSpec((rows // ROW_CUTS, part), lambda k, j=j: (j, k + first)) for j in range(ROW_CUTS)]
+
+
+def product_cost(rows, columns):
+    depth, width = columns.shape
+    return pl.CostEstimate(flops=2 * rows * depth * width, bytes_accessed=2 * rows * depth, transcendentals=0)
+
+
+def product_kernel(steps, order, splits, has_base, bit_ref, *refs):
+    a_refs, b_ref = refs[:ROW_CUTS], refs[ROW_CUTS]
+    base_ref = refs[ROW_CUTS + 1] if has_base else None
     out_refs, total_ref = refs[-1 - 2 * splits : -1], refs[-1]
     step = pl.program_id(0)
-    term = jnp.dot(a_ref[...], b_ref[...], preferred_element_type=jnp.float32)
-
-    @pl.when(step == 0)
-    def _():
-        total_ref[...] = term + base_ref[...] if has_base else term
-
-    @pl.when(step > 0)
-    def _():
-        total_ref[...] += term
+    add_product(a_refs, b_ref, total_ref, base_ref)
 
     @pl.when(step == steps - 1)
     def _():
@@ -83,27 +103,19 @@
         out_shape=[shape] * (2 * splits),
         in_specs=[
             pl.BlockSpec(memory_space=pltpu.SMEM),
-            pl.BlockSpec((rows, part), lambda k: (0, k + first)),
+            *row_blocks(rows, part, first),
             pl.BlockSpec((part, width), lambda k: (k, 0)),
         ]
         + [pl.BlockSpec((rows, width), lambda k: (0, 0)) for _ in bases],
         out_specs=[pl.BlockSpec(shape.shape, lambda k: (0, 0))] * (2 * splits),
         scratch_shapes=[pltpu.VMEM((rows, width), jnp.float32)],
         compiler_params=pltpu.CompilerParams(vmem_limit_bytes=PRODUCT_BYTES),
-        cost_estimate=pl.CostEstimate(flops=0, bytes_accessed=0, transcendentals=0),
-    )(bit, amplitudes, columns, *bases)
-
-
-def plain_kernel(a_ref, b_ref, out_ref):
-    term = jnp.dot(a_ref[...], b_ref[...], preferred_element_type=jnp.float32)
-
-    @pl.when(pl.program_id(0) == 0)
-    def _():
-        out_ref[...] = term
-
-    @pl.when(pl.program_id(0) > 0)
-    def _():
-        out_ref[...] += term
+        cost_estimate=product_cost(rows, columns) if splits == 1 else FREE,
+    )(bit, *[amplitudes] * ROW_CUTS, columns, *bases)
+
+
+def plain_kernel(*refs):
+    add_product(refs[:ROW_CUTS], refs[ROW_CUTS], refs[-1], None)
 
 
 def plain_product(amplitudes, columns):
@@ -115,13 +127,13 @@
         grid=(columns.shape[0] // part,),
         out_shape=jax.ShapeDtypeStruct((rows, width), jnp.float32),
         in_specs=[
-            pl.BlockSpec((rows, part), lambda k: (0, k)),
+            *row_blocks(rows, part, 0),
             pl.BlockSpec((part, width), lambda k: (k, 0)),
         ],
         out_specs=pl.BlockSpec((rows, width), lambda k: (0, 0)),
         compiler_params=pltpu.CompilerParams(vmem_limit_bytes=PRODUCT_BYTES),
-        cost_estimate=pl.CostEstimate(flops=0, bytes_accessed=0, transcendentals=0),
-    )(amplitudes, columns)
+        cost_estimate=product_cost(rows, columns),
+    )(*[amplitudes] * ROW_CUTS, columns)
 
 
 def halve_kernel(bit_ref, mine_ref, came_ref, keep_ref, send_ref):
@@ -140,7 +152,7 @@
         in_specs=[pl.BlockSpec(memory_space=pltpu.SMEM)] + [pl.BlockSpec(memory_space=pltpu.VMEM)] * 2,
         out_specs=[pl.BlockSpec(memory_space=pltpu.VMEM)] * 2,
         compiler_params=pltpu.CompilerParams(vmem_limit_bytes=SUM_BYTES),
-        cost_estimate=pl.CostEstimate(flops=0, bytes_accessed=0, transcendentals=0),
+        cost_estimate=FREE,
     )(bit, mine, came)
 
 
@@ -186,11 +198,10 @@
     own_product = multiplied(amplitudes, after(rest, pieces), bits[0], order, splits=OWN_SPLITS)
     own_sums = [exchanged_sum(own_product[2 * part : 2 * part + 2], bits)[0] for part in range(OWN_SPLITS)]
     sums = [own_sums] + [[] for _ in range(1, count)]
+    in_flight += [sent(after(piece, own_sums)) for piece in pieces[2:]]
     earlier, gates = own_sums, {}
     for step in range(len(pieces)):
         arrived, earlier = lax.optimization_barrier((in_flight[step], earlier))
-        if step + 2 < len(pieces):
-            in_flight.append(sent(after(pieces[step + 2], arrived)))
         if step == len(pieces) - 2:
             bases = [plain_product(amplitudes, columns) for columns in arrived]
             earlier = (stages[2], bases)
@@ -202,7 +213,7 @@
                 product = multiplied(amplitudes, arrived[shift - 1], bits[0], order, DEPTH_CUTS - 1, bases[shift - 1])
             total, stages = exchanged_sum(product, bits, gates)
             sums[shift].append(total)
-            earlier, gates = stages[2] if step < len(cuts) - 2 else stages[1], {1: total}
+            earlier, gates = stages[2] if step < len(cuts) - 2 else stages[0], {2: total}
 
     both = in_column_order([jnp.concatenate(parts, axis=1) for parts in sums], count)
     mine = jnp.where(upper, both[rows:], both[:rows])

time: 130 us -> 126 us (0.969)
  waiting for transfers between devices: 59.5 us -> 49.7 us
  Pallas kernels: 27.4 us -> 33.4 us
    ppermute x20, waiting for transfers between devices: 55.3 us -> 47.3 us  [flipped_along(): lax.ppermute(value, axis, [(source, source ^ bits) for source in range(co...]
    pallas_call x4, Pallas kernels: 22.3 us -> 27.6 us  [multiplied(): pl.pallas_call(functools.partial(product_kernel, steps, order, splits, ba...]
    ppermute x4, waiting for transfers between devices: 4.24 us -> 2.36 us  [passed_along(): return lax.ppermute(value, axis, pairs)]
  transfers between devices with their start and end apart: 24 -> 24, of which waited for: 17 -> 15; matrix products, arithmetic and copies ran while one was open for 3% -> 3% of each run, Pallas kernels for 19% -> 25%
where the time goes in v5:
time: 126 us
  waiting for transfers between devices  49.7 us (39%)
  Pallas kernels  33.4 us (27%)
  starting transfers between devices  33.3 us (26%)
  local copies, waits for them, and re-layouts  7.61 us (6%)
  other arithmetic  1.54 us (1%)
    ppermute x20, waiting for transfers between devices, flipped_along(): lax.ppermute(value, axis, [(source, source ^ bits) for source in range(co...  47.3 us
    pallas_call x4, Pallas kernels, multiplied(): pl.pallas_call(functools.partial(product_kernel, steps, order, splits, ba...  27.6 us
    ppermute x20, starting transfers between devices, flipped_along(): lax.ppermute(value, axis, [(source, source ^ bits) for source in range(co...  26.5 us
    ppermute x4, starting transfers between devices, passed_along(): return lax.ppermute(value, axis, pairs)  6.76 us
    pallas_call x1, Pallas kernels, plain_product(): pl.pallas_call(plain_kernel, grid=(columns.shape[0] // part,), out_shape=...  5.4 us
    slice x1, local copies, waits for them, and re-layouts, per_device(): first = integrals[:, cuts[0][0]:cuts[0][1]]  3.24 us
  transfers between devices with their start and end apart: 24, of which 15 were waited for; matrix products, arithmetic and copies ran while one was open for 3% of the time, Pallas kernels for 25%

profile of v5, /device:TPU:0, one launch (start us, length us, event | category | flops | bytes accessed | tf_op | source)
XLA Modules:
  0.0 125.8 jit_solution(12219545046160391954)
XLA Ops:
  0.0 3.2 %slice.20 = bf16[4096,256]{1,0:T(8,128)(2,1)} slice(bf16[4096,512]{1,0:T(8,128)(2,1)} %refs_4_), slice={[0:4096], [0:256]} | slice | bytes 4194304 | tf_op jit(solution)/shard_map/slice | solution.py:192
  3.2 3.0 %collective-permute-start = (bf16[4096,256]{1,0:T(8,128)(2,1)}, bf16[4096,256]{1,0:T(8,128)(2,1)}, u32[]{:S(2)}, u32[]{:S(2)}) collective-permute-start(bf16[4096,256]{1,0:T(8,128)(2,1)} %slice.20), channel_id=1, source_target_pairs={{0,16},{16,0},{1,17},{17,1},{2,18},{18,2},{3,19},{19,3},{4,20},{20... | collective-permute-start | bytes 6291464 | tf_op jit(solution)/shard_map/ppermute | solution.py:21
  6.2 1.1 slice.21
  7.4 1.0 slice.22
  8.4 0.7 slice.23
  9.1 9.7 %shard_map.73 = (f32[512,256]{1,0:T(8,128)S(1)}, f32[512,256]{1,0:T(8,128)S(1)}, f32[512,256]{1,0:T(8,128)S(1)}, f32[512,256]{1,0:T(8,128)S(1)}) custom-call(s32[1]{0:T(128)} %bitcast.2.bit_ref, bf16[1024,4096]{1,0:T(8,128)(2,1)} %refs_3_.9, bf16[1024,4096]{1,0:T(8,128)(2,1)} %refs_3_.9, bf16[1024,4096]{1,0:T(8,128)(2,1)} %refs_3_.9, ...), custom_call_target="tpu_custom_call" | custom-call | tf_op jit(solution)/shard_map/pallas_call | solution.py:100
  18.9 0.5 collective-permute-start.5
  19.4 1.4 %collective-permute-done.1.came_ref = f32[512,256]{1,0:T(8,128)S(1)} collective-permute-done((f32[512,256]{1,0:T(8,128)S(1)}, f32[512,256]{1,0:T(8,128)S(1)}, u32[]{:S(2)}, u32[]{:S(2)}) %collective-permute-start.1) | collective-permute-done | bytes 524320 | tf_op jit(solution)/shard_map/ppermute | solution.py:161
  20.9 1.6 %collective-permute-start.2 = (f32[256,256]{1,0:T(8,128)S(1)}, f32[256,256]{1,0:T(8,128)S(1)}, u32[]{:S(2)}, u32[]{:S(2)}) collective-permute-start(f32[256,256]{1,0:T(8,128)S(1)} %get-tuple-element.50), channel_id=1, source_target_pairs={{0,2},{1,3},{2,0},{3,1},{4,6},{5,7},{6,4},{7,5},{8,10},{9,11},{10,... | collective-permute-start | bytes 786440 | tf_op jit(solution)/shard_map/ppermute | solution.py:161
  22.5 0.7 collective-permute-start.6
  23.2 6.9 %collective-permute-done.2.came_ref = f32[256,256]{1,0:T(8,128)S(1)} collective-permute-done((f32[256,256]{1,0:T(8,128)S(1)}, f32[256,256]{1,0:T(8,128)S(1)}, u32[]{:S(2)}, u32[]{:S(2)}) %collective-permute-start.2) | collective-permute-done | bytes 262176 | tf_op jit(solution)/shard_map/ppermute | solution.py:161
  30.1 1.6 %collective-permute-start.3 = (f32[128,256]{1,0:T(8,128)S(1)}, f32[128,256]{1,0:T(8,128)S(1)}, u32[]{:S(2)}, u32[]{:S(2)}) collective-permute-start(f32[128,256]{1,0:T(8,128)S(1)} %get-tuple-element.52), channel_id=1, source_target_pairs={{0,4},{1,5},{2,6},{3,7},{4,0},{5,1},{6,2},{7,3},{8,12},{9,13},{10,... | collective-permute-start | bytes 393224 | tf_op jit(solution)/shard_map/ppermute | solution.py:161
  31.8 3.1 %collective-permute-done.6.came_ref = f32[256,256]{1,0:T(8,128)S(1)} collective-permute-done((f32[256,256]{1,0:T(8,128)S(1)}, f32[256,256]{1,0:T(8,128)S(1)}, u32[]{:S(2)}, u32[]{:S(2)}) %collective-permute-start.6) | collective-permute-done | bytes 262176 | tf_op jit(solution)/shard_map/ppermute | solution.py:161
  35.0 1.6 %collective-permute-start.7 = (f32[128,256]{1,0:T(8,128)S(1)}, f32[128,256]{1,0:T(8,128)S(1)}, u32[]{:S(2)}, u32[]{:S(2)}) collective-permute-start(f32[128,256]{1,0:T(8,128)S(1)} %get-tuple-element.58), channel_id=1, source_target_pairs={{0,4},{1,5},{2,6},{3,7},{4,0},{5,1},{6,2},{7,3},{8,12},{9,13},{10,... | collective-permute-start | bytes 393224 | tf_op jit(solution)/shard_map/ppermute | solution.py:161
  36.6 2.7 %collective-permute-start.4 = (f32[128,256]{1,0:T(8,128)S(1)}, f32[128,256]{1,0:T(8,128)S(1)}, u32[]{:S(2)}, u32[]{:S(2)}) collective-permute-start(f32[128,256]{1,0:T(8,128)S(1)} %add.65), channel_id=1, source_target_pairs={{0,8},{1,9},{2,10},{3,11},{4,12},{5,13},{6,14},{7,15},{8,0},{9,1},... | collective-permute-start | bytes 393224 | tf_op jit(solution)/shard_map/ppermute | solution.py:161
  39.3 2.2 %collective-permute-done.7 = f32[128,256]{1,0:T(8,128)S(1)} collective-permute-done((f32[128,256]{1,0:T(8,128)S(1)}, f32[128,256]{1,0:T(8,128)S(1)}, u32[]{:S(2)}, u32[]{:S(2)}) %collective-permute-start.7) | collective-permute-done | bytes 131104 | tf_op jit(solution)/shard_map/ppermute | solution.py:161
  41.5 2.4 %collective-permute-start.8 = (f32[128,256]{1,0:T(8,128)S(1)}, f32[128,256]{1,0:T(8,128)S(1)}, u32[]{:S(2)}, u32[]{:S(2)}) collective-permute-start(f32[128,256]{1,0:T(8,128)S(1)} %add.67), channel_id=1, source_target_pairs={{0,8},{1,9},{2,10},{3,11},{4,12},{5,13},{6,14},{7,15},{8,0},{9,1},... | collective-permute-start | bytes 393224 | tf_op jit(solution)/shard_map/ppermute | solution.py:161
  43.9 0.5 collective-permute-start.13
  44.4 4.3 %collective-permute-done.4 = f32[128,256]{1,0:T(8,128)S(1)} collective-permute-done((f32[128,256]{1,0:T(8,128)S(1)}, f32[128,256]{1,0:T(8,128)S(1)}, u32[]{:S(2)}, u32[]{:S(2)}) %collective-permute-start.4) | collective-permute-done | bytes 131104 | tf_op jit(solution)/shard_map/ppermute | solution.py:161
  48.7 1.9 %collective-permute-done.8 = f32[128,256]{1,0:T(8,128)S(1)} collective-permute-done((f32[128,256]{1,0:T(8,128)S(1)}, f32[128,256]{1,0:T(8,128)S(1)}, u32[]{:S(2)}, u32[]{:S(2)}) %collective-permute-start.8) | collective-permute-done | bytes 131104 | tf_op jit(solution)/shard_map/ppermute | solution.py:161
  50.6 2.4 %collective-permute-done.refs_4_ = bf16[4096,256]{1,0:T(8,128)(2,1)} collective-permute-done((bf16[4096,256]{1,0:T(8,128)(2,1)}, bf16[4096,256]{1,0:T(8,128)(2,1)}, u32[]{:S(2)}, u32[]{:S(2)}) %collective-permute-start) | collective-permute-done | bytes 2097184 | tf_op jit(solution)/shard_map/ppermute | solution.py:21
  53.0 8.8 %shard_map.78 = (f32[512,256]{1,0:T(8,128)S(1)}, f32[512,256]{1,0:T(8,128)S(1)}) custom-call(s32[1]{0:T(128)} %bitcast.2.bit_ref, bf16[1024,4096]{1,0:T(8,128)(2,1)} %refs_3_.9, bf16[1024,4096]{1,0:T(8,128)(2,1)} %refs_3_.9, bf16[1024,4096]{1,0:T(8,128)(2,1)} %refs_3_.9, bf16[1024,4096]{1,0:T(8,128)(2,1)} %refs_3_.9, ...), custom_call_target="tpu_custom_call" | custom-call | flops 2147483648 | bytes 8388608 | tf_op jit(solution)/shard_map/pallas_call | solution.py:100
  61.9 1.9 %collective-permute-done.9.came_ref = f32[512,256]{1,0:T(8,128)S(1)} collective-permute-done((f32[512,256]{1,0:T(8,128)S(1)}, f32[512,256]{1,0:T(8,128)S(1)}, u32[]{:S(2)}, u32[]{:S(2)}) %collective-permute-start.9) | collective-permute-done | bytes 524320 | tf_op jit(solution)/shard_map/ppermute | solution.py:161
  63.8 2.1 %collective-permute-start.10 = (f32[256,256]{1,0:T(8,128)S(1)}, f32[256,256]{1,0:T(8,128)S(1)}, u32[]{:S(2)}, u32[]{:S(2)}) collective-permute-start(f32[256,256]{1,0:T(8,128)S(1)} %get-tuple-element.63), channel_id=1, source_target_pairs={{0,2},{1,3},{2,0},{3,1},{4,6},{5,7},{6,4},{7,5},{8,10},{9,11},{10,... | collective-permute-start | bytes 786440 | tf_op jit(solution)/shard_map/ppermute | solution.py:161
  65.9 1.5 %collective-permute-start.19 = (bf16[3072,128]{1,0:T(8,128)(2,1)S(1)}, bf16[3072,128]{1,0:T(8,128)(2,1)S(1)}, u32[]{:S(2)}, u32[]{:S(2)}) collective-permute-start(bf16[3072,128]{1,0:T(8,128)(2,1)S(1)} %copy-done.1), channel_id=1, source_target_pairs={{0,16},{16,0},{1,17},{17,1},{2,18},{18,2},{3,19},{19,3},{4,20},{20... | collective-permute-start | bytes 2359304 | tf_op jit(solution)/shard_map/ppermute | solution.py:21
  67.5 5.1 %collective-permute-done.10.came_ref = f32[256,256]{1,0:T(8,128)S(1)} collective-permute-done((f32[256,256]{1,0:T(8,128)S(1)}, f32[256,256]{1,0:T(8,128)S(1)}, u32[]{:S(2)}, u32[]{:S(2)}) %collective-permute-start.10) | collective-permute-done | bytes 262176 | tf_op jit(solution)/shard_map/ppermute | solution.py:161
  72.6 1.9 %collective-permute-start.11 = (f32[128,256]{1,0:T(8,128)S(1)}, f32[128,256]{1,0:T(8,128)S(1)}, u32[]{:S(2)}, u32[]{:S(2)}) collective-permute-start(f32[128,256]{1,0:T(8,128)S(1)} %get-tuple-element.65), channel_id=1, source_target_pairs={{0,4},{1,5},{2,6},{3,7},{4,0},{5,1},{6,2},{7,3},{8,12},{9,13},{10,... | collective-permute-start | bytes 393224 | tf_op jit(solution)/shard_map/ppermute | solution.py:161
  74.5 3.2 %collective-permute-done.11 = f32[128,256]{1,0:T(8,128)S(1)} collective-permute-done((f32[128,256]{1,0:T(8,128)S(1)}, f32[128,256]{1,0:T(8,128)S(1)}, u32[]{:S(2)}, u32[]{:S(2)}) %collective-permute-start.11) | collective-permute-done | bytes 131104 | tf_op jit(solution)/shard_map/ppermute | solution.py:161
  77.7 6.8 %shard_map.81 = (f32[512,128]{1,0:T(8,128)S(1)}, f32[512,128]{1,0:T(8,128)S(1)}) custom-call(s32[1]{0:T(128)} %bitcast.2.bit_ref, bf16[1024,4096]{1,0:T(8,128)(2,1)} %refs_3_.9, bf16[1024,4096]{1,0:T(8,128)(2,1)} %refs_3_.9, bf16[1024,4096]{1,0:T(8,128)(2,1)} %refs_3_.9, bf16[1024,4096]{1,0:T(8,128)(2,1)} %refs_3_.9, ...), custom_call_target="tpu_custom_call" | custom-call | flops 1073741824 | bytes 8388608 | tf_op jit(solution)/shard_map/pallas_call | solution.py:100
  84.6 1.8 %collective-permute-start.18 = (bf16[1024,128]{1,0:T(8,128)(2,1)S(1)}, bf16[1024,128]{1,0:T(8,128)(2,1)S(1)}, u32[]{:S(2)}, u32[]{:S(2)}) collective-permute-start(bf16[1024,128]{1,0:T(8,128)(2,1)S(1)} %copy-done.2), channel_id=1, source_target_pairs={{0,16},{16,0},{1,17},{17,1},{2,18},{18,2},{3,19},{19,3},{4,20},{20... | collective-permute-start | bytes 786440 | tf_op jit(solution)/shard_map/ppermute | solution.py:21
  86.4 2.6 %collective-permute-start.12 = (f32[128,256]{1,0:T(8,128)S(1)}, f32[128,256]{1,0:T(8,128)S(1)}, u32[]{:S(2)}, u32[]{:S(2)}) collective-permute-start(f32[128,256]{1,0:T(8,128)S(1)} %add.69), channel_id=1, source_target_pairs={{0,8},{1,9},{2,10},{3,11},{4,12},{5,13},{6,14},{7,15},{8,0},{9,1},... | collective-permute-start | bytes 393224 | tf_op jit(solution)/shard_map/ppermute | solution.py:161
  89.0 1.6 %collective-permute-start.15 = (f32[256,128]{1,0:T(8,128)S(1)}, f32[256,128]{1,0:T(8,128)S(1)}, u32[]{:S(2)}, u32[]{:S(2)}) collective-permute-start(f32[256,128]{1,0:T(8,128)S(1)} %get-tuple-element.70), channel_id=1, source_target_pairs={{0,2},{1,3},{2,0},{3,1},{4,6},{5,7},{6,4},{7,5},{8,10},{9,11},{10,... | collective-permute-start | bytes 393224 | tf_op jit(solution)/shard_map/ppermute | solution.py:161
  90.6 5.1 %collective-permute-done.12 = f32[128,256]{1,0:T(8,128)S(1)} collective-permute-done((f32[128,256]{1,0:T(8,128)S(1)}, f32[128,256]{1,0:T(8,128)S(1)}, u32[]{:S(2)}, u32[]{:S(2)}) %collective-permute-start.12) | collective-permute-done | bytes 131104 | tf_op jit(solution)/shard_map/ppermute | solution.py:161
  95.7 0.8 collective-permute-start.16
  96.5 5.4 %shard_map.84.refs_5_ = f32[1024,128]{1,0:T(8,128)S(1)} custom-call(bf16[1024,4096]{1,0:T(8,128)(2,1)} %refs_3_.9, bf16[1024,4096]{1,0:T(8,128)(2,1)} %refs_3_.9, bf16[1024,4096]{1,0:T(8,128)(2,1)} %refs_3_.9, bf16[1024,4096]{1,0:T(8,128)(2,1)} %refs_3_.9, bf16[3072,128]{1,0:T(8,128)(2,1)S(1)} %collective-permute-done.19.refs_4_), custom_call_target="tpu_custom_call" | custom-call | flops 805306368 | bytes 6291456 | tf_op jit(solution)/shard_map/pallas_call | solution.py:125
  102.0 2.3 %shard_map.85 = (f32[512,128]{1,0:T(8,128)S(1)}, f32[512,128]{1,0:T(8,128)S(1)}) custom-call(s32[1]{0:T(128)} %bitcast.2.bit_ref, bf16[1024,4096]{1,0:T(8,128)(2,1)} %refs_3_.9, bf16[1024,4096]{1,0:T(8,128)(2,1)} %refs_3_.9, bf16[1024,4096]{1,0:T(8,128)(2,1)} %refs_3_.9, bf16[1024,4096]{1,0:T(8,128)(2,1)} %refs_3_.9, ...), custom_call_target="tpu_custom_call" | custom-call | flops 268435456 | bytes 2097152 | tf_op jit(solution)/shard_map/pallas_call | solution.py:100
  104.4 0.2 select_reduce_fusion.1
  104.6 3.4 %collective-permute-start.17 = (f32[128,128]{1,0:T(8,128)S(1)}, f32[128,128]{1,0:T(8,128)S(1)}, u32[]{:S(2)}, u32[]{:S(2)}) collective-permute-start(f32[128,128]{1,0:T(8,128)S(1)} %add.71), channel_id=1, source_target_pairs={{0,8},{1,9},{2,10},{3,11},{4,12},{5,13},{6,14},{7,15},{8,0},{9,1},... | collective-permute-start | bytes 196616 | tf_op jit(solution)/shard_map/ppermute | solution.py:161
  108.0 1.6 %collective-permute-start.21 = (f32[256,128]{1,0:T(8,128)S(1)}, f32[256,128]{1,0:T(8,128)S(1)}, u32[]{:S(2)}, u32[]{:S(2)}) collective-permute-start(f32[256,128]{1,0:T(8,128)S(1)} %get-tuple-element.81), channel_id=1, source_target_pairs={{0,2},{1,3},{2,0},{3,1},{4,6},{5,7},{6,4},{7,5},{8,10},{9,11},{10,... | collective-permute-start | bytes 393224 | tf_op jit(solution)/shard_map/ppermute | solution.py:161
  109.7 2.5 %collective-permute-done.17 = f32[128,128]{1,0:T(8,128)S(1)} collective-permute-done((f32[128,128]{1,0:T(8,128)S(1)}, f32[128,128]{1,0:T(8,128)S(1)}, u32[]{:S(2)}, u32[]{:S(2)}) %collective-permute-start.17) | collective-permute-done | bytes 65568 | tf_op jit(solution)/shard_map/ppermute | solution.py:161
  112.2 1.6 %collective-permute-done.21.came_ref = f32[256,128]{1,0:T(8,128)S(1)} collective-permute-done((f32[256,128]{1,0:T(8,128)S(1)}, f32[256,128]{1,0:T(8,128)S(1)}, u32[]{:S(2)}, u32[]{:S(2)}) %collective-permute-start.21) | collective-permute-done | bytes 131104 | tf_op jit(solution)/shard_map/ppermute | solution.py:161
  114.0 4.0 %collective-permute-done.22 = f32[128,128]{1,0:T(8,128)S(1)} collective-permute-done((f32[128,128]{1,0:T(8,128)S(1)}, f32[128,128]{1,0:T(8,128)S(1)}, u32[]{:S(2)}, u32[]{:S(2)}) %collective-permute-start.22) | collective-permute-done | bytes 65568 | tf_op jit(solution)/shard_map/ppermute | solution.py:161
  118.1 1.2 collective-permute-start.23
  119.3 4.2 %collective-permute-done.23 = f32[128,128]{1,0:T(8,128)S(1)} collective-permute-done((f32[128,128]{1,0:T(8,128)S(1)}, f32[128,128]{1,0:T(8,128)S(1)}, u32[]{:S(2)}, u32[]{:S(2)}) %collective-permute-start.23) | collective-permute-done | bytes 65568 | tf_op jit(solution)/shard_map/ppermute | solution.py:161
  123.6 0.7 gather_fusion
  124.3 0.2 copy.14
  124.5 0.3 copy.15
  125.0 0.8 subtract_divide_fusion
  (59 shorter events, 1.6 us)
Async XLA Ops:
  0.0 6.2 %copy-start = (bf16[4096,512]{1,0:T(8,128)(2,1)S(1)}, bf16[4096,512]{1,0:T(8,128)(2,1)}, u32[]{:S(2)}) copy-start(bf16[4096,512]{1,0:T(8,128)(2,1)} %refs_4_) | copy-start | bytes 12582916
  3.2 49.7 %collective-permute-start = (bf16[4096,256]{1,0:T(8,128)(2,1)}, bf16[4096,256]{1,0:T(8,128)(2,1)}, u32[]{:S(2)}, u32[]{:S(2)}) collective-permute-start(bf16[4096,256]{1,0:T(8,128)(2,1)} %slice.20), channel_id=1, source_target_pairs={{0,16},{16,0},{1,17},{17,1},{2,18},{18,2},{3,19},{19,3},{4,20},{20... | collective-permute-start | bytes 6291464 | tf_op jit(solution)/shard_map/ppermute | solution.py:21
  18.9 2.0 %collective-permute-start.1 = (f32[512,256]{1,0:T(8,128)S(1)}, f32[512,256]{1,0:T(8,128)S(1)}, u32[]{:S(2)}, u32[]{:S(2)}) collective-permute-start(f32[512,256]{1,0:T(8,128)S(1)} %get-tuple-element.48), channel_id=1, source_target_pairs={{0,1},{1,0},{2,3},{3,2},{4,5},{5,4},{6,7},{7,6},{8,9},{9,8},{10,11... | collective-permute-start | bytes 1572872 | tf_op jit(solution)/shard_map/ppermute | solution.py:161
  18.9 3.5 %collective-permute-start.5 = (f32[512,256]{1,0:T(8,128)S(1)}, f32[512,256]{1,0:T(8,128)S(1)}, u32[]{:S(2)}, u32[]{:S(2)}) collective-permute-start(f32[512,256]{1,0:T(8,128)S(1)} %get-tuple-element.54), channel_id=1, source_target_pairs={{0,1},{1,0},{2,3},{3,2},{4,5},{5,4},{6,7},{7,6},{8,9},{9,8},{10,11... | collective-permute-start | bytes 1572872 | tf_op jit(solution)/shard_map/ppermute | solution.py:161
  20.9 9.2 %collective-permute-start.2 = (f32[256,256]{1,0:T(8,128)S(1)}, f32[256,256]{1,0:T(8,128)S(1)}, u32[]{:S(2)}, u32[]{:S(2)}) collective-permute-start(f32[256,256]{1,0:T(8,128)S(1)} %get-tuple-element.50), channel_id=1, source_target_pairs={{0,2},{1,3},{2,0},{3,1},{4,6},{5,7},{6,4},{7,5},{8,10},{9,11},{10,... | collective-permute-start | bytes 786440 | tf_op jit(solution)/shard_map/ppermute | solution.py:161
  22.5 12.4 %collective-permute-start.6 = (f32[256,256]{1,0:T(8,128)S(1)}, f32[256,256]{1,0:T(8,128)S(1)}, u32[]{:S(2)}, u32[]{:S(2)}) collective-permute-start(f32[256,256]{1,0:T(8,128)S(1)} %get-tuple-element.56), channel_id=1, source_target_pairs={{0,2},{1,3},{2,0},{3,1},{4,6},{5,7},{6,4},{7,5},{8,10},{9,11},{10,... | collective-permute-start | bytes 786440 | tf_op jit(solution)/shard_map/ppermute | solution.py:161
  30.1 6.5 %collective-permute-start.3 = (f32[128,256]{1,0:T(8,128)S(1)}, f32[128,256]{1,0:T(8,128)S(1)}, u32[]{:S(2)}, u32[]{:S(2)}) collective-permute-start(f32[128,256]{1,0:T(8,128)S(1)} %get-tuple-element.52), channel_id=1, source_target_pairs={{0,4},{1,5},{2,6},{3,7},{4,0},{5,1},{6,2},{7,3},{8,12},{9,13},{10,... | collective-permute-start | bytes 393224 | tf_op jit(solution)/shard_map/ppermute | solution.py:161
  35.0 6.5 %collective-permute-start.7 = (f32[128,256]{1,0:T(8,128)S(1)}, f32[128,256]{1,0:T(8,128)S(1)}, u32[]{:S(2)}, u32[]{:S(2)}) collective-permute-start(f32[128,256]{1,0:T(8,128)S(1)} %get-tuple-element.58), channel_id=1, source_target_pairs={{0,4},{1,5},{2,6},{3,7},{4,0},{5,1},{6,2},{7,3},{8,12},{9,13},{10,... | collective-permute-start | bytes 393224 | tf_op jit(solution)/shard_map/ppermute | solution.py:161
  36.6 12.1 %collective-permute-start.4 = (f32[128,256]{1,0:T(8,128)S(1)}, f32[128,256]{1,0:T(8,128)S(1)}, u32[]{:S(2)}, u32[]{:S(2)}) collective-permute-start(f32[128,256]{1,0:T(8,128)S(1)} %add.65), channel_id=1, source_target_pairs={{0,8},{1,9},{2,10},{3,11},{4,12},{5,13},{6,14},{7,15},{8,0},{9,1},... | collective-permute-start | bytes 393224 | tf_op jit(solution)/shard_map/ppermute | solution.py:161
  41.5 9.1 %collective-permute-start.8 = (f32[128,256]{1,0:T(8,128)S(1)}, f32[128,256]{1,0:T(8,128)S(1)}, u32[]{:S(2)}, u32[]{:S(2)}) collective-permute-start(f32[128,256]{1,0:T(8,128)S(1)} %add.67), channel_id=1, source_target_pairs={{0,8},{1,9},{2,10},{3,11},{4,12},{5,13},{6,14},{7,15},{8,0},{9,1},... | collective-permute-start | bytes 393224 | tf_op jit(solution)/shard_map/ppermute | solution.py:161
  43.9 33.8 %collective-permute-start.13 = (bf16[4096,128]{1,0:T(8,128)(2,1)}, bf16[4096,128]{1,0:T(8,128)(2,1)S(1)}, u32[]{:S(2)}, u32[]{:S(2)}) collective-permute-start(bf16[4096,128]{1,0:T(8,128)(2,1)} %slice.21), channel_id=1, source_target_pairs={{0,16},{16,0},{1,17},{17,1},{2,18},{18,2},{3,19},{19,3},{4,20},{20... | collective-permute-start | bytes 3145736 | tf_op jit(solution)/shard_map/ppermute | solution.py:21
  50.6 15.3 %copy-start.1 = (bf16[3072,128]{1,0:T(8,128)(2,1)S(1)}, bf16[3072,128]{1,0:T(8,128)(2,1)}, u32[]{:S(2)}) copy-start(bf16[3072,128]{1,0:T(8,128)(2,1)} %slice.22) | copy-start | bytes 2359300
  61.8 2.0 %collective-permute-start.9 = (f32[512,256]{1,0:T(8,128)S(1)}, f32[512,256]{1,0:T(8,128)S(1)}, u32[]{:S(2)}, u32[]{:S(2)}) collective-permute-start(f32[512,256]{1,0:T(8,128)S(1)} %get-tuple-element.61), channel_id=1, source_target_pairs={{0,1},{1,0},{2,3},{3,2},{4,5},{5,4},{6,7},{7,6},{8,9},{9,8},{10,11... | collective-permute-start | bytes 1572872 | tf_op jit(solution)/shard_map/ppermute | solution.py:161
  63.8 8.7 %collective-permute-start.10 = (f32[256,256]{1,0:T(8,128)S(1)}, f32[256,256]{1,0:T(8,128)S(1)}, u32[]{:S(2)}, u32[]{:S(2)}) collective-permute-start(f32[256,256]{1,0:T(8,128)S(1)} %get-tuple-element.63), channel_id=1, source_target_pairs={{0,2},{1,3},{2,0},{3,1},{4,6},{5,7},{6,4},{7,5},{8,10},{9,11},{10,... | collective-permute-start | bytes 786440 | tf_op jit(solution)/shard_map/ppermute | solution.py:161
  65.9 29.7 %collective-permute-start.19 = (bf16[3072,128]{1,0:T(8,128)(2,1)S(1)}, bf16[3072,128]{1,0:T(8,128)(2,1)S(1)}, u32[]{:S(2)}, u32[]{:S(2)}) collective-permute-start(bf16[3072,128]{1,0:T(8,128)(2,1)S(1)} %copy-done.1), channel_id=1, source_target_pairs={{0,16},{16,0},{1,17},{17,1},{2,18},{18,2},{3,19},{19,3},{4,20},{20... | collective-permute-start | bytes 2359304 | tf_op jit(solution)/shard_map/ppermute | solution.py:21
  72.6 5.1 %collective-permute-start.11 = (f32[128,256]{1,0:T(8,128)S(1)}, f32[128,256]{1,0:T(8,128)S(1)}, u32[]{:S(2)}, u32[]{:S(2)}) collective-permute-start(f32[128,256]{1,0:T(8,128)S(1)} %get-tuple-element.65), channel_id=1, source_target_pairs={{0,4},{1,5},{2,6},{3,7},{4,0},{5,1},{6,2},{7,3},{8,12},{9,13},{10,... | collective-permute-start | bytes 393224 | tf_op jit(solution)/shard_map/ppermute | solution.py:161
  77.7 6.9 %copy-start.2 = (bf16[1024,128]{1,0:T(8,128)(2,1)S(1)}, bf16[1024,128]{1,0:T(8,128)(2,1)}, u32[]{:S(2)}) copy-start(bf16[1024,128]{1,0:T(8,128)(2,1)} %slice.23) | copy-start | bytes 786436
  84.5 4.5 %collective-permute-start.14 = (f32[512,128]{1,0:T(8,128)S(1)}, f32[512,128]{1,0:T(8,128)S(1)}, u32[]{:S(2)}, u32[]{:S(2)}) collective-permute-start(f32[512,128]{1,0:T(8,128)S(1)} %get-tuple-element.68), channel_id=1, source_target_pairs={{0,1},{1,0},{2,3},{3,2},{4,5},{5,4},{6,7},{7,6},{8,9},{9,8},{10,11... | collective-permute-start | bytes 786440 | tf_op jit(solution)/shard_map/ppermute | solution.py:161
  84.6 17.4 %collective-permute-start.18 = (bf16[1024,128]{1,0:T(8,128)(2,1)S(1)}, bf16[1024,128]{1,0:T(8,128)(2,1)S(1)}, u32[]{:S(2)}, u32[]{:S(2)}) collective-permute-start(bf16[1024,128]{1,0:T(8,128)(2,1)S(1)} %copy-done.2), channel_id=1, source_target_pairs={{0,16},{16,0},{1,17},{17,1},{2,18},{18,2},{3,19},{19,3},{4,20},{20... | collective-permute-start | bytes 786440 | tf_op jit(solution)/shard_map/ppermute | solution.py:21
  86.4 9.3 %collective-permute-start.12 = (f32[128,256]{1,0:T(8,128)S(1)}, f32[128,256]{1,0:T(8,128)S(1)}, u32[]{:S(2)}, u32[]{:S(2)}) collective-permute-start(f32[128,256]{1,0:T(8,128)S(1)} %add.69), channel_id=1, source_target_pairs={{0,8},{1,9},{2,10},{3,11},{4,12},{5,13},{6,14},{7,15},{8,0},{9,1},... | collective-permute-start | bytes 393224 | tf_op jit(solution)/shard_map/ppermute | solution.py:161
  89.0 6.7 %collective-permute-start.15 = (f32[256,128]{1,0:T(8,128)S(1)}, f32[256,128]{1,0:T(8,128)S(1)}, u32[]{:S(2)}, u32[]{:S(2)}) collective-permute-start(f32[256,128]{1,0:T(8,128)S(1)} %get-tuple-element.70), channel_id=1, source_target_pairs={{0,2},{1,3},{2,0},{3,1},{4,6},{5,7},{6,4},{7,5},{8,10},{9,11},{10,... | collective-permute-start | bytes 393224 | tf_op jit(solution)/shard_map/ppermute | solution.py:161
  95.7 6.2 %collective-permute-start.16 = (f32[128,128]{1,0:T(8,128)S(1)}, f32[128,128]{1,0:T(8,128)S(1)}, u32[]{:S(2)}, u32[]{:S(2)}) collective-permute-start(f32[128,128]{1,0:T(8,128)S(1)} %get-tuple-element.73), channel_id=1, source_target_pairs={{0,4},{1,5},{2,6},{3,7},{4,0},{5,1},{6,2},{7,3},{8,12},{9,13},{10,... | collective-permute-start | bytes 196616 | tf_op jit(solution)/shard_map/ppermute | solution.py:161
  101.9 2.4 %copy-start.3 = (f32[512]{0:T(512)S(1)}, f32[512]{0:T(512)}, u32[]{:S(2)}) copy-start(f32[512]{0:T(512)} %param.13) | copy-start | bytes 6148
  101.9 2.4 %copy-start.5 = (s32[32]{0:T(128)S(1)}, s32[32]{0:T(128)}, u32[]{:S(2)}) copy-start(s32[32]{0:T(128)} %param.11) | copy-start | bytes 388
  101.9 7.7 %copy-start.7 = (s32[64]{0:T(128)S(1)}, s32[64]{0:T(128)}, u32[]{:S(2)}) copy-start(s32[64]{0:T(128)} %param.10) | copy-start | bytes 772
  101.9 11.9 %copy-start.4 = (s32[64,2]{0,1:T(2,128)S(1)}, s32[64,2]{0,1:T(2,128)}, u32[]{:S(2)}) copy-start(s32[64,2]{0,1:T(2,128)} %param.9) | copy-start | bytes 1540
  102.0 11.9 %copy-start.6 = (f32[96]{0:T(128)S(1)}, f32[96]{0:T(128)}, u32[]{:S(2)}) copy-start(f32[96]{0:T(128)} %param.12) | copy-start | bytes 1156
  104.3 3.7 %collective-permute-start.20 = (f32[512,128]{1,0:T(8,128)S(1)}, f32[512,128]{1,0:T(8,128)S(1)}, u32[]{:S(2)}, u32[]{:S(2)}) collective-permute-start(f32[512,128]{1,0:T(8,128)S(1)} %get-tuple-element.79), channel_id=1, source_target_pairs={{0,1},{1,0},{2,3},{3,2},{4,5},{5,4},{6,7},{7,6},{8,9},{9,8},{10,11... | collective-permute-start | bytes 786440 | tf_op jit(solution)/shard_map/ppermute | solution.py:161
  104.6 7.5 %collective-permute-start.17 = (f32[128,128]{1,0:T(8,128)S(1)}, f32[128,128]{1,0:T(8,128)S(1)}, u32[]{:S(2)}, u32[]{:S(2)}) collective-permute-start(f32[128,128]{1,0:T(8,128)S(1)} %add.71), channel_id=1, source_target_pairs={{0,8},{1,9},{2,10},{3,11},{4,12},{5,13},{6,14},{7,15},{8,0},{9,1},... | collective-permute-start | bytes 196616 | tf_op jit(solution)/shard_map/ppermute | solution.py:161
  108.0 5.7 %collective-permute-start.21 = (f32[256,128]{1,0:T(8,128)S(1)}, f32[256,128]{1,0:T(8,128)S(1)}, u32[]{:S(2)}, u32[]{:S(2)}) collective-permute-start(f32[256,128]{1,0:T(8,128)S(1)} %get-tuple-element.81), channel_id=1, source_target_pairs={{0,2},{1,3},{2,0},{3,1},{4,6},{5,7},{6,4},{7,5},{8,10},{9,11},{10,... | collective-permute-start | bytes 393224 | tf_op jit(solution)/shard_map/ppermute | solution.py:161
  113.7 4.3 %collective-permute-start.22 = (f32[128,128]{1,0:T(8,128)S(1)}, f32[128,128]{1,0:T(8,128)S(1)}, u32[]{:S(2)}, u32[]{:S(2)}) collective-permute-start(f32[128,128]{1,0:T(8,128)S(1)} %get-tuple-element.84), channel_id=1, source_target_pairs={{0,4},{1,5},{2,6},{3,7},{4,0},{5,1},{6,2},{7,3},{8,12},{9,13},{10,... | collective-permute-start | bytes 196616 | tf_op jit(solution)/shard_map/ppermute | solution.py:161
  118.1 5.4 %collective-permute-start.23 = (f32[128,128]{1,0:T(8,128)S(1)}, f32[128,128]{1,0:T(8,128)S(1)}, u32[]{:S(2)}, u32[]{:S(2)}) collective-permute-start(f32[128,128]{1,0:T(8,128)S(1)} %add.73), channel_id=1, source_target_pairs={{0,8},{1,9},{2,10},{3,11},{4,12},{5,13},{6,14},{7,15},{8,0},{9,1},... | collective-permute-start | bytes 196616 | tf_op jit(solution)/shard_map/ppermute | solution.py:161

commit v6 on v5

--- a/solution.py
+++ b/solution.py
@@ -7,8 +7,9 @@
 from jax.experimental.pallas import tpu as pltpu
 from jax.sharding import PartitionSpec as P
 
+LANES = 128
 DEPTH_CUTS = 4
-ROW_CUTS = 4
+ROW_CUTS = 1
 FREE = pl.CostEstimate(flops=0, bytes_accessed=0, transcendentals=0)
 OWN_SPLITS = 2
 PRODUCT_BYTES = 51 * 1024 * 1024
@@ -174,6 +175,34 @@
     return total + flipped_along(total, "virt", 1 << (len(bits) - 1)), stages
 
 
+def cut_kernel(boxes, source_ref, *refs):
+    copies = []
+    for index, (rows, columns) in enumerate(boxes):
+        part = (rows[1] - rows[0]) // DEPTH_CUTS
+        for low in range(0, rows[1] - rows[0], part):
+            source = source_ref.at[rows[0] + low : rows[0] + low + part, columns[0] : columns[1]]
+            target = refs[index].at[low : low + part, :]
+            copies.append(pltpu.make_async_copy(source, target, refs[-1].at[len(copies)]))
+    for copy in copies:
+        copy.start()
+    for copy in copies:
+        copy.wait()
+
+
+def cut_out(source, boxes):
+    if any(edge % LANES for _, columns in boxes for edge in columns):
+        return [source[rows[0] : rows[1], columns[0] : columns[1]] for rows, columns in boxes]
+    anywhere = pl.BlockSpec(memory_space=pl.ANY)
+    return pl.pallas_call(
+        functools.partial(cut_kernel, boxes),
+        out_shape=[jax.ShapeDtypeStruct((r[1] - r[0], c[1] - c[0]), source.dtype) for r, c in boxes],
+        in_specs=[anywhere],
+        out_specs=[anywhere] * len(boxes),
+        scratch_shapes=[pltpu.SemaphoreType.DMA((len(boxes) * DEPTH_CUTS,))],
+        cost_estimate=FREE,
+    )(source)
+
+
 def per_device(amplitudes, integrals, occ_pairs, partners, virt_list, eps_occ, eps_virt):
     width = virt_list.shape[0]
     count = lax.axis_size("pair")
@@ -189,11 +218,11 @@
     def sent(piece):
         return [passed_along(piece, "pair", -shift) for shift in range(1, count)]
 
-    first = integrals[:, cuts[0][0] : cuts[0][1]]
+    depth = integrals.shape[0]
+    late = depth // DEPTH_CUTS * (DEPTH_CUTS - 1)
+    first = cut_out(integrals, [((0, depth), cuts[0])])[0]
     rest = after(integrals, first)
-    low, high = cuts[-1]
-    late = integrals.shape[0] // DEPTH_CUTS * (DEPTH_CUTS - 1)
-    pieces = [first] + [rest[:, low:high] for low, high in cuts[1:-1]] + [rest[:late, low:high], rest[late:, low:high]]
+    pieces = [first, *cut_out(rest, [((0, depth), cut) for cut in cuts[1:-1]] + [((0, late), cuts[-1]), ((late, depth), cuts[-1])])]
     in_flight = [sent(pieces[0]), sent(pieces[1])]
     own_product = multiplied(amplitudes, after(rest, pieces), bits[0], order, splits=OWN_SPLITS)
     own_sums = [exchanged_sum(own_product[2 * part : 2 * part + 2], bits)[0] for part in range(OWN_SPLITS)]

time: 126 us -> 239 us (1.90)
  Pallas kernels: 33.4 us -> 157 us
  starting transfers between devices: 33.3 us -> 26.2 us
  local copies, waits for them, and re-layouts: 7.61 us -> 1.48 us
    pallas_call x0 -> x2, Pallas kernels: none -> 129 us  [cut_out(): pl.pallas_call(functools.partial(cut_kernel, boxes), out_shape=[jax.Shape...]
    slice x4 -> x0, local copies, waits for them, and re-layouts: 6.13 us -> none  [the longest x1 3.24 us: per_device(): first = integrals[:, cuts[0][0]:cuts[0][1]]]
    pallas_call x4, Pallas kernels: 27.6 us -> 22.5 us  [multiplied(): pl.pallas_call(functools.partial(product_kernel, steps, order, splits, ba...]
    ppermute x20, starting transfers between devices: 26.5 us -> 21.6 us  [flipped_along(): lax.ppermute(value, axis, [(source, source ^ bits) for source in range(co...]
    ppermute x20, waiting for transfers between devices: 47.3 us -> 51.7 us  [flipped_along(): lax.ppermute(value, axis, [(source, source ^ bits) for source in range(co...]
  transfers between devices with their start and end apart: 24 -> 24, of which waited for: 15 -> 14; matrix products, arithmetic and copies ran while one was open for 3% -> 0% of each run, Pallas kernels for 25% -> 38%
where the time goes in v6:
time: 239 us; the launch traced here: 238 us
  Pallas kernels  157 us (66%)
  waiting for transfers between devices  51.7 us (22%)
  starting transfers between devices  26.2 us (11%)
    pallas_call x2, Pallas kernels, cut_out(): pl.pallas_call(functools.partial(cut_kernel, boxes), out_shape=[jax.Shape...  129 us
    ppermute x20, waiting for transfers between devices, flipped_along(): lax.ppermute(value, axis, [(source, source ^ bits) for source in range(co...  51.7 us
    pallas_call x4, Pallas kernels, multiplied(): pl.pallas_call(functools.partial(product_kernel, steps, order, splits, ba...  22.5 us
    ppermute x20, starting transfers between devices, flipped_along(): lax.ppermute(value, axis, [(source, source ^ bits) for source in range(co...  21.6 us
  transfers between devices with their start and end apart: 24, of which 14 were waited for; matrix products, arithmetic and copies ran while one was open for 0% of the time, Pallas kernels for 38%

profile of v6, /device:TPU:0, one launch (start us, length us, event | category | flops | bytes accessed | tf_op | source)
XLA Modules:
  0.0 238.3 jit_solution(11230795203960870135)
XLA Ops:
  0.0 64.7 %shard_map.73 = bf16[4096,256]{1,0:T(8,128)(2,1)} custom-call(bf16[4096,512]{1,0:T(8,128)(2,1)} %refs_1_), custom_call_target="tpu_custom_call" | custom-call | tf_op jit(solution)/shard_map/pallas_call | solution.py:196
  64.7 3.0 %collective-permute-start = (bf16[4096,256]{1,0:T(8,128)(2,1)}, bf16[4096,256]{1,0:T(8,128)(2,1)}, u32[]{:S(2)}, u32[]{:S(2)}) collective-permute-start(bf16[4096,256]{1,0:T(8,128)(2,1)} %shard_map.73), channel_id=1, source_target_pairs={{0,16},{16,0},{1,17},{17,1},{2,18},{18,2},{3,19},{19,3},{4,20},{20... | collective-permute-start | bytes 6291464 | tf_op jit(solution)/shard_map/ppermute | solution.py:22
  67.7 64.7 %shard_map.74 = (bf16[4096,128]{1,0:T(8,128)(2,1)}, bf16[3072,128]{1,0:T(8,128)(2,1)}, bf16[1024,128]{1,0:T(8,128)(2,1)}) custom-call(bf16[4096,512]{1,0:T(8,128)(2,1)} %refs_1_), custom_call_target="tpu_custom_call" | custom-call | tf_op jit(solution)/shard_map/pallas_call | solution.py:196
  132.5 8.3 %shard_map.75 = (f32[512,256]{1,0:T(8,128)S(1)}, f32[512,256]{1,0:T(8,128)S(1)}, f32[512,256]{1,0:T(8,128)S(1)}, f32[512,256]{1,0:T(8,128)S(1)}) custom-call(s32[1]{0:T(128)} %bitcast.2.bit_ref, bf16[1024,4096]{1,0:T(8,128)(2,1)} %refs_0_.9, bf16[4096,512]{1,0:T(8,128)(2,1)} %refs_1_), custom_call_target="tpu_custom_call" | custom-call | tf_op jit(solution)/shard_map/pallas_call | solution.py:101
  140.8 0.5 collective-permute-start.5
  141.3 1.4 collective-permute-done.1.came_ref
  142.8 1.6 collective-permute-start.2
  144.4 0.7 collective-permute-start.6
  145.1 6.9 %collective-permute-done.2.came_ref = f32[256,256]{1,0:T(8,128)S(1)} collective-permute-done((f32[256,256]{1,0:T(8,128)S(1)}, f32[256,256]{1,0:T(8,128)S(1)}, u32[]{:S(2)}, u32[]{:S(2)}) %collective-permute-start.2) | collective-permute-done | bytes 262176 | tf_op jit(solution)/shard_map/ppermute | solution.py:162
  152.0 1.6 collective-permute-start.3
  153.6 3.1 %collective-permute-done.6.came_ref = f32[256,256]{1,0:T(8,128)S(1)} collective-permute-done((f32[256,256]{1,0:T(8,128)S(1)}, f32[256,256]{1,0:T(8,128)S(1)}, u32[]{:S(2)}, u32[]{:S(2)}) %collective-permute-start.6) | collective-permute-done | bytes 262176 | tf_op jit(solution)/shard_map/ppermute | solution.py:162
  156.8 1.6 collective-permute-start.7
  158.5 2.7 %collective-permute-start.4 = (f32[128,256]{1,0:T(8,128)S(1)}, f32[128,256]{1,0:T(8,128)S(1)}, u32[]{:S(2)}, u32[]{:S(2)}) collective-permute-start(f32[128,256]{1,0:T(8,128)S(1)} %add.65), channel_id=1, source_target_pairs={{0,8},{1,9},{2,10},{3,11},{4,12},{5,13},{6,14},{7,15},{8,0},{9,1},... | collective-permute-start | bytes 393224 | tf_op jit(solution)/shard_map/ppermute | solution.py:162
  161.1 2.2 collective-permute-done.7
  163.4 2.3 collective-permute-start.8
  165.7 0.5 collective-permute-start.13
  166.2 4.5 %collective-permute-done.4 = f32[128,256]{1,0:T(8,128)S(1)} collective-permute-done((f32[128,256]{1,0:T(8,128)S(1)}, f32[128,256]{1,0:T(8,128)S(1)}, u32[]{:S(2)}, u32[]{:S(2)}) %collective-permute-start.4) | collective-permute-done | bytes 131104 | tf_op jit(solution)/shard_map/ppermute | solution.py:162
  170.7 1.6 collective-permute-done.8
  172.4 6.2 %shard_map.80 = (f32[512,256]{1,0:T(8,128)S(1)}, f32[512,256]{1,0:T(8,128)S(1)}) custom-call(s32[1]{0:T(128)} %bitcast.2.bit_ref, bf16[1024,4096]{1,0:T(8,128)(2,1)} %refs_0_.9, bf16[4096,256]{1,0:T(8,128)(2,1)} %collective-permute-done.refs_1_), custom_call_target="tpu_custom_call" | custom-call | flops 2147483648 | bytes 8388608 | tf_op jit(solution)/shard_map/pallas_call | solution.py:101
  178.6 1.9 collective-permute-done.9.came_ref
  180.6 1.6 collective-permute-start.10
  182.1 0.5 collective-permute-start.19
  182.7 6.3 %collective-permute-done.10.came_ref = f32[256,256]{1,0:T(8,128)S(1)} collective-permute-done((f32[256,256]{1,0:T(8,128)S(1)}, f32[256,256]{1,0:T(8,128)S(1)}, u32[]{:S(2)}, u32[]{:S(2)}) %collective-permute-start.10) | collective-permute-done | bytes 262176 | tf_op jit(solution)/shard_map/ppermute | solution.py:162
  189.1 5.0 %collective-permute-done.11 = f32[128,256]{1,0:T(8,128)S(1)} collective-permute-done((f32[128,256]{1,0:T(8,128)S(1)}, f32[128,256]{1,0:T(8,128)S(1)}, u32[]{:S(2)}, u32[]{:S(2)}) %collective-permute-start.11) | collective-permute-done | bytes 131104 | tf_op jit(solution)/shard_map/ppermute | solution.py:162
  194.1 5.7 %shard_map.83 = (f32[512,128]{1,0:T(8,128)S(1)}, f32[512,128]{1,0:T(8,128)S(1)}) custom-call(s32[1]{0:T(128)} %bitcast.2.bit_ref, bf16[1024,4096]{1,0:T(8,128)(2,1)} %refs_0_.9, bf16[4096,128]{1,0:T(8,128)(2,1)S(1)} %collective-permute-done.13.refs_1_), custom_call_target="tpu_custom_call" | custom-call | flops 1073741824 | bytes 8388608 | tf_op jit(solution)/shard_map/pallas_call | solution.py:101
  199.9 0.6 collective-permute-start.18
  200.5 1.1 collective-permute-start.12
  201.6 1.6 collective-permute-start.15
  203.1 6.5 %collective-permute-done.12 = f32[128,256]{1,0:T(8,128)S(1)} collective-permute-done((f32[128,256]{1,0:T(8,128)S(1)}, f32[128,256]{1,0:T(8,128)S(1)}, u32[]{:S(2)}, u32[]{:S(2)}) %collective-permute-start.12) | collective-permute-done | bytes 131104 | tf_op jit(solution)/shard_map/ppermute | solution.py:162
  209.7 0.9 collective-permute-start.16
  210.6 4.7 %shard_map.86.refs_2_ = f32[1024,128]{1,0:T(8,128)S(1)} custom-call(bf16[1024,4096]{1,0:T(8,128)(2,1)} %refs_0_.9, bf16[3072,128]{1,0:T(8,128)(2,1)S(1)} %collective-permute-done.19.refs_1_), custom_call_target="tpu_custom_call" | custom-call | flops 805306368 | bytes 6291456 | tf_op jit(solution)/shard_map/pallas_call | solution.py:126
  215.4 2.4 shard_map.87
  217.8 0.2 select_reduce_fusion.1
  218.0 0.1 broadcast_add_fusion
  218.1 1.9 collective-permute-start.17
  220.0 1.5 collective-permute-start.21
  221.6 3.3 %collective-permute-done.17 = f32[128,128]{1,0:T(8,128)S(1)} collective-permute-done((f32[128,128]{1,0:T(8,128)S(1)}, f32[128,128]{1,0:T(8,128)S(1)}, u32[]{:S(2)}, u32[]{:S(2)}) %collective-permute-start.17) | collective-permute-done | bytes 65568 | tf_op jit(solution)/shard_map/ppermute | solution.py:162
  224.9 0.8 collective-permute-done.21.came_ref
  225.7 0.6 collective-permute-start.22
  226.3 0.2 select_reduce_fusion
  226.4 3.6 %collective-permute-done.22 = f32[128,128]{1,0:T(8,128)S(1)} collective-permute-done((f32[128,128]{1,0:T(8,128)S(1)}, f32[128,128]{1,0:T(8,128)S(1)}, u32[]{:S(2)}, u32[]{:S(2)}) %collective-permute-start.22) | collective-permute-done | bytes 65568 | tf_op jit(solution)/shard_map/ppermute | solution.py:162
  230.0 1.2 collective-permute-start.23
  231.3 4.6 %collective-permute-done.23 = f32[128,128]{1,0:T(8,128)S(1)} collective-permute-done((f32[128,128]{1,0:T(8,128)S(1)}, f32[128,128]{1,0:T(8,128)S(1)}, u32[]{:S(2)}, u32[]{:S(2)}) %collective-permute-start.23) | collective-permute-done | bytes 65568 | tf_op jit(solution)/shard_map/ppermute | solution.py:162
  236.0 0.7 gather_fusion
  236.7 0.2 copy.14
  237.0 0.3 copy.15
  237.3 0.2 copy.16
  237.5 0.8 subtract_divide_fusion
  (55 shorter events, 1.1 us)
Async XLA Ops:
  64.7 107.7 %collective-permute-start = (bf16[4096,256]{1,0:T(8,128)(2,1)}, bf16[4096,256]{1,0:T(8,128)(2,1)}, u32[]{:S(2)}, u32[]{:S(2)}) collective-permute-start(bf16[4096,256]{1,0:T(8,128)(2,1)} %shard_map.73), channel_id=1, source_target_pairs={{0,16},{16,0},{1,17},{17,1},{2,18},{18,2},{3,19},{19,3},{4,20},{20... | collective-permute-start | bytes 6291464 | tf_op jit(solution)/shard_map/ppermute | solution.py:22
  140.7 2.0 collective-permute-start.1
  140.8 3.5 %collective-permute-start.5 = (f32[512,256]{1,0:T(8,128)S(1)}, f32[512,256]{1,0:T(8,128)S(1)}, u32[]{:S(2)}, u32[]{:S(2)}) collective-permute-start(f32[512,256]{1,0:T(8,128)S(1)} %get-tuple-element.60), channel_id=1, source_target_pairs={{0,1},{1,0},{2,3},{3,2},{4,5},{5,4},{6,7},{7,6},{8,9},{9,8},{10,11... | collective-permute-start | bytes 1572872 | tf_op jit(solution)/shard_map/ppermute | solution.py:162
  142.8 9.2 %collective-permute-start.2 = (f32[256,256]{1,0:T(8,128)S(1)}, f32[256,256]{1,0:T(8,128)S(1)}, u32[]{:S(2)}, u32[]{:S(2)}) collective-permute-start(f32[256,256]{1,0:T(8,128)S(1)} %get-tuple-element.56), channel_id=1, source_target_pairs={{0,2},{1,3},{2,0},{3,1},{4,6},{5,7},{6,4},{7,5},{8,10},{9,11},{10,... | collective-permute-start | bytes 786440 | tf_op jit(solution)/shard_map/ppermute | solution.py:162
  144.4 12.4 %collective-permute-start.6 = (f32[256,256]{1,0:T(8,128)S(1)}, f32[256,256]{1,0:T(8,128)S(1)}, u32[]{:S(2)}, u32[]{:S(2)}) collective-permute-start(f32[256,256]{1,0:T(8,128)S(1)} %get-tuple-element.62), channel_id=1, source_target_pairs={{0,2},{1,3},{2,0},{3,1},{4,6},{5,7},{6,4},{7,5},{8,10},{9,11},{10,... | collective-permute-start | bytes 786440 | tf_op jit(solution)/shard_map/ppermute | solution.py:162
  152.0 6.5 %collective-permute-start.3 = (f32[128,256]{1,0:T(8,128)S(1)}, f32[128,256]{1,0:T(8,128)S(1)}, u32[]{:S(2)}, u32[]{:S(2)}) collective-permute-start(f32[128,256]{1,0:T(8,128)S(1)} %get-tuple-element.58), channel_id=1, source_target_pairs={{0,4},{1,5},{2,6},{3,7},{4,0},{5,1},{6,2},{7,3},{8,12},{9,13},{10,... | collective-permute-start | bytes 393224 | tf_op jit(solution)/shard_map/ppermute | solution.py:162
  156.8 6.5 %collective-permute-start.7 = (f32[128,256]{1,0:T(8,128)S(1)}, f32[128,256]{1,0:T(8,128)S(1)}, u32[]{:S(2)}, u32[]{:S(2)}) collective-permute-start(f32[128,256]{1,0:T(8,128)S(1)} %get-tuple-element.64), channel_id=1, source_target_pairs={{0,4},{1,5},{2,6},{3,7},{4,0},{5,1},{6,2},{7,3},{8,12},{9,13},{10,... | collective-permute-start | bytes 393224 | tf_op jit(solution)/shard_map/ppermute | solution.py:162
  158.5 12.2 %collective-permute-start.4 = (f32[128,256]{1,0:T(8,128)S(1)}, f32[128,256]{1,0:T(8,128)S(1)}, u32[]{:S(2)}, u32[]{:S(2)}) collective-permute-start(f32[128,256]{1,0:T(8,128)S(1)} %add.65), channel_id=1, source_target_pairs={{0,8},{1,9},{2,10},{3,11},{4,12},{5,13},{6,14},{7,15},{8,0},{9,1},... | collective-permute-start | bytes 393224 | tf_op jit(solution)/shard_map/ppermute | solution.py:162
  163.4 9.0 %collective-permute-start.8 = (f32[128,256]{1,0:T(8,128)S(1)}, f32[128,256]{1,0:T(8,128)S(1)}, u32[]{:S(2)}, u32[]{:S(2)}) collective-permute-start(f32[128,256]{1,0:T(8,128)S(1)} %add.67), channel_id=1, source_target_pairs={{0,8},{1,9},{2,10},{3,11},{4,12},{5,13},{6,14},{7,15},{8,0},{9,1},... | collective-permute-start | bytes 393224 | tf_op jit(solution)/shard_map/ppermute | solution.py:162
  165.7 28.4 %collective-permute-start.13 = (bf16[4096,128]{1,0:T(8,128)(2,1)}, bf16[4096,128]{1,0:T(8,128)(2,1)S(1)}, u32[]{:S(2)}, u32[]{:S(2)}) collective-permute-start(bf16[4096,128]{1,0:T(8,128)(2,1)} %get-tuple-element.49), channel_id=1, source_target_pairs={{0,16},{16,0},{1,17},{17,1},{2,18},{18,2},{3,19},{19,3},{4,20},{20... | collective-permute-start | bytes 3145736 | tf_op jit(solution)/shard_map/ppermute | solution.py:22
  172.4 9.8 %copy-start.4 = (bf16[3072,128]{1,0:T(8,128)(2,1)S(1)}, bf16[3072,128]{1,0:T(8,128)(2,1)}, u32[]{:S(2)}) copy-start(bf16[3072,128]{1,0:T(8,128)(2,1)} %get-tuple-element.81) | copy-start | bytes 2359300
  178.5 2.0 collective-permute-start.9
  180.6 8.4 %collective-permute-start.10 = (f32[256,256]{1,0:T(8,128)S(1)}, f32[256,256]{1,0:T(8,128)S(1)}, u32[]{:S(2)}, u32[]{:S(2)}) collective-permute-start(f32[256,256]{1,0:T(8,128)S(1)} %get-tuple-element.69), channel_id=1, source_target_pairs={{0,2},{1,3},{2,0},{3,1},{4,6},{5,7},{6,4},{7,5},{8,10},{9,11},{10,... | collective-permute-start | bytes 786440 | tf_op jit(solution)/shard_map/ppermute | solution.py:162
  182.1 27.5 %collective-permute-start.19 = (bf16[3072,128]{1,0:T(8,128)(2,1)S(1)}, bf16[3072,128]{1,0:T(8,128)(2,1)S(1)}, u32[]{:S(2)}, u32[]{:S(2)}) collective-permute-start(bf16[3072,128]{1,0:T(8,128)(2,1)S(1)} %copy-done.4), channel_id=1, source_target_pairs={{0,16},{16,0},{1,17},{17,1},{2,18},{18,2},{3,19},{19,3},{4,20},{20... | collective-permute-start | bytes 2359304 | tf_op jit(solution)/shard_map/ppermute | solution.py:22
  189.0 5.0 %collective-permute-start.11 = (f32[128,256]{1,0:T(8,128)S(1)}, f32[128,256]{1,0:T(8,128)S(1)}, u32[]{:S(2)}, u32[]{:S(2)}) collective-permute-start(f32[128,256]{1,0:T(8,128)S(1)} %get-tuple-element.71), channel_id=1, source_target_pairs={{0,4},{1,5},{2,6},{3,7},{4,0},{5,1},{6,2},{7,3},{8,12},{9,13},{10,... | collective-permute-start | bytes 393224 | tf_op jit(solution)/shard_map/ppermute | solution.py:162
  194.1 5.8 %copy-start.5 = (bf16[1024,128]{1,0:T(8,128)(2,1)S(1)}, bf16[1024,128]{1,0:T(8,128)(2,1)}, u32[]{:S(2)}) copy-start(bf16[1024,128]{1,0:T(8,128)(2,1)} %get-tuple-element.80) | copy-start | bytes 786436
  199.8 1.7 collective-permute-start.14
  199.9 15.5 %collective-permute-start.18 = (bf16[1024,128]{1,0:T(8,128)(2,1)S(1)}, bf16[1024,128]{1,0:T(8,128)(2,1)S(1)}, u32[]{:S(2)}, u32[]{:S(2)}) collective-permute-start(bf16[1024,128]{1,0:T(8,128)(2,1)S(1)} %copy-done.5), channel_id=1, source_target_pairs={{0,16},{16,0},{1,17},{17,1},{2,18},{18,2},{3,19},{19,3},{4,20},{20... | collective-permute-start | bytes 786440 | tf_op jit(solution)/shard_map/ppermute | solution.py:22
  200.5 9.1 %collective-permute-start.12 = (f32[128,256]{1,0:T(8,128)S(1)}, f32[128,256]{1,0:T(8,128)S(1)}, u32[]{:S(2)}, u32[]{:S(2)}) collective-permute-start(f32[128,256]{1,0:T(8,128)S(1)} %add.69), channel_id=1, source_target_pairs={{0,8},{1,9},{2,10},{3,11},{4,12},{5,13},{6,14},{7,15},{8,0},{9,1},... | collective-permute-start | bytes 393224 | tf_op jit(solution)/shard_map/ppermute | solution.py:162
  201.6 8.1 %collective-permute-start.15 = (f32[256,128]{1,0:T(8,128)S(1)}, f32[256,128]{1,0:T(8,128)S(1)}, u32[]{:S(2)}, u32[]{:S(2)}) collective-permute-start(f32[256,128]{1,0:T(8,128)S(1)} %get-tuple-element.76), channel_id=1, source_target_pairs={{0,2},{1,3},{2,0},{3,1},{4,6},{5,7},{6,4},{7,5},{8,10},{9,11},{10,... | collective-permute-start | bytes 393224 | tf_op jit(solution)/shard_map/ppermute | solution.py:162
  209.7 5.6 %collective-permute-start.16 = (f32[128,128]{1,0:T(8,128)S(1)}, f32[128,128]{1,0:T(8,128)S(1)}, u32[]{:S(2)}, u32[]{:S(2)}) collective-permute-start(f32[128,128]{1,0:T(8,128)S(1)} %get-tuple-element.79), channel_id=1, source_target_pairs={{0,4},{1,5},{2,6},{3,7},{4,0},{5,1},{6,2},{7,3},{8,12},{9,13},{10,... | collective-permute-start | bytes 196616 | tf_op jit(solution)/shard_map/ppermute | solution.py:162
  215.3 2.5 %copy-start = (f32[512]{0:T(512)S(1)}, f32[512]{0:T(512)}, u32[]{:S(2)}) copy-start(f32[512]{0:T(512)} %param.13) | copy-start | bytes 6148
  215.3 2.5 %copy-start.2 = (s32[32]{0:T(128)S(1)}, s32[32]{0:T(128)}, u32[]{:S(2)}) copy-start(s32[32]{0:T(128)} %param.11) | copy-start | bytes 388
  215.3 6.2 %copy-start.6 = (s32[64]{0:T(128)S(1)}, s32[64]{0:T(128)}, u32[]{:S(2)}) copy-start(s32[64]{0:T(128)} %param.10) | copy-start | bytes 772
  215.3 10.9 %copy-start.1 = (s32[64,2]{0,1:T(2,128)S(1)}, s32[64,2]{0,1:T(2,128)}, u32[]{:S(2)}) copy-start(s32[64,2]{0,1:T(2,128)} %param.9) | copy-start | bytes 1540
  215.4 10.9 %copy-start.3 = (f32[96]{0:T(128)S(1)}, f32[96]{0:T(128)}, u32[]{:S(2)}) copy-start(f32[96]{0:T(128)} %param.12) | copy-start | bytes 1156
  217.7 2.2 collective-permute-start.20
  218.1 6.8 %collective-permute-start.17 = (f32[128,128]{1,0:T(8,128)S(1)}, f32[128,128]{1,0:T(8,128)S(1)}, u32[]{:S(2)}, u32[]{:S(2)}) collective-permute-start(f32[128,128]{1,0:T(8,128)S(1)} %add.71), channel_id=1, source_target_pairs={{0,8},{1,9},{2,10},{3,11},{4,12},{5,13},{6,14},{7,15},{8,0},{9,1},... | collective-permute-start | bytes 196616 | tf_op jit(solution)/shard_map/ppermute | solution.py:162
  220.0 5.7 %collective-permute-start.21 = (f32[256,128]{1,0:T(8,128)S(1)}, f32[256,128]{1,0:T(8,128)S(1)}, u32[]{:S(2)}, u32[]{:S(2)}) collective-permute-start(f32[256,128]{1,0:T(8,128)S(1)} %get-tuple-element.87), channel_id=1, source_target_pairs={{0,2},{1,3},{2,0},{3,1},{4,6},{5,7},{6,4},{7,5},{8,10},{9,11},{10,... | collective-permute-start | bytes 393224 | tf_op jit(solution)/shard_map/ppermute | solution.py:162
  225.7 4.3 %collective-permute-start.22 = (f32[128,128]{1,0:T(8,128)S(1)}, f32[128,128]{1,0:T(8,128)S(1)}, u32[]{:S(2)}, u32[]{:S(2)}) collective-permute-start(f32[128,128]{1,0:T(8,128)S(1)} %get-tuple-element.90), channel_id=1, source_target_pairs={{0,4},{1,5},{2,6},{3,7},{4,0},{5,1},{6,2},{7,3},{8,12},{9,13},{10,... | collective-permute-start | bytes 196616 | tf_op jit(solution)/shard_map/ppermute | solution.py:162
  230.0 5.9 %collective-permute-start.23 = (f32[128,128]{1,0:T(8,128)S(1)}, f32[128,128]{1,0:T(8,128)S(1)}, u32[]{:S(2)}, u32[]{:S(2)}) collective-permute-start(f32[128,128]{1,0:T(8,128)S(1)} %add.73), channel_id=1, source_target_pairs={{0,8},{1,9},{2,10},{3,11},{4,12},{5,13},{6,14},{7,15},{8,0},{9,1},... | collective-permute-start | bytes 196616 | tf_op jit(solution)/shard_map/ppermute | solution.py:162

commit v7 on v6

--- a/solution.py
+++ b/solution.py
@@ -13,6 +13,7 @@
 FREE = pl.CostEstimate(flops=0, bytes_accessed=0, transcendentals=0)
 OWN_SPLITS = 2
 PRODUCT_BYTES = 51 * 1024 * 1024
+CUT_BYTES = 56 * 1024 * 1024
 SUM_BYTES = 8 * 1024 * 1024
 
 
@@ -171,8 +172,10 @@
             came = after(came, gates[level])
         parts = halved(keep, came, bits[level]) if level < len(bits) - 1 else [keep + came]
         stages.append(parts[0])
-    total = parts[0]
-    return total + flipped_along(total, "virt", 1 << (len(bits) - 1)), stages
+    return (parts[0], flipped_along(parts[0], "virt", 1 << (len(bits) - 1))), stages
+
+
+WHOLE = pl.BlockSpec(memory_space=pltpu.VMEM)
 
 
 def cut_kernel(boxes, source_ref, *refs):
@@ -189,18 +192,62 @@
         copy.wait()
 
 
-def cut_out(source, boxes):
-    if any(edge % LANES for _, columns in boxes for edge in columns):
-        return [source[rows[0] : rows[1], columns[0] : columns[1]] for rows, columns in boxes]
-    anywhere = pl.BlockSpec(memory_space=pl.ANY)
-    return pl.pallas_call(
-        functools.partial(cut_kernel, boxes),
-        out_shape=[jax.ShapeDtypeStruct((r[1] - r[0], c[1] - c[0]), source.dtype) for r, c in boxes],
-        in_specs=[anywhere],
-        out_specs=[anywhere] * len(boxes),
-        scratch_shapes=[pltpu.SemaphoreType.DMA((len(boxes) * DEPTH_CUTS,))],
+def cut_out(source, rows, columns):
+    if columns[0] % LANES or columns[1] % LANES:
+        return source[rows[0] : rows[1], columns[0] : columns[1]]
+    return pl.pallas_call(
+        functools.partial(cut_kernel, [(rows, columns)]),
+        out_shape=[jax.ShapeDtypeStruct((rows[1] - rows[0], columns[1] - columns[0]), source.dtype)],
+        in_specs=[pl.BlockSpec(memory_space=pl.ANY)],
+        out_specs=[WHOLE],
+        scratch_shapes=[pltpu.SemaphoreType.DMA((DEPTH_CUTS,))],
+        compiler_params=pltpu.CompilerParams(vmem_limit_bytes=CUT_BYTES),
         cost_estimate=FREE,
-    )(source)
+    )(source)[0]
+
+
+def last_kernel(width, starts, where_ref, rows_ref, virt_ref, occ_ref, *refs):
+    blocks, (out_ref, both_ref, tall_ref, turned_ref) = refs[:-4], refs[-4:]
+    rows = out_ref.shape[0]
+    for index, start in enumerate(starts):
+        value = blocks[index][...]
+        if index == len(starts) - 1:
+            value = value + blocks[index + 1][...]
+        columns = out_ref.shape[1] // 2
+        side = where_ref[1] if start < columns else 1 - where_ref[1]
+        place = pl.multiple_of(side * columns + start % columns, LANES)
+        both_ref[:, pl.ds(place, value.shape[1])] = value
+    upper = where_ref[0]
+    mine = both_ref[pl.ds(pl.multiple_of(upper * rows, rows), rows), :]
+    other = both_ref[pl.ds(pl.multiple_of((1 - upper) * rows, rows), rows), :]
+    chosen = (rows_ref[...] == lax.broadcasted_iota(jnp.int32, (rows, rows), 1)).astype(jnp.float32)
+    flipped = jnp.dot(chosen, other, precision=lax.Precision.HIGHEST, preferred_element_type=jnp.float32)
+    tall_ref[...] = flipped.T
+    for b in range(width):
+        turned_ref[b * width : (b + 1) * width, :] = tall_ref[pl.ds(b, width, stride=width), :]
+    out_ref[...] = (mine + turned_ref[...].T) / (virt_ref[...] - occ_ref[...])
+
+
+def last_steps(blocks, where, local_rows, virt_sum, occ_sum, width):
+    rows = occ_sum.shape[0]
+    columns = virt_sum.shape[0]
+    starts, start = [], 0
+    for block in blocks[:-1]:
+        starts.append(start)
+        start += block.shape[1]
+    return pl.pallas_call(
+        functools.partial(last_kernel, width, starts),
+        out_shape=jax.ShapeDtypeStruct((rows, columns), jnp.float32),
+        in_specs=[pl.BlockSpec(memory_space=pltpu.SMEM)] + [WHOLE] * (3 + len(blocks)),
+        out_specs=WHOLE,
+        scratch_shapes=[
+            pltpu.VMEM((2 * rows, columns), jnp.float32),
+            pltpu.VMEM((columns, rows), jnp.float32),
+            pltpu.VMEM((columns, rows), jnp.float32),
+        ],
+        compiler_params=pltpu.CompilerParams(vmem_limit_bytes=SUM_BYTES),
+        cost_estimate=FREE,
+    )(where, local_rows.reshape(rows, 1), virt_sum.reshape(1, columns), occ_sum.reshape(rows, 1), *blocks)
 
 
 def per_device(amplitudes, integrals, occ_pairs, partners, virt_list, eps_occ, eps_virt):
@@ -220,12 +267,13 @@
 
     depth = integrals.shape[0]
     late = depth // DEPTH_CUTS * (DEPTH_CUTS - 1)
-    first = cut_out(integrals, [((0, depth), cuts[0])])[0]
+    first = cut_out(integrals, (0, depth), cuts[0])
     rest = after(integrals, first)
-    pieces = [first, *cut_out(rest, [((0, depth), cut) for cut in cuts[1:-1]] + [((0, late), cuts[-1]), ((late, depth), cuts[-1])])]
+    low, high = cuts[-1]
+    pieces = [first] + [rest[:, low:high] for low, high in cuts[1:-1]] + [rest[:late, low:high], rest[late:, low:high]]
     in_flight = [sent(pieces[0]), sent(pieces[1])]
     own_product = multiplied(amplitudes, after(rest, pieces), bits[0], order, splits=OWN_SPLITS)
-    own_sums = [exchanged_sum(own_product[2 * part : 2 * part + 2], bits)[0] for part in range(OWN_SPLITS)]
+    own_sums = [jnp.add(*exchanged_sum(own_product[2 * part : 2 * part + 2], bits)[0]) for part in range(OWN_SPLITS)]
     sums = [own_sums] + [[] for _ in range(1, count)]
     in_flight += [sent(after(piece, own_sums)) for piece in pieces[2:]]
     earlier, gates = own_sums, {}
@@ -240,15 +288,10 @@
                 product = multiplied(amplitudes, arrived[shift - 1], bits[0], order)
             else:
                 product = multiplied(amplitudes, arrived[shift - 1], bits[0], order, DEPTH_CUTS - 1, bases[shift - 1])
-            total, stages = exchanged_sum(product, bits, gates)
+            terms, stages = exchanged_sum(product, bits, gates)
+            total = jnp.add(*terms)
             sums[shift].append(total)
             earlier, gates = stages[2] if step < len(cuts) - 2 else stages[0], {2: total}
-
-    both = in_column_order([jnp.concatenate(parts, axis=1) for parts in sums], count)
-    mine = jnp.where(upper, both[rows:], both[:rows])
-    other = jnp.where(upper, both[:rows], both[rows:])
-    flipped = jnp.take(other, partners % mine.shape[0], axis=0)
-    total = mine + transpose_block(flipped, width)
 
     occ_ids = jnp.arange(eps_occ.shape[0], dtype=jnp.int32)
     occ_match = occ_pairs[:, :, None] == occ_ids[None, None, :]
@@ -257,6 +300,16 @@
     virt_match = virt_list[:, None] == virt_ids[None, :]
     virt_energy = jnp.sum(jnp.where(virt_match, eps_virt[None, :], 0.0), axis=1)
     virt_sum = (virt_energy[:, None] + virt_energy[None, :]).reshape(-1)
+    if count == 2 and all(block.shape[1] % LANES == 0 for parts in sums for block in parts):
+        where = jnp.stack([upper.astype(jnp.int32), lax.axis_index("pair").astype(jnp.int32)])
+        blocks = [*sums[0], *sums[1][:-1], *terms]
+        return last_steps(blocks, where, partners % rows, virt_sum, occ_sum, width)
+    both = in_column_order([jnp.concatenate(parts, axis=1) for parts in sums], count)
+    mine = jnp.where(upper, both[rows:], both[:rows])
+    other = jnp.where(upper, both[:rows], both[rows:])
+    flipped = jnp.take(other, partners % mine.shape[0], axis=0)
+    total = mine + transpose_block(flipped, width)
+
     denominator = virt_sum[None, :] - occ_sum[:, None]
     return total / denominator
 

time: 239 us -> 123 us (0.51)
  Pallas kernels: 157 us -> 32.6 us
  starting transfers between devices: 26.2 us -> 34.4 us
    pallas_call x2, Pallas kernels: 129 us -> 5.26 us  [the longest x1 3.05 us: cut_out(): pl.pallas_call(functools.partial(cut_kernel, [(rows, columns)]), out_shap...]
    ppermute x20, starting transfers between devices: 21.6 us -> 27.3 us  [flipped_along(): lax.ppermute(value, axis, [(source, source ^ bits) for source in range(co...]
    ppermute x20, waiting for transfers between devices: 51.7 us -> 47 us  [flipped_along(): lax.ppermute(value, axis, [(source, source ^ bits) for source in range(co...]
    ppermute x4, waiting for transfers between devices: 0.01 us -> 4.27 us  [passed_along(): return lax.ppermute(value, axis, pairs)]
    slice x0 -> x3, local copies, waits for them, and re-layouts: none -> 2.88 us  [the longest x1 1.15 us: per_device(): rest[:, low:high]]
    ppermute x4, starting transfers between devices: 4.63 us -> 7.18 us  [passed_along(): return lax.ppermute(value, axis, pairs)]
  transfers between devices with their start and end apart: 24 -> 24, of which waited for: 14 -> 16; matrix products, arithmetic and copies ran while one was open for 0% -> 3% of each run, Pallas kernels for 38% -> 20%
where the time goes in v7:
time: 123 us
  waiting for transfers between devices  51.3 us (42%)
  starting transfers between devices  34.4 us (28%)
  Pallas kernels  32.6 us (27%)
  local copies, waits for them, and re-layouts  3.2 us (3%)
    ppermute x20, waiting for transfers between devices, flipped_along(): lax.ppermute(value, axis, [(source, source ^ bits) for source in range(co...  47 us
    ppermute x20, starting transfers between devices, flipped_along(): lax.ppermute(value, axis, [(source, source ^ bits) for source in range(co...  27.3 us
    pallas_call x4, Pallas kernels, multiplied(): pl.pallas_call(functools.partial(product_kernel, steps, order, splits, ba...  22.3 us
    ppermute x4, starting transfers between devices, passed_along(): return lax.ppermute(value, axis, pairs)  7.18 us
    pallas_call x1, Pallas kernels, plain_product(): pl.pallas_call(plain_kernel, grid=(columns.shape[0] // part,), out_shape=...  4.7 us
    ppermute x4, waiting for transfers between devices, passed_along(): return lax.ppermute(value, axis, pairs)  4.27 us
    pallas_call x1, Pallas kernels, cut_out(): pl.pallas_call(functools.partial(cut_kernel, [(rows, columns)]), out_shap...  3.05 us
  transfers between devices with their start and end apart: 24, of which 16 were waited for; matrix products, arithmetic and copies ran while one was open for 3% of the time, Pallas kernels for 20%

profile of v7, /device:TPU:0, one launch (start us, length us, event | category | flops | bytes accessed | tf_op | source)
XLA Modules:
  0.0 122.5 jit_solution(9239680468406352076)
XLA Ops:
  0.0 3.1 %shard_map.73 = bf16[4096,256]{1,0:T(8,128)(2,1)} custom-call(bf16[4096,512]{1,0:T(8,128)(2,1)} %refs_1_), custom_call_target="tpu_custom_call" | custom-call | tf_op jit(solution)/shard_map/pallas_call | solution.py:198
  3.1 3.0 %collective-permute-start.8 = (bf16[4096,256]{1,0:T(8,128)(2,1)}, bf16[4096,256]{1,0:T(8,128)(2,1)}, u32[]{:S(2)}, u32[]{:S(2)}) collective-permute-start(bf16[4096,256]{1,0:T(8,128)(2,1)} %shard_map.73), channel_id=1, source_target_pairs={{0,16},{16,0},{1,17},{17,1},{2,18},{18,2},{3,19},{19,3},{4,20},{20... | collective-permute-start | bytes 6291464 | tf_op jit(solution)/shard_map/ppermute | solution.py:23
  6.1 1.1 slice.9
  7.2 1.0 slice.10
  8.2 0.7 slice.11
  9.0 8.2 %shard_map.74 = (f32[512,256]{1,0:T(8,128)S(1)}, f32[512,256]{1,0:T(8,128)S(1)}, f32[512,256]{1,0:T(8,128)S(1)}, f32[512,256]{1,0:T(8,128)S(1)}) custom-call(s32[1]{0:T(128)} %bitcast.6.bit_ref, bf16[1024,4096]{1,0:T(8,128)(2,1)} %refs_0_.9, bf16[4096,512]{1,0:T(8,128)(2,1)} %refs_1_), custom_call_target="tpu_custom_call" | custom-call | tf_op jit(solution)/shard_map/pallas_call | solution.py:102
  17.3 0.5 collective-permute-start
  17.8 1.4 %collective-permute-done.4.came_ref = f32[512,256]{1,0:T(8,128)S(1)} collective-permute-done((f32[512,256]{1,0:T(8,128)S(1)}, f32[512,256]{1,0:T(8,128)S(1)}, u32[]{:S(2)}, u32[]{:S(2)}) %collective-permute-start.4) | collective-permute-done | bytes 524320 | tf_op jit(solution)/shard_map/ppermute | solution.py:163
  19.3 1.6 %collective-permute-start.5 = (f32[256,256]{1,0:T(8,128)S(1)}, f32[256,256]{1,0:T(8,128)S(1)}, u32[]{:S(2)}, u32[]{:S(2)}) collective-permute-start(f32[256,256]{1,0:T(8,128)S(1)} %get-tuple-element.56), channel_id=1, source_target_pairs={{0,2},{1,3},{2,0},{3,1},{4,6},{5,7},{6,4},{7,5},{8,10},{9,11},{10,... | collective-permute-start | bytes 786440 | tf_op jit(solution)/shard_map/ppermute | solution.py:163
  20.9 0.7 collective-permute-start.1
  21.6 6.9 %collective-permute-done.5.came_ref = f32[256,256]{1,0:T(8,128)S(1)} collective-permute-done((f32[256,256]{1,0:T(8,128)S(1)}, f32[256,256]{1,0:T(8,128)S(1)}, u32[]{:S(2)}, u32[]{:S(2)}) %collective-permute-start.5) | collective-permute-done | bytes 262176 | tf_op jit(solution)/shard_map/ppermute | solution.py:163
  28.5 1.6 %collective-permute-start.6 = (f32[128,256]{1,0:T(8,128)S(1)}, f32[128,256]{1,0:T(8,128)S(1)}, u32[]{:S(2)}, u32[]{:S(2)}) collective-permute-start(f32[128,256]{1,0:T(8,128)S(1)} %get-tuple-element.58), channel_id=1, source_target_pairs={{0,4},{1,5},{2,6},{3,7},{4,0},{5,1},{6,2},{7,3},{8,12},{9,13},{10,... | collective-permute-start | bytes 393224 | tf_op jit(solution)/shard_map/ppermute | solution.py:163
  30.2 3.1 %collective-permute-done.1.came_ref = f32[256,256]{1,0:T(8,128)S(1)} collective-permute-done((f32[256,256]{1,0:T(8,128)S(1)}, f32[256,256]{1,0:T(8,128)S(1)}, u32[]{:S(2)}, u32[]{:S(2)}) %collective-permute-start.1) | collective-permute-done | bytes 262176 | tf_op jit(solution)/shard_map/ppermute | solution.py:163
  33.3 1.6 %collective-permute-start.2 = (f32[128,256]{1,0:T(8,128)S(1)}, f32[128,256]{1,0:T(8,128)S(1)}, u32[]{:S(2)}, u32[]{:S(2)}) collective-permute-start(f32[128,256]{1,0:T(8,128)S(1)} %get-tuple-element.52), channel_id=1, source_target_pairs={{0,4},{1,5},{2,6},{3,7},{4,0},{5,1},{6,2},{7,3},{8,12},{9,13},{10,... | collective-permute-start | bytes 393224 | tf_op jit(solution)/shard_map/ppermute | solution.py:163
  35.0 2.7 %collective-permute-start.7 = (f32[128,256]{1,0:T(8,128)S(1)}, f32[128,256]{1,0:T(8,128)S(1)}, u32[]{:S(2)}, u32[]{:S(2)}) collective-permute-start(f32[128,256]{1,0:T(8,128)S(1)} %add.63), channel_id=1, source_target_pairs={{0,8},{1,9},{2,10},{3,11},{4,12},{5,13},{6,14},{7,15},{8,0},{9,1},... | collective-permute-start | bytes 393224 | tf_op jit(solution)/shard_map/ppermute | solution.py:163
  37.7 2.2 %collective-permute-done.2 = f32[128,256]{1,0:T(8,128)S(1)} collective-permute-done((f32[128,256]{1,0:T(8,128)S(1)}, f32[128,256]{1,0:T(8,128)S(1)}, u32[]{:S(2)}, u32[]{:S(2)}) %collective-permute-start.2) | collective-permute-done | bytes 131104 | tf_op jit(solution)/shard_map/ppermute | solution.py:163
  39.9 2.4 %collective-permute-start.3 = (f32[128,256]{1,0:T(8,128)S(1)}, f32[128,256]{1,0:T(8,128)S(1)}, u32[]{:S(2)}, u32[]{:S(2)}) collective-permute-start(f32[128,256]{1,0:T(8,128)S(1)} %add.61), channel_id=1, source_target_pairs={{0,8},{1,9},{2,10},{3,11},{4,12},{5,13},{6,14},{7,15},{8,0},{9,1},... | collective-permute-start | bytes 393224 | tf_op jit(solution)/shard_map/ppermute | solution.py:163
  42.3 0.5 collective-permute-start.13
  42.8 4.3 %collective-permute-done.7 = f32[128,256]{1,0:T(8,128)S(1)} collective-permute-done((f32[128,256]{1,0:T(8,128)S(1)}, f32[128,256]{1,0:T(8,128)S(1)}, u32[]{:S(2)}, u32[]{:S(2)}) %collective-permute-start.7) | collective-permute-done | bytes 131104 | tf_op jit(solution)/shard_map/ppermute | solution.py:163
  47.1 1.9 %collective-permute-done.3 = f32[128,256]{1,0:T(8,128)S(1)} collective-permute-done((f32[128,256]{1,0:T(8,128)S(1)}, f32[128,256]{1,0:T(8,128)S(1)}, u32[]{:S(2)}, u32[]{:S(2)}) %collective-permute-start.3) | collective-permute-done | bytes 131104 | tf_op jit(solution)/shard_map/ppermute | solution.py:163
  49.0 3.9 %collective-permute-done.8.refs_1_ = bf16[4096,256]{1,0:T(8,128)(2,1)} collective-permute-done((bf16[4096,256]{1,0:T(8,128)(2,1)}, bf16[4096,256]{1,0:T(8,128)(2,1)}, u32[]{:S(2)}, u32[]{:S(2)}) %collective-permute-start.8) | collective-permute-done | bytes 2097184 | tf_op jit(solution)/shard_map/ppermute | solution.py:23
  52.9 6.1 %shard_map.79 = (f32[512,256]{1,0:T(8,128)S(1)}, f32[512,256]{1,0:T(8,128)S(1)}) custom-call(s32[1]{0:T(128)} %bitcast.6.bit_ref, bf16[1024,4096]{1,0:T(8,128)(2,1)} %refs_0_.9, bf16[4096,256]{1,0:T(8,128)(2,1)} %collective-permute-done.8.refs_1_), custom_call_target="tpu_custom_call" | custom-call | flops 2147483648 | bytes 8388608 | tf_op jit(solution)/shard_map/pallas_call | solution.py:102
  59.0 1.9 %collective-permute-done.9.came_ref = f32[512,256]{1,0:T(8,128)S(1)} collective-permute-done((f32[512,256]{1,0:T(8,128)S(1)}, f32[512,256]{1,0:T(8,128)S(1)}, u32[]{:S(2)}, u32[]{:S(2)}) %collective-permute-start.9) | collective-permute-done | bytes 524320 | tf_op jit(solution)/shard_map/ppermute | solution.py:163
  61.0 2.1 %collective-permute-start.10 = (f32[256,256]{1,0:T(8,128)S(1)}, f32[256,256]{1,0:T(8,128)S(1)}, u32[]{:S(2)}, u32[]{:S(2)}) collective-permute-start(f32[256,256]{1,0:T(8,128)S(1)} %get-tuple-element.63), channel_id=1, source_target_pairs={{0,2},{1,3},{2,0},{3,1},{4,6},{5,7},{6,4},{7,5},{8,10},{9,11},{10,... | collective-permute-start | bytes 786440 | tf_op jit(solution)/shard_map/ppermute | solution.py:163
  63.1 1.5 %collective-permute-start.19 = (bf16[3072,128]{1,0:T(8,128)(2,1)S(1)}, bf16[3072,128]{1,0:T(8,128)(2,1)S(1)}, u32[]{:S(2)}, u32[]{:S(2)}) collective-permute-start(bf16[3072,128]{1,0:T(8,128)(2,1)S(1)} %copy-done.1), channel_id=1, source_target_pairs={{0,16},{16,0},{1,17},{17,1},{2,18},{18,2},{3,19},{19,3},{4,20},{20... | collective-permute-start | bytes 2359304 | tf_op jit(solution)/shard_map/ppermute | solution.py:23
  64.6 5.1 %collective-permute-done.10.came_ref = f32[256,256]{1,0:T(8,128)S(1)} collective-permute-done((f32[256,256]{1,0:T(8,128)S(1)}, f32[256,256]{1,0:T(8,128)S(1)}, u32[]{:S(2)}, u32[]{:S(2)}) %collective-permute-start.10) | collective-permute-done | bytes 262176 | tf_op jit(solution)/shard_map/ppermute | solution.py:163
  69.7 1.9 %collective-permute-start.11 = (f32[128,256]{1,0:T(8,128)S(1)}, f32[128,256]{1,0:T(8,128)S(1)}, u32[]{:S(2)}, u32[]{:S(2)}) collective-permute-start(f32[128,256]{1,0:T(8,128)S(1)} %get-tuple-element.65), channel_id=1, source_target_pairs={{0,4},{1,5},{2,6},{3,7},{4,0},{5,1},{6,2},{7,3},{8,12},{9,13},{10,... | collective-permute-start | bytes 393224 | tf_op jit(solution)/shard_map/ppermute | solution.py:163
  71.6 3.2 %collective-permute-done.11 = f32[128,256]{1,0:T(8,128)S(1)} collective-permute-done((f32[128,256]{1,0:T(8,128)S(1)}, f32[128,256]{1,0:T(8,128)S(1)}, u32[]{:S(2)}, u32[]{:S(2)}) %collective-permute-start.11) | collective-permute-done | bytes 131104 | tf_op jit(solution)/shard_map/ppermute | solution.py:163
  74.9 0.4 collective-permute-done.13.refs_1_
  75.2 5.7 %shard_map.82 = (f32[512,128]{1,0:T(8,128)S(1)}, f32[512,128]{1,0:T(8,128)S(1)}) custom-call(s32[1]{0:T(128)} %bitcast.6.bit_ref, bf16[1024,4096]{1,0:T(8,128)(2,1)} %refs_0_.9, bf16[4096,128]{1,0:T(8,128)(2,1)S(1)} %collective-permute-done.13.refs_1_), custom_call_target="tpu_custom_call" | custom-call | flops 1073741824 | bytes 8388608 | tf_op jit(solution)/shard_map/pallas_call | solution.py:102
  81.0 2.1 %collective-permute-start.18 = (bf16[1024,128]{1,0:T(8,128)(2,1)S(1)}, bf16[1024,128]{1,0:T(8,128)(2,1)S(1)}, u32[]{:S(2)}, u32[]{:S(2)}) collective-permute-start(bf16[1024,128]{1,0:T(8,128)(2,1)S(1)} %copy-done.2), channel_id=1, source_target_pairs={{0,16},{16,0},{1,17},{17,1},{2,18},{18,2},{3,19},{19,3},{4,20},{20... | collective-permute-start | bytes 786440 | tf_op jit(solution)/shard_map/ppermute | solution.py:23
  83.1 2.6 %collective-permute-start.12 = (f32[128,256]{1,0:T(8,128)S(1)}, f32[128,256]{1,0:T(8,128)S(1)}, u32[]{:S(2)}, u32[]{:S(2)}) collective-permute-start(f32[128,256]{1,0:T(8,128)S(1)} %add.65), channel_id=1, source_target_pairs={{0,8},{1,9},{2,10},{3,11},{4,12},{5,13},{6,14},{7,15},{8,0},{9,1},... | collective-permute-start | bytes 393224 | tf_op jit(solution)/shard_map/ppermute | solution.py:163
  85.8 1.6 %collective-permute-start.15 = (f32[256,128]{1,0:T(8,128)S(1)}, f32[256,128]{1,0:T(8,128)S(1)}, u32[]{:S(2)}, u32[]{:S(2)}) collective-permute-start(f32[256,128]{1,0:T(8,128)S(1)} %get-tuple-element.70), channel_id=1, source_target_pairs={{0,2},{1,3},{2,0},{3,1},{4,6},{5,7},{6,4},{7,5},{8,10},{9,11},{10,... | collective-permute-start | bytes 393224 | tf_op jit(solution)/shard_map/ppermute | solution.py:163
  87.3 5.1 %collective-permute-done.12 = f32[128,256]{1,0:T(8,128)S(1)} collective-permute-done((f32[128,256]{1,0:T(8,128)S(1)}, f32[128,256]{1,0:T(8,128)S(1)}, u32[]{:S(2)}, u32[]{:S(2)}) %collective-permute-start.12) | collective-permute-done | bytes 131104 | tf_op jit(solution)/shard_map/ppermute | solution.py:163
  92.5 1.8 %collective-permute-start.16 = (f32[128,128]{1,0:T(8,128)S(1)}, f32[128,128]{1,0:T(8,128)S(1)}, u32[]{:S(2)}, u32[]{:S(2)}) collective-permute-start(f32[128,128]{1,0:T(8,128)S(1)} %get-tuple-element.73), channel_id=1, source_target_pairs={{0,4},{1,5},{2,6},{3,7},{4,0},{5,1},{6,2},{7,3},{8,12},{9,13},{10,... | collective-permute-start | bytes 196616 | tf_op jit(solution)/shard_map/ppermute | solution.py:163
  94.3 4.7 %shard_map.85.refs_2_ = f32[1024,128]{1,0:T(8,128)S(1)} custom-call(bf16[1024,4096]{1,0:T(8,128)(2,1)} %refs_0_.9, bf16[3072,128]{1,0:T(8,128)(2,1)S(1)} %collective-permute-done.19.refs_1_), custom_call_target="tpu_custom_call" | custom-call | flops 805306368 | bytes 6291456 | tf_op jit(solution)/shard_map/pallas_call | solution.py:127
  99.1 2.3 %shard_map.86 = (f32[512,128]{1,0:T(8,128)S(1)}, f32[512,128]{1,0:T(8,128)S(1)}) custom-call(s32[1]{0:T(128)} %bitcast.6.bit_ref, bf16[1024,4096]{1,0:T(8,128)(2,1)} %refs_0_.9, bf16[1024,128]{1,0:T(8,128)(2,1)S(1)} %collective-permute-done.18.refs_1_, f32[1024,128]{1,0:T(8,128)S(1)} %shard_map.85.refs_2_), custom_call_target="tpu_custom_call" | custom-call | flops 268435456 | bytes 2097152 | tf_op jit(solution)/shard_map/pallas_call | solution.py:102
  101.6 0.2 select_reduce_fusion.1
  101.8 2.6 %collective-permute-start.17 = (f32[128,128]{1,0:T(8,128)S(1)}, f32[128,128]{1,0:T(8,128)S(1)}, u32[]{:S(2)}, u32[]{:S(2)}) collective-permute-start(f32[128,128]{1,0:T(8,128)S(1)} %add.67), channel_id=1, source_target_pairs={{0,8},{1,9},{2,10},{3,11},{4,12},{5,13},{6,14},{7,15},{8,0},{9,1},... | collective-permute-start | bytes 196616 | tf_op jit(solution)/shard_map/ppermute | solution.py:163
  104.4 1.6 %collective-permute-start.21 = (f32[256,128]{1,0:T(8,128)S(1)}, f32[256,128]{1,0:T(8,128)S(1)}, u32[]{:S(2)}, u32[]{:S(2)}) collective-permute-start(f32[256,128]{1,0:T(8,128)S(1)} %get-tuple-element.81), channel_id=1, source_target_pairs={{0,2},{1,3},{2,0},{3,1},{4,6},{5,7},{6,4},{7,5},{8,10},{9,11},{10,... | collective-permute-start | bytes 393224 | tf_op jit(solution)/shard_map/ppermute | solution.py:163
  106.1 2.3 %collective-permute-done.17 = f32[128,128]{1,0:T(8,128)S(1)} collective-permute-done((f32[128,128]{1,0:T(8,128)S(1)}, f32[128,128]{1,0:T(8,128)S(1)}, u32[]{:S(2)}, u32[]{:S(2)}) %collective-permute-start.17) | collective-permute-done | bytes 65568 | tf_op jit(solution)/shard_map/ppermute | solution.py:163
  108.4 1.7 %collective-permute-done.21.came_ref = f32[256,128]{1,0:T(8,128)S(1)} collective-permute-done((f32[256,128]{1,0:T(8,128)S(1)}, f32[256,128]{1,0:T(8,128)S(1)}, u32[]{:S(2)}, u32[]{:S(2)}) %collective-permute-start.21) | collective-permute-done | bytes 131104 | tf_op jit(solution)/shard_map/ppermute | solution.py:163
  110.1 0.5 collective-permute-start.22
  110.7 0.2 select_reduce_fusion
  111.0 3.5 %collective-permute-done.22 = f32[128,128]{1,0:T(8,128)S(1)} collective-permute-done((f32[128,128]{1,0:T(8,128)S(1)}, f32[128,128]{1,0:T(8,128)S(1)}, u32[]{:S(2)}, u32[]{:S(2)}) %collective-permute-start.22) | collective-permute-done | bytes 65568 | tf_op jit(solution)/shard_map/ppermute | solution.py:163
  114.5 1.2 %collective-permute-start.23 = (f32[128,128]{1,0:T(8,128)S(1)}, f32[128,128]{1,0:T(8,128)S(1)}, u32[]{:S(2)}, u32[]{:S(2)}) collective-permute-start(f32[128,128]{1,0:T(8,128)S(1)} %add.69.refs_4_), channel_id=1, source_target_pairs={{0,8},{1,9},{2,10},{3,11},{4,12},{5,13},{6,14},{7,15},{8,0},{9,1},... | collective-permute-start | bytes 196616 | tf_op jit(solution)/shard_map/ppermute | solution.py:163
  115.8 4.5 %collective-permute-done.23.refs_5_ = f32[128,128]{1,0:T(8,128)S(1)} collective-permute-done((f32[128,128]{1,0:T(8,128)S(1)}, f32[128,128]{1,0:T(8,128)S(1)}, u32[]{:S(2)}, u32[]{:S(2)}) %collective-permute-start.23) | collective-permute-done | bytes 65568 | tf_op jit(solution)/shard_map/ppermute | solution.py:163
  120.3 2.2 %shard_map.89 = f32[64,1024]{1,0:T(8,128)} custom-call(s32[2]{0:T(128)S(1)} %pad_add_fusion.where_ref, s32[64,1]{1,0:T(8,128)S(1)} %copy.11.rows_ref, f32[1,1024]{1,0:T(1,128)S(1)} %add.60.virt_ref, f32[64,1]{1,0:T(8,128)S(1)} %copy.12.occ_ref, f32[128,256]{1,0:T(8,128)S(1)} %add.62.refs_0_, f32[128,256]{1,0:T(8,128)S(1)} %add.64.refs_1_, ...), custom_call_target="tpu_custom_call" | custom-call | tf_op jit(solution)/shard_map/pallas_call | solution.py:238
  (53 shorter events, 1.3 us)
Async XLA Ops:
  0.0 6.1 %copy-start = (bf16[4096,512]{1,0:T(8,128)(2,1)S(1)}, bf16[4096,512]{1,0:T(8,128)(2,1)}, u32[]{:S(2)}) copy-start(bf16[4096,512]{1,0:T(8,128)(2,1)} %refs_1_) | copy-start | bytes 12582916
  3.1 49.8 %collective-permute-start.8 = (bf16[4096,256]{1,0:T(8,128)(2,1)}, bf16[4096,256]{1,0:T(8,128)(2,1)}, u32[]{:S(2)}, u32[]{:S(2)}) collective-permute-start(bf16[4096,256]{1,0:T(8,128)(2,1)} %shard_map.73), channel_id=1, source_target_pairs={{0,16},{16,0},{1,17},{17,1},{2,18},{18,2},{3,19},{19,3},{4,20},{20... | collective-permute-start | bytes 6291464 | tf_op jit(solution)/shard_map/ppermute | solution.py:23
  17.2 2.0 %collective-permute-start.4 = (f32[512,256]{1,0:T(8,128)S(1)}, f32[512,256]{1,0:T(8,128)S(1)}, u32[]{:S(2)}, u32[]{:S(2)}) collective-permute-start(f32[512,256]{1,0:T(8,128)S(1)} %get-tuple-element.54), channel_id=1, source_target_pairs={{0,1},{1,0},{2,3},{3,2},{4,5},{5,4},{6,7},{7,6},{8,9},{9,8},{10,11... | collective-permute-start | bytes 1572872 | tf_op jit(solution)/shard_map/ppermute | solution.py:163
  17.3 3.5 %collective-permute-start = (f32[512,256]{1,0:T(8,128)S(1)}, f32[512,256]{1,0:T(8,128)S(1)}, u32[]{:S(2)}, u32[]{:S(2)}) collective-permute-start(f32[512,256]{1,0:T(8,128)S(1)} %get-tuple-element.48), channel_id=1, source_target_pairs={{0,1},{1,0},{2,3},{3,2},{4,5},{5,4},{6,7},{7,6},{8,9},{9,8},{10,11... | collective-permute-start | bytes 1572872 | tf_op jit(solution)/shard_map/ppermute | solution.py:163
  19.3 9.2 %collective-permute-start.5 = (f32[256,256]{1,0:T(8,128)S(1)}, f32[256,256]{1,0:T(8,128)S(1)}, u32[]{:S(2)}, u32[]{:S(2)}) collective-permute-start(f32[256,256]{1,0:T(8,128)S(1)} %get-tuple-element.56), channel_id=1, source_target_pairs={{0,2},{1,3},{2,0},{3,1},{4,6},{5,7},{6,4},{7,5},{8,10},{9,11},{10,... | collective-permute-start | bytes 786440 | tf_op jit(solution)/shard_map/ppermute | solution.py:163
  20.9 12.4 %collective-permute-start.1 = (f32[256,256]{1,0:T(8,128)S(1)}, f32[256,256]{1,0:T(8,128)S(1)}, u32[]{:S(2)}, u32[]{:S(2)}) collective-permute-start(f32[256,256]{1,0:T(8,128)S(1)} %get-tuple-element.50), channel_id=1, source_target_pairs={{0,2},{1,3},{2,0},{3,1},{4,6},{5,7},{6,4},{7,5},{8,10},{9,11},{10,... | collective-permute-start | bytes 786440 | tf_op jit(solution)/shard_map/ppermute | solution.py:163
  28.5 6.5 %collective-permute-start.6 = (f32[128,256]{1,0:T(8,128)S(1)}, f32[128,256]{1,0:T(8,128)S(1)}, u32[]{:S(2)}, u32[]{:S(2)}) collective-permute-start(f32[128,256]{1,0:T(8,128)S(1)} %get-tuple-element.58), channel_id=1, source_target_pairs={{0,4},{1,5},{2,6},{3,7},{4,0},{5,1},{6,2},{7,3},{8,12},{9,13},{10,... | collective-permute-start | bytes 393224 | tf_op jit(solution)/shard_map/ppermute | solution.py:163
  33.3 6.5 %collective-permute-start.2 = (f32[128,256]{1,0:T(8,128)S(1)}, f32[128,256]{1,0:T(8,128)S(1)}, u32[]{:S(2)}, u32[]{:S(2)}) collective-permute-start(f32[128,256]{1,0:T(8,128)S(1)} %get-tuple-element.52), channel_id=1, source_target_pairs={{0,4},{1,5},{2,6},{3,7},{4,0},{5,1},{6,2},{7,3},{8,12},{9,13},{10,... | collective-permute-start | bytes 393224 | tf_op jit(solution)/shard_map/ppermute | solution.py:163
  35.0 12.1 %collective-permute-start.7 = (f32[128,256]{1,0:T(8,128)S(1)}, f32[128,256]{1,0:T(8,128)S(1)}, u32[]{:S(2)}, u32[]{:S(2)}) collective-permute-start(f32[128,256]{1,0:T(8,128)S(1)} %add.63), channel_id=1, source_target_pairs={{0,8},{1,9},{2,10},{3,11},{4,12},{5,13},{6,14},{7,15},{8,0},{9,1},... | collective-permute-start | bytes 393224 | tf_op jit(solution)/shard_map/ppermute | solution.py:163
  39.9 9.1 %collective-permute-start.3 = (f32[128,256]{1,0:T(8,128)S(1)}, f32[128,256]{1,0:T(8,128)S(1)}, u32[]{:S(2)}, u32[]{:S(2)}) collective-permute-start(f32[128,256]{1,0:T(8,128)S(1)} %add.61), channel_id=1, source_target_pairs={{0,8},{1,9},{2,10},{3,11},{4,12},{5,13},{6,14},{7,15},{8,0},{9,1},... | collective-permute-start | bytes 393224 | tf_op jit(solution)/shard_map/ppermute | solution.py:163
  42.3 32.9 %collective-permute-start.13 = (bf16[4096,128]{1,0:T(8,128)(2,1)}, bf16[4096,128]{1,0:T(8,128)(2,1)S(1)}, u32[]{:S(2)}, u32[]{:S(2)}) collective-permute-start(bf16[4096,128]{1,0:T(8,128)(2,1)} %slice.9), channel_id=1, source_target_pairs={{0,16},{16,0},{1,17},{17,1},{2,18},{18,2},{3,19},{19,3},{4,20},{20... | collective-permute-start | bytes 3145736 | tf_op jit(solution)/shard_map/ppermute | solution.py:23
  49.0 14.1 %copy-start.1 = (bf16[3072,128]{1,0:T(8,128)(2,1)S(1)}, bf16[3072,128]{1,0:T(8,128)(2,1)}, u32[]{:S(2)}) copy-start(bf16[3072,128]{1,0:T(8,128)(2,1)} %slice.10) | copy-start | bytes 2359300
  59.0 2.0 %collective-permute-start.9 = (f32[512,256]{1,0:T(8,128)S(1)}, f32[512,256]{1,0:T(8,128)S(1)}, u32[]{:S(2)}, u32[]{:S(2)}) collective-permute-start(f32[512,256]{1,0:T(8,128)S(1)} %get-tuple-element.61), channel_id=1, source_target_pairs={{0,1},{1,0},{2,3},{3,2},{4,5},{5,4},{6,7},{7,6},{8,9},{9,8},{10,11... | collective-permute-start | bytes 1572872 | tf_op jit(solution)/shard_map/ppermute | solution.py:163
  61.0 8.7 %collective-permute-start.10 = (f32[256,256]{1,0:T(8,128)S(1)}, f32[256,256]{1,0:T(8,128)S(1)}, u32[]{:S(2)}, u32[]{:S(2)}) collective-permute-start(f32[256,256]{1,0:T(8,128)S(1)} %get-tuple-element.63), channel_id=1, source_target_pairs={{0,2},{1,3},{2,0},{3,1},{4,6},{5,7},{6,4},{7,5},{8,10},{9,11},{10,... | collective-permute-start | bytes 786440 | tf_op jit(solution)/shard_map/ppermute | solution.py:163
  63.1 29.3 %collective-permute-start.19 = (bf16[3072,128]{1,0:T(8,128)(2,1)S(1)}, bf16[3072,128]{1,0:T(8,128)(2,1)S(1)}, u32[]{:S(2)}, u32[]{:S(2)}) collective-permute-start(bf16[3072,128]{1,0:T(8,128)(2,1)S(1)} %copy-done.1), channel_id=1, source_target_pairs={{0,16},{16,0},{1,17},{17,1},{2,18},{18,2},{3,19},{19,3},{4,20},{20... | collective-permute-start | bytes 2359304 | tf_op jit(solution)/shard_map/ppermute | solution.py:23
  69.7 5.1 %collective-permute-start.11 = (f32[128,256]{1,0:T(8,128)S(1)}, f32[128,256]{1,0:T(8,128)S(1)}, u32[]{:S(2)}, u32[]{:S(2)}) collective-permute-start(f32[128,256]{1,0:T(8,128)S(1)} %get-tuple-element.65), channel_id=1, source_target_pairs={{0,4},{1,5},{2,6},{3,7},{4,0},{5,1},{6,2},{7,3},{8,12},{9,13},{10,... | collective-permute-start | bytes 393224 | tf_op jit(solution)/shard_map/ppermute | solution.py:163
  74.8 6.2 %copy-start.2 = (bf16[1024,128]{1,0:T(8,128)(2,1)S(1)}, bf16[1024,128]{1,0:T(8,128)(2,1)}, u32[]{:S(2)}) copy-start(bf16[1024,128]{1,0:T(8,128)(2,1)} %slice.11) | copy-start | bytes 786436
  80.9 4.8 %collective-permute-start.14 = (f32[512,128]{1,0:T(8,128)S(1)}, f32[512,128]{1,0:T(8,128)S(1)}, u32[]{:S(2)}, u32[]{:S(2)}) collective-permute-start(f32[512,128]{1,0:T(8,128)S(1)} %get-tuple-element.68), channel_id=1, source_target_pairs={{0,1},{1,0},{2,3},{3,2},{4,5},{5,4},{6,7},{7,6},{8,9},{9,8},{10,11... | collective-permute-start | bytes 786440 | tf_op jit(solution)/shard_map/ppermute | solution.py:163
  81.0 18.1 %collective-permute-start.18 = (bf16[1024,128]{1,0:T(8,128)(2,1)S(1)}, bf16[1024,128]{1,0:T(8,128)(2,1)S(1)}, u32[]{:S(2)}, u32[]{:S(2)}) collective-permute-start(bf16[1024,128]{1,0:T(8,128)(2,1)S(1)} %copy-done.2), channel_id=1, source_target_pairs={{0,16},{16,0},{1,17},{17,1},{2,18},{18,2},{3,19},{19,3},{4,20},{20... | collective-permute-start | bytes 786440 | tf_op jit(solution)/shard_map/ppermute | solution.py:23
  83.1 9.3 %collective-permute-start.12 = (f32[128,256]{1,0:T(8,128)S(1)}, f32[128,256]{1,0:T(8,128)S(1)}, u32[]{:S(2)}, u32[]{:S(2)}) collective-permute-start(f32[128,256]{1,0:T(8,128)S(1)} %add.65), channel_id=1, source_target_pairs={{0,8},{1,9},{2,10},{3,11},{4,12},{5,13},{6,14},{7,15},{8,0},{9,1},... | collective-permute-start | bytes 393224 | tf_op jit(solution)/shard_map/ppermute | solution.py:163
  85.8 6.7 %collective-permute-start.15 = (f32[256,128]{1,0:T(8,128)S(1)}, f32[256,128]{1,0:T(8,128)S(1)}, u32[]{:S(2)}, u32[]{:S(2)}) collective-permute-start(f32[256,128]{1,0:T(8,128)S(1)} %get-tuple-element.70), channel_id=1, source_target_pairs={{0,2},{1,3},{2,0},{3,1},{4,6},{5,7},{6,4},{7,5},{8,10},{9,11},{10,... | collective-permute-start | bytes 393224 | tf_op jit(solution)/shard_map/ppermute | solution.py:163
  92.5 6.5 %collective-permute-start.16 = (f32[128,128]{1,0:T(8,128)S(1)}, f32[128,128]{1,0:T(8,128)S(1)}, u32[]{:S(2)}, u32[]{:S(2)}) collective-permute-start(f32[128,128]{1,0:T(8,128)S(1)} %get-tuple-element.73), channel_id=1, source_target_pairs={{0,4},{1,5},{2,6},{3,7},{4,0},{5,1},{6,2},{7,3},{8,12},{9,13},{10,... | collective-permute-start | bytes 196616 | tf_op jit(solution)/shard_map/ppermute | solution.py:163
  99.0 2.5 %copy-start.3 = (f32[512]{0:T(512)S(1)}, f32[512]{0:T(512)}, u32[]{:S(2)}) copy-start(f32[512]{0:T(512)} %param.13) | copy-start | bytes 6148
  99.0 2.5 %copy-start.5 = (s32[32]{0:T(128)S(1)}, s32[32]{0:T(128)}, u32[]{:S(2)}) copy-start(s32[32]{0:T(128)} %param.11) | copy-start | bytes 388
  99.1 7.0 %copy-start.7 = (s32[64]{0:T(128)S(1)}, s32[64]{0:T(128)}, u32[]{:S(2)}) copy-start(s32[64]{0:T(128)} %param.10) | copy-start | bytes 772
  99.1 11.6 %copy-start.4 = (s32[64,2]{0,1:T(2,128)S(1)}, s32[64,2]{0,1:T(2,128)}, u32[]{:S(2)}) copy-start(s32[64,2]{0,1:T(2,128)} %param.9) | copy-start | bytes 1540
  99.1 11.6 %copy-start.6 = (f32[96]{0:T(128)S(1)}, f32[96]{0:T(128)}, u32[]{:S(2)}) copy-start(f32[96]{0:T(128)} %param.12) | copy-start | bytes 1156
  101.5 3.0 %collective-permute-start.20 = (f32[512,128]{1,0:T(8,128)S(1)}, f32[512,128]{1,0:T(8,128)S(1)}, u32[]{:S(2)}, u32[]{:S(2)}) collective-permute-start(f32[512,128]{1,0:T(8,128)S(1)} %get-tuple-element.79), channel_id=1, source_target_pairs={{0,1},{1,0},{2,3},{3,2},{4,5},{5,4},{6,7},{7,6},{8,9},{9,8},{10,11... | collective-permute-start | bytes 786440 | tf_op jit(solution)/shard_map/ppermute | solution.py:163
  101.8 6.6 %collective-permute-start.17 = (f32[128,128]{1,0:T(8,128)S(1)}, f32[128,128]{1,0:T(8,128)S(1)}, u32[]{:S(2)}, u32[]{:S(2)}) collective-permute-start(f32[128,128]{1,0:T(8,128)S(1)} %add.67), channel_id=1, source_target_pairs={{0,8},{1,9},{2,10},{3,11},{4,12},{5,13},{6,14},{7,15},{8,0},{9,1},... | collective-permute-start | bytes 196616 | tf_op jit(solution)/shard_map/ppermute | solution.py:163
  104.4 5.7 %collective-permute-start.21 = (f32[256,128]{1,0:T(8,128)S(1)}, f32[256,128]{1,0:T(8,128)S(1)}, u32[]{:S(2)}, u32[]{:S(2)}) collective-permute-start(f32[256,128]{1,0:T(8,128)S(1)} %get-tuple-element.81), channel_id=1, source_target_pairs={{0,2},{1,3},{2,0},{3,1},{4,6},{5,7},{6,4},{7,5},{8,10},{9,11},{10,... | collective-permute-start | bytes 393224 | tf_op jit(solution)/shard_map/ppermute | solution.py:163
  110.1 4.3 %collective-permute-start.22 = (f32[128,128]{1,0:T(8,128)S(1)}, f32[128,128]{1,0:T(8,128)S(1)}, u32[]{:S(2)}, u32[]{:S(2)}) collective-permute-start(f32[128,128]{1,0:T(8,128)S(1)} %get-tuple-element.84), channel_id=1, source_target_pairs={{0,4},{1,5},{2,6},{3,7},{4,0},{5,1},{6,2},{7,3},{8,12},{9,13},{10,... | collective-permute-start | bytes 196616 | tf_op jit(solution)/shard_map/ppermute | solution.py:163
  114.5 5.8 %collective-permute-start.23 = (f32[128,128]{1,0:T(8,128)S(1)}, f32[128,128]{1,0:T(8,128)S(1)}, u32[]{:S(2)}, u32[]{:S(2)}) collective-permute-start(f32[128,128]{1,0:T(8,128)S(1)} %add.69.refs_4_), channel_id=1, source_target_pairs={{0,8},{1,9},{2,10},{3,11},{4,12},{5,13},{6,14},{7,15},{8,0},{9,1},... | collective-permute-start | bytes 196616 | tf_op jit(solution)/shard_map/ppermute | solution.py:163

commit v8 on v7

--- a/solution.py
+++ b/solution.py
@@ -13,8 +13,12 @@
 FREE = pl.CostEstimate(flops=0, bytes_accessed=0, transcendentals=0)
 OWN_SPLITS = 2
 PRODUCT_BYTES = 51 * 1024 * 1024
+WHOLE_BYTES = 24 * 1024 * 1024
 CUT_BYTES = 56 * 1024 * 1024
 SUM_BYTES = 8 * 1024 * 1024
+
+
+WHOLE = pl.BlockSpec(memory_space=pltpu.VMEM)
 
 
 def passed_along(value, axis, steps):
@@ -116,26 +120,56 @@
     )(bit, *[amplitudes] * ROW_CUTS, columns, *bases)
 
 
-def plain_kernel(*refs):
-    add_product(refs[:ROW_CUTS], refs[ROW_CUTS], refs[-1], None)
-
-
-def plain_product(amplitudes, columns):
-    rows, depth = amplitudes.shape
+def add_whole(a_ref, b_ref, total_ref, first, base_ref):
+    depth = b_ref.shape[0]
+    part = a_ref.shape[1] // DEPTH_CUTS
+    for low in range(0, depth, part):
+        term = jnp.dot(a_ref[:, first + low : first + low + part], b_ref[low : low + part, :], preferred_element_type=jnp.float32)
+        if low > 0:
+            total_ref[...] += term
+        else:
+            total_ref[...] = term if base_ref is None else base_ref[...] + term
+
+
+def whole_kernel(order, first, has_base, bit_ref, a_ref, b_ref, *refs):
+    keep_ref, send_ref, total_ref = refs[-3:]
+    add_whole(a_ref, b_ref, total_ref, first, refs[0] if has_base else None)
+    rows = keep_ref.shape[0] // len(order)
+    for out_ref, bit in ((keep_ref, bit_ref[0]), (send_ref, 1 - bit_ref[0])):
+        for place, block in enumerate(order):
+            start = pl.multiple_of((block + bit) * rows, rows)
+            out_ref[place * rows : (place + 1) * rows, :] = total_ref[pl.ds(start, rows), :]
+
+
+def whole_multiplied(amplitudes, columns, bit, order, first=0, base=None):
+    rows = amplitudes.shape[0]
     width = columns.shape[1]
-    part = depth // DEPTH_CUTS
-    return pl.pallas_call(
-        plain_kernel,
-        grid=(columns.shape[0] // part,),
-        out_shape=jax.ShapeDtypeStruct((rows, width), jnp.float32),
-        in_specs=[
-            *row_blocks(rows, part, 0),
-            pl.BlockSpec((part, width), lambda k: (k, 0)),
-        ],
-        out_specs=pl.BlockSpec((rows, width), lambda k: (0, 0)),
-        compiler_params=pltpu.CompilerParams(vmem_limit_bytes=PRODUCT_BYTES),
+    bases = [] if base is None else [base]
+    return pl.pallas_call(
+        functools.partial(whole_kernel, order, first, base is not None),
+        out_shape=[jax.ShapeDtypeStruct((rows // 2, width), jnp.float32)] * 2,
+        in_specs=[pl.BlockSpec(memory_space=pltpu.SMEM)] + [WHOLE] * (2 + len(bases)),
+        out_specs=[WHOLE] * 2,
+        scratch_shapes=[pltpu.VMEM((rows, width), jnp.float32)],
+        compiler_params=pltpu.CompilerParams(vmem_limit_bytes=WHOLE_BYTES),
         cost_estimate=product_cost(rows, columns),
-    )(*[amplitudes] * ROW_CUTS, columns)
+    )(bit, amplitudes, columns, *bases)
+
+
+def whole_plain_kernel(a_ref, b_ref, out_ref):
+    add_whole(a_ref, b_ref, out_ref, 0, None)
+
+
+def whole_plain(amplitudes, columns):
+    rows = amplitudes.shape[0]
+    return pl.pallas_call(
+        whole_plain_kernel,
+        out_shape=jax.ShapeDtypeStruct((rows, columns.shape[1]), jnp.float32),
+        in_specs=[WHOLE] * 2,
+        out_specs=WHOLE,
+        compiler_params=pltpu.CompilerParams(vmem_limit_bytes=WHOLE_BYTES),
+        cost_estimate=product_cost(rows, columns),
+    )(amplitudes, columns)
 
 
 def halve_kernel(bit_ref, mine_ref, came_ref, keep_ref, send_ref):
@@ -173,9 +207,6 @@
         parts = halved(keep, came, bits[level]) if level < len(bits) - 1 else [keep + came]
         stages.append(parts[0])
     return (parts[0], flipped_along(parts[0], "virt", 1 << (len(bits) - 1))), stages
-
-
-WHOLE = pl.BlockSpec(memory_space=pltpu.VMEM)
 
 
 def cut_kernel(boxes, source_ref, *refs):
@@ -280,14 +311,14 @@
     for step in range(len(pieces)):
         arrived, earlier = lax.optimization_barrier((in_flight[step], earlier))
         if step == len(pieces) - 2:
-            bases = [plain_product(amplitudes, columns) for columns in arrived]
+            bases = [whole_plain(amplitudes, columns) for columns in arrived]
             earlier = (stages[2], bases)
             continue
         for shift in range(1, count):
             if step < len(cuts) - 1:
                 product = multiplied(amplitudes, arrived[shift - 1], bits[0], order)
             else:
-                product = multiplied(amplitudes, arrived[shift - 1], bits[0], order, DEPTH_CUTS - 1, bases[shift - 1])
+                product = whole_multiplied(amplitudes, arrived[shift - 1], bits[0], order, late, bases[shift - 1])
             terms, stages = exchanged_sum(product, bits, gates)
             total = jnp.add(*terms)
             sums[shift].append(total)

time: 123 us -> 118 us (0.959)
  Pallas kernels: 32.6 us -> 28.4 us
  starting transfers between devices: 34.4 us -> 35.7 us
    pallas_call x1 -> x2, Pallas kernels: 4.7 us -> 2.53 us  [the longest x1 1.78 us: whole_plain(): pl.pallas_call(whole_plain_kernel, out_shape=jax.ShapeDtypeStruct((rows,...]
    pallas_call x4 -> x3, Pallas kernels: 22.3 us -> 20.3 us  [multiplied(): pl.pallas_call(functools.partial(product_kernel, steps, order, splits, ba...]
    ppermute x20, starting transfers between devices: 27.3 us -> 28.5 us  [flipped_along(): lax.ppermute(value, axis, [(source, source ^ bits) for source in range(co...]
  transfers between devices with their start and end apart: 24 -> 24, of which waited for: 16 -> 17; matrix products, arithmetic and copies ran while one was open for 3% -> 3% of each run, Pallas kernels for 20% -> 19%
where the time goes in v8:
time: 118 us
  waiting for transfers between devices  50.1 us (42%)
  starting transfers between devices  35.7 us (30%)
  Pallas kernels  28.4 us (24%)
  local copies, waits for them, and re-layouts  3.19 us (3%)
    ppermute x20, waiting for transfers between devices, flipped_along(): lax.ppermute(value, axis, [(source, source ^ bits) for source in range(co...  46.1 us
    ppermute x20, starting transfers between devices, flipped_along(): lax.ppermute(value, axis, [(source, source ^ bits) for source in range(co...  28.5 us
    pallas_call x3, Pallas kernels, multiplied(): pl.pallas_call(functools.partial(product_kernel, steps, order, splits, ba...  20.3 us
    ppermute x4, starting transfers between devices, passed_along(): return lax.ppermute(value, axis, pairs)  7.18 us
    ppermute x4, waiting for transfers between devices, passed_along(): return lax.ppermute(value, axis, pairs)  4 us
    pallas_call x1, Pallas kernels, cut_out(): pl.pallas_call(functools.partial(cut_kernel, [(rows, columns)]), out_shap...  3.05 us
  transfers between devices with their start and end apart: 24, of which 17 were waited for; matrix products, arithmetic and copies ran while one was open for 3% of the time, Pallas kernels for 19%

profile of v8, /device:TPU:0, one launch (start us, length us, event | category | flops | bytes accessed | tf_op | source)
XLA Modules:
  0.0 118.3 jit_solution(5607435571570323426)
XLA Ops:
  0.0 3.1 %shard_map.73 = bf16[4096,256]{1,0:T(8,128)(2,1)} custom-call(bf16[4096,512]{1,0:T(8,128)(2,1)} %refs_1_), custom_call_target="tpu_custom_call" | custom-call | tf_op jit(solution)/shard_map/pallas_call | solution.py:229
  3.1 3.0 %collective-permute-start.8 = (bf16[4096,256]{1,0:T(8,128)(2,1)}, bf16[4096,256]{1,0:T(8,128)(2,1)}, u32[]{:S(2)}, u32[]{:S(2)}) collective-permute-start(bf16[4096,256]{1,0:T(8,128)(2,1)} %shard_map.73), channel_id=1, source_target_pairs={{0,16},{16,0},{1,17},{17,1},{2,18},{18,2},{3,19},{19,3},{4,20},{20... | collective-permute-start | bytes 6291464 | tf_op jit(solution)/shard_map/ppermute | solution.py:27
  6.1 1.1 slice.9
  7.2 1.0 slice.10
  8.2 0.7 slice.11
  9.0 8.3 %shard_map.74 = (f32[512,256]{1,0:T(8,128)S(1)}, f32[512,256]{1,0:T(8,128)S(1)}, f32[512,256]{1,0:T(8,128)S(1)}, f32[512,256]{1,0:T(8,128)S(1)}) custom-call(s32[1]{0:T(128)} %bitcast.6.bit_ref, bf16[1024,4096]{1,0:T(8,128)(2,1)} %a_ref.3, bf16[4096,512]{1,0:T(8,128)(2,1)} %refs_1_), custom_call_target="tpu_custom_call" | custom-call | tf_op jit(solution)/shard_map/pallas_call | solution.py:106
  17.3 0.5 collective-permute-start
  17.8 1.4 %collective-permute-done.4.came_ref = f32[512,256]{1,0:T(8,128)S(1)} collective-permute-done((f32[512,256]{1,0:T(8,128)S(1)}, f32[512,256]{1,0:T(8,128)S(1)}, u32[]{:S(2)}, u32[]{:S(2)}) %collective-permute-start.4) | collective-permute-done | bytes 524320 | tf_op jit(solution)/shard_map/ppermute | solution.py:197
  19.3 1.5 %collective-permute-start.5 = (f32[256,256]{1,0:T(8,128)S(1)}, f32[256,256]{1,0:T(8,128)S(1)}, u32[]{:S(2)}, u32[]{:S(2)}) collective-permute-start(f32[256,256]{1,0:T(8,128)S(1)} %get-tuple-element.56), channel_id=1, source_target_pairs={{0,2},{1,3},{2,0},{3,1},{4,6},{5,7},{6,4},{7,5},{8,10},{9,11},{10,... | collective-permute-start | bytes 786440 | tf_op jit(solution)/shard_map/ppermute | solution.py:197
  20.9 0.7 collective-permute-start.1
  21.6 6.9 %collective-permute-done.5.came_ref = f32[256,256]{1,0:T(8,128)S(1)} collective-permute-done((f32[256,256]{1,0:T(8,128)S(1)}, f32[256,256]{1,0:T(8,128)S(1)}, u32[]{:S(2)}, u32[]{:S(2)}) %collective-permute-start.5) | collective-permute-done | bytes 262176 | tf_op jit(solution)/shard_map/ppermute | solution.py:197
  28.5 1.6 %collective-permute-start.6 = (f32[128,256]{1,0:T(8,128)S(1)}, f32[128,256]{1,0:T(8,128)S(1)}, u32[]{:S(2)}, u32[]{:S(2)}) collective-permute-start(f32[128,256]{1,0:T(8,128)S(1)} %get-tuple-element.58), channel_id=1, source_target_pairs={{0,4},{1,5},{2,6},{3,7},{4,0},{5,1},{6,2},{7,3},{8,12},{9,13},{10,... | collective-permute-start | bytes 393224 | tf_op jit(solution)/shard_map/ppermute | solution.py:197
  30.1 3.1 %collective-permute-done.1.came_ref = f32[256,256]{1,0:T(8,128)S(1)} collective-permute-done((f32[256,256]{1,0:T(8,128)S(1)}, f32[256,256]{1,0:T(8,128)S(1)}, u32[]{:S(2)}, u32[]{:S(2)}) %collective-permute-start.1) | collective-permute-done | bytes 262176 | tf_op jit(solution)/shard_map/ppermute | solution.py:197
  33.3 1.6 %collective-permute-start.2 = (f32[128,256]{1,0:T(8,128)S(1)}, f32[128,256]{1,0:T(8,128)S(1)}, u32[]{:S(2)}, u32[]{:S(2)}) collective-permute-start(f32[128,256]{1,0:T(8,128)S(1)} %get-tuple-element.52), channel_id=1, source_target_pairs={{0,4},{1,5},{2,6},{3,7},{4,0},{5,1},{6,2},{7,3},{8,12},{9,13},{10,... | collective-permute-start | bytes 393224 | tf_op jit(solution)/shard_map/ppermute | solution.py:197
  35.0 2.6 %collective-permute-start.7 = (f32[128,256]{1,0:T(8,128)S(1)}, f32[128,256]{1,0:T(8,128)S(1)}, u32[]{:S(2)}, u32[]{:S(2)}) collective-permute-start(f32[128,256]{1,0:T(8,128)S(1)} %add.63), channel_id=1, source_target_pairs={{0,8},{1,9},{2,10},{3,11},{4,12},{5,13},{6,14},{7,15},{8,0},{9,1},... | collective-permute-start | bytes 393224 | tf_op jit(solution)/shard_map/ppermute | solution.py:197
  37.6 2.2 %collective-permute-done.2 = f32[128,256]{1,0:T(8,128)S(1)} collective-permute-done((f32[128,256]{1,0:T(8,128)S(1)}, f32[128,256]{1,0:T(8,128)S(1)}, u32[]{:S(2)}, u32[]{:S(2)}) %collective-permute-start.2) | collective-permute-done | bytes 131104 | tf_op jit(solution)/shard_map/ppermute | solution.py:197
  39.9 2.4 %collective-permute-start.3 = (f32[128,256]{1,0:T(8,128)S(1)}, f32[128,256]{1,0:T(8,128)S(1)}, u32[]{:S(2)}, u32[]{:S(2)}) collective-permute-start(f32[128,256]{1,0:T(8,128)S(1)} %add.61), channel_id=1, source_target_pairs={{0,8},{1,9},{2,10},{3,11},{4,12},{5,13},{6,14},{7,15},{8,0},{9,1},... | collective-permute-start | bytes 393224 | tf_op jit(solution)/shard_map/ppermute | solution.py:197
  42.3 0.5 collective-permute-start.13
  42.8 4.3 %collective-permute-done.7 = f32[128,256]{1,0:T(8,128)S(1)} collective-permute-done((f32[128,256]{1,0:T(8,128)S(1)}, f32[128,256]{1,0:T(8,128)S(1)}, u32[]{:S(2)}, u32[]{:S(2)}) %collective-permute-start.7) | collective-permute-done | bytes 131104 | tf_op jit(solution)/shard_map/ppermute | solution.py:197
  47.1 1.9 %collective-permute-done.3 = f32[128,256]{1,0:T(8,128)S(1)} collective-permute-done((f32[128,256]{1,0:T(8,128)S(1)}, f32[128,256]{1,0:T(8,128)S(1)}, u32[]{:S(2)}, u32[]{:S(2)}) %collective-permute-start.3) | collective-permute-done | bytes 131104 | tf_op jit(solution)/shard_map/ppermute | solution.py:197
  49.0 3.9 %collective-permute-done.8.refs_1_ = bf16[4096,256]{1,0:T(8,128)(2,1)} collective-permute-done((bf16[4096,256]{1,0:T(8,128)(2,1)}, bf16[4096,256]{1,0:T(8,128)(2,1)}, u32[]{:S(2)}, u32[]{:S(2)}) %collective-permute-start.8) | collective-permute-done | bytes 2097184 | tf_op jit(solution)/shard_map/ppermute | solution.py:27
  52.9 6.4 %shard_map.79 = (f32[512,256]{1,0:T(8,128)S(1)}, f32[512,256]{1,0:T(8,128)S(1)}) custom-call(s32[1]{0:T(128)} %bitcast.6.bit_ref, bf16[1024,4096]{1,0:T(8,128)(2,1)} %a_ref.3, bf16[4096,256]{1,0:T(8,128)(2,1)} %collective-permute-done.8.refs_1_), custom_call_target="tpu_custom_call" | custom-call | flops 2147483648 | bytes 8388608 | tf_op jit(solution)/shard_map/pallas_call | solution.py:106
  59.3 1.9 %collective-permute-done.9.came_ref = f32[512,256]{1,0:T(8,128)S(1)} collective-permute-done((f32[512,256]{1,0:T(8,128)S(1)}, f32[512,256]{1,0:T(8,128)S(1)}, u32[]{:S(2)}, u32[]{:S(2)}) %collective-permute-start.9) | collective-permute-done | bytes 524320 | tf_op jit(solution)/shard_map/ppermute | solution.py:197
  61.3 2.1 %collective-permute-start.10 = (f32[256,256]{1,0:T(8,128)S(1)}, f32[256,256]{1,0:T(8,128)S(1)}, u32[]{:S(2)}, u32[]{:S(2)}) collective-permute-start(f32[256,256]{1,0:T(8,128)S(1)} %get-tuple-element.63), channel_id=1, source_target_pairs={{0,2},{1,3},{2,0},{3,1},{4,6},{5,7},{6,4},{7,5},{8,10},{9,11},{10,... | collective-permute-start | bytes 786440 | tf_op jit(solution)/shard_map/ppermute | solution.py:197
  63.4 1.5 %collective-permute-start.19 = (bf16[3072,128]{1,0:T(8,128)(2,1)S(1)}, bf16[3072,128]{1,0:T(8,128)(2,1)S(1)}, u32[]{:S(2)}, u32[]{:S(2)}) collective-permute-start(bf16[3072,128]{1,0:T(8,128)(2,1)S(1)} %copy-done.1), channel_id=1, source_target_pairs={{0,16},{16,0},{1,17},{17,1},{2,18},{18,2},{3,19},{19,3},{4,20},{20... | collective-permute-start | bytes 2359304 | tf_op jit(solution)/shard_map/ppermute | solution.py:27
  64.9 5.1 %collective-permute-done.10.came_ref = f32[256,256]{1,0:T(8,128)S(1)} collective-permute-done((f32[256,256]{1,0:T(8,128)S(1)}, f32[256,256]{1,0:T(8,128)S(1)}, u32[]{:S(2)}, u32[]{:S(2)}) %collective-permute-start.10) | collective-permute-done | bytes 262176 | tf_op jit(solution)/shard_map/ppermute | solution.py:197
  70.0 1.9 %collective-permute-start.11 = (f32[128,256]{1,0:T(8,128)S(1)}, f32[128,256]{1,0:T(8,128)S(1)}, u32[]{:S(2)}, u32[]{:S(2)}) collective-permute-start(f32[128,256]{1,0:T(8,128)S(1)} %get-tuple-element.65), channel_id=1, source_target_pairs={{0,4},{1,5},{2,6},{3,7},{4,0},{5,1},{6,2},{7,3},{8,12},{9,13},{10,... | collective-permute-start | bytes 393224 | tf_op jit(solution)/shard_map/ppermute | solution.py:197
  71.9 3.2 %collective-permute-done.11 = f32[128,256]{1,0:T(8,128)S(1)} collective-permute-done((f32[128,256]{1,0:T(8,128)S(1)}, f32[128,256]{1,0:T(8,128)S(1)}, u32[]{:S(2)}, u32[]{:S(2)}) %collective-permute-start.11) | collective-permute-done | bytes 131104 | tf_op jit(solution)/shard_map/ppermute | solution.py:197
  75.2 5.7 %shard_map.82 = (f32[512,128]{1,0:T(8,128)S(1)}, f32[512,128]{1,0:T(8,128)S(1)}) custom-call(s32[1]{0:T(128)} %bitcast.6.bit_ref, bf16[1024,4096]{1,0:T(8,128)(2,1)} %a_ref.3, bf16[4096,128]{1,0:T(8,128)(2,1)S(1)} %collective-permute-done.13.refs_1_), custom_call_target="tpu_custom_call" | custom-call | flops 1073741824 | bytes 8388608 | tf_op jit(solution)/shard_map/pallas_call | solution.py:106
  81.0 2.1 %collective-permute-start.18 = (bf16[1024,128]{1,0:T(8,128)(2,1)S(1)}, bf16[1024,128]{1,0:T(8,128)(2,1)S(1)}, u32[]{:S(2)}, u32[]{:S(2)}) collective-permute-start(bf16[1024,128]{1,0:T(8,128)(2,1)S(1)} %copy-done.2), channel_id=1, source_target_pairs={{0,16},{16,0},{1,17},{17,1},{2,18},{18,2},{3,19},{19,3},{4,20},{20... | collective-permute-start | bytes 786440 | tf_op jit(solution)/shard_map/ppermute | solution.py:27
  83.1 2.6 %collective-permute-start.12 = (f32[128,256]{1,0:T(8,128)S(1)}, f32[128,256]{1,0:T(8,128)S(1)}, u32[]{:S(2)}, u32[]{:S(2)}) collective-permute-start(f32[128,256]{1,0:T(8,128)S(1)} %add.65), channel_id=1, source_target_pairs={{0,8},{1,9},{2,10},{3,11},{4,12},{5,13},{6,14},{7,15},{8,0},{9,1},... | collective-permute-start | bytes 393224 | tf_op jit(solution)/shard_map/ppermute | solution.py:197
  85.8 1.6 %collective-permute-start.15 = (f32[256,128]{1,0:T(8,128)S(1)}, f32[256,128]{1,0:T(8,128)S(1)}, u32[]{:S(2)}, u32[]{:S(2)}) collective-permute-start(f32[256,128]{1,0:T(8,128)S(1)} %get-tuple-element.70), channel_id=1, source_target_pairs={{0,2},{1,3},{2,0},{3,1},{4,6},{5,7},{6,4},{7,5},{8,10},{9,11},{10,... | collective-permute-start | bytes 393224 | tf_op jit(solution)/shard_map/ppermute | solution.py:197
  87.3 5.1 %collective-permute-done.12 = f32[128,256]{1,0:T(8,128)S(1)} collective-permute-done((f32[128,256]{1,0:T(8,128)S(1)}, f32[128,256]{1,0:T(8,128)S(1)}, u32[]{:S(2)}, u32[]{:S(2)}) %collective-permute-start.12) | collective-permute-done | bytes 131104 | tf_op jit(solution)/shard_map/ppermute | solution.py:197
  92.5 1.8 %collective-permute-start.16 = (f32[128,128]{1,0:T(8,128)S(1)}, f32[128,128]{1,0:T(8,128)S(1)}, u32[]{:S(2)}, u32[]{:S(2)}) collective-permute-start(f32[128,128]{1,0:T(8,128)S(1)} %get-tuple-element.73), channel_id=1, source_target_pairs={{0,4},{1,5},{2,6},{3,7},{4,0},{5,1},{6,2},{7,3},{8,12},{9,13},{10,... | collective-permute-start | bytes 196616 | tf_op jit(solution)/shard_map/ppermute | solution.py:197
  94.3 1.8 %shard_map.85.refs_0_ = f32[1024,128]{1,0:T(8,128)S(1)} custom-call(bf16[1024,4096]{1,0:T(8,128)(2,1)S(1)} %bitcast.9, bf16[3072,128]{1,0:T(8,128)(2,1)S(1)} %collective-permute-done.19.b_ref), custom_call_target="tpu_custom_call" | custom-call | flops 805306368 | bytes 6291456 | tf_op jit(solution)/shard_map/pallas_call | solution.py:165
  96.1 0.7 collective-permute-done.16
  96.9 0.7 shard_map.86
  97.7 0.2 select_reduce_fusion.1
  98.0 2.8 %collective-permute-start.17 = (f32[128,128]{1,0:T(8,128)S(1)}, f32[128,128]{1,0:T(8,128)S(1)}, u32[]{:S(2)}, u32[]{:S(2)}) collective-permute-start(f32[128,128]{1,0:T(8,128)S(1)} %add.67), channel_id=1, source_target_pairs={{0,8},{1,9},{2,10},{3,11},{4,12},{5,13},{6,14},{7,15},{8,0},{9,1},... | collective-permute-start | bytes 196616 | tf_op jit(solution)/shard_map/ppermute | solution.py:197
  100.8 1.6 %collective-permute-start.21 = (f32[256,128]{1,0:T(8,128)S(1)}, f32[256,128]{1,0:T(8,128)S(1)}, u32[]{:S(2)}, u32[]{:S(2)}) collective-permute-start(f32[256,128]{1,0:T(8,128)S(1)} %get-tuple-element.81), channel_id=1, source_target_pairs={{0,2},{1,3},{2,0},{3,1},{4,6},{5,7},{6,4},{7,5},{8,10},{9,11},{10,... | collective-permute-start | bytes 393224 | tf_op jit(solution)/shard_map/ppermute | solution.py:197
  102.5 2.4 %collective-permute-done.17 = f32[128,128]{1,0:T(8,128)S(1)} collective-permute-done((f32[128,128]{1,0:T(8,128)S(1)}, f32[128,128]{1,0:T(8,128)S(1)}, u32[]{:S(2)}, u32[]{:S(2)}) %collective-permute-start.17) | collective-permute-done | bytes 65568 | tf_op jit(solution)/shard_map/ppermute | solution.py:197
  105.0 1.6 %collective-permute-done.21.came_ref = f32[256,128]{1,0:T(8,128)S(1)} collective-permute-done((f32[256,128]{1,0:T(8,128)S(1)}, f32[256,128]{1,0:T(8,128)S(1)}, u32[]{:S(2)}, u32[]{:S(2)}) %collective-permute-start.21) | collective-permute-done | bytes 131104 | tf_op jit(solution)/shard_map/ppermute | solution.py:197
  106.5 1.6 %collective-permute-start.22 = (f32[128,128]{1,0:T(8,128)S(1)}, f32[128,128]{1,0:T(8,128)S(1)}, u32[]{:S(2)}, u32[]{:S(2)}) collective-permute-start(f32[128,128]{1,0:T(8,128)S(1)} %get-tuple-element.84), channel_id=1, source_target_pairs={{0,4},{1,5},{2,6},{3,7},{4,0},{5,1},{6,2},{7,3},{8,12},{9,13},{10,... | collective-permute-start | bytes 196616 | tf_op jit(solution)/shard_map/ppermute | solution.py:197
  108.2 0.2 select_reduce_fusion
  108.5 2.3 %collective-permute-done.22 = f32[128,128]{1,0:T(8,128)S(1)} collective-permute-done((f32[128,128]{1,0:T(8,128)S(1)}, f32[128,128]{1,0:T(8,128)S(1)}, u32[]{:S(2)}, u32[]{:S(2)}) %collective-permute-start.22) | collective-permute-done | bytes 65568 | tf_op jit(solution)/shard_map/ppermute | solution.py:197
  110.9 1.2 %collective-permute-start.23 = (f32[128,128]{1,0:T(8,128)S(1)}, f32[128,128]{1,0:T(8,128)S(1)}, u32[]{:S(2)}, u32[]{:S(2)}) collective-permute-start(f32[128,128]{1,0:T(8,128)S(1)} %add.69.refs_4_), channel_id=1, source_target_pairs={{0,8},{1,9},{2,10},{3,11},{4,12},{5,13},{6,14},{7,15},{8,0},{9,1},... | collective-permute-start | bytes 196616 | tf_op jit(solution)/shard_map/ppermute | solution.py:197
  112.2 3.9 %collective-permute-done.23.refs_5_ = f32[128,128]{1,0:T(8,128)S(1)} collective-permute-done((f32[128,128]{1,0:T(8,128)S(1)}, f32[128,128]{1,0:T(8,128)S(1)}, u32[]{:S(2)}, u32[]{:S(2)}) %collective-permute-start.23) | collective-permute-done | bytes 65568 | tf_op jit(solution)/shard_map/ppermute | solution.py:197
  116.1 2.2 %shard_map.89 = f32[64,1024]{1,0:T(8,128)} custom-call(s32[2]{0:T(128)S(1)} %pad_add_fusion.where_ref, s32[64,1]{1,0:T(8,128)S(1)} %copy.11.rows_ref, f32[1,1024]{1,0:T(1,128)S(1)} %add.60.virt_ref, f32[64,1]{1,0:T(8,128)S(1)} %copy.12.occ_ref, f32[128,256]{1,0:T(8,128)S(1)} %add.62.refs_0_, f32[128,256]{1,0:T(8,128)S(1)} %add.64.refs_1_, ...), custom_call_target="tpu_custom_call" | custom-call | tf_op jit(solution)/shard_map/pallas_call | solution.py:269
  (58 shorter events, 1.4 us)
Async XLA Ops:
  0.0 6.1 %copy-start = (bf16[4096,512]{1,0:T(8,128)(2,1)S(1)}, bf16[4096,512]{1,0:T(8,128)(2,1)}, u32[]{:S(2)}) copy-start(bf16[4096,512]{1,0:T(8,128)(2,1)} %refs_1_) | copy-start | bytes 12582916
  3.1 49.8 %collective-permute-start.8 = (bf16[4096,256]{1,0:T(8,128)(2,1)}, bf16[4096,256]{1,0:T(8,128)(2,1)}, u32[]{:S(2)}, u32[]{:S(2)}) collective-permute-start(bf16[4096,256]{1,0:T(8,128)(2,1)} %shard_map.73), channel_id=1, source_target_pairs={{0,16},{16,0},{1,17},{17,1},{2,18},{18,2},{3,19},{19,3},{4,20},{20... | collective-permute-start | bytes 6291464 | tf_op jit(solution)/shard_map/ppermute | solution.py:27
  17.2 2.0 %collective-permute-start.4 = (f32[512,256]{1,0:T(8,128)S(1)}, f32[512,256]{1,0:T(8,128)S(1)}, u32[]{:S(2)}, u32[]{:S(2)}) collective-permute-start(f32[512,256]{1,0:T(8,128)S(1)} %get-tuple-element.54), channel_id=1, source_target_pairs={{0,1},{1,0},{2,3},{3,2},{4,5},{5,4},{6,7},{7,6},{8,9},{9,8},{10,11... | collective-permute-start | bytes 1572872 | tf_op jit(solution)/shard_map/ppermute | solution.py:197
  17.3 3.5 %collective-permute-start = (f32[512,256]{1,0:T(8,128)S(1)}, f32[512,256]{1,0:T(8,128)S(1)}, u32[]{:S(2)}, u32[]{:S(2)}) collective-permute-start(f32[512,256]{1,0:T(8,128)S(1)} %get-tuple-element.48), channel_id=1, source_target_pairs={{0,1},{1,0},{2,3},{3,2},{4,5},{5,4},{6,7},{7,6},{8,9},{9,8},{10,11... | collective-permute-start | bytes 1572872 | tf_op jit(solution)/shard_map/ppermute | solution.py:197
  19.3 9.2 %collective-permute-start.5 = (f32[256,256]{1,0:T(8,128)S(1)}, f32[256,256]{1,0:T(8,128)S(1)}, u32[]{:S(2)}, u32[]{:S(2)}) collective-permute-start(f32[256,256]{1,0:T(8,128)S(1)} %get-tuple-element.56), channel_id=1, source_target_pairs={{0,2},{1,3},{2,0},{3,1},{4,6},{5,7},{6,4},{7,5},{8,10},{9,11},{10,... | collective-permute-start | bytes 786440 | tf_op jit(solution)/shard_map/ppermute | solution.py:197
  20.9 12.4 %collective-permute-start.1 = (f32[256,256]{1,0:T(8,128)S(1)}, f32[256,256]{1,0:T(8,128)S(1)}, u32[]{:S(2)}, u32[]{:S(2)}) collective-permute-start(f32[256,256]{1,0:T(8,128)S(1)} %get-tuple-element.50), channel_id=1, source_target_pairs={{0,2},{1,3},{2,0},{3,1},{4,6},{5,7},{6,4},{7,5},{8,10},{9,11},{10,... | collective-permute-start | bytes 786440 | tf_op jit(solution)/shard_map/ppermute | solution.py:197
  28.5 6.5 %collective-permute-start.6 = (f32[128,256]{1,0:T(8,128)S(1)}, f32[128,256]{1,0:T(8,128)S(1)}, u32[]{:S(2)}, u32[]{:S(2)}) collective-permute-start(f32[128,256]{1,0:T(8,128)S(1)} %get-tuple-element.58), channel_id=1, source_target_pairs={{0,4},{1,5},{2,6},{3,7},{4,0},{5,1},{6,2},{7,3},{8,12},{9,13},{10,... | collective-permute-start | bytes 393224 | tf_op jit(solution)/shard_map/ppermute | solution.py:197
  33.3 6.5 %collective-permute-start.2 = (f32[128,256]{1,0:T(8,128)S(1)}, f32[128,256]{1,0:T(8,128)S(1)}, u32[]{:S(2)}, u32[]{:S(2)}) collective-permute-start(f32[128,256]{1,0:T(8,128)S(1)} %get-tuple-element.52), channel_id=1, source_target_pairs={{0,4},{1,5},{2,6},{3,7},{4,0},{5,1},{6,2},{7,3},{8,12},{9,13},{10,... | collective-permute-start | bytes 393224 | tf_op jit(solution)/shard_map/ppermute | solution.py:197
  35.0 12.1 %collective-permute-start.7 = (f32[128,256]{1,0:T(8,128)S(1)}, f32[128,256]{1,0:T(8,128)S(1)}, u32[]{:S(2)}, u32[]{:S(2)}) collective-permute-start(f32[128,256]{1,0:T(8,128)S(1)} %add.63), channel_id=1, source_target_pairs={{0,8},{1,9},{2,10},{3,11},{4,12},{5,13},{6,14},{7,15},{8,0},{9,1},... | collective-permute-start | bytes 393224 | tf_op jit(solution)/shard_map/ppermute | solution.py:197
  39.9 9.1 %collective-permute-start.3 = (f32[128,256]{1,0:T(8,128)S(1)}, f32[128,256]{1,0:T(8,128)S(1)}, u32[]{:S(2)}, u32[]{:S(2)}) collective-permute-start(f32[128,256]{1,0:T(8,128)S(1)} %add.61), channel_id=1, source_target_pairs={{0,8},{1,9},{2,10},{3,11},{4,12},{5,13},{6,14},{7,15},{8,0},{9,1},... | collective-permute-start | bytes 393224 | tf_op jit(solution)/shard_map/ppermute | solution.py:197
  42.3 33.0 %collective-permute-start.13 = (bf16[4096,128]{1,0:T(8,128)(2,1)}, bf16[4096,128]{1,0:T(8,128)(2,1)S(1)}, u32[]{:S(2)}, u32[]{:S(2)}) collective-permute-start(bf16[4096,128]{1,0:T(8,128)(2,1)} %slice.9), channel_id=1, source_target_pairs={{0,16},{16,0},{1,17},{17,1},{2,18},{18,2},{3,19},{19,3},{4,20},{20... | collective-permute-start | bytes 3145736 | tf_op jit(solution)/shard_map/ppermute | solution.py:27
  49.0 14.4 %copy-start.1 = (bf16[3072,128]{1,0:T(8,128)(2,1)S(1)}, bf16[3072,128]{1,0:T(8,128)(2,1)}, u32[]{:S(2)}) copy-start(bf16[3072,128]{1,0:T(8,128)(2,1)} %slice.10) | copy-start | bytes 2359300
  52.9 41.4 %slice-start = ((s8[8388608]{0:T(1024)(128)(4,1)}), s8[4194304]{0:T(1024)(128)(4,1)S(1)}, s32[]{:S(2)}) async-start(s8[8388608]{0:T(1024)(128)(4,1)} %bitcast.8), calls=%async_computation | async-start | bytes 8388608
  59.2 2.0 %collective-permute-start.9 = (f32[512,256]{1,0:T(8,128)S(1)}, f32[512,256]{1,0:T(8,128)S(1)}, u32[]{:S(2)}, u32[]{:S(2)}) collective-permute-start(f32[512,256]{1,0:T(8,128)S(1)} %get-tuple-element.61), channel_id=1, source_target_pairs={{0,1},{1,0},{2,3},{3,2},{4,5},{5,4},{6,7},{7,6},{8,9},{9,8},{10,11... | collective-permute-start | bytes 1572872 | tf_op jit(solution)/shard_map/ppermute | solution.py:197
  61.3 8.7 %collective-permute-start.10 = (f32[256,256]{1,0:T(8,128)S(1)}, f32[256,256]{1,0:T(8,128)S(1)}, u32[]{:S(2)}, u32[]{:S(2)}) collective-permute-start(f32[256,256]{1,0:T(8,128)S(1)} %get-tuple-element.63), channel_id=1, source_target_pairs={{0,2},{1,3},{2,0},{3,1},{4,6},{5,7},{6,4},{7,5},{8,10},{9,11},{10,... | collective-permute-start | bytes 786440 | tf_op jit(solution)/shard_map/ppermute | solution.py:197
  63.4 29.0 %collective-permute-start.19 = (bf16[3072,128]{1,0:T(8,128)(2,1)S(1)}, bf16[3072,128]{1,0:T(8,128)(2,1)S(1)}, u32[]{:S(2)}, u32[]{:S(2)}) collective-permute-start(bf16[3072,128]{1,0:T(8,128)(2,1)S(1)} %copy-done.1), channel_id=1, source_target_pairs={{0,16},{16,0},{1,17},{17,1},{2,18},{18,2},{3,19},{19,3},{4,20},{20... | collective-permute-start | bytes 2359304 | tf_op jit(solution)/shard_map/ppermute | solution.py:27
  70.0 24.3 %slice-start.1 = ((s8[8388608]{0:T(1024)(128)(4,1)}), s8[4194304]{0:T(1024)(128)(4,1)S(1)}, s32[]{:S(2)}) async-start(s8[8388608]{0:T(1024)(128)(4,1)} %bitcast.8), calls=%async_computation.1 | async-start | bytes 8388608
  70.0 5.1 %collective-permute-start.11 = (f32[128,256]{1,0:T(8,128)S(1)}, f32[128,256]{1,0:T(8,128)S(1)}, u32[]{:S(2)}, u32[]{:S(2)}) collective-permute-start(f32[128,256]{1,0:T(8,128)S(1)} %get-tuple-element.65), channel_id=1, source_target_pairs={{0,4},{1,5},{2,6},{3,7},{4,0},{5,1},{6,2},{7,3},{8,12},{9,13},{10,... | collective-permute-start | bytes 393224 | tf_op jit(solution)/shard_map/ppermute | solution.py:197
  75.1 5.9 %copy-start.2 = (bf16[1024,128]{1,0:T(8,128)(2,1)S(1)}, bf16[1024,128]{1,0:T(8,128)(2,1)}, u32[]{:S(2)}) copy-start(bf16[1024,128]{1,0:T(8,128)(2,1)} %slice.11) | copy-start | bytes 786436
  80.9 4.8 %collective-permute-start.14 = (f32[512,128]{1,0:T(8,128)S(1)}, f32[512,128]{1,0:T(8,128)S(1)}, u32[]{:S(2)}, u32[]{:S(2)}) collective-permute-start(f32[512,128]{1,0:T(8,128)S(1)} %get-tuple-element.68), channel_id=1, source_target_pairs={{0,1},{1,0},{2,3},{3,2},{4,5},{5,4},{6,7},{7,6},{8,9},{9,8},{10,11... | collective-permute-start | bytes 786440 | tf_op jit(solution)/shard_map/ppermute | solution.py:197
  81.0 15.9 %collective-permute-start.18 = (bf16[1024,128]{1,0:T(8,128)(2,1)S(1)}, bf16[1024,128]{1,0:T(8,128)(2,1)S(1)}, u32[]{:S(2)}, u32[]{:S(2)}) collective-permute-start(bf16[1024,128]{1,0:T(8,128)(2,1)S(1)} %copy-done.2), channel_id=1, source_target_pairs={{0,16},{16,0},{1,17},{17,1},{2,18},{18,2},{3,19},{19,3},{4,20},{20... | collective-permute-start | bytes 786440 | tf_op jit(solution)/shard_map/ppermute | solution.py:27
  83.1 9.3 %collective-permute-start.12 = (f32[128,256]{1,0:T(8,128)S(1)}, f32[128,256]{1,0:T(8,128)S(1)}, u32[]{:S(2)}, u32[]{:S(2)}) collective-permute-start(f32[128,256]{1,0:T(8,128)S(1)} %add.65), channel_id=1, source_target_pairs={{0,8},{1,9},{2,10},{3,11},{4,12},{5,13},{6,14},{7,15},{8,0},{9,1},... | collective-permute-start | bytes 393224 | tf_op jit(solution)/shard_map/ppermute | solution.py:197
  85.8 6.7 %collective-permute-start.15 = (f32[256,128]{1,0:T(8,128)S(1)}, f32[256,128]{1,0:T(8,128)S(1)}, u32[]{:S(2)}, u32[]{:S(2)}) collective-permute-start(f32[256,128]{1,0:T(8,128)S(1)} %get-tuple-element.70), channel_id=1, source_target_pairs={{0,2},{1,3},{2,0},{3,1},{4,6},{5,7},{6,4},{7,5},{8,10},{9,11},{10,... | collective-permute-start | bytes 393224 | tf_op jit(solution)/shard_map/ppermute | solution.py:197
  92.5 4.3 %collective-permute-start.16 = (f32[128,128]{1,0:T(8,128)S(1)}, f32[128,128]{1,0:T(8,128)S(1)}, u32[]{:S(2)}, u32[]{:S(2)}) collective-permute-start(f32[128,128]{1,0:T(8,128)S(1)} %get-tuple-element.73), channel_id=1, source_target_pairs={{0,4},{1,5},{2,6},{3,7},{4,0},{5,1},{6,2},{7,3},{8,12},{9,13},{10,... | collective-permute-start | bytes 196616 | tf_op jit(solution)/shard_map/ppermute | solution.py:197
  96.8 0.9 copy-start.3
  96.8 0.9 copy-start.5
  96.8 5.6 %copy-start.7 = (s32[64]{0:T(128)S(1)}, s32[64]{0:T(128)}, u32[]{:S(2)}) copy-start(s32[64]{0:T(128)} %param.10) | copy-start | bytes 772
  96.8 11.3 %copy-start.4 = (s32[64,2]{0,1:T(2,128)S(1)}, s32[64,2]{0,1:T(2,128)}, u32[]{:S(2)}) copy-start(s32[64,2]{0,1:T(2,128)} %param.9) | copy-start | bytes 1540
  96.9 11.3 %copy-start.6 = (f32[96]{0:T(128)S(1)}, f32[96]{0:T(128)}, u32[]{:S(2)}) copy-start(f32[96]{0:T(128)} %param.12) | copy-start | bytes 1156
  97.6 3.2 %collective-permute-start.20 = (f32[512,128]{1,0:T(8,128)S(1)}, f32[512,128]{1,0:T(8,128)S(1)}, u32[]{:S(2)}, u32[]{:S(2)}) collective-permute-start(f32[512,128]{1,0:T(8,128)S(1)} %get-tuple-element.79), channel_id=1, source_target_pairs={{0,1},{1,0},{2,3},{3,2},{4,5},{5,4},{6,7},{7,6},{8,9},{9,8},{10,11... | collective-permute-start | bytes 786440 | tf_op jit(solution)/shard_map/ppermute | solution.py:197
  98.0 7.0 %collective-permute-start.17 = (f32[128,128]{1,0:T(8,128)S(1)}, f32[128,128]{1,0:T(8,128)S(1)}, u32[]{:S(2)}, u32[]{:S(2)}) collective-permute-start(f32[128,128]{1,0:T(8,128)S(1)} %add.67), channel_id=1, source_target_pairs={{0,8},{1,9},{2,10},{3,11},{4,12},{5,13},{6,14},{7,15},{8,0},{9,1},... | collective-permute-start | bytes 196616 | tf_op jit(solution)/shard_map/ppermute | solution.py:197
  100.8 5.7 %collective-permute-start.21 = (f32[256,128]{1,0:T(8,128)S(1)}, f32[256,128]{1,0:T(8,128)S(1)}, u32[]{:S(2)}, u32[]{:S(2)}) collective-permute-start(f32[256,128]{1,0:T(8,128)S(1)} %get-tuple-element.81), channel_id=1, source_target_pairs={{0,2},{1,3},{2,0},{3,1},{4,6},{5,7},{6,4},{7,5},{8,10},{9,11},{10,... | collective-permute-start | bytes 393224 | tf_op jit(solution)/shard_map/ppermute | solution.py:197
  106.5 4.3 %collective-permute-start.22 = (f32[128,128]{1,0:T(8,128)S(1)}, f32[128,128]{1,0:T(8,128)S(1)}, u32[]{:S(2)}, u32[]{:S(2)}) collective-permute-start(f32[128,128]{1,0:T(8,128)S(1)} %get-tuple-element.84), channel_id=1, source_target_pairs={{0,4},{1,5},{2,6},{3,7},{4,0},{5,1},{6,2},{7,3},{8,12},{9,13},{10,... | collective-permute-start | bytes 196616 | tf_op jit(solution)/shard_map/ppermute | solution.py:197
  110.9 5.2 %collective-permute-start.23 = (f32[128,128]{1,0:T(8,128)S(1)}, f32[128,128]{1,0:T(8,128)S(1)}, u32[]{:S(2)}, u32[]{:S(2)}) collective-permute-start(f32[128,128]{1,0:T(8,128)S(1)} %add.69.refs_4_), channel_id=1, source_target_pairs={{0,8},{1,9},{2,10},{3,11},{4,12},{5,13},{6,14},{7,15},{8,0},{9,1},... | collective-permute-start | bytes 196616 | tf_op jit(solution)/shard_map/ppermute | solution.py:197

commit v9 on v8

--- a/solution.py
+++ b/solution.py
@@ -9,6 +9,8 @@
 
 LANES = 128
 DEPTH_CUTS = 4
+CUT_STEPS = 8
+ROW_STEPS = 4
 ROW_CUTS = 1
 FREE = pl.CostEstimate(flops=0, bytes_accessed=0, transcendentals=0)
 OWN_SPLITS = 2
@@ -120,6 +122,45 @@
     )(bit, *[amplitudes] * ROW_CUTS, columns, *bases)
 
 
+def rowwise_kernel(steps, order, bit_ref, a_ref, b_ref, keep_ref, send_ref, total_ref):
+    step = pl.program_id(0)
+    rows = a_ref.shape[0]
+    term = jnp.dot(a_ref[...], b_ref[...], preferred_element_type=jnp.float32)
+    total_ref[pl.ds(pl.multiple_of(step * rows, rows), rows), :] = term
+
+    @pl.when(step == steps - 1)
+    def _():
+        share_out(order, bit_ref, total_ref, keep_ref, send_ref)
+
+
+def share_out(order, bit_ref, total_ref, keep_ref, send_ref):
+    rows = keep_ref.shape[0] // len(order)
+    for out_ref, bit in ((keep_ref, bit_ref[0]), (send_ref, 1 - bit_ref[0])):
+        for place, block in enumerate(order):
+            start = pl.multiple_of((block + bit) * rows, rows)
+            out_ref[place * rows : (place + 1) * rows, :] = total_ref[pl.ds(start, rows), :]
+
+
+def rowwise_multiplied(amplitudes, columns, bit, order):
+    rows, depth = amplitudes.shape
+    width = columns.shape[1]
+    shape = jax.ShapeDtypeStruct((rows // 2, width), jnp.float32)
+    return pl.pallas_call(
+        functools.partial(rowwise_kernel, ROW_STEPS, order),
+        grid=(ROW_STEPS,),
+        out_shape=[shape] * 2,
+        in_specs=[
+            pl.BlockSpec(memory_space=pltpu.SMEM),
+            pl.BlockSpec((rows // ROW_STEPS, depth), lambda m: (m, 0)),
+            pl.BlockSpec((depth, width), lambda m: (0, 0)),
+        ],
+        out_specs=[pl.BlockSpec(shape.shape, lambda m: (0, 0))] * 2,
+        scratch_shapes=[pltpu.VMEM((rows, width), jnp.float32)],
+        compiler_params=pltpu.CompilerParams(vmem_limit_bytes=PRODUCT_BYTES),
+        cost_estimate=product_cost(rows, columns),
+    )(bit, amplitudes, columns)
+
+
 def add_whole(a_ref, b_ref, total_ref, first, base_ref):
     depth = b_ref.shape[0]
     part = a_ref.shape[1] // DEPTH_CUTS
@@ -134,11 +175,7 @@
 def whole_kernel(order, first, has_base, bit_ref, a_ref, b_ref, *refs):
     keep_ref, send_ref, total_ref = refs[-3:]
     add_whole(a_ref, b_ref, total_ref, first, refs[0] if has_base else None)
-    rows = keep_ref.shape[0] // len(order)
-    for out_ref, bit in ((keep_ref, bit_ref[0]), (send_ref, 1 - bit_ref[0])):
-        for place, block in enumerate(order):
-            start = pl.multiple_of((block + bit) * rows, rows)
-            out_ref[place * rows : (place + 1) * rows, :] = total_ref[pl.ds(start, rows), :]
+    share_out(order, bit_ref, total_ref, keep_ref, send_ref)
 
 
 def whole_multiplied(amplitudes, columns, bit, order, first=0, base=None):
@@ -209,32 +246,24 @@
     return (parts[0], flipped_along(parts[0], "virt", 1 << (len(bits) - 1))), stages
 
 
-def cut_kernel(boxes, source_ref, *refs):
-    copies = []
-    for index, (rows, columns) in enumerate(boxes):
-        part = (rows[1] - rows[0]) // DEPTH_CUTS
-        for low in range(0, rows[1] - rows[0], part):
-            source = source_ref.at[rows[0] + low : rows[0] + low + part, columns[0] : columns[1]]
-            target = refs[index].at[low : low + part, :]
-            copies.append(pltpu.make_async_copy(source, target, refs[-1].at[len(copies)]))
-    for copy in copies:
-        copy.start()
-    for copy in copies:
-        copy.wait()
-
-
-def cut_out(source, rows, columns):
-    if columns[0] % LANES or columns[1] % LANES:
-        return source[rows[0] : rows[1], columns[0] : columns[1]]
-    return pl.pallas_call(
-        functools.partial(cut_kernel, [(rows, columns)]),
-        out_shape=[jax.ShapeDtypeStruct((rows[1] - rows[0], columns[1] - columns[0]), source.dtype)],
-        in_specs=[pl.BlockSpec(memory_space=pl.ANY)],
-        out_specs=[WHOLE],
-        scratch_shapes=[pltpu.SemaphoreType.DMA((DEPTH_CUTS,))],
+def cut_kernel(source_ref, piece_ref):
+    piece_ref[...] = source_ref[...]
+
+
+def first_columns(source, width):
+    if width % LANES:
+        return source[:, :width]
+    depth = source.shape[0]
+    block = pl.BlockSpec((depth // CUT_STEPS, width), lambda k: (k, 0))
+    return pl.pallas_call(
+        cut_kernel,
+        grid=(CUT_STEPS,),
+        out_shape=jax.ShapeDtypeStruct((depth, width), source.dtype),
+        in_specs=[block],
+        out_specs=block,
         compiler_params=pltpu.CompilerParams(vmem_limit_bytes=CUT_BYTES),
         cost_estimate=FREE,
-    )(source)[0]
+    )(source)
 
 
 def last_kernel(width, starts, where_ref, rows_ref, virt_ref, occ_ref, *refs):
@@ -298,7 +327,7 @@
 
     depth = integrals.shape[0]
     late = depth // DEPTH_CUTS * (DEPTH_CUTS - 1)
-    first = cut_out(integrals, (0, depth), cuts[0])
+    first = first_columns(integrals, cuts[0][1])
     rest = after(integrals, first)
     low, high = cuts[-1]
     pieces = [first] + [rest[:, low:high] for low, high in cuts[1:-1]] + [rest[:late, low:high], rest[late:, low:high]]
@@ -316,7 +345,7 @@
             continue
         for shift in range(1, count):
             if step < len(cuts) - 1:
-                product = multiplied(amplitudes, arrived[shift - 1], bits[0], order)
+                product = rowwise_multiplied(amplitudes, arrived[shift - 1], bits[0], order)
             else:
                 product = whole_multiplied(amplitudes, arrived[shift - 1], bits[0], order, late, bases[shift - 1])
             terms, stages = exchanged_sum(product, bits, gates)

time: 118 us -> 121 us (1.025)
  Pallas kernels: 28.4 us -> 31.3 us
    pallas_call x1 -> x3, Pallas kernels: 3.05 us -> 17.9 us  [the longest x2 11.9 us: rowwise_multiplied(): pl.pallas_call(functools.partial(rowwise_kernel, ROW_STEPS, order), grid=...]
    pallas_call x3 -> x1, Pallas kernels: 20.3 us -> 8.26 us  [multiplied(): pl.pallas_call(functools.partial(product_kernel, steps, order, splits, ba...]
  transfers between devices with their start and end apart: 24 -> 24, of which waited for: 17 -> 18; matrix products, arithmetic and copies ran while one was open for 3% -> 3% of each run, Pallas kernels for 19% -> 18%
where the time goes in v9:
time: 121 us
  waiting for transfers between devices  50.1 us (41%)
  starting transfers between devices  35.8 us (30%)
  Pallas kernels  31.3 us (26%)
  local copies, waits for them, and re-layouts  3.19 us (3%)
    ppermute x20, waiting for transfers between devices, flipped_along(): lax.ppermute(value, axis, [(source, source ^ bits) for source in range(co...  45.9 us
    ppermute x20, starting transfers between devices, flipped_along(): lax.ppermute(value, axis, [(source, source ^ bits) for source in range(co...  28.7 us
    pallas_call x2, Pallas kernels, rowwise_multiplied(): pl.pallas_call(functools.partial(rowwise_kernel, ROW_STEPS, order), grid=...  11.9 us
    pallas_call x1, Pallas kernels, multiplied(): pl.pallas_call(functools.partial(product_kernel, steps, order, splits, ba...  8.26 us
    ppermute x4, starting transfers between devices, passed_along(): return lax.ppermute(value, axis, pairs)  7.13 us
    pallas_call x1, Pallas kernels, first_columns(): pl.pallas_call(cut_kernel, grid=(CUT_STEPS,), out_shape=jax.ShapeDtypeStr...  6.05 us
    ppermute x4, waiting for transfers between devices, passed_along(): return lax.ppermute(value, axis, pairs)  4.12 us
  transfers between devices with their start and end apart: 24, of which 18 were waited for; matrix products, arithmetic and copies ran while one was open for 3% of the time, Pallas kernels for 18%

profile of v9, /device:TPU:0, one launch (start us, length us, event | category | flops | bytes accessed | tf_op | source)
XLA Modules:
  0.0 121.2 jit_solution(2242845439558986455)
XLA Ops:
  0.0 6.0 %shard_map.73 = bf16[4096,256]{1,0:T(8,128)(2,1)} custom-call(bf16[4096,512]{1,0:T(8,128)(2,1)} %refs_1_), custom_call_target="tpu_custom_call" | custom-call | tf_op jit(solution)/shard_map/pallas_call | solution.py:258
  6.1 3.0 %collective-permute-start.8 = (bf16[4096,256]{1,0:T(8,128)(2,1)}, bf16[4096,256]{1,0:T(8,128)(2,1)}, u32[]{:S(2)}, u32[]{:S(2)}) collective-permute-start(bf16[4096,256]{1,0:T(8,128)(2,1)} %shard_map.73), channel_id=1, source_target_pairs={{0,16},{16,0},{1,17},{17,1},{2,18},{18,2},{3,19},{19,3},{4,20},{20... | collective-permute-start | bytes 6291464 | tf_op jit(solution)/shard_map/ppermute | solution.py:29
  9.0 1.1 slice.9
  10.2 1.0 slice.10
  11.1 0.7 slice.11
  11.9 8.3 %shard_map.74 = (f32[512,256]{1,0:T(8,128)S(1)}, f32[512,256]{1,0:T(8,128)S(1)}, f32[512,256]{1,0:T(8,128)S(1)}, f32[512,256]{1,0:T(8,128)S(1)}) custom-call(s32[1]{0:T(128)} %bitcast.6.bit_ref, bf16[1024,4096]{1,0:T(8,128)(2,1)} %a_ref.7, bf16[4096,512]{1,0:T(8,128)(2,1)} %refs_1_), custom_call_target="tpu_custom_call" | custom-call | tf_op jit(solution)/shard_map/pallas_call | solution.py:108
  20.2 0.5 collective-permute-start
  20.7 1.4 %collective-permute-done.4.came_ref = f32[512,256]{1,0:T(8,128)S(1)} collective-permute-done((f32[512,256]{1,0:T(8,128)S(1)}, f32[512,256]{1,0:T(8,128)S(1)}, u32[]{:S(2)}, u32[]{:S(2)}) %collective-permute-start.4) | collective-permute-done | bytes 524320 | tf_op jit(solution)/shard_map/ppermute | solution.py:234
  22.2 1.5 %collective-permute-start.5 = (f32[256,256]{1,0:T(8,128)S(1)}, f32[256,256]{1,0:T(8,128)S(1)}, u32[]{:S(2)}, u32[]{:S(2)}) collective-permute-start(f32[256,256]{1,0:T(8,128)S(1)} %get-tuple-element.56), channel_id=1, source_target_pairs={{0,2},{1,3},{2,0},{3,1},{4,6},{5,7},{6,4},{7,5},{8,10},{9,11},{10,... | collective-permute-start | bytes 786440 | tf_op jit(solution)/shard_map/ppermute | solution.py:234
  23.8 0.7 collective-permute-start.1
  24.5 6.9 %collective-permute-done.5.came_ref = f32[256,256]{1,0:T(8,128)S(1)} collective-permute-done((f32[256,256]{1,0:T(8,128)S(1)}, f32[256,256]{1,0:T(8,128)S(1)}, u32[]{:S(2)}, u32[]{:S(2)}) %collective-permute-start.5) | collective-permute-done | bytes 262176 | tf_op jit(solution)/shard_map/ppermute | solution.py:234
  31.4 1.6 %collective-permute-start.6 = (f32[128,256]{1,0:T(8,128)S(1)}, f32[128,256]{1,0:T(8,128)S(1)}, u32[]{:S(2)}, u32[]{:S(2)}) collective-permute-start(f32[128,256]{1,0:T(8,128)S(1)} %get-tuple-element.58), channel_id=1, source_target_pairs={{0,4},{1,5},{2,6},{3,7},{4,0},{5,1},{6,2},{7,3},{8,12},{9,13},{10,... | collective-permute-start | bytes 393224 | tf_op jit(solution)/shard_map/ppermute | solution.py:234
  33.1 3.1 %collective-permute-done.1.came_ref = f32[256,256]{1,0:T(8,128)S(1)} collective-permute-done((f32[256,256]{1,0:T(8,128)S(1)}, f32[256,256]{1,0:T(8,128)S(1)}, u32[]{:S(2)}, u32[]{:S(2)}) %collective-permute-start.1) | collective-permute-done | bytes 262176 | tf_op jit(solution)/shard_map/ppermute | solution.py:234
  36.2 1.6 %collective-permute-start.2 = (f32[128,256]{1,0:T(8,128)S(1)}, f32[128,256]{1,0:T(8,128)S(1)}, u32[]{:S(2)}, u32[]{:S(2)}) collective-permute-start(f32[128,256]{1,0:T(8,128)S(1)} %get-tuple-element.52), channel_id=1, source_target_pairs={{0,4},{1,5},{2,6},{3,7},{4,0},{5,1},{6,2},{7,3},{8,12},{9,13},{10,... | collective-permute-start | bytes 393224 | tf_op jit(solution)/shard_map/ppermute | solution.py:234
  37.9 2.6 %collective-permute-start.7 = (f32[128,256]{1,0:T(8,128)S(1)}, f32[128,256]{1,0:T(8,128)S(1)}, u32[]{:S(2)}, u32[]{:S(2)}) collective-permute-start(f32[128,256]{1,0:T(8,128)S(1)} %add.63), channel_id=1, source_target_pairs={{0,8},{1,9},{2,10},{3,11},{4,12},{5,13},{6,14},{7,15},{8,0},{9,1},... | collective-permute-start | bytes 393224 | tf_op jit(solution)/shard_map/ppermute | solution.py:234
  40.6 2.2 %collective-permute-done.2 = f32[128,256]{1,0:T(8,128)S(1)} collective-permute-done((f32[128,256]{1,0:T(8,128)S(1)}, f32[128,256]{1,0:T(8,128)S(1)}, u32[]{:S(2)}, u32[]{:S(2)}) %collective-permute-start.2) | collective-permute-done | bytes 131104 | tf_op jit(solution)/shard_map/ppermute | solution.py:234
  42.8 2.4 %collective-permute-start.3 = (f32[128,256]{1,0:T(8,128)S(1)}, f32[128,256]{1,0:T(8,128)S(1)}, u32[]{:S(2)}, u32[]{:S(2)}) collective-permute-start(f32[128,256]{1,0:T(8,128)S(1)} %add.61), channel_id=1, source_target_pairs={{0,8},{1,9},{2,10},{3,11},{4,12},{5,13},{6,14},{7,15},{8,0},{9,1},... | collective-permute-start | bytes 393224 | tf_op jit(solution)/shard_map/ppermute | solution.py:234
  45.2 0.5 collective-permute-start.13
  45.7 4.3 %collective-permute-done.7 = f32[128,256]{1,0:T(8,128)S(1)} collective-permute-done((f32[128,256]{1,0:T(8,128)S(1)}, f32[128,256]{1,0:T(8,128)S(1)}, u32[]{:S(2)}, u32[]{:S(2)}) %collective-permute-start.7) | collective-permute-done | bytes 131104 | tf_op jit(solution)/shard_map/ppermute | solution.py:234
  50.0 1.9 %collective-permute-done.3 = f32[128,256]{1,0:T(8,128)S(1)} collective-permute-done((f32[128,256]{1,0:T(8,128)S(1)}, f32[128,256]{1,0:T(8,128)S(1)}, u32[]{:S(2)}, u32[]{:S(2)}) %collective-permute-start.3) | collective-permute-done | bytes 131104 | tf_op jit(solution)/shard_map/ppermute | solution.py:234
  51.9 3.9 %collective-permute-done.8.b_ref = bf16[4096,256]{1,0:T(8,128)(2,1)} collective-permute-done((bf16[4096,256]{1,0:T(8,128)(2,1)}, bf16[4096,256]{1,0:T(8,128)(2,1)}, u32[]{:S(2)}, u32[]{:S(2)}) %collective-permute-start.8) | collective-permute-done | bytes 2097184 | tf_op jit(solution)/shard_map/ppermute | solution.py:29
  55.8 6.4 %shard_map.79 = (f32[512,256]{1,0:T(8,128)S(1)}, f32[512,256]{1,0:T(8,128)S(1)}) custom-call(s32[1]{0:T(128)} %bitcast.6.bit_ref, bf16[1024,4096]{1,0:T(8,128)(2,1)} %a_ref.7, bf16[4096,256]{1,0:T(8,128)(2,1)} %collective-permute-done.8.b_ref), custom_call_target="tpu_custom_call" | custom-call | flops 2147483648 | bytes 8388608 | tf_op jit(solution)/shard_map/pallas_call | solution.py:148
  62.2 1.9 %collective-permute-done.9.came_ref = f32[512,256]{1,0:T(8,128)S(1)} collective-permute-done((f32[512,256]{1,0:T(8,128)S(1)}, f32[512,256]{1,0:T(8,128)S(1)}, u32[]{:S(2)}, u32[]{:S(2)}) %collective-permute-start.9) | collective-permute-done | bytes 524320 | tf_op jit(solution)/shard_map/ppermute | solution.py:234
  64.2 2.1 %collective-permute-start.10 = (f32[256,256]{1,0:T(8,128)S(1)}, f32[256,256]{1,0:T(8,128)S(1)}, u32[]{:S(2)}, u32[]{:S(2)}) collective-permute-start(f32[256,256]{1,0:T(8,128)S(1)} %get-tuple-element.63), channel_id=1, source_target_pairs={{0,2},{1,3},{2,0},{3,1},{4,6},{5,7},{6,4},{7,5},{8,10},{9,11},{10,... | collective-permute-start | bytes 786440 | tf_op jit(solution)/shard_map/ppermute | solution.py:234
  66.3 1.5 %collective-permute-start.19 = (bf16[3072,128]{1,0:T(8,128)(2,1)S(1)}, bf16[3072,128]{1,0:T(8,128)(2,1)S(1)}, u32[]{:S(2)}, u32[]{:S(2)}) collective-permute-start(bf16[3072,128]{1,0:T(8,128)(2,1)S(1)} %copy-done.1), channel_id=1, source_target_pairs={{0,16},{16,0},{1,17},{17,1},{2,18},{18,2},{3,19},{19,3},{4,20},{20... | collective-permute-start | bytes 2359304 | tf_op jit(solution)/shard_map/ppermute | solution.py:29
  67.8 5.1 %collective-permute-done.10.came_ref = f32[256,256]{1,0:T(8,128)S(1)} collective-permute-done((f32[256,256]{1,0:T(8,128)S(1)}, f32[256,256]{1,0:T(8,128)S(1)}, u32[]{:S(2)}, u32[]{:S(2)}) %collective-permute-start.10) | collective-permute-done | bytes 262176 | tf_op jit(solution)/shard_map/ppermute | solution.py:234
  72.9 1.9 %collective-permute-start.11 = (f32[128,256]{1,0:T(8,128)S(1)}, f32[128,256]{1,0:T(8,128)S(1)}, u32[]{:S(2)}, u32[]{:S(2)}) collective-permute-start(f32[128,256]{1,0:T(8,128)S(1)} %get-tuple-element.65), channel_id=1, source_target_pairs={{0,4},{1,5},{2,6},{3,7},{4,0},{5,1},{6,2},{7,3},{8,12},{9,13},{10,... | collective-permute-start | bytes 393224 | tf_op jit(solution)/shard_map/ppermute | solution.py:234
  74.8 3.2 %collective-permute-done.11 = f32[128,256]{1,0:T(8,128)S(1)} collective-permute-done((f32[128,256]{1,0:T(8,128)S(1)}, f32[128,256]{1,0:T(8,128)S(1)}, u32[]{:S(2)}, u32[]{:S(2)}) %collective-permute-start.11) | collective-permute-done | bytes 131104 | tf_op jit(solution)/shard_map/ppermute | solution.py:234
  78.2 5.5 %shard_map.82 = (f32[512,128]{1,0:T(8,128)S(1)}, f32[512,128]{1,0:T(8,128)S(1)}) custom-call(s32[1]{0:T(128)} %bitcast.6.bit_ref, bf16[1024,4096]{1,0:T(8,128)(2,1)} %a_ref.7, bf16[4096,128]{1,0:T(8,128)(2,1)S(1)} %collective-permute-done.13.b_ref), custom_call_target="tpu_custom_call" | custom-call | flops 1073741824 | bytes 8388608 | tf_op jit(solution)/shard_map/pallas_call | solution.py:148
  83.8 2.1 %collective-permute-start.18 = (bf16[1024,128]{1,0:T(8,128)(2,1)S(1)}, bf16[1024,128]{1,0:T(8,128)(2,1)S(1)}, u32[]{:S(2)}, u32[]{:S(2)}) collective-permute-start(bf16[1024,128]{1,0:T(8,128)(2,1)S(1)} %copy-done.2), channel_id=1, source_target_pairs={{0,16},{16,0},{1,17},{17,1},{2,18},{18,2},{3,19},{19,3},{4,20},{20... | collective-permute-start | bytes 786440 | tf_op jit(solution)/shard_map/ppermute | solution.py:29
  85.9 2.6 %collective-permute-start.12 = (f32[128,256]{1,0:T(8,128)S(1)}, f32[128,256]{1,0:T(8,128)S(1)}, u32[]{:S(2)}, u32[]{:S(2)}) collective-permute-start(f32[128,256]{1,0:T(8,128)S(1)} %add.65), channel_id=1, source_target_pairs={{0,8},{1,9},{2,10},{3,11},{4,12},{5,13},{6,14},{7,15},{8,0},{9,1},... | collective-permute-start | bytes 393224 | tf_op jit(solution)/shard_map/ppermute | solution.py:234
  88.5 1.6 %collective-permute-start.15 = (f32[256,128]{1,0:T(8,128)S(1)}, f32[256,128]{1,0:T(8,128)S(1)}, u32[]{:S(2)}, u32[]{:S(2)}) collective-permute-start(f32[256,128]{1,0:T(8,128)S(1)} %get-tuple-element.70), channel_id=1, source_target_pairs={{0,2},{1,3},{2,0},{3,1},{4,6},{5,7},{6,4},{7,5},{8,10},{9,11},{10,... | collective-permute-start | bytes 393224 | tf_op jit(solution)/shard_map/ppermute | solution.py:234
  90.1 5.1 %collective-permute-done.12 = f32[128,256]{1,0:T(8,128)S(1)} collective-permute-done((f32[128,256]{1,0:T(8,128)S(1)}, f32[128,256]{1,0:T(8,128)S(1)}, u32[]{:S(2)}, u32[]{:S(2)}) %collective-permute-start.12) | collective-permute-done | bytes 131104 | tf_op jit(solution)/shard_map/ppermute | solution.py:234
  95.2 2.0 %collective-permute-start.16 = (f32[128,128]{1,0:T(8,128)S(1)}, f32[128,128]{1,0:T(8,128)S(1)}, u32[]{:S(2)}, u32[]{:S(2)}) collective-permute-start(f32[128,128]{1,0:T(8,128)S(1)} %get-tuple-element.73), channel_id=1, source_target_pairs={{0,4},{1,5},{2,6},{3,7},{4,0},{5,1},{6,2},{7,3},{8,12},{9,13},{10,... | collective-permute-start | bytes 196616 | tf_op jit(solution)/shard_map/ppermute | solution.py:234
  97.2 1.8 %shard_map.85.refs_0_ = f32[1024,128]{1,0:T(8,128)S(1)} custom-call(bf16[1024,4096]{1,0:T(8,128)(2,1)S(1)} %bitcast.9, bf16[3072,128]{1,0:T(8,128)(2,1)S(1)} %collective-permute-done.19.b_ref), custom_call_target="tpu_custom_call" | custom-call | flops 805306368 | bytes 6291456 | tf_op jit(solution)/shard_map/pallas_call | solution.py:202
  99.0 0.6 collective-permute-done.16
  99.8 0.7 shard_map.86
  100.6 0.2 select_reduce_fusion.1
  100.9 2.8 %collective-permute-start.17 = (f32[128,128]{1,0:T(8,128)S(1)}, f32[128,128]{1,0:T(8,128)S(1)}, u32[]{:S(2)}, u32[]{:S(2)}) collective-permute-start(f32[128,128]{1,0:T(8,128)S(1)} %add.67), channel_id=1, source_target_pairs={{0,8},{1,9},{2,10},{3,11},{4,12},{5,13},{6,14},{7,15},{8,0},{9,1},... | collective-permute-start | bytes 196616 | tf_op jit(solution)/shard_map/ppermute | solution.py:234
  103.8 1.6 %collective-permute-start.21 = (f32[256,128]{1,0:T(8,128)S(1)}, f32[256,128]{1,0:T(8,128)S(1)}, u32[]{:S(2)}, u32[]{:S(2)}) collective-permute-start(f32[256,128]{1,0:T(8,128)S(1)} %get-tuple-element.81), channel_id=1, source_target_pairs={{0,2},{1,3},{2,0},{3,1},{4,6},{5,7},{6,4},{7,5},{8,10},{9,11},{10,... | collective-permute-start | bytes 393224 | tf_op jit(solution)/shard_map/ppermute | solution.py:234
  105.4 2.4 %collective-permute-done.17 = f32[128,128]{1,0:T(8,128)S(1)} collective-permute-done((f32[128,128]{1,0:T(8,128)S(1)}, f32[128,128]{1,0:T(8,128)S(1)}, u32[]{:S(2)}, u32[]{:S(2)}) %collective-permute-start.17) | collective-permute-done | bytes 65568 | tf_op jit(solution)/shard_map/ppermute | solution.py:234
  107.9 1.6 %collective-permute-done.21.came_ref = f32[256,128]{1,0:T(8,128)S(1)} collective-permute-done((f32[256,128]{1,0:T(8,128)S(1)}, f32[256,128]{1,0:T(8,128)S(1)}, u32[]{:S(2)}, u32[]{:S(2)}) %collective-permute-start.21) | collective-permute-done | bytes 131104 | tf_op jit(solution)/shard_map/ppermute | solution.py:234
  109.4 1.6 %collective-permute-start.22 = (f32[128,128]{1,0:T(8,128)S(1)}, f32[128,128]{1,0:T(8,128)S(1)}, u32[]{:S(2)}, u32[]{:S(2)}) collective-permute-start(f32[128,128]{1,0:T(8,128)S(1)} %get-tuple-element.84), channel_id=1, source_target_pairs={{0,4},{1,5},{2,6},{3,7},{4,0},{5,1},{6,2},{7,3},{8,12},{9,13},{10,... | collective-permute-start | bytes 196616 | tf_op jit(solution)/shard_map/ppermute | solution.py:234
  111.1 0.2 select_reduce_fusion
  111.5 2.3 %collective-permute-done.22 = f32[128,128]{1,0:T(8,128)S(1)} collective-permute-done((f32[128,128]{1,0:T(8,128)S(1)}, f32[128,128]{1,0:T(8,128)S(1)}, u32[]{:S(2)}, u32[]{:S(2)}) %collective-permute-start.22) | collective-permute-done | bytes 65568 | tf_op jit(solution)/shard_map/ppermute | solution.py:234
  113.8 1.2 %collective-permute-start.23 = (f32[128,128]{1,0:T(8,128)S(1)}, f32[128,128]{1,0:T(8,128)S(1)}, u32[]{:S(2)}, u32[]{:S(2)}) collective-permute-start(f32[128,128]{1,0:T(8,128)S(1)} %add.69.refs_4_), channel_id=1, source_target_pairs={{0,8},{1,9},{2,10},{3,11},{4,12},{5,13},{6,14},{7,15},{8,0},{9,1},... | collective-permute-start | bytes 196616 | tf_op jit(solution)/shard_map/ppermute | solution.py:234
  115.1 3.9 %collective-permute-done.23.refs_5_ = f32[128,128]{1,0:T(8,128)S(1)} collective-permute-done((f32[128,128]{1,0:T(8,128)S(1)}, f32[128,128]{1,0:T(8,128)S(1)}, u32[]{:S(2)}, u32[]{:S(2)}) %collective-permute-start.23) | collective-permute-done | bytes 65568 | tf_op jit(solution)/shard_map/ppermute | solution.py:234
  119.0 2.2 %shard_map.89 = f32[64,1024]{1,0:T(8,128)} custom-call(s32[2]{0:T(128)S(1)} %pad_add_fusion.where_ref, s32[64,1]{1,0:T(8,128)S(1)} %copy.11.rows_ref, f32[1,1024]{1,0:T(1,128)S(1)} %add.60.virt_ref, f32[64,1]{1,0:T(8,128)S(1)} %copy.12.occ_ref, f32[128,256]{1,0:T(8,128)S(1)} %add.62.refs_0_, f32[128,256]{1,0:T(8,128)S(1)} %add.64.refs_1_, ...), custom_call_target="tpu_custom_call" | custom-call | tf_op jit(solution)/shard_map/pallas_call | solution.py:298
  (58 shorter events, 1.5 us)
Async XLA Ops:
  0.0 9.0 %copy-start = (bf16[4096,512]{1,0:T(8,128)(2,1)S(1)}, bf16[4096,512]{1,0:T(8,128)(2,1)}, u32[]{:S(2)}) copy-start(bf16[4096,512]{1,0:T(8,128)(2,1)} %refs_1_) | copy-start | bytes 12582916
  6.1 49.7 %collective-permute-start.8 = (bf16[4096,256]{1,0:T(8,128)(2,1)}, bf16[4096,256]{1,0:T(8,128)(2,1)}, u32[]{:S(2)}, u32[]{:S(2)}) collective-permute-start(bf16[4096,256]{1,0:T(8,128)(2,1)} %shard_map.73), channel_id=1, source_target_pairs={{0,16},{16,0},{1,17},{17,1},{2,18},{18,2},{3,19},{19,3},{4,20},{20... | collective-permute-start | bytes 6291464 | tf_op jit(solution)/shard_map/ppermute | solution.py:29
  20.1 2.0 %collective-permute-start.4 = (f32[512,256]{1,0:T(8,128)S(1)}, f32[512,256]{1,0:T(8,128)S(1)}, u32[]{:S(2)}, u32[]{:S(2)}) collective-permute-start(f32[512,256]{1,0:T(8,128)S(1)} %get-tuple-element.54), channel_id=1, source_target_pairs={{0,1},{1,0},{2,3},{3,2},{4,5},{5,4},{6,7},{7,6},{8,9},{9,8},{10,11... | collective-permute-start | bytes 1572872 | tf_op jit(solution)/shard_map/ppermute | solution.py:234
  20.2 3.5 %collective-permute-start = (f32[512,256]{1,0:T(8,128)S(1)}, f32[512,256]{1,0:T(8,128)S(1)}, u32[]{:S(2)}, u32[]{:S(2)}) collective-permute-start(f32[512,256]{1,0:T(8,128)S(1)} %get-tuple-element.48), channel_id=1, source_target_pairs={{0,1},{1,0},{2,3},{3,2},{4,5},{5,4},{6,7},{7,6},{8,9},{9,8},{10,11... | collective-permute-start | bytes 1572872 | tf_op jit(solution)/shard_map/ppermute | solution.py:234
  22.2 9.2 %collective-permute-start.5 = (f32[256,256]{1,0:T(8,128)S(1)}, f32[256,256]{1,0:T(8,128)S(1)}, u32[]{:S(2)}, u32[]{:S(2)}) collective-permute-start(f32[256,256]{1,0:T(8,128)S(1)} %get-tuple-element.56), channel_id=1, source_target_pairs={{0,2},{1,3},{2,0},{3,1},{4,6},{5,7},{6,4},{7,5},{8,10},{9,11},{10,... | collective-permute-start | bytes 786440 | tf_op jit(solution)/shard_map/ppermute | solution.py:234
  23.8 12.4 %collective-permute-start.1 = (f32[256,256]{1,0:T(8,128)S(1)}, f32[256,256]{1,0:T(8,128)S(1)}, u32[]{:S(2)}, u32[]{:S(2)}) collective-permute-start(f32[256,256]{1,0:T(8,128)S(1)} %get-tuple-element.50), channel_id=1, source_target_pairs={{0,2},{1,3},{2,0},{3,1},{4,6},{5,7},{6,4},{7,5},{8,10},{9,11},{10,... | collective-permute-start | bytes 786440 | tf_op jit(solution)/shard_map/ppermute | solution.py:234
  31.4 6.5 %collective-permute-start.6 = (f32[128,256]{1,0:T(8,128)S(1)}, f32[128,256]{1,0:T(8,128)S(1)}, u32[]{:S(2)}, u32[]{:S(2)}) collective-permute-start(f32[128,256]{1,0:T(8,128)S(1)} %get-tuple-element.58), channel_id=1, source_target_pairs={{0,4},{1,5},{2,6},{3,7},{4,0},{5,1},{6,2},{7,3},{8,12},{9,13},{10,... | collective-permute-start | bytes 393224 | tf_op jit(solution)/shard_map/ppermute | solution.py:234
  36.2 6.5 %collective-permute-start.2 = (f32[128,256]{1,0:T(8,128)S(1)}, f32[128,256]{1,0:T(8,128)S(1)}, u32[]{:S(2)}, u32[]{:S(2)}) collective-permute-start(f32[128,256]{1,0:T(8,128)S(1)} %get-tuple-element.52), channel_id=1, source_target_pairs={{0,4},{1,5},{2,6},{3,7},{4,0},{5,1},{6,2},{7,3},{8,12},{9,13},{10,... | collective-permute-start | bytes 393224 | tf_op jit(solution)/shard_map/ppermute | solution.py:234
  37.9 12.1 %collective-permute-start.7 = (f32[128,256]{1,0:T(8,128)S(1)}, f32[128,256]{1,0:T(8,128)S(1)}, u32[]{:S(2)}, u32[]{:S(2)}) collective-permute-start(f32[128,256]{1,0:T(8,128)S(1)} %add.63), channel_id=1, source_target_pairs={{0,8},{1,9},{2,10},{3,11},{4,12},{5,13},{6,14},{7,15},{8,0},{9,1},... | collective-permute-start | bytes 393224 | tf_op jit(solution)/shard_map/ppermute | solution.py:234
  42.8 9.1 %collective-permute-start.3 = (f32[128,256]{1,0:T(8,128)S(1)}, f32[128,256]{1,0:T(8,128)S(1)}, u32[]{:S(2)}, u32[]{:S(2)}) collective-permute-start(f32[128,256]{1,0:T(8,128)S(1)} %add.61), channel_id=1, source_target_pairs={{0,8},{1,9},{2,10},{3,11},{4,12},{5,13},{6,14},{7,15},{8,0},{9,1},... | collective-permute-start | bytes 393224 | tf_op jit(solution)/shard_map/ppermute | solution.py:234
  45.2 33.0 %collective-permute-start.13 = (bf16[4096,128]{1,0:T(8,128)(2,1)}, bf16[4096,128]{1,0:T(8,128)(2,1)S(1)}, u32[]{:S(2)}, u32[]{:S(2)}) collective-permute-start(bf16[4096,128]{1,0:T(8,128)(2,1)} %slice.9), channel_id=1, source_target_pairs={{0,16},{16,0},{1,17},{17,1},{2,18},{18,2},{3,19},{19,3},{4,20},{20... | collective-permute-start | bytes 3145736 | tf_op jit(solution)/shard_map/ppermute | solution.py:29
  51.9 14.4 %copy-start.1 = (bf16[3072,128]{1,0:T(8,128)(2,1)S(1)}, bf16[3072,128]{1,0:T(8,128)(2,1)}, u32[]{:S(2)}) copy-start(bf16[3072,128]{1,0:T(8,128)(2,1)} %slice.10) | copy-start | bytes 2359300
  55.8 41.4 %slice-start = ((s8[8388608]{0:T(1024)(128)(4,1)}), s8[4194304]{0:T(1024)(128)(4,1)S(1)}, s32[]{:S(2)}) async-start(s8[8388608]{0:T(1024)(128)(4,1)} %bitcast.8), calls=%async_computation | async-start | bytes 8388608
  62.2 2.0 %collective-permute-start.9 = (f32[512,256]{1,0:T(8,128)S(1)}, f32[512,256]{1,0:T(8,128)S(1)}, u32[]{:S(2)}, u32[]{:S(2)}) collective-permute-start(f32[512,256]{1,0:T(8,128)S(1)} %get-tuple-element.61), channel_id=1, source_target_pairs={{0,1},{1,0},{2,3},{3,2},{4,5},{5,4},{6,7},{7,6},{8,9},{9,8},{10,11... | collective-permute-start | bytes 1572872 | tf_op jit(solution)/shard_map/ppermute | solution.py:234
  64.2 8.7 %collective-permute-start.10 = (f32[256,256]{1,0:T(8,128)S(1)}, f32[256,256]{1,0:T(8,128)S(1)}, u32[]{:S(2)}, u32[]{:S(2)}) collective-permute-start(f32[256,256]{1,0:T(8,128)S(1)} %get-tuple-element.63), channel_id=1, source_target_pairs={{0,2},{1,3},{2,0},{3,1},{4,6},{5,7},{6,4},{7,5},{8,10},{9,11},{10,... | collective-permute-start | bytes 786440 | tf_op jit(solution)/shard_map/ppermute | solution.py:234
  66.3 28.9 %collective-permute-start.19 = (bf16[3072,128]{1,0:T(8,128)(2,1)S(1)}, bf16[3072,128]{1,0:T(8,128)(2,1)S(1)}, u32[]{:S(2)}, u32[]{:S(2)}) collective-permute-start(bf16[3072,128]{1,0:T(8,128)(2,1)S(1)} %copy-done.1), channel_id=1, source_target_pairs={{0,16},{16,0},{1,17},{17,1},{2,18},{18,2},{3,19},{19,3},{4,20},{20... | collective-permute-start | bytes 2359304 | tf_op jit(solution)/shard_map/ppermute | solution.py:29
  72.9 24.3 %slice-start.1 = ((s8[8388608]{0:T(1024)(128)(4,1)}), s8[4194304]{0:T(1024)(128)(4,1)S(1)}, s32[]{:S(2)}) async-start(s8[8388608]{0:T(1024)(128)(4,1)} %bitcast.8), calls=%async_computation.1 | async-start | bytes 8388608
  72.9 5.1 %collective-permute-start.11 = (f32[128,256]{1,0:T(8,128)S(1)}, f32[128,256]{1,0:T(8,128)S(1)}, u32[]{:S(2)}, u32[]{:S(2)}) collective-permute-start(f32[128,256]{1,0:T(8,128)S(1)} %get-tuple-element.65), channel_id=1, source_target_pairs={{0,4},{1,5},{2,6},{3,7},{4,0},{5,1},{6,2},{7,3},{8,12},{9,13},{10,... | collective-permute-start | bytes 393224 | tf_op jit(solution)/shard_map/ppermute | solution.py:234
  78.0 5.7 %copy-start.2 = (bf16[1024,128]{1,0:T(8,128)(2,1)S(1)}, bf16[1024,128]{1,0:T(8,128)(2,1)}, u32[]{:S(2)}) copy-start(bf16[1024,128]{1,0:T(8,128)(2,1)} %slice.11) | copy-start | bytes 786436
  83.7 4.8 %collective-permute-start.14 = (f32[512,128]{1,0:T(8,128)S(1)}, f32[512,128]{1,0:T(8,128)S(1)}, u32[]{:S(2)}, u32[]{:S(2)}) collective-permute-start(f32[512,128]{1,0:T(8,128)S(1)} %get-tuple-element.68), channel_id=1, source_target_pairs={{0,1},{1,0},{2,3},{3,2},{4,5},{5,4},{6,7},{7,6},{8,9},{9,8},{10,11... | collective-permute-start | bytes 786440 | tf_op jit(solution)/shard_map/ppermute | solution.py:234
  83.8 16.0 %collective-permute-start.18 = (bf16[1024,128]{1,0:T(8,128)(2,1)S(1)}, bf16[1024,128]{1,0:T(8,128)(2,1)S(1)}, u32[]{:S(2)}, u32[]{:S(2)}) collective-permute-start(bf16[1024,128]{1,0:T(8,128)(2,1)S(1)} %copy-done.2), channel_id=1, source_target_pairs={{0,16},{16,0},{1,17},{17,1},{2,18},{18,2},{3,19},{19,3},{4,20},{20... | collective-permute-start | bytes 786440 | tf_op jit(solution)/shard_map/ppermute | solution.py:29
  85.9 9.3 %collective-permute-start.12 = (f32[128,256]{1,0:T(8,128)S(1)}, f32[128,256]{1,0:T(8,128)S(1)}, u32[]{:S(2)}, u32[]{:S(2)}) collective-permute-start(f32[128,256]{1,0:T(8,128)S(1)} %add.65), channel_id=1, source_target_pairs={{0,8},{1,9},{2,10},{3,11},{4,12},{5,13},{6,14},{7,15},{8,0},{9,1},... | collective-permute-start | bytes 393224 | tf_op jit(solution)/shard_map/ppermute | solution.py:234
  88.5 6.7 %collective-permute-start.15 = (f32[256,128]{1,0:T(8,128)S(1)}, f32[256,128]{1,0:T(8,128)S(1)}, u32[]{:S(2)}, u32[]{:S(2)}) collective-permute-start(f32[256,128]{1,0:T(8,128)S(1)} %get-tuple-element.70), channel_id=1, source_target_pairs={{0,2},{1,3},{2,0},{3,1},{4,6},{5,7},{6,4},{7,5},{8,10},{9,11},{10,... | collective-permute-start | bytes 393224 | tf_op jit(solution)/shard_map/ppermute | solution.py:234
  95.2 4.3 %collective-permute-start.16 = (f32[128,128]{1,0:T(8,128)S(1)}, f32[128,128]{1,0:T(8,128)S(1)}, u32[]{:S(2)}, u32[]{:S(2)}) collective-permute-start(f32[128,128]{1,0:T(8,128)S(1)} %get-tuple-element.73), channel_id=1, source_target_pairs={{0,4},{1,5},{2,6},{3,7},{4,0},{5,1},{6,2},{7,3},{8,12},{9,13},{10,... | collective-permute-start | bytes 196616 | tf_op jit(solution)/shard_map/ppermute | solution.py:234
  99.6 1.0 copy-start.3
  99.6 1.0 copy-start.5
  99.6 5.7 %copy-start.7 = (s32[64]{0:T(128)S(1)}, s32[64]{0:T(128)}, u32[]{:S(2)}) copy-start(s32[64]{0:T(128)} %param.10) | copy-start | bytes 772
  99.6 11.5 %copy-start.4 = (s32[64,2]{0,1:T(2,128)S(1)}, s32[64,2]{0,1:T(2,128)}, u32[]{:S(2)}) copy-start(s32[64,2]{0,1:T(2,128)} %param.9) | copy-start | bytes 1540
  99.6 11.5 %copy-start.6 = (f32[96]{0:T(128)S(1)}, f32[96]{0:T(128)}, u32[]{:S(2)}) copy-start(f32[96]{0:T(128)} %param.12) | copy-start | bytes 1156
  100.5 3.2 %collective-permute-start.20 = (f32[512,128]{1,0:T(8,128)S(1)}, f32[512,128]{1,0:T(8,128)S(1)}, u32[]{:S(2)}, u32[]{:S(2)}) collective-permute-start(f32[512,128]{1,0:T(8,128)S(1)} %get-tuple-element.79), channel_id=1, source_target_pairs={{0,1},{1,0},{2,3},{3,2},{4,5},{5,4},{6,7},{7,6},{8,9},{9,8},{10,11... | collective-permute-start | bytes 786440 | tf_op jit(solution)/shard_map/ppermute | solution.py:234
  100.9 7.0 %collective-permute-start.17 = (f32[128,128]{1,0:T(8,128)S(1)}, f32[128,128]{1,0:T(8,128)S(1)}, u32[]{:S(2)}, u32[]{:S(2)}) collective-permute-start(f32[128,128]{1,0:T(8,128)S(1)} %add.67), channel_id=1, source_target_pairs={{0,8},{1,9},{2,10},{3,11},{4,12},{5,13},{6,14},{7,15},{8,0},{9,1},... | collective-permute-start | bytes 196616 | tf_op jit(solution)/shard_map/ppermute | solution.py:234
  103.8 5.7 %collective-permute-start.21 = (f32[256,128]{1,0:T(8,128)S(1)}, f32[256,128]{1,0:T(8,128)S(1)}, u32[]{:S(2)}, u32[]{:S(2)}) collective-permute-start(f32[256,128]{1,0:T(8,128)S(1)} %get-tuple-element.81), channel_id=1, source_target_pairs={{0,2},{1,3},{2,0},{3,1},{4,6},{5,7},{6,4},{7,5},{8,10},{9,11},{10,... | collective-permute-start | bytes 393224 | tf_op jit(solution)/shard_map/ppermute | solution.py:234
  109.4 4.3 %collective-permute-start.22 = (f32[128,128]{1,0:T(8,128)S(1)}, f32[128,128]{1,0:T(8,128)S(1)}, u32[]{:S(2)}, u32[]{:S(2)}) collective-permute-start(f32[128,128]{1,0:T(8,128)S(1)} %get-tuple-element.84), channel_id=1, source_target_pairs={{0,4},{1,5},{2,6},{3,7},{4,0},{5,1},{6,2},{7,3},{8,12},{9,13},{10,... | collective-permute-start | bytes 196616 | tf_op jit(solution)/shard_map/ppermute | solution.py:234
  113.8 5.2 %collective-permute-start.23 = (f32[128,128]{1,0:T(8,128)S(1)}, f32[128,128]{1,0:T(8,128)S(1)}, u32[]{:S(2)}, u32[]{:S(2)}) collective-permute-start(f32[128,128]{1,0:T(8,128)S(1)} %add.69.refs_4_), channel_id=1, source_target_pairs={{0,8},{1,9},{2,10},{3,11},{4,12},{5,13},{6,14},{7,15},{8,0},{9,1},... | collective-permute-start | bytes 196616 | tf_op jit(solution)/shard_map/ppermute | solution.py:234

commit v10 on v8

--- a/solution.py
+++ b/solution.py
@@ -223,18 +223,18 @@
         copy.wait()
 
 
-def cut_out(source, rows, columns):
-    if columns[0] % LANES or columns[1] % LANES:
-        return source[rows[0] : rows[1], columns[0] : columns[1]]
-    return pl.pallas_call(
-        functools.partial(cut_kernel, [(rows, columns)]),
-        out_shape=[jax.ShapeDtypeStruct((rows[1] - rows[0], columns[1] - columns[0]), source.dtype)],
+def cut_out(source, boxes):
+    if any(edge % LANES for _, columns in boxes for edge in columns):
+        return [source[rows[0] : rows[1], columns[0] : columns[1]] for rows, columns in boxes]
+    return pl.pallas_call(
+        functools.partial(cut_kernel, boxes),
+        out_shape=[jax.ShapeDtypeStruct((r[1] - r[0], c[1] - c[0]), source.dtype) for r, c in boxes],
         in_specs=[pl.BlockSpec(memory_space=pl.ANY)],
-        out_specs=[WHOLE],
-        scratch_shapes=[pltpu.SemaphoreType.DMA((DEPTH_CUTS,))],
+        out_specs=[WHOLE] * len(boxes),
+        scratch_shapes=[pltpu.SemaphoreType.DMA((DEPTH_CUTS * len(boxes),))],
         compiler_params=pltpu.CompilerParams(vmem_limit_bytes=CUT_BYTES),
         cost_estimate=FREE,
-    )(source)[0]
+    )(source)
 
 
 def last_kernel(width, starts, where_ref, rows_ref, virt_ref, occ_ref, *refs):
@@ -298,10 +298,10 @@
 
     depth = integrals.shape[0]
     late = depth // DEPTH_CUTS * (DEPTH_CUTS - 1)
-    first = cut_out(integrals, (0, depth), cuts[0])
+    (first,) = cut_out(integrals, [((0, depth), cuts[0])])
     rest = after(integrals, first)
-    low, high = cuts[-1]
-    pieces = [first] + [rest[:, low:high] for low, high in cuts[1:-1]] + [rest[:late, low:high], rest[late:, low:high]]
+    boxes = [((0, depth), cut) for cut in cuts[1:-1]] + [((0, late), cuts[-1]), ((late, depth), cuts[-1])]
+    pieces = [first, *cut_out(rest, boxes)]
     in_flight = [sent(pieces[0]), sent(pieces[1])]
     own_product = multiplied(amplitudes, after(rest, pieces), bits[0], order, splits=OWN_SPLITS)
     own_sums = [jnp.add(*exchanged_sum(own_product[2 * part : 2 * part + 2], bits)[0]) for part in range(OWN_SPLITS)]

time: 118 us -> 118 us (level)
  local copies, waits for them, and re-layouts: 3.19 us -> 0.32 us
  Pallas kernels: 28.4 us -> 31.2 us
    slice x3 -> x0, local copies, waits for them, and re-layouts: 2.86 us -> none  [the longest x1 1.14 us: per_device(): rest[:, low:high]]
    pallas_call x1 -> x2, Pallas kernels: 3.05 us -> 5.83 us  [cut_out(): pl.pallas_call(functools.partial(cut_kernel, boxes), out_shape=[jax.Shape...]
  transfers between devices with their start and end apart: 24 -> 24, of which waited for: 17 -> 17; matrix products, arithmetic and copies ran while one was open for 3% -> 1% of each run, Pallas kernels for 19% -> 21%
where the time goes in v10:
time: 118 us
  waiting for transfers between devices  50 us (42%)
  starting transfers between devices  35.8 us (30%)
  Pallas kernels  31.2 us (26%)
    ppermute x20, waiting for transfers between devices, flipped_along(): lax.ppermute(value, axis, [(source, source ^ bits) for source in range(co...  46 us
    ppermute x20, starting transfers between devices, flipped_along(): lax.ppermute(value, axis, [(source, source ^ bits) for source in range(co...  28.6 us
    pallas_call x3, Pallas kernels, multiplied(): pl.pallas_call(functools.partial(product_kernel, steps, order, splits, ba...  20.3 us
    ppermute x4, starting transfers between devices, passed_along(): return lax.ppermute(value, axis, pairs)  7.18 us
    pallas_call x2, Pallas kernels, cut_out(): pl.pallas_call(functools.partial(cut_kernel, boxes), out_shape=[jax.Shape...  5.83 us
    ppermute x4, waiting for transfers between devices, passed_along(): return lax.ppermute(value, axis, pairs)  3.92 us
  transfers between devices with their start and end apart: 24, of which 17 were waited for; matrix products, arithmetic and copies ran while one was open for 1% of the time, Pallas kernels for 21%

profile of v10, /device:TPU:0, one launch (start us, length us, event | category | flops | bytes accessed | tf_op | source)
XLA Modules:
  0.0 118.2 jit_solution(10579099322649587912)
XLA Ops:
  0.0 2.9 %shard_map.73 = bf16[4096,256]{1,0:T(8,128)(2,1)} custom-call(bf16[4096,512]{1,0:T(8,128)(2,1)} %refs_1_), custom_call_target="tpu_custom_call" | custom-call | tf_op jit(solution)/shard_map/pallas_call | solution.py:229
  2.9 3.0 %collective-permute-start.8 = (bf16[4096,256]{1,0:T(8,128)(2,1)}, bf16[4096,256]{1,0:T(8,128)(2,1)}, u32[]{:S(2)}, u32[]{:S(2)}) collective-permute-start(bf16[4096,256]{1,0:T(8,128)(2,1)} %shard_map.73), channel_id=1, source_target_pairs={{0,16},{16,0},{1,17},{17,1},{2,18},{18,2},{3,19},{19,3},{4,20},{20... | collective-permute-start | bytes 6291464 | tf_op jit(solution)/shard_map/ppermute | solution.py:27
  5.9 2.9 %shard_map.74 = (bf16[4096,128]{1,0:T(8,128)(2,1)}, bf16[3072,128]{1,0:T(8,128)(2,1)}, bf16[1024,128]{1,0:T(8,128)(2,1)}) custom-call(bf16[4096,512]{1,0:T(8,128)(2,1)} %refs_1_), custom_call_target="tpu_custom_call" | custom-call | tf_op jit(solution)/shard_map/pallas_call | solution.py:229
  8.9 8.3 %shard_map.75 = (f32[512,256]{1,0:T(8,128)S(1)}, f32[512,256]{1,0:T(8,128)S(1)}, f32[512,256]{1,0:T(8,128)S(1)}, f32[512,256]{1,0:T(8,128)S(1)}) custom-call(s32[1]{0:T(128)} %bitcast.6.bit_ref, bf16[1024,4096]{1,0:T(8,128)(2,1)} %a_ref.3, bf16[4096,512]{1,0:T(8,128)(2,1)} %refs_1_), custom_call_target="tpu_custom_call" | custom-call | tf_op jit(solution)/shard_map/pallas_call | solution.py:106
  17.2 0.5 collective-permute-start
  17.7 1.4 %collective-permute-done.4.came_ref = f32[512,256]{1,0:T(8,128)S(1)} collective-permute-done((f32[512,256]{1,0:T(8,128)S(1)}, f32[512,256]{1,0:T(8,128)S(1)}, u32[]{:S(2)}, u32[]{:S(2)}) %collective-permute-start.4) | collective-permute-done | bytes 524320 | tf_op jit(solution)/shard_map/ppermute | solution.py:197
  19.2 1.6 %collective-permute-start.5 = (f32[256,256]{1,0:T(8,128)S(1)}, f32[256,256]{1,0:T(8,128)S(1)}, u32[]{:S(2)}, u32[]{:S(2)}) collective-permute-start(f32[256,256]{1,0:T(8,128)S(1)} %get-tuple-element.62), channel_id=1, source_target_pairs={{0,2},{1,3},{2,0},{3,1},{4,6},{5,7},{6,4},{7,5},{8,10},{9,11},{10,... | collective-permute-start | bytes 786440 | tf_op jit(solution)/shard_map/ppermute | solution.py:197
  20.8 0.7 collective-permute-start.1
  21.5 6.9 %collective-permute-done.5.came_ref = f32[256,256]{1,0:T(8,128)S(1)} collective-permute-done((f32[256,256]{1,0:T(8,128)S(1)}, f32[256,256]{1,0:T(8,128)S(1)}, u32[]{:S(2)}, u32[]{:S(2)}) %collective-permute-start.5) | collective-permute-done | bytes 262176 | tf_op jit(solution)/shard_map/ppermute | solution.py:197
  28.4 1.6 %collective-permute-start.6 = (f32[128,256]{1,0:T(8,128)S(1)}, f32[128,256]{1,0:T(8,128)S(1)}, u32[]{:S(2)}, u32[]{:S(2)}) collective-permute-start(f32[128,256]{1,0:T(8,128)S(1)} %get-tuple-element.64), channel_id=1, source_target_pairs={{0,4},{1,5},{2,6},{3,7},{4,0},{5,1},{6,2},{7,3},{8,12},{9,13},{10,... | collective-permute-start | bytes 393224 | tf_op jit(solution)/shard_map/ppermute | solution.py:197
  30.1 3.1 %collective-permute-done.1.came_ref = f32[256,256]{1,0:T(8,128)S(1)} collective-permute-done((f32[256,256]{1,0:T(8,128)S(1)}, f32[256,256]{1,0:T(8,128)S(1)}, u32[]{:S(2)}, u32[]{:S(2)}) %collective-permute-start.1) | collective-permute-done | bytes 262176 | tf_op jit(solution)/shard_map/ppermute | solution.py:197
  33.2 1.6 %collective-permute-start.2 = (f32[128,256]{1,0:T(8,128)S(1)}, f32[128,256]{1,0:T(8,128)S(1)}, u32[]{:S(2)}, u32[]{:S(2)}) collective-permute-start(f32[128,256]{1,0:T(8,128)S(1)} %get-tuple-element.58), channel_id=1, source_target_pairs={{0,4},{1,5},{2,6},{3,7},{4,0},{5,1},{6,2},{7,3},{8,12},{9,13},{10,... | collective-permute-start | bytes 393224 | tf_op jit(solution)/shard_map/ppermute | solution.py:197
  34.9 2.7 %collective-permute-start.7 = (f32[128,256]{1,0:T(8,128)S(1)}, f32[128,256]{1,0:T(8,128)S(1)}, u32[]{:S(2)}, u32[]{:S(2)}) collective-permute-start(f32[128,256]{1,0:T(8,128)S(1)} %add.63), channel_id=1, source_target_pairs={{0,8},{1,9},{2,10},{3,11},{4,12},{5,13},{6,14},{7,15},{8,0},{9,1},... | collective-permute-start | bytes 393224 | tf_op jit(solution)/shard_map/ppermute | solution.py:197
  37.6 2.2 %collective-permute-done.2 = f32[128,256]{1,0:T(8,128)S(1)} collective-permute-done((f32[128,256]{1,0:T(8,128)S(1)}, f32[128,256]{1,0:T(8,128)S(1)}, u32[]{:S(2)}, u32[]{:S(2)}) %collective-permute-start.2) | collective-permute-done | bytes 131104 | tf_op jit(solution)/shard_map/ppermute | solution.py:197
  39.8 2.4 %collective-permute-start.3 = (f32[128,256]{1,0:T(8,128)S(1)}, f32[128,256]{1,0:T(8,128)S(1)}, u32[]{:S(2)}, u32[]{:S(2)}) collective-permute-start(f32[128,256]{1,0:T(8,128)S(1)} %add.61), channel_id=1, source_target_pairs={{0,8},{1,9},{2,10},{3,11},{4,12},{5,13},{6,14},{7,15},{8,0},{9,1},... | collective-permute-start | bytes 393224 | tf_op jit(solution)/shard_map/ppermute | solution.py:197
  42.2 0.5 collective-permute-start.13
  42.7 4.3 %collective-permute-done.7 = f32[128,256]{1,0:T(8,128)S(1)} collective-permute-done((f32[128,256]{1,0:T(8,128)S(1)}, f32[128,256]{1,0:T(8,128)S(1)}, u32[]{:S(2)}, u32[]{:S(2)}) %collective-permute-start.7) | collective-permute-done | bytes 131104 | tf_op jit(solution)/shard_map/ppermute | solution.py:197
  47.0 1.9 %collective-permute-done.3 = f32[128,256]{1,0:T(8,128)S(1)} collective-permute-done((f32[128,256]{1,0:T(8,128)S(1)}, f32[128,256]{1,0:T(8,128)S(1)}, u32[]{:S(2)}, u32[]{:S(2)}) %collective-permute-start.3) | collective-permute-done | bytes 131104 | tf_op jit(solution)/shard_map/ppermute | solution.py:197
  48.9 3.8 %collective-permute-done.8.refs_1_ = bf16[4096,256]{1,0:T(8,128)(2,1)} collective-permute-done((bf16[4096,256]{1,0:T(8,128)(2,1)}, bf16[4096,256]{1,0:T(8,128)(2,1)}, u32[]{:S(2)}, u32[]{:S(2)}) %collective-permute-start.8) | collective-permute-done | bytes 2097184 | tf_op jit(solution)/shard_map/ppermute | solution.py:27
  52.7 6.4 %shard_map.80 = (f32[512,256]{1,0:T(8,128)S(1)}, f32[512,256]{1,0:T(8,128)S(1)}) custom-call(s32[1]{0:T(128)} %bitcast.6.bit_ref, bf16[1024,4096]{1,0:T(8,128)(2,1)} %a_ref.3, bf16[4096,256]{1,0:T(8,128)(2,1)} %collective-permute-done.8.refs_1_), custom_call_target="tpu_custom_call" | custom-call | flops 2147483648 | bytes 8388608 | tf_op jit(solution)/shard_map/pallas_call | solution.py:106
  59.2 1.9 %collective-permute-done.9.came_ref = f32[512,256]{1,0:T(8,128)S(1)} collective-permute-done((f32[512,256]{1,0:T(8,128)S(1)}, f32[512,256]{1,0:T(8,128)S(1)}, u32[]{:S(2)}, u32[]{:S(2)}) %collective-permute-start.9) | collective-permute-done | bytes 524320 | tf_op jit(solution)/shard_map/ppermute | solution.py:197
  61.1 2.1 %collective-permute-start.10 = (f32[256,256]{1,0:T(8,128)S(1)}, f32[256,256]{1,0:T(8,128)S(1)}, u32[]{:S(2)}, u32[]{:S(2)}) collective-permute-start(f32[256,256]{1,0:T(8,128)S(1)} %get-tuple-element.69), channel_id=1, source_target_pairs={{0,2},{1,3},{2,0},{3,1},{4,6},{5,7},{6,4},{7,5},{8,10},{9,11},{10,... | collective-permute-start | bytes 786440 | tf_op jit(solution)/shard_map/ppermute | solution.py:197
  63.2 1.5 %collective-permute-start.19 = (bf16[3072,128]{1,0:T(8,128)(2,1)S(1)}, bf16[3072,128]{1,0:T(8,128)(2,1)S(1)}, u32[]{:S(2)}, u32[]{:S(2)}) collective-permute-start(bf16[3072,128]{1,0:T(8,128)(2,1)S(1)} %copy-done.4), channel_id=1, source_target_pairs={{0,16},{16,0},{1,17},{17,1},{2,18},{18,2},{3,19},{19,3},{4,20},{20... | collective-permute-start | bytes 2359304 | tf_op jit(solution)/shard_map/ppermute | solution.py:27
  64.7 5.1 %collective-permute-done.10.came_ref = f32[256,256]{1,0:T(8,128)S(1)} collective-permute-done((f32[256,256]{1,0:T(8,128)S(1)}, f32[256,256]{1,0:T(8,128)S(1)}, u32[]{:S(2)}, u32[]{:S(2)}) %collective-permute-start.10) | collective-permute-done | bytes 262176 | tf_op jit(solution)/shard_map/ppermute | solution.py:197
  69.9 1.9 %collective-permute-start.11 = (f32[128,256]{1,0:T(8,128)S(1)}, f32[128,256]{1,0:T(8,128)S(1)}, u32[]{:S(2)}, u32[]{:S(2)}) collective-permute-start(f32[128,256]{1,0:T(8,128)S(1)} %get-tuple-element.71), channel_id=1, source_target_pairs={{0,4},{1,5},{2,6},{3,7},{4,0},{5,1},{6,2},{7,3},{8,12},{9,13},{10,... | collective-permute-start | bytes 393224 | tf_op jit(solution)/shard_map/ppermute | solution.py:197
  71.7 3.2 %collective-permute-done.11 = f32[128,256]{1,0:T(8,128)S(1)} collective-permute-done((f32[128,256]{1,0:T(8,128)S(1)}, f32[128,256]{1,0:T(8,128)S(1)}, u32[]{:S(2)}, u32[]{:S(2)}) %collective-permute-start.11) | collective-permute-done | bytes 131104 | tf_op jit(solution)/shard_map/ppermute | solution.py:197
  75.0 0.1 collective-permute-done.13.refs_1_
  75.1 5.7 %shard_map.83 = (f32[512,128]{1,0:T(8,128)S(1)}, f32[512,128]{1,0:T(8,128)S(1)}) custom-call(s32[1]{0:T(128)} %bitcast.6.bit_ref, bf16[1024,4096]{1,0:T(8,128)(2,1)} %a_ref.3, bf16[4096,128]{1,0:T(8,128)(2,1)S(1)} %collective-permute-done.13.refs_1_), custom_call_target="tpu_custom_call" | custom-call | flops 1073741824 | bytes 8388608 | tf_op jit(solution)/shard_map/pallas_call | solution.py:106
  80.8 2.1 %collective-permute-start.18 = (bf16[1024,128]{1,0:T(8,128)(2,1)S(1)}, bf16[1024,128]{1,0:T(8,128)(2,1)S(1)}, u32[]{:S(2)}, u32[]{:S(2)}) collective-permute-start(bf16[1024,128]{1,0:T(8,128)(2,1)S(1)} %copy-done.5), channel_id=1, source_target_pairs={{0,16},{16,0},{1,17},{17,1},{2,18},{18,2},{3,19},{19,3},{4,20},{20... | collective-permute-start | bytes 786440 | tf_op jit(solution)/shard_map/ppermute | solution.py:27
  83.0 2.6 %collective-permute-start.12 = (f32[128,256]{1,0:T(8,128)S(1)}, f32[128,256]{1,0:T(8,128)S(1)}, u32[]{:S(2)}, u32[]{:S(2)}) collective-permute-start(f32[128,256]{1,0:T(8,128)S(1)} %add.65), channel_id=1, source_target_pairs={{0,8},{1,9},{2,10},{3,11},{4,12},{5,13},{6,14},{7,15},{8,0},{9,1},... | collective-permute-start | bytes 393224 | tf_op jit(solution)/shard_map/ppermute | solution.py:197
  85.6 1.6 %collective-permute-start.15 = (f32[256,128]{1,0:T(8,128)S(1)}, f32[256,128]{1,0:T(8,128)S(1)}, u32[]{:S(2)}, u32[]{:S(2)}) collective-permute-start(f32[256,128]{1,0:T(8,128)S(1)} %get-tuple-element.76), channel_id=1, source_target_pairs={{0,2},{1,3},{2,0},{3,1},{4,6},{5,7},{6,4},{7,5},{8,10},{9,11},{10,... | collective-permute-start | bytes 393224 | tf_op jit(solution)/shard_map/ppermute | solution.py:197
  87.2 5.1 %collective-permute-done.12 = f32[128,256]{1,0:T(8,128)S(1)} collective-permute-done((f32[128,256]{1,0:T(8,128)S(1)}, f32[128,256]{1,0:T(8,128)S(1)}, u32[]{:S(2)}, u32[]{:S(2)}) %collective-permute-start.12) | collective-permute-done | bytes 131104 | tf_op jit(solution)/shard_map/ppermute | solution.py:197
  92.3 1.8 %collective-permute-start.16 = (f32[128,128]{1,0:T(8,128)S(1)}, f32[128,128]{1,0:T(8,128)S(1)}, u32[]{:S(2)}, u32[]{:S(2)}) collective-permute-start(f32[128,128]{1,0:T(8,128)S(1)} %get-tuple-element.79), channel_id=1, source_target_pairs={{0,4},{1,5},{2,6},{3,7},{4,0},{5,1},{6,2},{7,3},{8,12},{9,13},{10,... | collective-permute-start | bytes 196616 | tf_op jit(solution)/shard_map/ppermute | solution.py:197
  94.1 1.8 %shard_map.86.refs_0_ = f32[1024,128]{1,0:T(8,128)S(1)} custom-call(bf16[1024,4096]{1,0:T(8,128)(2,1)S(1)} %bitcast.9, bf16[3072,128]{1,0:T(8,128)(2,1)S(1)} %collective-permute-done.19.b_ref), custom_call_target="tpu_custom_call" | custom-call | flops 805306368 | bytes 6291456 | tf_op jit(solution)/shard_map/pallas_call | solution.py:165
  95.9 0.7 collective-permute-done.16
  96.7 0.7 shard_map.87
  97.6 0.2 select_reduce_fusion.1
  97.8 2.8 %collective-permute-start.17 = (f32[128,128]{1,0:T(8,128)S(1)}, f32[128,128]{1,0:T(8,128)S(1)}, u32[]{:S(2)}, u32[]{:S(2)}) collective-permute-start(f32[128,128]{1,0:T(8,128)S(1)} %add.67), channel_id=1, source_target_pairs={{0,8},{1,9},{2,10},{3,11},{4,12},{5,13},{6,14},{7,15},{8,0},{9,1},... | collective-permute-start | bytes 196616 | tf_op jit(solution)/shard_map/ppermute | solution.py:197
  100.7 1.6 %collective-permute-start.21 = (f32[256,128]{1,0:T(8,128)S(1)}, f32[256,128]{1,0:T(8,128)S(1)}, u32[]{:S(2)}, u32[]{:S(2)}) collective-permute-start(f32[256,128]{1,0:T(8,128)S(1)} %get-tuple-element.87), channel_id=1, source_target_pairs={{0,2},{1,3},{2,0},{3,1},{4,6},{5,7},{6,4},{7,5},{8,10},{9,11},{10,... | collective-permute-start | bytes 393224 | tf_op jit(solution)/shard_map/ppermute | solution.py:197
  102.4 2.4 %collective-permute-done.17 = f32[128,128]{1,0:T(8,128)S(1)} collective-permute-done((f32[128,128]{1,0:T(8,128)S(1)}, f32[128,128]{1,0:T(8,128)S(1)}, u32[]{:S(2)}, u32[]{:S(2)}) %collective-permute-start.17) | collective-permute-done | bytes 65568 | tf_op jit(solution)/shard_map/ppermute | solution.py:197
  104.8 1.6 %collective-permute-done.21.came_ref = f32[256,128]{1,0:T(8,128)S(1)} collective-permute-done((f32[256,128]{1,0:T(8,128)S(1)}, f32[256,128]{1,0:T(8,128)S(1)}, u32[]{:S(2)}, u32[]{:S(2)}) %collective-permute-start.21) | collective-permute-done | bytes 131104 | tf_op jit(solution)/shard_map/ppermute | solution.py:197
  106.4 1.6 %collective-permute-start.22 = (f32[128,128]{1,0:T(8,128)S(1)}, f32[128,128]{1,0:T(8,128)S(1)}, u32[]{:S(2)}, u32[]{:S(2)}) collective-permute-start(f32[128,128]{1,0:T(8,128)S(1)} %get-tuple-element.90), channel_id=1, source_target_pairs={{0,4},{1,5},{2,6},{3,7},{4,0},{5,1},{6,2},{7,3},{8,12},{9,13},{10,... | collective-permute-start | bytes 196616 | tf_op jit(solution)/shard_map/ppermute | solution.py:197
  108.0 0.2 select_reduce_fusion
  108.2 0.1 copy.12.occ_ref
  108.4 2.3 %collective-permute-done.22 = f32[128,128]{1,0:T(8,128)S(1)} collective-permute-done((f32[128,128]{1,0:T(8,128)S(1)}, f32[128,128]{1,0:T(8,128)S(1)}, u32[]{:S(2)}, u32[]{:S(2)}) %collective-permute-start.22) | collective-permute-done | bytes 65568 | tf_op jit(solution)/shard_map/ppermute | solution.py:197
  110.7 1.2 %collective-permute-start.23 = (f32[128,128]{1,0:T(8,128)S(1)}, f32[128,128]{1,0:T(8,128)S(1)}, u32[]{:S(2)}, u32[]{:S(2)}) collective-permute-start(f32[128,128]{1,0:T(8,128)S(1)} %add.69.refs_4_), channel_id=1, source_target_pairs={{0,8},{1,9},{2,10},{3,11},{4,12},{5,13},{6,14},{7,15},{8,0},{9,1},... | collective-permute-start | bytes 196616 | tf_op jit(solution)/shard_map/ppermute | solution.py:197
  112.0 3.9 %collective-permute-done.23.refs_5_ = f32[128,128]{1,0:T(8,128)S(1)} collective-permute-done((f32[128,128]{1,0:T(8,128)S(1)}, f32[128,128]{1,0:T(8,128)S(1)}, u32[]{:S(2)}, u32[]{:S(2)}) %collective-permute-start.23) | collective-permute-done | bytes 65568 | tf_op jit(solution)/shard_map/ppermute | solution.py:197
  116.0 2.2 %shard_map.90 = f32[64,1024]{1,0:T(8,128)} custom-call(s32[2]{0:T(128)S(1)} %pad_add_fusion.where_ref, s32[64,1]{1,0:T(8,128)S(1)} %copy.11.rows_ref, f32[1,1024]{1,0:T(1,128)S(1)} %add.60.virt_ref, f32[64,1]{1,0:T(8,128)S(1)} %copy.12.occ_ref, f32[128,256]{1,0:T(8,128)S(1)} %add.62.refs_0_, f32[128,256]{1,0:T(8,128)S(1)} %add.64.refs_1_, ...), custom_call_target="tpu_custom_call" | custom-call | tf_op jit(solution)/shard_map/pallas_call | solution.py:269
  (54 shorter events, 1.2 us)
Async XLA Ops:
  2.9 49.8 %collective-permute-start.8 = (bf16[4096,256]{1,0:T(8,128)(2,1)}, bf16[4096,256]{1,0:T(8,128)(2,1)}, u32[]{:S(2)}, u32[]{:S(2)}) collective-permute-start(bf16[4096,256]{1,0:T(8,128)(2,1)} %shard_map.73), channel_id=1, source_target_pairs={{0,16},{16,0},{1,17},{17,1},{2,18},{18,2},{3,19},{19,3},{4,20},{20... | collective-permute-start | bytes 6291464 | tf_op jit(solution)/shard_map/ppermute | solution.py:27
  17.1 2.0 %collective-permute-start.4 = (f32[512,256]{1,0:T(8,128)S(1)}, f32[512,256]{1,0:T(8,128)S(1)}, u32[]{:S(2)}, u32[]{:S(2)}) collective-permute-start(f32[512,256]{1,0:T(8,128)S(1)} %get-tuple-element.60), channel_id=1, source_target_pairs={{0,1},{1,0},{2,3},{3,2},{4,5},{5,4},{6,7},{7,6},{8,9},{9,8},{10,11... | collective-permute-start | bytes 1572872 | tf_op jit(solution)/shard_map/ppermute | solution.py:197
  17.2 3.5 %collective-permute-start = (f32[512,256]{1,0:T(8,128)S(1)}, f32[512,256]{1,0:T(8,128)S(1)}, u32[]{:S(2)}, u32[]{:S(2)}) collective-permute-start(f32[512,256]{1,0:T(8,128)S(1)} %get-tuple-element.54), channel_id=1, source_target_pairs={{0,1},{1,0},{2,3},{3,2},{4,5},{5,4},{6,7},{7,6},{8,9},{9,8},{10,11... | collective-permute-start | bytes 1572872 | tf_op jit(solution)/shard_map/ppermute | solution.py:197
  19.2 9.2 %collective-permute-start.5 = (f32[256,256]{1,0:T(8,128)S(1)}, f32[256,256]{1,0:T(8,128)S(1)}, u32[]{:S(2)}, u32[]{:S(2)}) collective-permute-start(f32[256,256]{1,0:T(8,128)S(1)} %get-tuple-element.62), channel_id=1, source_target_pairs={{0,2},{1,3},{2,0},{3,1},{4,6},{5,7},{6,4},{7,5},{8,10},{9,11},{10,... | collective-permute-start | bytes 786440 | tf_op jit(solution)/shard_map/ppermute | solution.py:197
  20.8 12.4 %collective-permute-start.1 = (f32[256,256]{1,0:T(8,128)S(1)}, f32[256,256]{1,0:T(8,128)S(1)}, u32[]{:S(2)}, u32[]{:S(2)}) collective-permute-start(f32[256,256]{1,0:T(8,128)S(1)} %get-tuple-element.56), channel_id=1, source_target_pairs={{0,2},{1,3},{2,0},{3,1},{4,6},{5,7},{6,4},{7,5},{8,10},{9,11},{10,... | collective-permute-start | bytes 786440 | tf_op jit(solution)/shard_map/ppermute | solution.py:197
  28.4 6.5 %collective-permute-start.6 = (f32[128,256]{1,0:T(8,128)S(1)}, f32[128,256]{1,0:T(8,128)S(1)}, u32[]{:S(2)}, u32[]{:S(2)}) collective-permute-start(f32[128,256]{1,0:T(8,128)S(1)} %get-tuple-element.64), channel_id=1, source_target_pairs={{0,4},{1,5},{2,6},{3,7},{4,0},{5,1},{6,2},{7,3},{8,12},{9,13},{10,... | collective-permute-start | bytes 393224 | tf_op jit(solution)/shard_map/ppermute | solution.py:197
  33.2 6.5 %collective-permute-start.2 = (f32[128,256]{1,0:T(8,128)S(1)}, f32[128,256]{1,0:T(8,128)S(1)}, u32[]{:S(2)}, u32[]{:S(2)}) collective-permute-start(f32[128,256]{1,0:T(8,128)S(1)} %get-tuple-element.58), channel_id=1, source_target_pairs={{0,4},{1,5},{2,6},{3,7},{4,0},{5,1},{6,2},{7,3},{8,12},{9,13},{10,... | collective-permute-start | bytes 393224 | tf_op jit(solution)/shard_map/ppermute | solution.py:197
  34.9 12.1 %collective-permute-start.7 = (f32[128,256]{1,0:T(8,128)S(1)}, f32[128,256]{1,0:T(8,128)S(1)}, u32[]{:S(2)}, u32[]{:S(2)}) collective-permute-start(f32[128,256]{1,0:T(8,128)S(1)} %add.63), channel_id=1, source_target_pairs={{0,8},{1,9},{2,10},{3,11},{4,12},{5,13},{6,14},{7,15},{8,0},{9,1},... | collective-permute-start | bytes 393224 | tf_op jit(solution)/shard_map/ppermute | solution.py:197
  39.8 9.1 %collective-permute-start.3 = (f32[128,256]{1,0:T(8,128)S(1)}, f32[128,256]{1,0:T(8,128)S(1)}, u32[]{:S(2)}, u32[]{:S(2)}) collective-permute-start(f32[128,256]{1,0:T(8,128)S(1)} %add.61), channel_id=1, source_target_pairs={{0,8},{1,9},{2,10},{3,11},{4,12},{5,13},{6,14},{7,15},{8,0},{9,1},... | collective-permute-start | bytes 393224 | tf_op jit(solution)/shard_map/ppermute | solution.py:197
  42.2 32.9 %collective-permute-start.13 = (bf16[4096,128]{1,0:T(8,128)(2,1)}, bf16[4096,128]{1,0:T(8,128)(2,1)S(1)}, u32[]{:S(2)}, u32[]{:S(2)}) collective-permute-start(bf16[4096,128]{1,0:T(8,128)(2,1)} %get-tuple-element.49), channel_id=1, source_target_pairs={{0,16},{16,0},{1,17},{17,1},{2,18},{18,2},{3,19},{19,3},{4,20},{20... | collective-permute-start | bytes 3145736 | tf_op jit(solution)/shard_map/ppermute | solution.py:27
  48.9 14.3 %copy-start.4 = (bf16[3072,128]{1,0:T(8,128)(2,1)S(1)}, bf16[3072,128]{1,0:T(8,128)(2,1)}, u32[]{:S(2)}) copy-start(bf16[3072,128]{1,0:T(8,128)(2,1)} %get-tuple-element.81) | copy-start | bytes 2359300
  52.7 41.4 %slice-start = ((s8[8388608]{0:T(1024)(128)(4,1)}), s8[4194304]{0:T(1024)(128)(4,1)S(1)}, s32[]{:S(2)}) async-start(s8[8388608]{0:T(1024)(128)(4,1)} %bitcast.8), calls=%async_computation | async-start | bytes 8388608
  59.1 2.0 %collective-permute-start.9 = (f32[512,256]{1,0:T(8,128)S(1)}, f32[512,256]{1,0:T(8,128)S(1)}, u32[]{:S(2)}, u32[]{:S(2)}) collective-permute-start(f32[512,256]{1,0:T(8,128)S(1)} %get-tuple-element.67), channel_id=1, source_target_pairs={{0,1},{1,0},{2,3},{3,2},{4,5},{5,4},{6,7},{7,6},{8,9},{9,8},{10,11... | collective-permute-start | bytes 1572872 | tf_op jit(solution)/shard_map/ppermute | solution.py:197
  61.1 8.7 %collective-permute-start.10 = (f32[256,256]{1,0:T(8,128)S(1)}, f32[256,256]{1,0:T(8,128)S(1)}, u32[]{:S(2)}, u32[]{:S(2)}) collective-permute-start(f32[256,256]{1,0:T(8,128)S(1)} %get-tuple-element.69), channel_id=1, source_target_pairs={{0,2},{1,3},{2,0},{3,1},{4,6},{5,7},{6,4},{7,5},{8,10},{9,11},{10,... | collective-permute-start | bytes 786440 | tf_op jit(solution)/shard_map/ppermute | solution.py:197
  63.2 29.0 %collective-permute-start.19 = (bf16[3072,128]{1,0:T(8,128)(2,1)S(1)}, bf16[3072,128]{1,0:T(8,128)(2,1)S(1)}, u32[]{:S(2)}, u32[]{:S(2)}) collective-permute-start(bf16[3072,128]{1,0:T(8,128)(2,1)S(1)} %copy-done.4), channel_id=1, source_target_pairs={{0,16},{16,0},{1,17},{17,1},{2,18},{18,2},{3,19},{19,3},{4,20},{20... | collective-permute-start | bytes 2359304 | tf_op jit(solution)/shard_map/ppermute | solution.py:27
  69.8 24.3 %slice-start.1 = ((s8[8388608]{0:T(1024)(128)(4,1)}), s8[4194304]{0:T(1024)(128)(4,1)S(1)}, s32[]{:S(2)}) async-start(s8[8388608]{0:T(1024)(128)(4,1)} %bitcast.8), calls=%async_computation.1 | async-start | bytes 8388608
  69.9 5.1 %collective-permute-start.11 = (f32[128,256]{1,0:T(8,128)S(1)}, f32[128,256]{1,0:T(8,128)S(1)}, u32[]{:S(2)}, u32[]{:S(2)}) collective-permute-start(f32[128,256]{1,0:T(8,128)S(1)} %get-tuple-element.71), channel_id=1, source_target_pairs={{0,4},{1,5},{2,6},{3,7},{4,0},{5,1},{6,2},{7,3},{8,12},{9,13},{10,... | collective-permute-start | bytes 393224 | tf_op jit(solution)/shard_map/ppermute | solution.py:197
  75.0 5.9 %copy-start.5 = (bf16[1024,128]{1,0:T(8,128)(2,1)S(1)}, bf16[1024,128]{1,0:T(8,128)(2,1)}, u32[]{:S(2)}) copy-start(bf16[1024,128]{1,0:T(8,128)(2,1)} %get-tuple-element.80) | copy-start | bytes 786436
  80.8 4.8 %collective-permute-start.14 = (f32[512,128]{1,0:T(8,128)S(1)}, f32[512,128]{1,0:T(8,128)S(1)}, u32[]{:S(2)}, u32[]{:S(2)}) collective-permute-start(f32[512,128]{1,0:T(8,128)S(1)} %get-tuple-element.74), channel_id=1, source_target_pairs={{0,1},{1,0},{2,3},{3,2},{4,5},{5,4},{6,7},{7,6},{8,9},{9,8},{10,11... | collective-permute-start | bytes 786440 | tf_op jit(solution)/shard_map/ppermute | solution.py:197
  80.8 15.9 %collective-permute-start.18 = (bf16[1024,128]{1,0:T(8,128)(2,1)S(1)}, bf16[1024,128]{1,0:T(8,128)(2,1)S(1)}, u32[]{:S(2)}, u32[]{:S(2)}) collective-permute-start(bf16[1024,128]{1,0:T(8,128)(2,1)S(1)} %copy-done.5), channel_id=1, source_target_pairs={{0,16},{16,0},{1,17},{17,1},{2,18},{18,2},{3,19},{19,3},{4,20},{20... | collective-permute-start | bytes 786440 | tf_op jit(solution)/shard_map/ppermute | solution.py:27
  83.0 9.3 %collective-permute-start.12 = (f32[128,256]{1,0:T(8,128)S(1)}, f32[128,256]{1,0:T(8,128)S(1)}, u32[]{:S(2)}, u32[]{:S(2)}) collective-permute-start(f32[128,256]{1,0:T(8,128)S(1)} %add.65), channel_id=1, source_target_pairs={{0,8},{1,9},{2,10},{3,11},{4,12},{5,13},{6,14},{7,15},{8,0},{9,1},... | collective-permute-start | bytes 393224 | tf_op jit(solution)/shard_map/ppermute | solution.py:197
  85.6 6.7 %collective-permute-start.15 = (f32[256,128]{1,0:T(8,128)S(1)}, f32[256,128]{1,0:T(8,128)S(1)}, u32[]{:S(2)}, u32[]{:S(2)}) collective-permute-start(f32[256,128]{1,0:T(8,128)S(1)} %get-tuple-element.76), channel_id=1, source_target_pairs={{0,2},{1,3},{2,0},{3,1},{4,6},{5,7},{6,4},{7,5},{8,10},{9,11},{10,... | collective-permute-start | bytes 393224 | tf_op jit(solution)/shard_map/ppermute | solution.py:197
  92.3 4.3 %collective-permute-start.16 = (f32[128,128]{1,0:T(8,128)S(1)}, f32[128,128]{1,0:T(8,128)S(1)}, u32[]{:S(2)}, u32[]{:S(2)}) collective-permute-start(f32[128,128]{1,0:T(8,128)S(1)} %get-tuple-element.79), channel_id=1, source_target_pairs={{0,4},{1,5},{2,6},{3,7},{4,0},{5,1},{6,2},{7,3},{8,12},{9,13},{10,... | collective-permute-start | bytes 196616 | tf_op jit(solution)/shard_map/ppermute | solution.py:197
  96.7 0.9 copy-start
  96.7 0.9 copy-start.2
  96.7 5.6 %copy-start.6 = (s32[64]{0:T(128)S(1)}, s32[64]{0:T(128)}, u32[]{:S(2)}) copy-start(s32[64]{0:T(128)} %param.10) | copy-start | bytes 772
  96.7 11.3 %copy-start.1 = (s32[64,2]{0,1:T(2,128)S(1)}, s32[64,2]{0,1:T(2,128)}, u32[]{:S(2)}) copy-start(s32[64,2]{0,1:T(2,128)} %param.9) | copy-start | bytes 1540
  96.7 11.3 %copy-start.3 = (f32[96]{0:T(128)S(1)}, f32[96]{0:T(128)}, u32[]{:S(2)}) copy-start(f32[96]{0:T(128)} %param.12) | copy-start | bytes 1156
  97.5 3.2 %collective-permute-start.20 = (f32[512,128]{1,0:T(8,128)S(1)}, f32[512,128]{1,0:T(8,128)S(1)}, u32[]{:S(2)}, u32[]{:S(2)}) collective-permute-start(f32[512,128]{1,0:T(8,128)S(1)} %get-tuple-element.85), channel_id=1, source_target_pairs={{0,1},{1,0},{2,3},{3,2},{4,5},{5,4},{6,7},{7,6},{8,9},{9,8},{10,11... | collective-permute-start | bytes 786440 | tf_op jit(solution)/shard_map/ppermute | solution.py:197
  97.8 7.0 %collective-permute-start.17 = (f32[128,128]{1,0:T(8,128)S(1)}, f32[128,128]{1,0:T(8,128)S(1)}, u32[]{:S(2)}, u32[]{:S(2)}) collective-permute-start(f32[128,128]{1,0:T(8,128)S(1)} %add.67), channel_id=1, source_target_pairs={{0,8},{1,9},{2,10},{3,11},{4,12},{5,13},{6,14},{7,15},{8,0},{9,1},... | collective-permute-start | bytes 196616 | tf_op jit(solution)/shard_map/ppermute | solution.py:197
  100.7 5.7 %collective-permute-start.21 = (f32[256,128]{1,0:T(8,128)S(1)}, f32[256,128]{1,0:T(8,128)S(1)}, u32[]{:S(2)}, u32[]{:S(2)}) collective-permute-start(f32[256,128]{1,0:T(8,128)S(1)} %get-tuple-element.87), channel_id=1, source_target_pairs={{0,2},{1,3},{2,0},{3,1},{4,6},{5,7},{6,4},{7,5},{8,10},{9,11},{10,... | collective-permute-start | bytes 393224 | tf_op jit(solution)/shard_map/ppermute | solution.py:197
  106.4 4.3 %collective-permute-start.22 = (f32[128,128]{1,0:T(8,128)S(1)}, f32[128,128]{1,0:T(8,128)S(1)}, u32[]{:S(2)}, u32[]{:S(2)}) collective-permute-start(f32[128,128]{1,0:T(8,128)S(1)} %get-tuple-element.90), channel_id=1, source_target_pairs={{0,4},{1,5},{2,6},{3,7},{4,0},{5,1},{6,2},{7,3},{8,12},{9,13},{10,... | collective-permute-start | bytes 196616 | tf_op jit(solution)/shard_map/ppermute | solution.py:197
  110.7 5.2 %collective-permute-start.23 = (f32[128,128]{1,0:T(8,128)S(1)}, f32[128,128]{1,0:T(8,128)S(1)}, u32[]{:S(2)}, u32[]{:S(2)}) collective-permute-start(f32[128,128]{1,0:T(8,128)S(1)} %add.69.refs_4_), channel_id=1, source_target_pairs={{0,8},{1,9},{2,10},{3,11},{4,12},{5,13},{6,14},{7,15},{8,0},{9,1},... | collective-permute-start | bytes 196616 | tf_op jit(solution)/shard_map/ppermute | solution.py:197

commit v11 on v10

--- a/solution.py
+++ b/solution.py
@@ -91,8 +91,8 @@
         for index, out_ref in enumerate(out_refs):
             bit = 1 - bit_ref[0] if index % 2 else bit_ref[0]
             columns = slice(index // 2 * width, (index // 2 + 1) * width)
-            for place, block in enumerate(order):
-                start = pl.multiple_of((block + bit) * rows, rows)
+            for place, (even, odd) in enumerate(order):
+                start = pl.multiple_of((even + bit * (odd - even + 1)) * rows, rows)
                 out_ref[place * rows : (place + 1) * rows, :] = total_ref[pl.ds(start, rows), columns]
 
 
@@ -136,8 +136,8 @@
     add_whole(a_ref, b_ref, total_ref, first, refs[0] if has_base else None)
     rows = keep_ref.shape[0] // len(order)
     for out_ref, bit in ((keep_ref, bit_ref[0]), (send_ref, 1 - bit_ref[0])):
-        for place, block in enumerate(order):
-            start = pl.multiple_of((block + bit) * rows, rows)
+        for place, (even, odd) in enumerate(order):
+            start = pl.multiple_of((even + bit * (odd - even + 1)) * rows, rows)
             out_ref[place * rows : (place + 1) * rows, :] = total_ref[pl.ds(start, rows), :]
 
 
@@ -192,21 +192,21 @@
     )(bit, mine, came)
 
 
-def flipped_along(value, axis, bits):
+def flipped_along(value, axis, flip):
     count = lax.axis_size(axis)
-    return lax.ppermute(value, axis, [(source, source ^ bits) for source in range(count)])
-
-
-def exchanged_sum(parts, bits, gates=()):
+    return lax.ppermute(value, axis, [(source, source ^ flip[source % 2]) for source in range(count)])
+
+
+def exchanged_sum(parts, bits, flips, gates=()):
     stages = []
     for level in range(1, len(bits)):
         keep, send = parts
-        came = flipped_along(send, "virt", 1 << (level - 1))
+        came = flipped_along(send, "virt", flips[level - 1])
         if level in gates:
             came = after(came, gates[level])
         parts = halved(keep, came, bits[level]) if level < len(bits) - 1 else [keep + came]
         stages.append(parts[0])
-    return (parts[0], flipped_along(parts[0], "virt", 1 << (len(bits) - 1))), stages
+    return (parts[0], flipped_along(parts[0], "virt", flips[-1])), stages
 
 
 def cut_kernel(boxes, source_ref, *refs):
@@ -289,8 +289,17 @@
     cuts = column_cuts(integrals.shape[1])
     me = lax.axis_index("virt").astype(jnp.int32)
     levels = size.bit_length() - 1
-    bits = [((me >> level) & 1).reshape(1) for level in range(levels)]
-    order = [sum(((place >> (levels - 1 - level)) & 1) << level for level in range(1, levels)) for place in range(size // 2)]
+    steps = [list(range(1, levels)), list(range(1, levels))]
+    if levels > 3:
+        steps[1][0:2] = [2, 1]
+    own_bits = [(me >> level) & 1 for level in range(levels)]
+    bits = [own_bits[0]] + [jnp.where(own_bits[0] == 1, own_bits[odd], own_bits[even]) for even, odd in zip(*steps)]
+    bits = [bit.reshape(1) for bit in bits]
+    flips = [[1, 1]] + [[1 << even, 1 << odd] for even, odd in zip(*steps)]
+    order = [
+        tuple(sum(((place >> (levels - 2 - index)) & 1) << level for index, level in enumerate(taken)) for taken in steps)
+        for place in range(size // 2)
+    ]
     upper = me >= size // 2
 
     def sent(piece):
@@ -304,7 +313,7 @@
     pieces = [first, *cut_out(rest, boxes)]
     in_flight = [sent(pieces[0]), sent(pieces[1])]
     own_product = multiplied(amplitudes, after(rest, pieces), bits[0], order, splits=OWN_SPLITS)
-    own_sums = [jnp.add(*exchanged_sum(own_product[2 * part : 2 * part + 2], bits)[0]) for part in range(OWN_SPLITS)]
+    own_sums = [jnp.add(*exchanged_sum(own_product[2 * part : 2 * part + 2], bits, flips)[0]) for part in range(OWN_SPLITS)]
     sums = [own_sums] + [[] for _ in range(1, count)]
     in_flight += [sent(after(piece, own_sums)) for piece in pieces[2:]]
     earlier, gates = own_sums, {}
@@ -319,7 +328,7 @@
                 product = multiplied(amplitudes, arrived[shift - 1], bits[0], order)
             else:
                 product = whole_multiplied(amplitudes, arrived[shift - 1], bits[0], order, late, bases[shift - 1])
-            terms, stages = exchanged_sum(product, bits, gates)
+            terms, stages = exchanged_sum(product, bits, flips, gates)
             total = jnp.add(*terms)
             sums[shift].append(total)
             earlier, gates = stages[2] if step < len(cuts) - 2 else stages[0], {2: total}

time: 118 us -> 118 us (level)
  waiting for transfers between devices: 50 us -> 48.6 us
    ppermute x20, waiting for transfers between devices: 46 us -> 38.4 us  [flipped_along(): lax.ppermute(value, axis, [(source, source ^ flip[source % 2]) for source...]
    ppermute x4, waiting for transfers between devices: 3.92 us -> 10.1 us  [passed_along(): return lax.ppermute(value, axis, pairs)]
  transfers between devices with their start and end apart: 24 -> 24, of which waited for: 17 -> 17; matrix products, arithmetic and copies ran while one was open for 1% -> 1% of each run, Pallas kernels for 21% -> 22%
where the time goes in v11:
time: 118 us
  waiting for transfers between devices  48.6 us (41%)
  starting transfers between devices  36.5 us (31%)
  Pallas kernels  31.2 us (26%)
    ppermute x20, waiting for transfers between devices, flipped_along(): lax.ppermute(value, axis, [(source, source ^ flip[source % 2]) for source...  38.4 us
    ppermute x20, starting transfers between devices, flipped_along(): lax.ppermute(value, axis, [(source, source ^ flip[source % 2]) for source...  29.3 us
    pallas_call x3, Pallas kernels, multiplied(): pl.pallas_call(functools.partial(product_kernel, steps, order, splits, ba...  20.3 us
    ppermute x4, waiting for transfers between devices, passed_along(): return lax.ppermute(value, axis, pairs)  10.1 us
    ppermute x4, starting transfers between devices, passed_along(): return lax.ppermute(value, axis, pairs)  7.18 us
    pallas_call x2, Pallas kernels, cut_out(): pl.pallas_call(functools.partial(cut_kernel, boxes), out_shape=[jax.Shape...  5.83 us
  transfers between devices with their start and end apart: 24, of which 17 were waited for; matrix products, arithmetic and copies ran while one was open for 1% of the time, Pallas kernels for 22%

profile of v11, /device:TPU:0, one launch (start us, length us, event | category | flops | bytes accessed | tf_op | source)
XLA Modules:
  0.0 117.5 jit_solution(7066073336404297742)
XLA Ops:
  0.0 2.9 %shard_map.73 = bf16[4096,256]{1,0:T(8,128)(2,1)} custom-call(bf16[4096,512]{1,0:T(8,128)(2,1)} %refs_1_), custom_call_target="tpu_custom_call" | custom-call | tf_op jit(solution)/shard_map/pallas_call | solution.py:229
  2.9 3.0 %collective-permute-start.8 = (bf16[4096,256]{1,0:T(8,128)(2,1)}, bf16[4096,256]{1,0:T(8,128)(2,1)}, u32[]{:S(2)}, u32[]{:S(2)}) collective-permute-start(bf16[4096,256]{1,0:T(8,128)(2,1)} %shard_map.73), channel_id=1, source_target_pairs={{0,16},{16,0},{1,17},{17,1},{2,18},{18,2},{3,19},{19,3},{4,20},{20... | collective-permute-start | bytes 6291464 | tf_op jit(solution)/shard_map/ppermute | solution.py:27
  5.9 2.9 %shard_map.74 = (bf16[4096,128]{1,0:T(8,128)(2,1)}, bf16[3072,128]{1,0:T(8,128)(2,1)}, bf16[1024,128]{1,0:T(8,128)(2,1)}) custom-call(bf16[4096,512]{1,0:T(8,128)(2,1)} %refs_1_), custom_call_target="tpu_custom_call" | custom-call | tf_op jit(solution)/shard_map/pallas_call | solution.py:229
  8.9 8.3 %shard_map.75 = (f32[512,256]{1,0:T(8,128)S(1)}, f32[512,256]{1,0:T(8,128)S(1)}, f32[512,256]{1,0:T(8,128)S(1)}, f32[512,256]{1,0:T(8,128)S(1)}) custom-call(s32[1]{0:T(128)} %bitcast.6.bit_ref, bf16[1024,4096]{1,0:T(8,128)(2,1)} %a_ref.3, bf16[4096,512]{1,0:T(8,128)(2,1)} %refs_1_), custom_call_target="tpu_custom_call" | custom-call | tf_op jit(solution)/shard_map/pallas_call | solution.py:106
  17.2 0.5 collective-permute-start
  17.7 1.4 %collective-permute-done.4.came_ref = f32[512,256]{1,0:T(8,128)S(1)} collective-permute-done((f32[512,256]{1,0:T(8,128)S(1)}, f32[512,256]{1,0:T(8,128)S(1)}, u32[]{:S(2)}, u32[]{:S(2)}) %collective-permute-start.4) | collective-permute-done | bytes 524320 | tf_op jit(solution)/shard_map/ppermute | solution.py:197
  19.2 1.6 %collective-permute-start.5 = (f32[256,256]{1,0:T(8,128)S(1)}, f32[256,256]{1,0:T(8,128)S(1)}, u32[]{:S(2)}, u32[]{:S(2)}) collective-permute-start(f32[256,256]{1,0:T(8,128)S(1)} %get-tuple-element.62), channel_id=1, source_target_pairs={{0,2},{1,5},{2,0},{3,7},{4,6},{5,1},{6,4},{7,3},{8,10},{9,13},{10,... | collective-permute-start | bytes 786440 | tf_op jit(solution)/shard_map/ppermute | solution.py:197
  20.8 0.7 collective-permute-start.1
  21.5 4.1 %collective-permute-done.5.came_ref = f32[256,256]{1,0:T(8,128)S(1)} collective-permute-done((f32[256,256]{1,0:T(8,128)S(1)}, f32[256,256]{1,0:T(8,128)S(1)}, u32[]{:S(2)}, u32[]{:S(2)}) %collective-permute-start.5) | collective-permute-done | bytes 262176 | tf_op jit(solution)/shard_map/ppermute | solution.py:197
  25.6 1.6 %collective-permute-start.6 = (f32[128,256]{1,0:T(8,128)S(1)}, f32[128,256]{1,0:T(8,128)S(1)}, u32[]{:S(2)}, u32[]{:S(2)}) collective-permute-start(f32[128,256]{1,0:T(8,128)S(1)} %get-tuple-element.64), channel_id=1, source_target_pairs={{0,4},{1,3},{2,6},{3,1},{4,0},{5,7},{6,2},{7,5},{8,12},{9,11},{10,... | collective-permute-start | bytes 393224 | tf_op jit(solution)/shard_map/ppermute | solution.py:197
  27.3 1.8 %collective-permute-done.1.came_ref = f32[256,256]{1,0:T(8,128)S(1)} collective-permute-done((f32[256,256]{1,0:T(8,128)S(1)}, f32[256,256]{1,0:T(8,128)S(1)}, u32[]{:S(2)}, u32[]{:S(2)}) %collective-permute-start.1) | collective-permute-done | bytes 262176 | tf_op jit(solution)/shard_map/ppermute | solution.py:197
  29.1 1.6 %collective-permute-start.2 = (f32[128,256]{1,0:T(8,128)S(1)}, f32[128,256]{1,0:T(8,128)S(1)}, u32[]{:S(2)}, u32[]{:S(2)}) collective-permute-start(f32[128,256]{1,0:T(8,128)S(1)} %get-tuple-element.58), channel_id=1, source_target_pairs={{0,4},{1,3},{2,6},{3,1},{4,0},{5,7},{6,2},{7,5},{8,12},{9,11},{10,... | collective-permute-start | bytes 393224 | tf_op jit(solution)/shard_map/ppermute | solution.py:197
  30.8 2.7 %collective-permute-start.7 = (f32[128,256]{1,0:T(8,128)S(1)}, f32[128,256]{1,0:T(8,128)S(1)}, u32[]{:S(2)}, u32[]{:S(2)}) collective-permute-start(f32[128,256]{1,0:T(8,128)S(1)} %add.63), channel_id=1, source_target_pairs={{0,8},{1,9},{2,10},{3,11},{4,12},{5,13},{6,14},{7,15},{8,0},{9,1},... | collective-permute-start | bytes 393224 | tf_op jit(solution)/shard_map/ppermute | solution.py:197
  33.4 2.0 %collective-permute-done.2 = f32[128,256]{1,0:T(8,128)S(1)} collective-permute-done((f32[128,256]{1,0:T(8,128)S(1)}, f32[128,256]{1,0:T(8,128)S(1)}, u32[]{:S(2)}, u32[]{:S(2)}) %collective-permute-start.2) | collective-permute-done | bytes 131104 | tf_op jit(solution)/shard_map/ppermute | solution.py:197
  35.5 2.7 %collective-permute-start.3 = (f32[128,256]{1,0:T(8,128)S(1)}, f32[128,256]{1,0:T(8,128)S(1)}, u32[]{:S(2)}, u32[]{:S(2)}) collective-permute-start(f32[128,256]{1,0:T(8,128)S(1)} %add.61), channel_id=1, source_target_pairs={{0,8},{1,9},{2,10},{3,11},{4,12},{5,13},{6,14},{7,15},{8,0},{9,1},... | collective-permute-start | bytes 393224 | tf_op jit(solution)/shard_map/ppermute | solution.py:197
  38.2 0.5 collective-permute-start.13
  38.7 4.6 %collective-permute-done.7 = f32[128,256]{1,0:T(8,128)S(1)} collective-permute-done((f32[128,256]{1,0:T(8,128)S(1)}, f32[128,256]{1,0:T(8,128)S(1)}, u32[]{:S(2)}, u32[]{:S(2)}) %collective-permute-start.7) | collective-permute-done | bytes 131104 | tf_op jit(solution)/shard_map/ppermute | solution.py:197
  43.3 1.6 %collective-permute-done.3 = f32[128,256]{1,0:T(8,128)S(1)} collective-permute-done((f32[128,256]{1,0:T(8,128)S(1)}, f32[128,256]{1,0:T(8,128)S(1)}, u32[]{:S(2)}, u32[]{:S(2)}) %collective-permute-start.3) | collective-permute-done | bytes 131104 | tf_op jit(solution)/shard_map/ppermute | solution.py:197
  44.9 7.8 %collective-permute-done.8.refs_1_ = bf16[4096,256]{1,0:T(8,128)(2,1)} collective-permute-done((bf16[4096,256]{1,0:T(8,128)(2,1)}, bf16[4096,256]{1,0:T(8,128)(2,1)}, u32[]{:S(2)}, u32[]{:S(2)}) %collective-permute-start.8) | collective-permute-done | bytes 2097184 | tf_op jit(solution)/shard_map/ppermute | solution.py:27
  52.7 6.4 %shard_map.80 = (f32[512,256]{1,0:T(8,128)S(1)}, f32[512,256]{1,0:T(8,128)S(1)}) custom-call(s32[1]{0:T(128)} %bitcast.6.bit_ref, bf16[1024,4096]{1,0:T(8,128)(2,1)} %a_ref.3, bf16[4096,256]{1,0:T(8,128)(2,1)} %collective-permute-done.8.refs_1_), custom_call_target="tpu_custom_call" | custom-call | flops 2147483648 | bytes 8388608 | tf_op jit(solution)/shard_map/pallas_call | solution.py:106
  59.2 1.9 %collective-permute-done.9.came_ref = f32[512,256]{1,0:T(8,128)S(1)} collective-permute-done((f32[512,256]{1,0:T(8,128)S(1)}, f32[512,256]{1,0:T(8,128)S(1)}, u32[]{:S(2)}, u32[]{:S(2)}) %collective-permute-start.9) | collective-permute-done | bytes 524320 | tf_op jit(solution)/shard_map/ppermute | solution.py:197
  61.1 2.1 %collective-permute-start.10 = (f32[256,256]{1,0:T(8,128)S(1)}, f32[256,256]{1,0:T(8,128)S(1)}, u32[]{:S(2)}, u32[]{:S(2)}) collective-permute-start(f32[256,256]{1,0:T(8,128)S(1)} %get-tuple-element.69), channel_id=1, source_target_pairs={{0,2},{1,5},{2,0},{3,7},{4,6},{5,1},{6,4},{7,3},{8,10},{9,13},{10,... | collective-permute-start | bytes 786440 | tf_op jit(solution)/shard_map/ppermute | solution.py:197
  63.2 1.5 %collective-permute-start.19 = (bf16[3072,128]{1,0:T(8,128)(2,1)S(1)}, bf16[3072,128]{1,0:T(8,128)(2,1)S(1)}, u32[]{:S(2)}, u32[]{:S(2)}) collective-permute-start(bf16[3072,128]{1,0:T(8,128)(2,1)S(1)} %copy-done.4), channel_id=1, source_target_pairs={{0,16},{16,0},{1,17},{17,1},{2,18},{18,2},{3,19},{19,3},{4,20},{20... | collective-permute-start | bytes 2359304 | tf_op jit(solution)/shard_map/ppermute | solution.py:27
  64.7 2.8 %collective-permute-done.10.came_ref = f32[256,256]{1,0:T(8,128)S(1)} collective-permute-done((f32[256,256]{1,0:T(8,128)S(1)}, f32[256,256]{1,0:T(8,128)S(1)}, u32[]{:S(2)}, u32[]{:S(2)}) %collective-permute-start.10) | collective-permute-done | bytes 262176 | tf_op jit(solution)/shard_map/ppermute | solution.py:197
  67.6 2.2 %collective-permute-start.11 = (f32[128,256]{1,0:T(8,128)S(1)}, f32[128,256]{1,0:T(8,128)S(1)}, u32[]{:S(2)}, u32[]{:S(2)}) collective-permute-start(f32[128,256]{1,0:T(8,128)S(1)} %get-tuple-element.71), channel_id=1, source_target_pairs={{0,4},{1,3},{2,6},{3,1},{4,0},{5,7},{6,2},{7,5},{8,12},{9,11},{10,... | collective-permute-start | bytes 393224 | tf_op jit(solution)/shard_map/ppermute | solution.py:197
  69.8 2.9 %collective-permute-done.11 = f32[128,256]{1,0:T(8,128)S(1)} collective-permute-done((f32[128,256]{1,0:T(8,128)S(1)}, f32[128,256]{1,0:T(8,128)S(1)}, u32[]{:S(2)}, u32[]{:S(2)}) %collective-permute-start.11) | collective-permute-done | bytes 131104 | tf_op jit(solution)/shard_map/ppermute | solution.py:197
  72.8 2.3 %collective-permute-done.13.refs_1_ = bf16[4096,128]{1,0:T(8,128)(2,1)S(1)} collective-permute-done((bf16[4096,128]{1,0:T(8,128)(2,1)}, bf16[4096,128]{1,0:T(8,128)(2,1)S(1)}, u32[]{:S(2)}, u32[]{:S(2)}) %collective-permute-start.13) | collective-permute-done | bytes 1048608 | tf_op jit(solution)/shard_map/ppermute | solution.py:27
  75.1 5.7 %shard_map.83 = (f32[512,128]{1,0:T(8,128)S(1)}, f32[512,128]{1,0:T(8,128)S(1)}) custom-call(s32[1]{0:T(128)} %bitcast.6.bit_ref, bf16[1024,4096]{1,0:T(8,128)(2,1)} %a_ref.3, bf16[4096,128]{1,0:T(8,128)(2,1)S(1)} %collective-permute-done.13.refs_1_), custom_call_target="tpu_custom_call" | custom-call | flops 1073741824 | bytes 8388608 | tf_op jit(solution)/shard_map/pallas_call | solution.py:106
  80.8 2.1 %collective-permute-start.18 = (bf16[1024,128]{1,0:T(8,128)(2,1)S(1)}, bf16[1024,128]{1,0:T(8,128)(2,1)S(1)}, u32[]{:S(2)}, u32[]{:S(2)}) collective-permute-start(bf16[1024,128]{1,0:T(8,128)(2,1)S(1)} %copy-done.5), channel_id=1, source_target_pairs={{0,16},{16,0},{1,17},{17,1},{2,18},{18,2},{3,19},{19,3},{4,20},{20... | collective-permute-start | bytes 786440 | tf_op jit(solution)/shard_map/ppermute | solution.py:27
  83.0 2.6 %collective-permute-start.12 = (f32[128,256]{1,0:T(8,128)S(1)}, f32[128,256]{1,0:T(8,128)S(1)}, u32[]{:S(2)}, u32[]{:S(2)}) collective-permute-start(f32[128,256]{1,0:T(8,128)S(1)} %add.65), channel_id=1, source_target_pairs={{0,8},{1,9},{2,10},{3,11},{4,12},{5,13},{6,14},{7,15},{8,0},{9,1},... | collective-permute-start | bytes 393224 | tf_op jit(solution)/shard_map/ppermute | solution.py:197
  85.6 1.6 %collective-permute-start.15 = (f32[256,128]{1,0:T(8,128)S(1)}, f32[256,128]{1,0:T(8,128)S(1)}, u32[]{:S(2)}, u32[]{:S(2)}) collective-permute-start(f32[256,128]{1,0:T(8,128)S(1)} %get-tuple-element.76), channel_id=1, source_target_pairs={{0,2},{1,5},{2,0},{3,7},{4,6},{5,1},{6,4},{7,3},{8,10},{9,13},{10,... | collective-permute-start | bytes 393224 | tf_op jit(solution)/shard_map/ppermute | solution.py:197
  87.2 5.1 %collective-permute-done.12 = f32[128,256]{1,0:T(8,128)S(1)} collective-permute-done((f32[128,256]{1,0:T(8,128)S(1)}, f32[128,256]{1,0:T(8,128)S(1)}, u32[]{:S(2)}, u32[]{:S(2)}) %collective-permute-start.12) | collective-permute-done | bytes 131104 | tf_op jit(solution)/shard_map/ppermute | solution.py:197
  92.3 1.8 %collective-permute-start.16 = (f32[128,128]{1,0:T(8,128)S(1)}, f32[128,128]{1,0:T(8,128)S(1)}, u32[]{:S(2)}, u32[]{:S(2)}) collective-permute-start(f32[128,128]{1,0:T(8,128)S(1)} %get-tuple-element.79), channel_id=1, source_target_pairs={{0,4},{1,3},{2,6},{3,1},{4,0},{5,7},{6,2},{7,5},{8,12},{9,11},{10,... | collective-permute-start | bytes 196616 | tf_op jit(solution)/shard_map/ppermute | solution.py:197
  94.1 1.8 %shard_map.86.refs_0_ = f32[1024,128]{1,0:T(8,128)S(1)} custom-call(bf16[1024,4096]{1,0:T(8,128)(2,1)S(1)} %bitcast.9, bf16[3072,128]{1,0:T(8,128)(2,1)S(1)} %collective-permute-done.19.b_ref), custom_call_target="tpu_custom_call" | custom-call | flops 805306368 | bytes 6291456 | tf_op jit(solution)/shard_map/pallas_call | solution.py:165
  95.9 0.7 collective-permute-done.16
  96.7 0.7 shard_map.87
  97.6 0.2 select_reduce_fusion.1
  97.8 2.8 %collective-permute-start.17 = (f32[128,128]{1,0:T(8,128)S(1)}, f32[128,128]{1,0:T(8,128)S(1)}, u32[]{:S(2)}, u32[]{:S(2)}) collective-permute-start(f32[128,128]{1,0:T(8,128)S(1)} %add.67), channel_id=1, source_target_pairs={{0,8},{1,9},{2,10},{3,11},{4,12},{5,13},{6,14},{7,15},{8,0},{9,1},... | collective-permute-start | bytes 196616 | tf_op jit(solution)/shard_map/ppermute | solution.py:197
  100.7 1.6 %collective-permute-start.21 = (f32[256,128]{1,0:T(8,128)S(1)}, f32[256,128]{1,0:T(8,128)S(1)}, u32[]{:S(2)}, u32[]{:S(2)}) collective-permute-start(f32[256,128]{1,0:T(8,128)S(1)} %get-tuple-element.87), channel_id=1, source_target_pairs={{0,2},{1,5},{2,0},{3,7},{4,6},{5,1},{6,4},{7,3},{8,10},{9,13},{10,... | collective-permute-start | bytes 393224 | tf_op jit(solution)/shard_map/ppermute | solution.py:197
  102.4 2.3 %collective-permute-done.17 = f32[128,128]{1,0:T(8,128)S(1)} collective-permute-done((f32[128,128]{1,0:T(8,128)S(1)}, f32[128,128]{1,0:T(8,128)S(1)}, u32[]{:S(2)}, u32[]{:S(2)}) %collective-permute-start.17) | collective-permute-done | bytes 65568 | tf_op jit(solution)/shard_map/ppermute | solution.py:197
  104.7 1.0 collective-permute-done.21.came_ref
  105.7 1.6 %collective-permute-start.22 = (f32[128,128]{1,0:T(8,128)S(1)}, f32[128,128]{1,0:T(8,128)S(1)}, u32[]{:S(2)}, u32[]{:S(2)}) collective-permute-start(f32[128,128]{1,0:T(8,128)S(1)} %get-tuple-element.90), channel_id=1, source_target_pairs={{0,4},{1,3},{2,6},{3,1},{4,0},{5,7},{6,2},{7,5},{8,12},{9,11},{10,... | collective-permute-start | bytes 196616 | tf_op jit(solution)/shard_map/ppermute | solution.py:197
  107.4 0.2 select_reduce_fusion
  107.6 0.1 copy.12.occ_ref
  107.7 2.3 %collective-permute-done.22 = f32[128,128]{1,0:T(8,128)S(1)} collective-permute-done((f32[128,128]{1,0:T(8,128)S(1)}, f32[128,128]{1,0:T(8,128)S(1)}, u32[]{:S(2)}, u32[]{:S(2)}) %collective-permute-start.22) | collective-permute-done | bytes 65568 | tf_op jit(solution)/shard_map/ppermute | solution.py:197
  110.1 1.4 %collective-permute-start.23 = (f32[128,128]{1,0:T(8,128)S(1)}, f32[128,128]{1,0:T(8,128)S(1)}, u32[]{:S(2)}, u32[]{:S(2)}) collective-permute-start(f32[128,128]{1,0:T(8,128)S(1)} %add.69.refs_4_), channel_id=1, source_target_pairs={{0,8},{1,9},{2,10},{3,11},{4,12},{5,13},{6,14},{7,15},{8,0},{9,1},... | collective-permute-start | bytes 196616 | tf_op jit(solution)/shard_map/ppermute | solution.py:197
  111.5 3.8 %collective-permute-done.23.refs_5_ = f32[128,128]{1,0:T(8,128)S(1)} collective-permute-done((f32[128,128]{1,0:T(8,128)S(1)}, f32[128,128]{1,0:T(8,128)S(1)}, u32[]{:S(2)}, u32[]{:S(2)}) %collective-permute-start.23) | collective-permute-done | bytes 65568 | tf_op jit(solution)/shard_map/ppermute | solution.py:197
  115.3 2.2 %shard_map.90 = f32[64,1024]{1,0:T(8,128)} custom-call(s32[2]{0:T(128)S(1)} %pad_add_fusion.where_ref, s32[64,1]{1,0:T(8,128)S(1)} %copy.11.rows_ref, f32[1,1024]{1,0:T(1,128)S(1)} %add.60.virt_ref, f32[64,1]{1,0:T(8,128)S(1)} %copy.12.occ_ref, f32[128,256]{1,0:T(8,128)S(1)} %add.62.refs_0_, f32[128,256]{1,0:T(8,128)S(1)} %add.64.refs_1_, ...), custom_call_target="tpu_custom_call" | custom-call | tf_op jit(solution)/shard_map/pallas_call | solution.py:269
  (54 shorter events, 1.2 us)
Async XLA Ops:
  2.9 49.8 %collective-permute-start.8 = (bf16[4096,256]{1,0:T(8,128)(2,1)}, bf16[4096,256]{1,0:T(8,128)(2,1)}, u32[]{:S(2)}, u32[]{:S(2)}) collective-permute-start(bf16[4096,256]{1,0:T(8,128)(2,1)} %shard_map.73), channel_id=1, source_target_pairs={{0,16},{16,0},{1,17},{17,1},{2,18},{18,2},{3,19},{19,3},{4,20},{20... | collective-permute-start | bytes 6291464 | tf_op jit(solution)/shard_map/ppermute | solution.py:27
  17.1 2.0 %collective-permute-start.4 = (f32[512,256]{1,0:T(8,128)S(1)}, f32[512,256]{1,0:T(8,128)S(1)}, u32[]{:S(2)}, u32[]{:S(2)}) collective-permute-start(f32[512,256]{1,0:T(8,128)S(1)} %get-tuple-element.60), channel_id=1, source_target_pairs={{0,1},{1,0},{2,3},{3,2},{4,5},{5,4},{6,7},{7,6},{8,9},{9,8},{10,11... | collective-permute-start | bytes 1572872 | tf_op jit(solution)/shard_map/ppermute | solution.py:197
  17.2 3.5 %collective-permute-start = (f32[512,256]{1,0:T(8,128)S(1)}, f32[512,256]{1,0:T(8,128)S(1)}, u32[]{:S(2)}, u32[]{:S(2)}) collective-permute-start(f32[512,256]{1,0:T(8,128)S(1)} %get-tuple-element.54), channel_id=1, source_target_pairs={{0,1},{1,0},{2,3},{3,2},{4,5},{5,4},{6,7},{7,6},{8,9},{9,8},{10,11... | collective-permute-start | bytes 1572872 | tf_op jit(solution)/shard_map/ppermute | solution.py:197
  19.2 6.4 %collective-permute-start.5 = (f32[256,256]{1,0:T(8,128)S(1)}, f32[256,256]{1,0:T(8,128)S(1)}, u32[]{:S(2)}, u32[]{:S(2)}) collective-permute-start(f32[256,256]{1,0:T(8,128)S(1)} %get-tuple-element.62), channel_id=1, source_target_pairs={{0,2},{1,5},{2,0},{3,7},{4,6},{5,1},{6,4},{7,3},{8,10},{9,13},{10,... | collective-permute-start | bytes 786440 | tf_op jit(solution)/shard_map/ppermute | solution.py:197
  20.8 8.3 %collective-permute-start.1 = (f32[256,256]{1,0:T(8,128)S(1)}, f32[256,256]{1,0:T(8,128)S(1)}, u32[]{:S(2)}, u32[]{:S(2)}) collective-permute-start(f32[256,256]{1,0:T(8,128)S(1)} %get-tuple-element.56), channel_id=1, source_target_pairs={{0,2},{1,5},{2,0},{3,7},{4,6},{5,1},{6,4},{7,3},{8,10},{9,13},{10,... | collective-permute-start | bytes 786440 | tf_op jit(solution)/shard_map/ppermute | solution.py:197
  25.6 5.1 %collective-permute-start.6 = (f32[128,256]{1,0:T(8,128)S(1)}, f32[128,256]{1,0:T(8,128)S(1)}, u32[]{:S(2)}, u32[]{:S(2)}) collective-permute-start(f32[128,256]{1,0:T(8,128)S(1)} %get-tuple-element.64), channel_id=1, source_target_pairs={{0,4},{1,3},{2,6},{3,1},{4,0},{5,7},{6,2},{7,5},{8,12},{9,11},{10,... | collective-permute-start | bytes 393224 | tf_op jit(solution)/shard_map/ppermute | solution.py:197
  29.1 6.3 %collective-permute-start.2 = (f32[128,256]{1,0:T(8,128)S(1)}, f32[128,256]{1,0:T(8,128)S(1)}, u32[]{:S(2)}, u32[]{:S(2)}) collective-permute-start(f32[128,256]{1,0:T(8,128)S(1)} %get-tuple-element.58), channel_id=1, source_target_pairs={{0,4},{1,3},{2,6},{3,1},{4,0},{5,7},{6,2},{7,5},{8,12},{9,11},{10,... | collective-permute-start | bytes 393224 | tf_op jit(solution)/shard_map/ppermute | solution.py:197
  30.8 12.5 %collective-permute-start.7 = (f32[128,256]{1,0:T(8,128)S(1)}, f32[128,256]{1,0:T(8,128)S(1)}, u32[]{:S(2)}, u32[]{:S(2)}) collective-permute-start(f32[128,256]{1,0:T(8,128)S(1)} %add.63), channel_id=1, source_target_pairs={{0,8},{1,9},{2,10},{3,11},{4,12},{5,13},{6,14},{7,15},{8,0},{9,1},... | collective-permute-start | bytes 393224 | tf_op jit(solution)/shard_map/ppermute | solution.py:197
  35.5 9.4 %collective-permute-start.3 = (f32[128,256]{1,0:T(8,128)S(1)}, f32[128,256]{1,0:T(8,128)S(1)}, u32[]{:S(2)}, u32[]{:S(2)}) collective-permute-start(f32[128,256]{1,0:T(8,128)S(1)} %add.61), channel_id=1, source_target_pairs={{0,8},{1,9},{2,10},{3,11},{4,12},{5,13},{6,14},{7,15},{8,0},{9,1},... | collective-permute-start | bytes 393224 | tf_op jit(solution)/shard_map/ppermute | solution.py:197
  38.2 36.9 %collective-permute-start.13 = (bf16[4096,128]{1,0:T(8,128)(2,1)}, bf16[4096,128]{1,0:T(8,128)(2,1)S(1)}, u32[]{:S(2)}, u32[]{:S(2)}) collective-permute-start(bf16[4096,128]{1,0:T(8,128)(2,1)} %get-tuple-element.49), channel_id=1, source_target_pairs={{0,16},{16,0},{1,17},{17,1},{2,18},{18,2},{3,19},{19,3},{4,20},{20... | collective-permute-start | bytes 3145736 | tf_op jit(solution)/shard_map/ppermute | solution.py:27
  44.9 18.3 %copy-start.4 = (bf16[3072,128]{1,0:T(8,128)(2,1)S(1)}, bf16[3072,128]{1,0:T(8,128)(2,1)}, u32[]{:S(2)}) copy-start(bf16[3072,128]{1,0:T(8,128)(2,1)} %get-tuple-element.81) | copy-start | bytes 2359300
  52.7 41.4 %slice-start = ((s8[8388608]{0:T(1024)(128)(4,1)}), s8[4194304]{0:T(1024)(128)(4,1)S(1)}, s32[]{:S(2)}) async-start(s8[8388608]{0:T(1024)(128)(4,1)} %bitcast.8), calls=%async_computation | async-start | bytes 8388608
  59.1 2.0 %collective-permute-start.9 = (f32[512,256]{1,0:T(8,128)S(1)}, f32[512,256]{1,0:T(8,128)S(1)}, u32[]{:S(2)}, u32[]{:S(2)}) collective-permute-start(f32[512,256]{1,0:T(8,128)S(1)} %get-tuple-element.67), channel_id=1, source_target_pairs={{0,1},{1,0},{2,3},{3,2},{4,5},{5,4},{6,7},{7,6},{8,9},{9,8},{10,11... | collective-permute-start | bytes 1572872 | tf_op jit(solution)/shard_map/ppermute | solution.py:197
  61.1 6.4 %collective-permute-start.10 = (f32[256,256]{1,0:T(8,128)S(1)}, f32[256,256]{1,0:T(8,128)S(1)}, u32[]{:S(2)}, u32[]{:S(2)}) collective-permute-start(f32[256,256]{1,0:T(8,128)S(1)} %get-tuple-element.69), channel_id=1, source_target_pairs={{0,2},{1,5},{2,0},{3,7},{4,6},{5,1},{6,4},{7,3},{8,10},{9,13},{10,... | collective-permute-start | bytes 786440 | tf_op jit(solution)/shard_map/ppermute | solution.py:197
  63.2 29.0 %collective-permute-start.19 = (bf16[3072,128]{1,0:T(8,128)(2,1)S(1)}, bf16[3072,128]{1,0:T(8,128)(2,1)S(1)}, u32[]{:S(2)}, u32[]{:S(2)}) collective-permute-start(bf16[3072,128]{1,0:T(8,128)(2,1)S(1)} %copy-done.4), channel_id=1, source_target_pairs={{0,16},{16,0},{1,17},{17,1},{2,18},{18,2},{3,19},{19,3},{4,20},{20... | collective-permute-start | bytes 2359304 | tf_op jit(solution)/shard_map/ppermute | solution.py:27
  67.6 26.6 %slice-start.1 = ((s8[8388608]{0:T(1024)(128)(4,1)}), s8[4194304]{0:T(1024)(128)(4,1)S(1)}, s32[]{:S(2)}) async-start(s8[8388608]{0:T(1024)(128)(4,1)} %bitcast.8), calls=%async_computation.1 | async-start | bytes 8388608
  67.6 5.1 %collective-permute-start.11 = (f32[128,256]{1,0:T(8,128)S(1)}, f32[128,256]{1,0:T(8,128)S(1)}, u32[]{:S(2)}, u32[]{:S(2)}) collective-permute-start(f32[128,256]{1,0:T(8,128)S(1)} %get-tuple-element.71), channel_id=1, source_target_pairs={{0,4},{1,3},{2,6},{3,1},{4,0},{5,7},{6,2},{7,5},{8,12},{9,11},{10,... | collective-permute-start | bytes 393224 | tf_op jit(solution)/shard_map/ppermute | solution.py:197
  72.7 8.1 %copy-start.5 = (bf16[1024,128]{1,0:T(8,128)(2,1)S(1)}, bf16[1024,128]{1,0:T(8,128)(2,1)}, u32[]{:S(2)}) copy-start(bf16[1024,128]{1,0:T(8,128)(2,1)} %get-tuple-element.80) | copy-start | bytes 786436
  80.8 4.8 %collective-permute-start.14 = (f32[512,128]{1,0:T(8,128)S(1)}, f32[512,128]{1,0:T(8,128)S(1)}, u32[]{:S(2)}, u32[]{:S(2)}) collective-permute-start(f32[512,128]{1,0:T(8,128)S(1)} %get-tuple-element.74), channel_id=1, source_target_pairs={{0,1},{1,0},{2,3},{3,2},{4,5},{5,4},{6,7},{7,6},{8,9},{9,8},{10,11... | collective-permute-start | bytes 786440 | tf_op jit(solution)/shard_map/ppermute | solution.py:197
  80.8 15.9 %collective-permute-start.18 = (bf16[1024,128]{1,0:T(8,128)(2,1)S(1)}, bf16[1024,128]{1,0:T(8,128)(2,1)S(1)}, u32[]{:S(2)}, u32[]{:S(2)}) collective-permute-start(bf16[1024,128]{1,0:T(8,128)(2,1)S(1)} %copy-done.5), channel_id=1, source_target_pairs={{0,16},{16,0},{1,17},{17,1},{2,18},{18,2},{3,19},{19,3},{4,20},{20... | collective-permute-start | bytes 786440 | tf_op jit(solution)/shard_map/ppermute | solution.py:27
  83.0 9.3 %collective-permute-start.12 = (f32[128,256]{1,0:T(8,128)S(1)}, f32[128,256]{1,0:T(8,128)S(1)}, u32[]{:S(2)}, u32[]{:S(2)}) collective-permute-start(f32[128,256]{1,0:T(8,128)S(1)} %add.65), channel_id=1, source_target_pairs={{0,8},{1,9},{2,10},{3,11},{4,12},{5,13},{6,14},{7,15},{8,0},{9,1},... | collective-permute-start | bytes 393224 | tf_op jit(solution)/shard_map/ppermute | solution.py:197
  85.6 6.7 %collective-permute-start.15 = (f32[256,128]{1,0:T(8,128)S(1)}, f32[256,128]{1,0:T(8,128)S(1)}, u32[]{:S(2)}, u32[]{:S(2)}) collective-permute-start(f32[256,128]{1,0:T(8,128)S(1)} %get-tuple-element.76), channel_id=1, source_target_pairs={{0,2},{1,5},{2,0},{3,7},{4,6},{5,1},{6,4},{7,3},{8,10},{9,13},{10,... | collective-permute-start | bytes 393224 | tf_op jit(solution)/shard_map/ppermute | solution.py:197
  92.3 4.3 %collective-permute-start.16 = (f32[128,128]{1,0:T(8,128)S(1)}, f32[128,128]{1,0:T(8,128)S(1)}, u32[]{:S(2)}, u32[]{:S(2)}) collective-permute-start(f32[128,128]{1,0:T(8,128)S(1)} %get-tuple-element.79), channel_id=1, source_target_pairs={{0,4},{1,3},{2,6},{3,1},{4,0},{5,7},{6,2},{7,5},{8,12},{9,11},{10,... | collective-permute-start | bytes 196616 | tf_op jit(solution)/shard_map/ppermute | solution.py:197
  96.7 0.9 copy-start
  96.7 0.9 copy-start.2
  96.7 5.6 %copy-start.6 = (s32[64]{0:T(128)S(1)}, s32[64]{0:T(128)}, u32[]{:S(2)}) copy-start(s32[64]{0:T(128)} %param.10) | copy-start | bytes 772
  96.7 10.7 %copy-start.1 = (s32[64,2]{0,1:T(2,128)S(1)}, s32[64,2]{0,1:T(2,128)}, u32[]{:S(2)}) copy-start(s32[64,2]{0,1:T(2,128)} %param.9) | copy-start | bytes 1540
  96.7 10.7 %copy-start.3 = (f32[96]{0:T(128)S(1)}, f32[96]{0:T(128)}, u32[]{:S(2)}) copy-start(f32[96]{0:T(128)} %param.12) | copy-start | bytes 1156
  97.5 3.2 %collective-permute-start.20 = (f32[512,128]{1,0:T(8,128)S(1)}, f32[512,128]{1,0:T(8,128)S(1)}, u32[]{:S(2)}, u32[]{:S(2)}) collective-permute-start(f32[512,128]{1,0:T(8,128)S(1)} %get-tuple-element.85), channel_id=1, source_target_pairs={{0,1},{1,0},{2,3},{3,2},{4,5},{5,4},{6,7},{7,6},{8,9},{9,8},{10,11... | collective-permute-start | bytes 786440 | tf_op jit(solution)/shard_map/ppermute | solution.py:197
  97.8 6.8 %collective-permute-start.17 = (f32[128,128]{1,0:T(8,128)S(1)}, f32[128,128]{1,0:T(8,128)S(1)}, u32[]{:S(2)}, u32[]{:S(2)}) collective-permute-start(f32[128,128]{1,0:T(8,128)S(1)} %add.67), channel_id=1, source_target_pairs={{0,8},{1,9},{2,10},{3,11},{4,12},{5,13},{6,14},{7,15},{8,0},{9,1},... | collective-permute-start | bytes 196616 | tf_op jit(solution)/shard_map/ppermute | solution.py:197
  100.7 5.0 %collective-permute-start.21 = (f32[256,128]{1,0:T(8,128)S(1)}, f32[256,128]{1,0:T(8,128)S(1)}, u32[]{:S(2)}, u32[]{:S(2)}) collective-permute-start(f32[256,128]{1,0:T(8,128)S(1)} %get-tuple-element.87), channel_id=1, source_target_pairs={{0,2},{1,5},{2,0},{3,7},{4,6},{5,1},{6,4},{7,3},{8,10},{9,13},{10,... | collective-permute-start | bytes 393224 | tf_op jit(solution)/shard_map/ppermute | solution.py:197
  105.7 4.3 %collective-permute-start.22 = (f32[128,128]{1,0:T(8,128)S(1)}, f32[128,128]{1,0:T(8,128)S(1)}, u32[]{:S(2)}, u32[]{:S(2)}) collective-permute-start(f32[128,128]{1,0:T(8,128)S(1)} %get-tuple-element.90), channel_id=1, source_target_pairs={{0,4},{1,3},{2,6},{3,1},{4,0},{5,7},{6,2},{7,5},{8,12},{9,11},{10,... | collective-permute-start | bytes 196616 | tf_op jit(solution)/shard_map/ppermute | solution.py:197
  110.1 5.2 %collective-permute-start.23 = (f32[128,128]{1,0:T(8,128)S(1)}, f32[128,128]{1,0:T(8,128)S(1)}, u32[]{:S(2)}, u32[]{:S(2)}) collective-permute-start(f32[128,128]{1,0:T(8,128)S(1)} %add.69.refs_4_), channel_id=1, source_target_pairs={{0,8},{1,9},{2,10},{3,11},{4,12},{5,13},{6,14},{7,15},{8,0},{9,1},... | collective-permute-start | bytes 196616 | tf_op jit(solution)/shard_map/ppermute | solution.py:197

commit v12 on v11

--- a/solution.py
+++ b/solution.py
@@ -9,6 +9,8 @@
 
 LANES = 128
 DEPTH_CUTS = 4
+DEPTH_PART = 1024
+LATE_GATE = 3
 ROW_CUTS = 1
 FREE = pl.CostEstimate(flops=0, bytes_accessed=0, transcendentals=0)
 OWN_SPLITS = 2
@@ -122,7 +124,7 @@
 
 def add_whole(a_ref, b_ref, total_ref, first, base_ref):
     depth = b_ref.shape[0]
-    part = a_ref.shape[1] // DEPTH_CUTS
+    part = min(depth, DEPTH_PART)
     for low in range(0, depth, part):
         term = jnp.dot(a_ref[:, first + low : first + low + part], b_ref[low : low + part, :], preferred_element_type=jnp.float32)
         if low > 0:
@@ -203,10 +205,10 @@
         keep, send = parts
         came = flipped_along(send, "virt", flips[level - 1])
         if level in gates:
-            came = after(came, gates[level])
+            came = after(came, gates[level](stages))
         parts = halved(keep, came, bits[level]) if level < len(bits) - 1 else [keep + came]
         stages.append(parts[0])
-    return (parts[0], flipped_along(parts[0], "virt", flips[-1])), stages
+    return parts[0], stages
 
 
 def cut_kernel(boxes, source_ref, *refs):
@@ -281,6 +283,10 @@
     )(where, local_rows.reshape(rows, 1), virt_sum.reshape(1, columns), occ_sum.reshape(rows, 1), *blocks)
 
 
+def both_halves(part, flips):
+    return part + flipped_along(part, "virt", flips[-1])
+
+
 def per_device(amplitudes, integrals, occ_pairs, partners, virt_list, eps_occ, eps_virt):
     width = virt_list.shape[0]
     count = lax.axis_size("pair")
@@ -313,25 +319,40 @@
     pieces = [first, *cut_out(rest, boxes)]
     in_flight = [sent(pieces[0]), sent(pieces[1])]
     own_product = multiplied(amplitudes, after(rest, pieces), bits[0], order, splits=OWN_SPLITS)
-    own_sums = [jnp.add(*exchanged_sum(own_product[2 * part : 2 * part + 2], bits, flips)[0]) for part in range(OWN_SPLITS)]
+    own_sums = [both_halves(exchanged_sum(own_product[2 * part : 2 * part + 2], bits, flips)[0], flips) for part in range(OWN_SPLITS)]
     sums = [own_sums] + [[] for _ in range(1, count)]
     in_flight += [sent(after(piece, own_sums)) for piece in pieces[2:]]
-    earlier, gates = own_sums, {}
+    later = after(amplitudes, own_product)
+    first_part, last_part = later[:, :late], later[:, late:]
+    earlier, gates = (own_sums, first_part, last_part), {}
     for step in range(len(pieces)):
         arrived, earlier = lax.optimization_barrier((in_flight[step], earlier))
         if step == len(pieces) - 2:
-            bases = [whole_plain(amplitudes, columns) for columns in arrived]
+            bases = [whole_plain(first_part, columns) for columns in arrived]
             earlier = (stages[2], bases)
             continue
         for shift in range(1, count):
             if step < len(cuts) - 1:
                 product = multiplied(amplitudes, arrived[shift - 1], bits[0], order)
             else:
-                product = whole_multiplied(amplitudes, arrived[shift - 1], bits[0], order, late, bases[shift - 1])
-            terms, stages = exchanged_sum(product, bits, flips, gates)
-            total = jnp.add(*terms)
-            sums[shift].append(total)
-            earlier, gates = stages[2] if step < len(cuts) - 2 else stages[0], {2: total}
+                product = whole_multiplied(last_part, arrived[shift - 1], bits[0], order, 0, bases[shift - 1])
+            part, stages = exchanged_sum(product, bits, flips, gates)
+            if step == 0 or (step < len(cuts) - 1 and shift < count - 1):
+                total = both_halves(part, flips)
+                sums[shift].append(total)
+                earlier, gates = stages[2], {2: lambda _, total=total: total}
+            elif step < len(cuts) - 1:
+
+                def finished(later, part=part, shift=shift):
+                    total = both_halves(after(part, later[0]), flips)
+                    sums[shift].append(total)
+                    return total
+
+                earlier, gates = stages[0], {LATE_GATE: finished}
+            else:
+                terms = part, flipped_along(part, "virt", flips[-1])
+                sums[shift].append(jnp.add(*terms))
+                gates = {}
 
     occ_ids = jnp.arange(eps_occ.shape[0], dtype=jnp.int32)
     occ_match = occ_pairs[:, :, None] == occ_ids[None, None, :]

time: 118 us -> 116 us (0.983)
  waiting for transfers between devices: 48.6 us -> 40.5 us
  local copies, waits for them, and re-layouts: 0.32 us -> 5.31 us
  starting transfers between devices: 36.5 us -> 38.2 us
    ppermute x20, waiting for transfers between devices: 38.4 us -> 30.1 us  [flipped_along(): lax.ppermute(value, axis, [(source, source ^ flip[source % 2]) for source...]
    slice x0 -> x2, local copies, waits for them, and re-layouts: none -> 4.99 us  [per_device(): first_part, last_part = (later[:, :late], later[:, late:])]
    ppermute x20, starting transfers between devices: 29.3 us -> 31 us  [flipped_along(): lax.ppermute(value, axis, [(source, source ^ flip[source % 2]) for source...]
  transfers between devices with their start and end apart: 24 -> 24, of which waited for: 17 -> 17; matrix products, arithmetic and copies ran while one was open for 1% -> 5% of each run, Pallas kernels for 22% -> 22%
where the time goes in v12:
time: 116 us
  waiting for transfers between devices  40.5 us (35%)
  starting transfers between devices  38.2 us (33%)
  Pallas kernels  30.9 us (27%)
  local copies, waits for them, and re-layouts  5.31 us (5%)
    ppermute x20, starting transfers between devices, flipped_along(): lax.ppermute(value, axis, [(source, source ^ flip[source % 2]) for source...  31 us
    ppermute x20, waiting for transfers between devices, flipped_along(): lax.ppermute(value, axis, [(source, source ^ flip[source % 2]) for source...  30.1 us
    pallas_call x3, Pallas kernels, multiplied(): pl.pallas_call(functools.partial(product_kernel, steps, order, splits, ba...  20 us
    ppermute x4, waiting for transfers between devices, passed_along(): return lax.ppermute(value, axis, pairs)  10.4 us
    ppermute x4, starting transfers between devices, passed_along(): return lax.ppermute(value, axis, pairs)  7.2 us
    pallas_call x2, Pallas kernels, cut_out(): pl.pallas_call(functools.partial(cut_kernel, boxes), out_shape=[jax.Shape...  5.83 us
    slice x2, local copies, waits for them, and re-layouts, per_device(): first_part, last_part = (later[:, :late], later[:, late:])  4.99 us
  transfers between devices with their start and end apart: 24, of which 17 were waited for; matrix products, arithmetic and copies ran while one was open for 5% of the time, Pallas kernels for 22%

profile of v12, /device:TPU:0, one launch (start us, length us, event | category | flops | bytes accessed | tf_op | source)
XLA Modules:
  0.0 115.9 jit_solution(17687391053004991461)
XLA Ops:
  0.0 2.9 %shard_map.73 = bf16[4096,256]{1,0:T(8,128)(2,1)} custom-call(bf16[4096,512]{1,0:T(8,128)(2,1)} %refs_1_), custom_call_target="tpu_custom_call" | custom-call | tf_op jit(solution)/shard_map/pallas_call | solution.py:231
  2.9 3.0 %collective-permute-start.8 = (bf16[4096,256]{1,0:T(8,128)(2,1)}, bf16[4096,256]{1,0:T(8,128)(2,1)}, u32[]{:S(2)}, u32[]{:S(2)}) collective-permute-start(bf16[4096,256]{1,0:T(8,128)(2,1)} %shard_map.73), channel_id=1, source_target_pairs={{0,16},{16,0},{1,17},{17,1},{2,18},{18,2},{3,19},{19,3},{4,20},{20... | collective-permute-start | bytes 6291464 | tf_op jit(solution)/shard_map/ppermute | solution.py:29
  5.9 2.9 %shard_map.74 = (bf16[4096,128]{1,0:T(8,128)(2,1)}, bf16[3072,128]{1,0:T(8,128)(2,1)}, bf16[1024,128]{1,0:T(8,128)(2,1)}) custom-call(bf16[4096,512]{1,0:T(8,128)(2,1)} %refs_1_), custom_call_target="tpu_custom_call" | custom-call | tf_op jit(solution)/shard_map/pallas_call | solution.py:231
  8.9 8.3 %shard_map.75 = (f32[512,256]{1,0:T(8,128)S(1)}, f32[512,256]{1,0:T(8,128)S(1)}, f32[512,256]{1,0:T(8,128)S(1)}, f32[512,256]{1,0:T(8,128)S(1)}) custom-call(s32[1]{0:T(128)} %bitcast.6.bit_ref, bf16[1024,4096]{1,0:T(8,128)(2,1)} %refs_0_.5, bf16[4096,512]{1,0:T(8,128)(2,1)} %refs_1_), custom_call_target="tpu_custom_call" | custom-call | tf_op jit(solution)/shard_map/pallas_call | solution.py:108
  17.2 0.5 collective-permute-start.4
  17.7 1.4 %collective-permute-done.came_ref = f32[512,256]{1,0:T(8,128)S(1)} collective-permute-done((f32[512,256]{1,0:T(8,128)S(1)}, f32[512,256]{1,0:T(8,128)S(1)}, u32[]{:S(2)}, u32[]{:S(2)}) %collective-permute-start) | collective-permute-done | bytes 524320 | tf_op jit(solution)/shard_map/ppermute | solution.py:199
  19.2 1.6 %collective-permute-start.1 = (f32[256,256]{1,0:T(8,128)S(1)}, f32[256,256]{1,0:T(8,128)S(1)}, u32[]{:S(2)}, u32[]{:S(2)}) collective-permute-start(f32[256,256]{1,0:T(8,128)S(1)} %get-tuple-element.58), channel_id=1, source_target_pairs={{0,2},{1,5},{2,0},{3,7},{4,6},{5,1},{6,4},{7,3},{8,10},{9,13},{10,... | collective-permute-start | bytes 786440 | tf_op jit(solution)/shard_map/ppermute | solution.py:199
  20.8 0.7 collective-permute-start.5
  21.5 4.1 %collective-permute-done.1.came_ref = f32[256,256]{1,0:T(8,128)S(1)} collective-permute-done((f32[256,256]{1,0:T(8,128)S(1)}, f32[256,256]{1,0:T(8,128)S(1)}, u32[]{:S(2)}, u32[]{:S(2)}) %collective-permute-start.1) | collective-permute-done | bytes 262176 | tf_op jit(solution)/shard_map/ppermute | solution.py:199
  25.6 1.6 %collective-permute-start.2 = (f32[128,256]{1,0:T(8,128)S(1)}, f32[128,256]{1,0:T(8,128)S(1)}, u32[]{:S(2)}, u32[]{:S(2)}) collective-permute-start(f32[128,256]{1,0:T(8,128)S(1)} %get-tuple-element.60), channel_id=1, source_target_pairs={{0,4},{1,3},{2,6},{3,1},{4,0},{5,7},{6,2},{7,5},{8,12},{9,11},{10,... | collective-permute-start | bytes 393224 | tf_op jit(solution)/shard_map/ppermute | solution.py:199
  27.3 1.8 %collective-permute-done.5.came_ref = f32[256,256]{1,0:T(8,128)S(1)} collective-permute-done((f32[256,256]{1,0:T(8,128)S(1)}, f32[256,256]{1,0:T(8,128)S(1)}, u32[]{:S(2)}, u32[]{:S(2)}) %collective-permute-start.5) | collective-permute-done | bytes 262176 | tf_op jit(solution)/shard_map/ppermute | solution.py:199
  29.1 1.6 %collective-permute-start.6 = (f32[128,256]{1,0:T(8,128)S(1)}, f32[128,256]{1,0:T(8,128)S(1)}, u32[]{:S(2)}, u32[]{:S(2)}) collective-permute-start(f32[128,256]{1,0:T(8,128)S(1)} %get-tuple-element.66), channel_id=1, source_target_pairs={{0,4},{1,3},{2,6},{3,1},{4,0},{5,7},{6,2},{7,5},{8,12},{9,11},{10,... | collective-permute-start | bytes 393224 | tf_op jit(solution)/shard_map/ppermute | solution.py:199
  30.8 2.7 %collective-permute-start.3 = (f32[128,256]{1,0:T(8,128)S(1)}, f32[128,256]{1,0:T(8,128)S(1)}, u32[]{:S(2)}, u32[]{:S(2)}) collective-permute-start(f32[128,256]{1,0:T(8,128)S(1)} %add.61), channel_id=1, source_target_pairs={{0,8},{1,9},{2,10},{3,11},{4,12},{5,13},{6,14},{7,15},{8,0},{9,1},... | collective-permute-start | bytes 393224 | tf_op jit(solution)/shard_map/ppermute | solution.py:199
  33.4 2.0 %collective-permute-done.6 = f32[128,256]{1,0:T(8,128)S(1)} collective-permute-done((f32[128,256]{1,0:T(8,128)S(1)}, f32[128,256]{1,0:T(8,128)S(1)}, u32[]{:S(2)}, u32[]{:S(2)}) %collective-permute-start.6) | collective-permute-done | bytes 131104 | tf_op jit(solution)/shard_map/ppermute | solution.py:199
  35.5 2.7 %collective-permute-start.7 = (f32[128,256]{1,0:T(8,128)S(1)}, f32[128,256]{1,0:T(8,128)S(1)}, u32[]{:S(2)}, u32[]{:S(2)}) collective-permute-start(f32[128,256]{1,0:T(8,128)S(1)} %add.63), channel_id=1, source_target_pairs={{0,8},{1,9},{2,10},{3,11},{4,12},{5,13},{6,14},{7,15},{8,0},{9,1},... | collective-permute-start | bytes 393224 | tf_op jit(solution)/shard_map/ppermute | solution.py:199
  38.2 0.5 collective-permute-start.13
  38.8 1.8 %slice.7.a_ref = bf16[1024,1024]{1,0:T(8,128)(2,1)S(1)} slice(bf16[1024,4096]{1,0:T(8,128)(2,1)} %refs_0_.5), slice={[0:1024], [3072:4096]} | slice | bytes 4194304 | tf_op jit(solution)/shard_map/slice | solution.py:326
  40.5 3.2 %slice.6.a_ref = bf16[1024,3072]{1,0:T(8,128)(2,1)S(1)} slice(bf16[1024,4096]{1,0:T(8,128)(2,1)} %refs_0_.5), slice={[0:1024], [0:3072]} | slice | bytes 12582912 | tf_op jit(solution)/shard_map/slice | solution.py:326
  43.8 1.1 collective-permute-done.7
  44.9 7.8 %collective-permute-done.8.refs_1_ = bf16[4096,256]{1,0:T(8,128)(2,1)} collective-permute-done((bf16[4096,256]{1,0:T(8,128)(2,1)}, bf16[4096,256]{1,0:T(8,128)(2,1)}, u32[]{:S(2)}, u32[]{:S(2)}) %collective-permute-start.8) | collective-permute-done | bytes 2097184 | tf_op jit(solution)/shard_map/ppermute | solution.py:29
  52.7 6.1 %shard_map.80 = (f32[512,256]{1,0:T(8,128)S(1)}, f32[512,256]{1,0:T(8,128)S(1)}) custom-call(s32[1]{0:T(128)} %bitcast.6.bit_ref, bf16[1024,4096]{1,0:T(8,128)(2,1)} %refs_0_.5, bf16[4096,256]{1,0:T(8,128)(2,1)} %collective-permute-done.8.refs_1_), custom_call_target="tpu_custom_call" | custom-call | flops 2147483648 | bytes 8388608 | tf_op jit(solution)/shard_map/pallas_call | solution.py:108
  58.9 1.9 %collective-permute-done.9.came_ref = f32[512,256]{1,0:T(8,128)S(1)} collective-permute-done((f32[512,256]{1,0:T(8,128)S(1)}, f32[512,256]{1,0:T(8,128)S(1)}, u32[]{:S(2)}, u32[]{:S(2)}) %collective-permute-start.9) | collective-permute-done | bytes 524320 | tf_op jit(solution)/shard_map/ppermute | solution.py:199
  60.8 2.1 %collective-permute-start.10 = (f32[256,256]{1,0:T(8,128)S(1)}, f32[256,256]{1,0:T(8,128)S(1)}, u32[]{:S(2)}, u32[]{:S(2)}) collective-permute-start(f32[256,256]{1,0:T(8,128)S(1)} %get-tuple-element.72), channel_id=1, source_target_pairs={{0,2},{1,5},{2,0},{3,7},{4,6},{5,1},{6,4},{7,3},{8,10},{9,13},{10,... | collective-permute-start | bytes 786440 | tf_op jit(solution)/shard_map/ppermute | solution.py:199
  62.9 1.5 %collective-permute-start.18 = (bf16[3072,128]{1,0:T(8,128)(2,1)S(1)}, bf16[3072,128]{1,0:T(8,128)(2,1)S(1)}, u32[]{:S(2)}, u32[]{:S(2)}) collective-permute-start(bf16[3072,128]{1,0:T(8,128)(2,1)S(1)} %copy-done.4), channel_id=1, source_target_pairs={{0,16},{16,0},{1,17},{17,1},{2,18},{18,2},{3,19},{19,3},{4,20},{20... | collective-permute-start | bytes 2359304 | tf_op jit(solution)/shard_map/ppermute | solution.py:29
  64.5 2.8 %collective-permute-done.10.came_ref = f32[256,256]{1,0:T(8,128)S(1)} collective-permute-done((f32[256,256]{1,0:T(8,128)S(1)}, f32[256,256]{1,0:T(8,128)S(1)}, u32[]{:S(2)}, u32[]{:S(2)}) %collective-permute-start.10) | collective-permute-done | bytes 262176 | tf_op jit(solution)/shard_map/ppermute | solution.py:199
  67.3 2.2 %collective-permute-start.11 = (f32[128,256]{1,0:T(8,128)S(1)}, f32[128,256]{1,0:T(8,128)S(1)}, u32[]{:S(2)}, u32[]{:S(2)}) collective-permute-start(f32[128,256]{1,0:T(8,128)S(1)} %get-tuple-element.74), channel_id=1, source_target_pairs={{0,4},{1,3},{2,6},{3,1},{4,0},{5,7},{6,2},{7,5},{8,12},{9,11},{10,... | collective-permute-start | bytes 393224 | tf_op jit(solution)/shard_map/ppermute | solution.py:199
  69.5 2.9 %collective-permute-done.11 = f32[128,256]{1,0:T(8,128)S(1)} collective-permute-done((f32[128,256]{1,0:T(8,128)S(1)}, f32[128,256]{1,0:T(8,128)S(1)}, u32[]{:S(2)}, u32[]{:S(2)}) %collective-permute-start.11) | collective-permute-done | bytes 131104 | tf_op jit(solution)/shard_map/ppermute | solution.py:199
  72.5 2.6 %collective-permute-done.13.refs_1_ = bf16[4096,128]{1,0:T(8,128)(2,1)S(1)} collective-permute-done((bf16[4096,128]{1,0:T(8,128)(2,1)}, bf16[4096,128]{1,0:T(8,128)(2,1)S(1)}, u32[]{:S(2)}, u32[]{:S(2)}) %collective-permute-start.13) | collective-permute-done | bytes 1048608 | tf_op jit(solution)/shard_map/ppermute | solution.py:29
  75.1 5.7 %shard_map.83 = (f32[512,128]{1,0:T(8,128)S(1)}, f32[512,128]{1,0:T(8,128)S(1)}) custom-call(s32[1]{0:T(128)} %bitcast.6.bit_ref, bf16[1024,4096]{1,0:T(8,128)(2,1)} %refs_0_.5, bf16[4096,128]{1,0:T(8,128)(2,1)S(1)} %collective-permute-done.13.refs_1_), custom_call_target="tpu_custom_call" | custom-call | flops 1073741824 | bytes 8388608 | tf_op jit(solution)/shard_map/pallas_call | solution.py:108
  80.9 2.1 %collective-permute-start.17 = (bf16[1024,128]{1,0:T(8,128)(2,1)S(1)}, bf16[1024,128]{1,0:T(8,128)(2,1)S(1)}, u32[]{:S(2)}, u32[]{:S(2)}) collective-permute-start(bf16[1024,128]{1,0:T(8,128)(2,1)S(1)} %copy-done.5), channel_id=1, source_target_pairs={{0,16},{16,0},{1,17},{17,1},{2,18},{18,2},{3,19},{19,3},{4,20},{20... | collective-permute-start | bytes 786440 | tf_op jit(solution)/shard_map/ppermute | solution.py:29
  83.0 2.6 %collective-permute-start.12 = (f32[128,256]{1,0:T(8,128)S(1)}, f32[128,256]{1,0:T(8,128)S(1)}, u32[]{:S(2)}, u32[]{:S(2)}) collective-permute-start(f32[128,256]{1,0:T(8,128)S(1)} %add.65), channel_id=1, source_target_pairs={{0,8},{1,9},{2,10},{3,11},{4,12},{5,13},{6,14},{7,15},{8,0},{9,1},... | collective-permute-start | bytes 393224 | tf_op jit(solution)/shard_map/ppermute | solution.py:199
  85.6 1.6 %collective-permute-start.15 = (f32[256,128]{1,0:T(8,128)S(1)}, f32[256,128]{1,0:T(8,128)S(1)}, u32[]{:S(2)}, u32[]{:S(2)}) collective-permute-start(f32[256,128]{1,0:T(8,128)S(1)} %get-tuple-element.79), channel_id=1, source_target_pairs={{0,2},{1,5},{2,0},{3,7},{4,6},{5,1},{6,4},{7,3},{8,10},{9,13},{10,... | collective-permute-start | bytes 393224 | tf_op jit(solution)/shard_map/ppermute | solution.py:199
  87.2 5.1 %collective-permute-done.12 = f32[128,256]{1,0:T(8,128)S(1)} collective-permute-done((f32[128,256]{1,0:T(8,128)S(1)}, f32[128,256]{1,0:T(8,128)S(1)}, u32[]{:S(2)}, u32[]{:S(2)}) %collective-permute-start.12) | collective-permute-done | bytes 131104 | tf_op jit(solution)/shard_map/ppermute | solution.py:199
  92.4 1.8 %collective-permute-start.16 = (f32[128,128]{1,0:T(8,128)S(1)}, f32[128,128]{1,0:T(8,128)S(1)}, u32[]{:S(2)}, u32[]{:S(2)}) collective-permute-start(f32[128,128]{1,0:T(8,128)S(1)} %get-tuple-element.82), channel_id=1, source_target_pairs={{0,4},{1,3},{2,6},{3,1},{4,0},{5,7},{6,2},{7,5},{8,12},{9,11},{10,... | collective-permute-start | bytes 196616 | tf_op jit(solution)/shard_map/ppermute | solution.py:199
  94.2 1.8 %shard_map.86.refs_0_ = f32[1024,128]{1,0:T(8,128)S(1)} custom-call(bf16[1024,3072]{1,0:T(8,128)(2,1)S(1)} %slice.6.a_ref, bf16[3072,128]{1,0:T(8,128)(2,1)S(1)} %collective-permute-done.18.b_ref), custom_call_target="tpu_custom_call" | custom-call | flops 805306368 | bytes 6291456 | tf_op jit(solution)/shard_map/pallas_call | solution.py:167
  96.0 0.7 collective-permute-done.16
  96.7 0.7 shard_map.87
  97.6 0.2 select_reduce_fusion.1
  97.9 1.2 collective-permute-done.19.came_ref
  99.1 1.8 %collective-permute-start.21 = (f32[256,128]{1,0:T(8,128)S(1)}, f32[256,128]{1,0:T(8,128)S(1)}, u32[]{:S(2)}, u32[]{:S(2)}) collective-permute-start(f32[256,128]{1,0:T(8,128)S(1)} %get-tuple-element.91), channel_id=1, source_target_pairs={{0,2},{1,5},{2,0},{3,7},{4,6},{5,1},{6,4},{7,3},{8,10},{9,13},{10,... | collective-permute-start | bytes 393224 | tf_op jit(solution)/shard_map/ppermute | solution.py:199
  101.0 2.6 %collective-permute-start.20 = (f32[128,128]{1,0:T(8,128)S(1)}, f32[128,128]{1,0:T(8,128)S(1)}, u32[]{:S(2)}, u32[]{:S(2)}) collective-permute-start(f32[128,128]{1,0:T(8,128)S(1)} %add.67), channel_id=1, source_target_pairs={{0,8},{1,9},{2,10},{3,11},{4,12},{5,13},{6,14},{7,15},{8,0},{9,1},... | collective-permute-start | bytes 196616 | tf_op jit(solution)/shard_map/ppermute | solution.py:199
  103.6 0.5 collective-permute-done.21.came_ref
  104.2 1.9 %collective-permute-start.22 = (f32[128,128]{1,0:T(8,128)S(1)}, f32[128,128]{1,0:T(8,128)S(1)}, u32[]{:S(2)}, u32[]{:S(2)}) collective-permute-start(f32[128,128]{1,0:T(8,128)S(1)} %get-tuple-element.93), channel_id=1, source_target_pairs={{0,4},{1,3},{2,6},{3,1},{4,0},{5,7},{6,2},{7,5},{8,12},{9,11},{10,... | collective-permute-start | bytes 196616 | tf_op jit(solution)/shard_map/ppermute | solution.py:199
  106.3 1.3 %collective-permute-done.20 = f32[128,128]{1,0:T(8,128)S(1)} collective-permute-done((f32[128,128]{1,0:T(8,128)S(1)}, f32[128,128]{1,0:T(8,128)S(1)}, u32[]{:S(2)}, u32[]{:S(2)}) %collective-permute-start.20) | collective-permute-done | bytes 65568 | tf_op jit(solution)/shard_map/ppermute | solution.py:199
  107.6 0.9 collective-permute-done.22
  108.5 2.9 %collective-permute-start.23 = (f32[128,128]{1,0:T(8,128)S(1)}, f32[128,128]{1,0:T(8,128)S(1)}, u32[]{:S(2)}, u32[]{:S(2)}) collective-permute-start(f32[128,128]{1,0:T(8,128)S(1)} %add.69.refs_4_), channel_id=1, source_target_pairs={{0,8},{1,9},{2,10},{3,11},{4,12},{5,13},{6,14},{7,15},{8,0},{9,1},... | collective-permute-start | bytes 196616 | tf_op jit(solution)/shard_map/ppermute | solution.py:199
  111.5 2.3 %collective-permute-done.23.refs_5_ = f32[128,128]{1,0:T(8,128)S(1)} collective-permute-done((f32[128,128]{1,0:T(8,128)S(1)}, f32[128,128]{1,0:T(8,128)S(1)}, u32[]{:S(2)}, u32[]{:S(2)}) %collective-permute-start.23) | collective-permute-done | bytes 65568 | tf_op jit(solution)/shard_map/ppermute | solution.py:199
  113.7 2.2 %shard_map.90 = f32[64,1024]{1,0:T(8,128)} custom-call(s32[2]{0:T(128)S(1)} %pad_add_fusion.where_ref, s32[64,1]{1,0:T(8,128)S(1)} %copy.11.rows_ref, f32[1,1024]{1,0:T(1,128)S(1)} %add.60.virt_ref, f32[64,1]{1,0:T(8,128)S(1)} %copy.12.occ_ref, f32[128,256]{1,0:T(8,128)S(1)} %add.62.refs_0_, f32[128,256]{1,0:T(8,128)S(1)} %add.64.refs_1_, ...), custom_call_target="tpu_custom_call" | custom-call | tf_op jit(solution)/shard_map/pallas_call | solution.py:271
  (51 shorter events, 1.4 us)
Async XLA Ops:
  2.9 49.8 %collective-permute-start.8 = (bf16[4096,256]{1,0:T(8,128)(2,1)}, bf16[4096,256]{1,0:T(8,128)(2,1)}, u32[]{:S(2)}, u32[]{:S(2)}) collective-permute-start(bf16[4096,256]{1,0:T(8,128)(2,1)} %shard_map.73), channel_id=1, source_target_pairs={{0,16},{16,0},{1,17},{17,1},{2,18},{18,2},{3,19},{19,3},{4,20},{20... | collective-permute-start | bytes 6291464 | tf_op jit(solution)/shard_map/ppermute | solution.py:29
  17.1 2.0 %collective-permute-start = (f32[512,256]{1,0:T(8,128)S(1)}, f32[512,256]{1,0:T(8,128)S(1)}, u32[]{:S(2)}, u32[]{:S(2)}) collective-permute-start(f32[512,256]{1,0:T(8,128)S(1)} %get-tuple-element.56), channel_id=1, source_target_pairs={{0,1},{1,0},{2,3},{3,2},{4,5},{5,4},{6,7},{7,6},{8,9},{9,8},{10,11... | collective-permute-start | bytes 1572872 | tf_op jit(solution)/shard_map/ppermute | solution.py:199
  17.2 3.5 %collective-permute-start.4 = (f32[512,256]{1,0:T(8,128)S(1)}, f32[512,256]{1,0:T(8,128)S(1)}, u32[]{:S(2)}, u32[]{:S(2)}) collective-permute-start(f32[512,256]{1,0:T(8,128)S(1)} %get-tuple-element.62), channel_id=1, source_target_pairs={{0,1},{1,0},{2,3},{3,2},{4,5},{5,4},{6,7},{7,6},{8,9},{9,8},{10,11... | collective-permute-start | bytes 1572872 | tf_op jit(solution)/shard_map/ppermute | solution.py:199
  19.2 6.4 %collective-permute-start.1 = (f32[256,256]{1,0:T(8,128)S(1)}, f32[256,256]{1,0:T(8,128)S(1)}, u32[]{:S(2)}, u32[]{:S(2)}) collective-permute-start(f32[256,256]{1,0:T(8,128)S(1)} %get-tuple-element.58), channel_id=1, source_target_pairs={{0,2},{1,5},{2,0},{3,7},{4,6},{5,1},{6,4},{7,3},{8,10},{9,13},{10,... | collective-permute-start | bytes 786440 | tf_op jit(solution)/shard_map/ppermute | solution.py:199
  20.8 8.3 %collective-permute-start.5 = (f32[256,256]{1,0:T(8,128)S(1)}, f32[256,256]{1,0:T(8,128)S(1)}, u32[]{:S(2)}, u32[]{:S(2)}) collective-permute-start(f32[256,256]{1,0:T(8,128)S(1)} %get-tuple-element.64), channel_id=1, source_target_pairs={{0,2},{1,5},{2,0},{3,7},{4,6},{5,1},{6,4},{7,3},{8,10},{9,13},{10,... | collective-permute-start | bytes 786440 | tf_op jit(solution)/shard_map/ppermute | solution.py:199
  25.6 5.1 %collective-permute-start.2 = (f32[128,256]{1,0:T(8,128)S(1)}, f32[128,256]{1,0:T(8,128)S(1)}, u32[]{:S(2)}, u32[]{:S(2)}) collective-permute-start(f32[128,256]{1,0:T(8,128)S(1)} %get-tuple-element.60), channel_id=1, source_target_pairs={{0,4},{1,3},{2,6},{3,1},{4,0},{5,7},{6,2},{7,5},{8,12},{9,11},{10,... | collective-permute-start | bytes 393224 | tf_op jit(solution)/shard_map/ppermute | solution.py:199
  29.1 6.3 %collective-permute-start.6 = (f32[128,256]{1,0:T(8,128)S(1)}, f32[128,256]{1,0:T(8,128)S(1)}, u32[]{:S(2)}, u32[]{:S(2)}) collective-permute-start(f32[128,256]{1,0:T(8,128)S(1)} %get-tuple-element.66), channel_id=1, source_target_pairs={{0,4},{1,3},{2,6},{3,1},{4,0},{5,7},{6,2},{7,5},{8,12},{9,11},{10,... | collective-permute-start | bytes 393224 | tf_op jit(solution)/shard_map/ppermute | solution.py:199
  30.8 13.0 %collective-permute-start.3 = (f32[128,256]{1,0:T(8,128)S(1)}, f32[128,256]{1,0:T(8,128)S(1)}, u32[]{:S(2)}, u32[]{:S(2)}) collective-permute-start(f32[128,256]{1,0:T(8,128)S(1)} %add.61), channel_id=1, source_target_pairs={{0,8},{1,9},{2,10},{3,11},{4,12},{5,13},{6,14},{7,15},{8,0},{9,1},... | collective-permute-start | bytes 393224 | tf_op jit(solution)/shard_map/ppermute | solution.py:199
  35.5 9.4 %collective-permute-start.7 = (f32[128,256]{1,0:T(8,128)S(1)}, f32[128,256]{1,0:T(8,128)S(1)}, u32[]{:S(2)}, u32[]{:S(2)}) collective-permute-start(f32[128,256]{1,0:T(8,128)S(1)} %add.63), channel_id=1, source_target_pairs={{0,8},{1,9},{2,10},{3,11},{4,12},{5,13},{6,14},{7,15},{8,0},{9,1},... | collective-permute-start | bytes 393224 | tf_op jit(solution)/shard_map/ppermute | solution.py:199
  38.2 36.9 %collective-permute-start.13 = (bf16[4096,128]{1,0:T(8,128)(2,1)}, bf16[4096,128]{1,0:T(8,128)(2,1)S(1)}, u32[]{:S(2)}, u32[]{:S(2)}) collective-permute-start(bf16[4096,128]{1,0:T(8,128)(2,1)} %get-tuple-element.51), channel_id=1, source_target_pairs={{0,16},{16,0},{1,17},{17,1},{2,18},{18,2},{3,19},{19,3},{4,20},{20... | collective-permute-start | bytes 3145736 | tf_op jit(solution)/shard_map/ppermute | solution.py:29
  44.9 18.0 %copy-start.4 = (bf16[3072,128]{1,0:T(8,128)(2,1)S(1)}, bf16[3072,128]{1,0:T(8,128)(2,1)}, u32[]{:S(2)}) copy-start(bf16[3072,128]{1,0:T(8,128)(2,1)} %get-tuple-element.84) | copy-start | bytes 2359300
  58.8 2.0 %collective-permute-start.9 = (f32[512,256]{1,0:T(8,128)S(1)}, f32[512,256]{1,0:T(8,128)S(1)}, u32[]{:S(2)}, u32[]{:S(2)}) collective-permute-start(f32[512,256]{1,0:T(8,128)S(1)} %get-tuple-element.70), channel_id=1, source_target_pairs={{0,1},{1,0},{2,3},{3,2},{4,5},{5,4},{6,7},{7,6},{8,9},{9,8},{10,11... | collective-permute-start | bytes 1572872 | tf_op jit(solution)/shard_map/ppermute | solution.py:199
  60.8 6.4 %collective-permute-start.10 = (f32[256,256]{1,0:T(8,128)S(1)}, f32[256,256]{1,0:T(8,128)S(1)}, u32[]{:S(2)}, u32[]{:S(2)}) collective-permute-start(f32[256,256]{1,0:T(8,128)S(1)} %get-tuple-element.72), channel_id=1, source_target_pairs={{0,2},{1,5},{2,0},{3,7},{4,6},{5,1},{6,4},{7,3},{8,10},{9,13},{10,... | collective-permute-start | bytes 786440 | tf_op jit(solution)/shard_map/ppermute | solution.py:199
  62.9 29.3 %collective-permute-start.18 = (bf16[3072,128]{1,0:T(8,128)(2,1)S(1)}, bf16[3072,128]{1,0:T(8,128)(2,1)S(1)}, u32[]{:S(2)}, u32[]{:S(2)}) collective-permute-start(bf16[3072,128]{1,0:T(8,128)(2,1)S(1)} %copy-done.4), channel_id=1, source_target_pairs={{0,16},{16,0},{1,17},{17,1},{2,18},{18,2},{3,19},{19,3},{4,20},{20... | collective-permute-start | bytes 2359304 | tf_op jit(solution)/shard_map/ppermute | solution.py:29
  67.3 5.1 %collective-permute-start.11 = (f32[128,256]{1,0:T(8,128)S(1)}, f32[128,256]{1,0:T(8,128)S(1)}, u32[]{:S(2)}, u32[]{:S(2)}) collective-permute-start(f32[128,256]{1,0:T(8,128)S(1)} %get-tuple-element.74), channel_id=1, source_target_pairs={{0,4},{1,3},{2,6},{3,1},{4,0},{5,7},{6,2},{7,5},{8,12},{9,11},{10,... | collective-permute-start | bytes 393224 | tf_op jit(solution)/shard_map/ppermute | solution.py:199
  72.5 8.4 %copy-start.5 = (bf16[1024,128]{1,0:T(8,128)(2,1)S(1)}, bf16[1024,128]{1,0:T(8,128)(2,1)}, u32[]{:S(2)}) copy-start(bf16[1024,128]{1,0:T(8,128)(2,1)} %get-tuple-element.83) | copy-start | bytes 786436
  80.8 4.8 %collective-permute-start.14 = (f32[512,128]{1,0:T(8,128)S(1)}, f32[512,128]{1,0:T(8,128)S(1)}, u32[]{:S(2)}, u32[]{:S(2)}) collective-permute-start(f32[512,128]{1,0:T(8,128)S(1)} %get-tuple-element.77), channel_id=1, source_target_pairs={{0,1},{1,0},{2,3},{3,2},{4,5},{5,4},{6,7},{7,6},{8,9},{9,8},{10,11... | collective-permute-start | bytes 786440 | tf_op jit(solution)/shard_map/ppermute | solution.py:199
  80.9 15.9 %collective-permute-start.17 = (bf16[1024,128]{1,0:T(8,128)(2,1)S(1)}, bf16[1024,128]{1,0:T(8,128)(2,1)S(1)}, u32[]{:S(2)}, u32[]{:S(2)}) collective-permute-start(bf16[1024,128]{1,0:T(8,128)(2,1)S(1)} %copy-done.5), channel_id=1, source_target_pairs={{0,16},{16,0},{1,17},{17,1},{2,18},{18,2},{3,19},{19,3},{4,20},{20... | collective-permute-start | bytes 786440 | tf_op jit(solution)/shard_map/ppermute | solution.py:29
  83.0 9.3 %collective-permute-start.12 = (f32[128,256]{1,0:T(8,128)S(1)}, f32[128,256]{1,0:T(8,128)S(1)}, u32[]{:S(2)}, u32[]{:S(2)}) collective-permute-start(f32[128,256]{1,0:T(8,128)S(1)} %add.65), channel_id=1, source_target_pairs={{0,8},{1,9},{2,10},{3,11},{4,12},{5,13},{6,14},{7,15},{8,0},{9,1},... | collective-permute-start | bytes 393224 | tf_op jit(solution)/shard_map/ppermute | solution.py:199
  85.6 6.7 %collective-permute-start.15 = (f32[256,128]{1,0:T(8,128)S(1)}, f32[256,128]{1,0:T(8,128)S(1)}, u32[]{:S(2)}, u32[]{:S(2)}) collective-permute-start(f32[256,128]{1,0:T(8,128)S(1)} %get-tuple-element.79), channel_id=1, source_target_pairs={{0,2},{1,5},{2,0},{3,7},{4,6},{5,1},{6,4},{7,3},{8,10},{9,13},{10,... | collective-permute-start | bytes 393224 | tf_op jit(solution)/shard_map/ppermute | solution.py:199
  92.3 5.3 %copy-start = (f32[512]{0:T(512)S(1)}, f32[512]{0:T(512)}, u32[]{:S(2)}) copy-start(f32[512]{0:T(512)} %param.13) | copy-start | bytes 6148
  92.3 5.3 %copy-start.2 = (s32[32]{0:T(128)S(1)}, s32[32]{0:T(128)}, u32[]{:S(2)}) copy-start(s32[32]{0:T(128)} %param.11) | copy-start | bytes 388
  92.3 8.6 %copy-start.6 = (s32[64]{0:T(128)S(1)}, s32[64]{0:T(128)}, u32[]{:S(2)}) copy-start(s32[64]{0:T(128)} %param.10) | copy-start | bytes 772
  92.3 13.7 %copy-start.1 = (s32[64,2]{0,1:T(2,128)S(1)}, s32[64,2]{0,1:T(2,128)}, u32[]{:S(2)}) copy-start(s32[64,2]{0,1:T(2,128)} %param.9) | copy-start | bytes 1540
  92.4 13.7 %copy-start.3 = (f32[96]{0:T(128)S(1)}, f32[96]{0:T(128)}, u32[]{:S(2)}) copy-start(f32[96]{0:T(128)} %param.12) | copy-start | bytes 1156
  92.4 4.3 %collective-permute-start.16 = (f32[128,128]{1,0:T(8,128)S(1)}, f32[128,128]{1,0:T(8,128)S(1)}, u32[]{:S(2)}, u32[]{:S(2)}) collective-permute-start(f32[128,128]{1,0:T(8,128)S(1)} %get-tuple-element.82), channel_id=1, source_target_pairs={{0,4},{1,3},{2,6},{3,1},{4,0},{5,7},{6,2},{7,5},{8,12},{9,11},{10,... | collective-permute-start | bytes 196616 | tf_op jit(solution)/shard_map/ppermute | solution.py:199
  97.5 1.6 %collective-permute-start.19 = (f32[512,128]{1,0:T(8,128)S(1)}, f32[512,128]{1,0:T(8,128)S(1)}, u32[]{:S(2)}, u32[]{:S(2)}) collective-permute-start(f32[512,128]{1,0:T(8,128)S(1)} %get-tuple-element.88), channel_id=1, source_target_pairs={{0,1},{1,0},{2,3},{3,2},{4,5},{5,4},{6,7},{7,6},{8,9},{9,8},{10,11... | collective-permute-start | bytes 786440 | tf_op jit(solution)/shard_map/ppermute | solution.py:199
  99.1 5.0 %collective-permute-start.21 = (f32[256,128]{1,0:T(8,128)S(1)}, f32[256,128]{1,0:T(8,128)S(1)}, u32[]{:S(2)}, u32[]{:S(2)}) collective-permute-start(f32[256,128]{1,0:T(8,128)S(1)} %get-tuple-element.91), channel_id=1, source_target_pairs={{0,2},{1,5},{2,0},{3,7},{4,6},{5,1},{6,4},{7,3},{8,10},{9,13},{10,... | collective-permute-start | bytes 393224 | tf_op jit(solution)/shard_map/ppermute | solution.py:199
  101.0 6.6 %collective-permute-start.20 = (f32[128,128]{1,0:T(8,128)S(1)}, f32[128,128]{1,0:T(8,128)S(1)}, u32[]{:S(2)}, u32[]{:S(2)}) collective-permute-start(f32[128,128]{1,0:T(8,128)S(1)} %add.67), channel_id=1, source_target_pairs={{0,8},{1,9},{2,10},{3,11},{4,12},{5,13},{6,14},{7,15},{8,0},{9,1},... | collective-permute-start | bytes 196616 | tf_op jit(solution)/shard_map/ppermute | solution.py:199
  104.2 4.3 %collective-permute-start.22 = (f32[128,128]{1,0:T(8,128)S(1)}, f32[128,128]{1,0:T(8,128)S(1)}, u32[]{:S(2)}, u32[]{:S(2)}) collective-permute-start(f32[128,128]{1,0:T(8,128)S(1)} %get-tuple-element.93), channel_id=1, source_target_pairs={{0,4},{1,3},{2,6},{3,1},{4,0},{5,7},{6,2},{7,5},{8,12},{9,11},{10,... | collective-permute-start | bytes 196616 | tf_op jit(solution)/shard_map/ppermute | solution.py:199
  108.5 5.2 %collective-permute-start.23 = (f32[128,128]{1,0:T(8,128)S(1)}, f32[128,128]{1,0:T(8,128)S(1)}, u32[]{:S(2)}, u32[]{:S(2)}) collective-permute-start(f32[128,128]{1,0:T(8,128)S(1)} %add.69.refs_4_), channel_id=1, source_target_pairs={{0,8},{1,9},{2,10},{3,11},{4,12},{5,13},{6,14},{7,15},{8,0},{9,1},... | collective-permute-start | bytes 196616 | tf_op jit(solution)/shard_map/ppermute | solution.py:199

commit v13 on v12

--- a/solution.py
+++ b/solution.py
@@ -9,6 +9,7 @@
 
 LANES = 128
 DEPTH_CUTS = 4
+CUT_PARTS = 16
 DEPTH_PART = 1024
 LATE_GATE = 3
 ROW_CUTS = 1
@@ -214,7 +215,7 @@
 def cut_kernel(boxes, source_ref, *refs):
     copies = []
     for index, (rows, columns) in enumerate(boxes):
-        part = (rows[1] - rows[0]) // DEPTH_CUTS
+        part = (rows[1] - rows[0]) // CUT_PARTS
         for low in range(0, rows[1] - rows[0], part):
             source = source_ref.at[rows[0] + low : rows[0] + low + part, columns[0] : columns[1]]
             target = refs[index].at[low : low + part, :]
@@ -233,7 +234,7 @@
         out_shape=[jax.ShapeDtypeStruct((r[1] - r[0], c[1] - c[0]), source.dtype) for r, c in boxes],
         in_specs=[pl.BlockSpec(memory_space=pl.ANY)],
         out_specs=[WHOLE] * len(boxes),
-        scratch_shapes=[pltpu.SemaphoreType.DMA((DEPTH_CUTS * len(boxes),))],
+        scratch_shapes=[pltpu.SemaphoreType.DMA((CUT_PARTS * len(boxes),))],
         compiler_params=pltpu.CompilerParams(vmem_limit_bytes=CUT_BYTES),
         cost_estimate=FREE,
     )(source)

time: 116 us -> 117 us (level)
  no operation moved by 1% of the time
where the time goes in v13:
time: 117 us; the launch traced here: 116 us
  waiting for transfers between devices  40.2 us (34%)
  starting transfers between devices  38.2 us (33%)
  Pallas kernels  31.4 us (27%)
  local copies, waits for them, and re-layouts  5.31 us (5%)
    ppermute x20, starting transfers between devices, flipped_along(): lax.ppermute(value, axis, [(source, source ^ flip[source % 2]) for source...  31.1 us
    ppermute x20, waiting for transfers between devices, flipped_along(): lax.ppermute(value, axis, [(source, source ^ flip[source % 2]) for source...  30.1 us
    pallas_call x3, Pallas kernels, multiplied(): pl.pallas_call(functools.partial(product_kernel, steps, order, splits, ba...  20 us
    ppermute x4, waiting for transfers between devices, passed_along(): return lax.ppermute(value, axis, pairs)  10.1 us
    ppermute x4, starting transfers between devices, passed_along(): return lax.ppermute(value, axis, pairs)  7.19 us
    pallas_call x2, Pallas kernels, cut_out(): pl.pallas_call(functools.partial(cut_kernel, boxes), out_shape=[jax.Shape...  6.33 us
    slice x2, local copies, waits for them, and re-layouts, per_device(): first_part, last_part = (later[:, :late], later[:, late:])  4.99 us
  transfers between devices with their start and end apart: 24, of which 17 were waited for; matrix products, arithmetic and copies ran while one was open for 5% of the time, Pallas kernels for 22%

profile of v13, /device:TPU:0, one launch (start us, length us, event | category | flops | bytes accessed | tf_op | source)
XLA Modules:
  0.0 116.1 jit_solution(10722825052455834764)
XLA Ops:
  0.0 3.1 %shard_map.73 = bf16[4096,256]{1,0:T(8,128)(2,1)} custom-call(bf16[4096,512]{1,0:T(8,128)(2,1)} %refs_1_), custom_call_target="tpu_custom_call" | custom-call | tf_op jit(solution)/shard_map/pallas_call | solution.py:232
  3.1 3.0 %collective-permute-start.8 = (bf16[4096,256]{1,0:T(8,128)(2,1)}, bf16[4096,256]{1,0:T(8,128)(2,1)}, u32[]{:S(2)}, u32[]{:S(2)}) collective-permute-start(bf16[4096,256]{1,0:T(8,128)(2,1)} %shard_map.73), channel_id=1, source_target_pairs={{0,16},{16,0},{1,17},{17,1},{2,18},{18,2},{3,19},{19,3},{4,20},{20... | collective-permute-start | bytes 6291464 | tf_op jit(solution)/shard_map/ppermute | solution.py:30
  6.1 3.2 %shard_map.74 = (bf16[4096,128]{1,0:T(8,128)(2,1)}, bf16[3072,128]{1,0:T(8,128)(2,1)}, bf16[1024,128]{1,0:T(8,128)(2,1)}) custom-call(bf16[4096,512]{1,0:T(8,128)(2,1)} %refs_1_), custom_call_target="tpu_custom_call" | custom-call | tf_op jit(solution)/shard_map/pallas_call | solution.py:232
  9.4 8.3 %shard_map.75 = (f32[512,256]{1,0:T(8,128)S(1)}, f32[512,256]{1,0:T(8,128)S(1)}, f32[512,256]{1,0:T(8,128)S(1)}, f32[512,256]{1,0:T(8,128)S(1)}) custom-call(s32[1]{0:T(128)} %bitcast.6.bit_ref, bf16[1024,4096]{1,0:T(8,128)(2,1)} %refs_0_.5, bf16[4096,512]{1,0:T(8,128)(2,1)} %refs_1_), custom_call_target="tpu_custom_call" | custom-call | tf_op jit(solution)/shard_map/pallas_call | solution.py:109
  17.7 0.5 collective-permute-start.4
  18.2 1.4 %collective-permute-done.came_ref = f32[512,256]{1,0:T(8,128)S(1)} collective-permute-done((f32[512,256]{1,0:T(8,128)S(1)}, f32[512,256]{1,0:T(8,128)S(1)}, u32[]{:S(2)}, u32[]{:S(2)}) %collective-permute-start) | collective-permute-done | bytes 524320 | tf_op jit(solution)/shard_map/ppermute | solution.py:200
  19.7 1.6 %collective-permute-start.1 = (f32[256,256]{1,0:T(8,128)S(1)}, f32[256,256]{1,0:T(8,128)S(1)}, u32[]{:S(2)}, u32[]{:S(2)}) collective-permute-start(f32[256,256]{1,0:T(8,128)S(1)} %get-tuple-element.58), channel_id=1, source_target_pairs={{0,2},{1,5},{2,0},{3,7},{4,6},{5,1},{6,4},{7,3},{8,10},{9,13},{10,... | collective-permute-start | bytes 786440 | tf_op jit(solution)/shard_map/ppermute | solution.py:200
  21.3 0.7 collective-permute-start.5
  22.0 4.1 %collective-permute-done.1.came_ref = f32[256,256]{1,0:T(8,128)S(1)} collective-permute-done((f32[256,256]{1,0:T(8,128)S(1)}, f32[256,256]{1,0:T(8,128)S(1)}, u32[]{:S(2)}, u32[]{:S(2)}) %collective-permute-start.1) | collective-permute-done | bytes 262176 | tf_op jit(solution)/shard_map/ppermute | solution.py:200
  26.2 1.6 %collective-permute-start.2 = (f32[128,256]{1,0:T(8,128)S(1)}, f32[128,256]{1,0:T(8,128)S(1)}, u32[]{:S(2)}, u32[]{:S(2)}) collective-permute-start(f32[128,256]{1,0:T(8,128)S(1)} %get-tuple-element.60), channel_id=1, source_target_pairs={{0,4},{1,3},{2,6},{3,1},{4,0},{5,7},{6,2},{7,5},{8,12},{9,11},{10,... | collective-permute-start | bytes 393224 | tf_op jit(solution)/shard_map/ppermute | solution.py:200
  27.8 1.8 %collective-permute-done.5.came_ref = f32[256,256]{1,0:T(8,128)S(1)} collective-permute-done((f32[256,256]{1,0:T(8,128)S(1)}, f32[256,256]{1,0:T(8,128)S(1)}, u32[]{:S(2)}, u32[]{:S(2)}) %collective-permute-start.5) | collective-permute-done | bytes 262176 | tf_op jit(solution)/shard_map/ppermute | solution.py:200
  29.6 1.6 %collective-permute-start.6 = (f32[128,256]{1,0:T(8,128)S(1)}, f32[128,256]{1,0:T(8,128)S(1)}, u32[]{:S(2)}, u32[]{:S(2)}) collective-permute-start(f32[128,256]{1,0:T(8,128)S(1)} %get-tuple-element.66), channel_id=1, source_target_pairs={{0,4},{1,3},{2,6},{3,1},{4,0},{5,7},{6,2},{7,5},{8,12},{9,11},{10,... | collective-permute-start | bytes 393224 | tf_op jit(solution)/shard_map/ppermute | solution.py:200
  31.3 2.7 %collective-permute-start.3 = (f32[128,256]{1,0:T(8,128)S(1)}, f32[128,256]{1,0:T(8,128)S(1)}, u32[]{:S(2)}, u32[]{:S(2)}) collective-permute-start(f32[128,256]{1,0:T(8,128)S(1)} %add.61), channel_id=1, source_target_pairs={{0,8},{1,9},{2,10},{3,11},{4,12},{5,13},{6,14},{7,15},{8,0},{9,1},... | collective-permute-start | bytes 393224 | tf_op jit(solution)/shard_map/ppermute | solution.py:200
  33.9 2.0 %collective-permute-done.6 = f32[128,256]{1,0:T(8,128)S(1)} collective-permute-done((f32[128,256]{1,0:T(8,128)S(1)}, f32[128,256]{1,0:T(8,128)S(1)}, u32[]{:S(2)}, u32[]{:S(2)}) %collective-permute-start.6) | collective-permute-done | bytes 131104 | tf_op jit(solution)/shard_map/ppermute | solution.py:200
  36.0 2.7 %collective-permute-start.7 = (f32[128,256]{1,0:T(8,128)S(1)}, f32[128,256]{1,0:T(8,128)S(1)}, u32[]{:S(2)}, u32[]{:S(2)}) collective-permute-start(f32[128,256]{1,0:T(8,128)S(1)} %add.63), channel_id=1, source_target_pairs={{0,8},{1,9},{2,10},{3,11},{4,12},{5,13},{6,14},{7,15},{8,0},{9,1},... | collective-permute-start | bytes 393224 | tf_op jit(solution)/shard_map/ppermute | solution.py:200
  38.7 0.5 collective-permute-start.13
  39.2 1.8 %slice.7.a_ref = bf16[1024,1024]{1,0:T(8,128)(2,1)S(1)} slice(bf16[1024,4096]{1,0:T(8,128)(2,1)} %refs_0_.5), slice={[0:1024], [3072:4096]} | slice | bytes 4194304 | tf_op jit(solution)/shard_map/slice | solution.py:327
  41.0 3.2 %slice.6.a_ref = bf16[1024,3072]{1,0:T(8,128)(2,1)S(1)} slice(bf16[1024,4096]{1,0:T(8,128)(2,1)} %refs_0_.5), slice={[0:1024], [0:3072]} | slice | bytes 12582912 | tf_op jit(solution)/shard_map/slice | solution.py:327
  44.3 1.1 collective-permute-done.7
  45.4 7.5 %collective-permute-done.8.refs_1_ = bf16[4096,256]{1,0:T(8,128)(2,1)} collective-permute-done((bf16[4096,256]{1,0:T(8,128)(2,1)}, bf16[4096,256]{1,0:T(8,128)(2,1)}, u32[]{:S(2)}, u32[]{:S(2)}) %collective-permute-start.8) | collective-permute-done | bytes 2097184 | tf_op jit(solution)/shard_map/ppermute | solution.py:30
  52.9 6.1 %shard_map.80 = (f32[512,256]{1,0:T(8,128)S(1)}, f32[512,256]{1,0:T(8,128)S(1)}) custom-call(s32[1]{0:T(128)} %bitcast.6.bit_ref, bf16[1024,4096]{1,0:T(8,128)(2,1)} %refs_0_.5, bf16[4096,256]{1,0:T(8,128)(2,1)} %collective-permute-done.8.refs_1_), custom_call_target="tpu_custom_call" | custom-call | flops 2147483648 | bytes 8388608 | tf_op jit(solution)/shard_map/pallas_call | solution.py:109
  59.1 1.9 %collective-permute-done.9.came_ref = f32[512,256]{1,0:T(8,128)S(1)} collective-permute-done((f32[512,256]{1,0:T(8,128)S(1)}, f32[512,256]{1,0:T(8,128)S(1)}, u32[]{:S(2)}, u32[]{:S(2)}) %collective-permute-start.9) | collective-permute-done | bytes 524320 | tf_op jit(solution)/shard_map/ppermute | solution.py:200
  61.0 2.1 %collective-permute-start.10 = (f32[256,256]{1,0:T(8,128)S(1)}, f32[256,256]{1,0:T(8,128)S(1)}, u32[]{:S(2)}, u32[]{:S(2)}) collective-permute-start(f32[256,256]{1,0:T(8,128)S(1)} %get-tuple-element.72), channel_id=1, source_target_pairs={{0,2},{1,5},{2,0},{3,7},{4,6},{5,1},{6,4},{7,3},{8,10},{9,13},{10,... | collective-permute-start | bytes 786440 | tf_op jit(solution)/shard_map/ppermute | solution.py:200
  63.1 1.5 %collective-permute-start.18 = (bf16[3072,128]{1,0:T(8,128)(2,1)S(1)}, bf16[3072,128]{1,0:T(8,128)(2,1)S(1)}, u32[]{:S(2)}, u32[]{:S(2)}) collective-permute-start(bf16[3072,128]{1,0:T(8,128)(2,1)S(1)} %copy-done.4), channel_id=1, source_target_pairs={{0,16},{16,0},{1,17},{17,1},{2,18},{18,2},{3,19},{19,3},{4,20},{20... | collective-permute-start | bytes 2359304 | tf_op jit(solution)/shard_map/ppermute | solution.py:30
  64.6 2.8 %collective-permute-done.10.came_ref = f32[256,256]{1,0:T(8,128)S(1)} collective-permute-done((f32[256,256]{1,0:T(8,128)S(1)}, f32[256,256]{1,0:T(8,128)S(1)}, u32[]{:S(2)}, u32[]{:S(2)}) %collective-permute-start.10) | collective-permute-done | bytes 262176 | tf_op jit(solution)/shard_map/ppermute | solution.py:200
  67.5 2.2 %collective-permute-start.11 = (f32[128,256]{1,0:T(8,128)S(1)}, f32[128,256]{1,0:T(8,128)S(1)}, u32[]{:S(2)}, u32[]{:S(2)}) collective-permute-start(f32[128,256]{1,0:T(8,128)S(1)} %get-tuple-element.74), channel_id=1, source_target_pairs={{0,4},{1,3},{2,6},{3,1},{4,0},{5,7},{6,2},{7,5},{8,12},{9,11},{10,... | collective-permute-start | bytes 393224 | tf_op jit(solution)/shard_map/ppermute | solution.py:200
  69.7 2.9 %collective-permute-done.11 = f32[128,256]{1,0:T(8,128)S(1)} collective-permute-done((f32[128,256]{1,0:T(8,128)S(1)}, f32[128,256]{1,0:T(8,128)S(1)}, u32[]{:S(2)}, u32[]{:S(2)}) %collective-permute-start.11) | collective-permute-done | bytes 131104 | tf_op jit(solution)/shard_map/ppermute | solution.py:200
  72.6 2.6 %collective-permute-done.13.refs_1_ = bf16[4096,128]{1,0:T(8,128)(2,1)S(1)} collective-permute-done((bf16[4096,128]{1,0:T(8,128)(2,1)}, bf16[4096,128]{1,0:T(8,128)(2,1)S(1)}, u32[]{:S(2)}, u32[]{:S(2)}) %collective-permute-start.13) | collective-permute-done | bytes 1048608 | tf_op jit(solution)/shard_map/ppermute | solution.py:30
  75.3 5.7 %shard_map.83 = (f32[512,128]{1,0:T(8,128)S(1)}, f32[512,128]{1,0:T(8,128)S(1)}) custom-call(s32[1]{0:T(128)} %bitcast.6.bit_ref, bf16[1024,4096]{1,0:T(8,128)(2,1)} %refs_0_.5, bf16[4096,128]{1,0:T(8,128)(2,1)S(1)} %collective-permute-done.13.refs_1_), custom_call_target="tpu_custom_call" | custom-call | flops 1073741824 | bytes 8388608 | tf_op jit(solution)/shard_map/pallas_call | solution.py:109
  81.0 2.1 %collective-permute-start.17 = (bf16[1024,128]{1,0:T(8,128)(2,1)S(1)}, bf16[1024,128]{1,0:T(8,128)(2,1)S(1)}, u32[]{:S(2)}, u32[]{:S(2)}) collective-permute-start(bf16[1024,128]{1,0:T(8,128)(2,1)S(1)} %copy-done.5), channel_id=1, source_target_pairs={{0,16},{16,0},{1,17},{17,1},{2,18},{18,2},{3,19},{19,3},{4,20},{20... | collective-permute-start | bytes 786440 | tf_op jit(solution)/shard_map/ppermute | solution.py:30
  83.2 2.6 %collective-permute-start.12 = (f32[128,256]{1,0:T(8,128)S(1)}, f32[128,256]{1,0:T(8,128)S(1)}, u32[]{:S(2)}, u32[]{:S(2)}) collective-permute-start(f32[128,256]{1,0:T(8,128)S(1)} %add.65), channel_id=1, source_target_pairs={{0,8},{1,9},{2,10},{3,11},{4,12},{5,13},{6,14},{7,15},{8,0},{9,1},... | collective-permute-start | bytes 393224 | tf_op jit(solution)/shard_map/ppermute | solution.py:200
  85.8 1.6 %collective-permute-start.15 = (f32[256,128]{1,0:T(8,128)S(1)}, f32[256,128]{1,0:T(8,128)S(1)}, u32[]{:S(2)}, u32[]{:S(2)}) collective-permute-start(f32[256,128]{1,0:T(8,128)S(1)} %get-tuple-element.79), channel_id=1, source_target_pairs={{0,2},{1,5},{2,0},{3,7},{4,6},{5,1},{6,4},{7,3},{8,10},{9,13},{10,... | collective-permute-start | bytes 393224 | tf_op jit(solution)/shard_map/ppermute | solution.py:200
  87.3 5.1 %collective-permute-done.12 = f32[128,256]{1,0:T(8,128)S(1)} collective-permute-done((f32[128,256]{1,0:T(8,128)S(1)}, f32[128,256]{1,0:T(8,128)S(1)}, u32[]{:S(2)}, u32[]{:S(2)}) %collective-permute-start.12) | collective-permute-done | bytes 131104 | tf_op jit(solution)/shard_map/ppermute | solution.py:200
  92.6 1.8 %collective-permute-start.16 = (f32[128,128]{1,0:T(8,128)S(1)}, f32[128,128]{1,0:T(8,128)S(1)}, u32[]{:S(2)}, u32[]{:S(2)}) collective-permute-start(f32[128,128]{1,0:T(8,128)S(1)} %get-tuple-element.82), channel_id=1, source_target_pairs={{0,4},{1,3},{2,6},{3,1},{4,0},{5,7},{6,2},{7,5},{8,12},{9,11},{10,... | collective-permute-start | bytes 196616 | tf_op jit(solution)/shard_map/ppermute | solution.py:200
  94.4 1.8 %shard_map.86.refs_0_ = f32[1024,128]{1,0:T(8,128)S(1)} custom-call(bf16[1024,3072]{1,0:T(8,128)(2,1)S(1)} %slice.6.a_ref, bf16[3072,128]{1,0:T(8,128)(2,1)S(1)} %collective-permute-done.18.b_ref), custom_call_target="tpu_custom_call" | custom-call | flops 805306368 | bytes 6291456 | tf_op jit(solution)/shard_map/pallas_call | solution.py:168
  96.2 0.7 collective-permute-done.16
  96.9 0.7 shard_map.87
  97.8 0.2 select_reduce_fusion.1
  98.1 1.2 collective-permute-done.19.came_ref
  99.3 1.8 %collective-permute-start.21 = (f32[256,128]{1,0:T(8,128)S(1)}, f32[256,128]{1,0:T(8,128)S(1)}, u32[]{:S(2)}, u32[]{:S(2)}) collective-permute-start(f32[256,128]{1,0:T(8,128)S(1)} %get-tuple-element.91), channel_id=1, source_target_pairs={{0,2},{1,5},{2,0},{3,7},{4,6},{5,1},{6,4},{7,3},{8,10},{9,13},{10,... | collective-permute-start | bytes 393224 | tf_op jit(solution)/shard_map/ppermute | solution.py:200
  101.2 2.6 %collective-permute-start.20 = (f32[128,128]{1,0:T(8,128)S(1)}, f32[128,128]{1,0:T(8,128)S(1)}, u32[]{:S(2)}, u32[]{:S(2)}) collective-permute-start(f32[128,128]{1,0:T(8,128)S(1)} %add.67), channel_id=1, source_target_pairs={{0,8},{1,9},{2,10},{3,11},{4,12},{5,13},{6,14},{7,15},{8,0},{9,1},... | collective-permute-start | bytes 196616 | tf_op jit(solution)/shard_map/ppermute | solution.py:200
  103.8 0.5 collective-permute-done.21.came_ref
  104.4 1.9 %collective-permute-start.22 = (f32[128,128]{1,0:T(8,128)S(1)}, f32[128,128]{1,0:T(8,128)S(1)}, u32[]{:S(2)}, u32[]{:S(2)}) collective-permute-start(f32[128,128]{1,0:T(8,128)S(1)} %get-tuple-element.93), channel_id=1, source_target_pairs={{0,4},{1,3},{2,6},{3,1},{4,0},{5,7},{6,2},{7,5},{8,12},{9,11},{10,... | collective-permute-start | bytes 196616 | tf_op jit(solution)/shard_map/ppermute | solution.py:200
  106.5 1.3 %collective-permute-done.20 = f32[128,128]{1,0:T(8,128)S(1)} collective-permute-done((f32[128,128]{1,0:T(8,128)S(1)}, f32[128,128]{1,0:T(8,128)S(1)}, u32[]{:S(2)}, u32[]{:S(2)}) %collective-permute-start.20) | collective-permute-done | bytes 65568 | tf_op jit(solution)/shard_map/ppermute | solution.py:200
  107.8 0.9 collective-permute-done.22
  108.7 2.9 %collective-permute-start.23 = (f32[128,128]{1,0:T(8,128)S(1)}, f32[128,128]{1,0:T(8,128)S(1)}, u32[]{:S(2)}, u32[]{:S(2)}) collective-permute-start(f32[128,128]{1,0:T(8,128)S(1)} %add.69.refs_4_), channel_id=1, source_target_pairs={{0,8},{1,9},{2,10},{3,11},{4,12},{5,13},{6,14},{7,15},{8,0},{9,1},... | collective-permute-start | bytes 196616 | tf_op jit(solution)/shard_map/ppermute | solution.py:200
  111.6 2.3 %collective-permute-done.23.refs_5_ = f32[128,128]{1,0:T(8,128)S(1)} collective-permute-done((f32[128,128]{1,0:T(8,128)S(1)}, f32[128,128]{1,0:T(8,128)S(1)}, u32[]{:S(2)}, u32[]{:S(2)}) %collective-permute-start.23) | collective-permute-done | bytes 65568 | tf_op jit(solution)/shard_map/ppermute | solution.py:200
  113.9 2.2 %shard_map.90 = f32[64,1024]{1,0:T(8,128)} custom-call(s32[2]{0:T(128)S(1)} %pad_add_fusion.where_ref, s32[64,1]{1,0:T(8,128)S(1)} %copy.11.rows_ref, f32[1,1024]{1,0:T(1,128)S(1)} %add.60.virt_ref, f32[64,1]{1,0:T(8,128)S(1)} %copy.12.occ_ref, f32[128,256]{1,0:T(8,128)S(1)} %add.62.refs_0_, f32[128,256]{1,0:T(8,128)S(1)} %add.64.refs_1_, ...), custom_call_target="tpu_custom_call" | custom-call | tf_op jit(solution)/shard_map/pallas_call | solution.py:272
  (51 shorter events, 1.4 us)
Async XLA Ops:
  3.1 49.8 %collective-permute-start.8 = (bf16[4096,256]{1,0:T(8,128)(2,1)}, bf16[4096,256]{1,0:T(8,128)(2,1)}, u32[]{:S(2)}, u32[]{:S(2)}) collective-permute-start(bf16[4096,256]{1,0:T(8,128)(2,1)} %shard_map.73), channel_id=1, source_target_pairs={{0,16},{16,0},{1,17},{17,1},{2,18},{18,2},{3,19},{19,3},{4,20},{20... | collective-permute-start | bytes 6291464 | tf_op jit(solution)/shard_map/ppermute | solution.py:30
  17.6 2.0 %collective-permute-start = (f32[512,256]{1,0:T(8,128)S(1)}, f32[512,256]{1,0:T(8,128)S(1)}, u32[]{:S(2)}, u32[]{:S(2)}) collective-permute-start(f32[512,256]{1,0:T(8,128)S(1)} %get-tuple-element.56), channel_id=1, source_target_pairs={{0,1},{1,0},{2,3},{3,2},{4,5},{5,4},{6,7},{7,6},{8,9},{9,8},{10,11... | collective-permute-start | bytes 1572872 | tf_op jit(solution)/shard_map/ppermute | solution.py:200
  17.7 3.5 %collective-permute-start.4 = (f32[512,256]{1,0:T(8,128)S(1)}, f32[512,256]{1,0:T(8,128)S(1)}, u32[]{:S(2)}, u32[]{:S(2)}) collective-permute-start(f32[512,256]{1,0:T(8,128)S(1)} %get-tuple-element.62), channel_id=1, source_target_pairs={{0,1},{1,0},{2,3},{3,2},{4,5},{5,4},{6,7},{7,6},{8,9},{9,8},{10,11... | collective-permute-start | bytes 1572872 | tf_op jit(solution)/shard_map/ppermute | solution.py:200
  19.7 6.4 %collective-permute-start.1 = (f32[256,256]{1,0:T(8,128)S(1)}, f32[256,256]{1,0:T(8,128)S(1)}, u32[]{:S(2)}, u32[]{:S(2)}) collective-permute-start(f32[256,256]{1,0:T(8,128)S(1)} %get-tuple-element.58), channel_id=1, source_target_pairs={{0,2},{1,5},{2,0},{3,7},{4,6},{5,1},{6,4},{7,3},{8,10},{9,13},{10,... | collective-permute-start | bytes 786440 | tf_op jit(solution)/shard_map/ppermute | solution.py:200
  21.3 8.3 %collective-permute-start.5 = (f32[256,256]{1,0:T(8,128)S(1)}, f32[256,256]{1,0:T(8,128)S(1)}, u32[]{:S(2)}, u32[]{:S(2)}) collective-permute-start(f32[256,256]{1,0:T(8,128)S(1)} %get-tuple-element.64), channel_id=1, source_target_pairs={{0,2},{1,5},{2,0},{3,7},{4,6},{5,1},{6,4},{7,3},{8,10},{9,13},{10,... | collective-permute-start | bytes 786440 | tf_op jit(solution)/shard_map/ppermute | solution.py:200
  26.2 5.1 %collective-permute-start.2 = (f32[128,256]{1,0:T(8,128)S(1)}, f32[128,256]{1,0:T(8,128)S(1)}, u32[]{:S(2)}, u32[]{:S(2)}) collective-permute-start(f32[128,256]{1,0:T(8,128)S(1)} %get-tuple-element.60), channel_id=1, source_target_pairs={{0,4},{1,3},{2,6},{3,1},{4,0},{5,7},{6,2},{7,5},{8,12},{9,11},{10,... | collective-permute-start | bytes 393224 | tf_op jit(solution)/shard_map/ppermute | solution.py:200
  29.6 6.3 %collective-permute-start.6 = (f32[128,256]{1,0:T(8,128)S(1)}, f32[128,256]{1,0:T(8,128)S(1)}, u32[]{:S(2)}, u32[]{:S(2)}) collective-permute-start(f32[128,256]{1,0:T(8,128)S(1)} %get-tuple-element.66), channel_id=1, source_target_pairs={{0,4},{1,3},{2,6},{3,1},{4,0},{5,7},{6,2},{7,5},{8,12},{9,11},{10,... | collective-permute-start | bytes 393224 | tf_op jit(solution)/shard_map/ppermute | solution.py:200
  31.3 13.0 %collective-permute-start.3 = (f32[128,256]{1,0:T(8,128)S(1)}, f32[128,256]{1,0:T(8,128)S(1)}, u32[]{:S(2)}, u32[]{:S(2)}) collective-permute-start(f32[128,256]{1,0:T(8,128)S(1)} %add.61), channel_id=1, source_target_pairs={{0,8},{1,9},{2,10},{3,11},{4,12},{5,13},{6,14},{7,15},{8,0},{9,1},... | collective-permute-start | bytes 393224 | tf_op jit(solution)/shard_map/ppermute | solution.py:200
  36.0 9.4 %collective-permute-start.7 = (f32[128,256]{1,0:T(8,128)S(1)}, f32[128,256]{1,0:T(8,128)S(1)}, u32[]{:S(2)}, u32[]{:S(2)}) collective-permute-start(f32[128,256]{1,0:T(8,128)S(1)} %add.63), channel_id=1, source_target_pairs={{0,8},{1,9},{2,10},{3,11},{4,12},{5,13},{6,14},{7,15},{8,0},{9,1},... | collective-permute-start | bytes 393224 | tf_op jit(solution)/shard_map/ppermute | solution.py:200
  38.7 36.5 %collective-permute-start.13 = (bf16[4096,128]{1,0:T(8,128)(2,1)}, bf16[4096,128]{1,0:T(8,128)(2,1)S(1)}, u32[]{:S(2)}, u32[]{:S(2)}) collective-permute-start(bf16[4096,128]{1,0:T(8,128)(2,1)} %get-tuple-element.51), channel_id=1, source_target_pairs={{0,16},{16,0},{1,17},{17,1},{2,18},{18,2},{3,19},{19,3},{4,20},{20... | collective-permute-start | bytes 3145736 | tf_op jit(solution)/shard_map/ppermute | solution.py:30
  45.4 17.7 %copy-start.4 = (bf16[3072,128]{1,0:T(8,128)(2,1)S(1)}, bf16[3072,128]{1,0:T(8,128)(2,1)}, u32[]{:S(2)}) copy-start(bf16[3072,128]{1,0:T(8,128)(2,1)} %get-tuple-element.84) | copy-start | bytes 2359300
  59.0 2.0 %collective-permute-start.9 = (f32[512,256]{1,0:T(8,128)S(1)}, f32[512,256]{1,0:T(8,128)S(1)}, u32[]{:S(2)}, u32[]{:S(2)}) collective-permute-start(f32[512,256]{1,0:T(8,128)S(1)} %get-tuple-element.70), channel_id=1, source_target_pairs={{0,1},{1,0},{2,3},{3,2},{4,5},{5,4},{6,7},{7,6},{8,9},{9,8},{10,11... | collective-permute-start | bytes 1572872 | tf_op jit(solution)/shard_map/ppermute | solution.py:200
  61.0 6.4 %collective-permute-start.10 = (f32[256,256]{1,0:T(8,128)S(1)}, f32[256,256]{1,0:T(8,128)S(1)}, u32[]{:S(2)}, u32[]{:S(2)}) collective-permute-start(f32[256,256]{1,0:T(8,128)S(1)} %get-tuple-element.72), channel_id=1, source_target_pairs={{0,2},{1,5},{2,0},{3,7},{4,6},{5,1},{6,4},{7,3},{8,10},{9,13},{10,... | collective-permute-start | bytes 786440 | tf_op jit(solution)/shard_map/ppermute | solution.py:200
  63.1 29.3 %collective-permute-start.18 = (bf16[3072,128]{1,0:T(8,128)(2,1)S(1)}, bf16[3072,128]{1,0:T(8,128)(2,1)S(1)}, u32[]{:S(2)}, u32[]{:S(2)}) collective-permute-start(bf16[3072,128]{1,0:T(8,128)(2,1)S(1)} %copy-done.4), channel_id=1, source_target_pairs={{0,16},{16,0},{1,17},{17,1},{2,18},{18,2},{3,19},{19,3},{4,20},{20... | collective-permute-start | bytes 2359304 | tf_op jit(solution)/shard_map/ppermute | solution.py:30
  67.5 5.1 %collective-permute-start.11 = (f32[128,256]{1,0:T(8,128)S(1)}, f32[128,256]{1,0:T(8,128)S(1)}, u32[]{:S(2)}, u32[]{:S(2)}) collective-permute-start(f32[128,256]{1,0:T(8,128)S(1)} %get-tuple-element.74), channel_id=1, source_target_pairs={{0,4},{1,3},{2,6},{3,1},{4,0},{5,7},{6,2},{7,5},{8,12},{9,11},{10,... | collective-permute-start | bytes 393224 | tf_op jit(solution)/shard_map/ppermute | solution.py:200
  72.6 8.4 %copy-start.5 = (bf16[1024,128]{1,0:T(8,128)(2,1)S(1)}, bf16[1024,128]{1,0:T(8,128)(2,1)}, u32[]{:S(2)}) copy-start(bf16[1024,128]{1,0:T(8,128)(2,1)} %get-tuple-element.83) | copy-start | bytes 786436
  80.9 4.8 %collective-permute-start.14 = (f32[512,128]{1,0:T(8,128)S(1)}, f32[512,128]{1,0:T(8,128)S(1)}, u32[]{:S(2)}, u32[]{:S(2)}) collective-permute-start(f32[512,128]{1,0:T(8,128)S(1)} %get-tuple-element.77), channel_id=1, source_target_pairs={{0,1},{1,0},{2,3},{3,2},{4,5},{5,4},{6,7},{7,6},{8,9},{9,8},{10,11... | collective-permute-start | bytes 786440 | tf_op jit(solution)/shard_map/ppermute | solution.py:200
  81.0 15.9 %collective-permute-start.17 = (bf16[1024,128]{1,0:T(8,128)(2,1)S(1)}, bf16[1024,128]{1,0:T(8,128)(2,1)S(1)}, u32[]{:S(2)}, u32[]{:S(2)}) collective-permute-start(bf16[1024,128]{1,0:T(8,128)(2,1)S(1)} %copy-done.5), channel_id=1, source_target_pairs={{0,16},{16,0},{1,17},{17,1},{2,18},{18,2},{3,19},{19,3},{4,20},{20... | collective-permute-start | bytes 786440 | tf_op jit(solution)/shard_map/ppermute | solution.py:30
  83.2 9.3 %collective-permute-start.12 = (f32[128,256]{1,0:T(8,128)S(1)}, f32[128,256]{1,0:T(8,128)S(1)}, u32[]{:S(2)}, u32[]{:S(2)}) collective-permute-start(f32[128,256]{1,0:T(8,128)S(1)} %add.65), channel_id=1, source_target_pairs={{0,8},{1,9},{2,10},{3,11},{4,12},{5,13},{6,14},{7,15},{8,0},{9,1},... | collective-permute-start | bytes 393224 | tf_op jit(solution)/shard_map/ppermute | solution.py:200
  85.8 6.7 %collective-permute-start.15 = (f32[256,128]{1,0:T(8,128)S(1)}, f32[256,128]{1,0:T(8,128)S(1)}, u32[]{:S(2)}, u32[]{:S(2)}) collective-permute-start(f32[256,128]{1,0:T(8,128)S(1)} %get-tuple-element.79), channel_id=1, source_target_pairs={{0,2},{1,5},{2,0},{3,7},{4,6},{5,1},{6,4},{7,3},{8,10},{9,13},{10,... | collective-permute-start | bytes 393224 | tf_op jit(solution)/shard_map/ppermute | solution.py:200
  92.5 5.3 %copy-start = (f32[512]{0:T(512)S(1)}, f32[512]{0:T(512)}, u32[]{:S(2)}) copy-start(f32[512]{0:T(512)} %param.13) | copy-start | bytes 6148
  92.5 5.2 %copy-start.2 = (s32[32]{0:T(128)S(1)}, s32[32]{0:T(128)}, u32[]{:S(2)}) copy-start(s32[32]{0:T(128)} %param.11) | copy-start | bytes 388
  92.5 8.6 %copy-start.6 = (s32[64]{0:T(128)S(1)}, s32[64]{0:T(128)}, u32[]{:S(2)}) copy-start(s32[64]{0:T(128)} %param.10) | copy-start | bytes 772
  92.5 13.7 %copy-start.1 = (s32[64,2]{0,1:T(2,128)S(1)}, s32[64,2]{0,1:T(2,128)}, u32[]{:S(2)}) copy-start(s32[64,2]{0,1:T(2,128)} %param.9) | copy-start | bytes 1540
  92.5 13.7 %copy-start.3 = (f32[96]{0:T(128)S(1)}, f32[96]{0:T(128)}, u32[]{:S(2)}) copy-start(f32[96]{0:T(128)} %param.12) | copy-start | bytes 1156
  92.6 4.3 %collective-permute-start.16 = (f32[128,128]{1,0:T(8,128)S(1)}, f32[128,128]{1,0:T(8,128)S(1)}, u32[]{:S(2)}, u32[]{:S(2)}) collective-permute-start(f32[128,128]{1,0:T(8,128)S(1)} %get-tuple-element.82), channel_id=1, source_target_pairs={{0,4},{1,3},{2,6},{3,1},{4,0},{5,7},{6,2},{7,5},{8,12},{9,11},{10,... | collective-permute-start | bytes 196616 | tf_op jit(solution)/shard_map/ppermute | solution.py:200
  97.7 1.6 %collective-permute-start.19 = (f32[512,128]{1,0:T(8,128)S(1)}, f32[512,128]{1,0:T(8,128)S(1)}, u32[]{:S(2)}, u32[]{:S(2)}) collective-permute-start(f32[512,128]{1,0:T(8,128)S(1)} %get-tuple-element.88), channel_id=1, source_target_pairs={{0,1},{1,0},{2,3},{3,2},{4,5},{5,4},{6,7},{7,6},{8,9},{9,8},{10,11... | collective-permute-start | bytes 786440 | tf_op jit(solution)/shard_map/ppermute | solution.py:200
  99.3 5.0 %collective-permute-start.21 = (f32[256,128]{1,0:T(8,128)S(1)}, f32[256,128]{1,0:T(8,128)S(1)}, u32[]{:S(2)}, u32[]{:S(2)}) collective-permute-start(f32[256,128]{1,0:T(8,128)S(1)} %get-tuple-element.91), channel_id=1, source_target_pairs={{0,2},{1,5},{2,0},{3,7},{4,6},{5,1},{6,4},{7,3},{8,10},{9,13},{10,... | collective-permute-start | bytes 393224 | tf_op jit(solution)/shard_map/ppermute | solution.py:200
  101.2 6.6 %collective-permute-start.20 = (f32[128,128]{1,0:T(8,128)S(1)}, f32[128,128]{1,0:T(8,128)S(1)}, u32[]{:S(2)}, u32[]{:S(2)}) collective-permute-start(f32[128,128]{1,0:T(8,128)S(1)} %add.67), channel_id=1, source_target_pairs={{0,8},{1,9},{2,10},{3,11},{4,12},{5,13},{6,14},{7,15},{8,0},{9,1},... | collective-permute-start | bytes 196616 | tf_op jit(solution)/shard_map/ppermute | solution.py:200
  104.4 4.3 %collective-permute-start.22 = (f32[128,128]{1,0:T(8,128)S(1)}, f32[128,128]{1,0:T(8,128)S(1)}, u32[]{:S(2)}, u32[]{:S(2)}) collective-permute-start(f32[128,128]{1,0:T(8,128)S(1)} %get-tuple-element.93), channel_id=1, source_target_pairs={{0,4},{1,3},{2,6},{3,1},{4,0},{5,7},{6,2},{7,5},{8,12},{9,11},{10,... | collective-permute-start | bytes 196616 | tf_op jit(solution)/shard_map/ppermute | solution.py:200
  108.7 5.2 %collective-permute-start.23 = (f32[128,128]{1,0:T(8,128)S(1)}, f32[128,128]{1,0:T(8,128)S(1)}, u32[]{:S(2)}, u32[]{:S(2)}) collective-permute-start(f32[128,128]{1,0:T(8,128)S(1)} %add.69.refs_4_), channel_id=1, source_target_pairs={{0,8},{1,9},{2,10},{3,11},{4,12},{5,13},{6,14},{7,15},{8,0},{9,1},... | collective-permute-start | bytes 196616 | tf_op jit(solution)/shard_map/ppermute | solution.py:200
